TPU v7x, 32 devices: a whole 2x2x4 slice. The times are simulated.
32 devices in a mesh: grp: 2 (over y), pair: 4 (over z), orb: 4 (over x, core).
Axes of the slice: x: 2, y: 2, z: 4, core: 2. Of those that a mesh axis runs over, the one named last changes fastest.
Arguments:
- integrals: bfloat16 [64, 8, 4096], P(('grp', 'pair', 'orb')), parts along dimension 0, may hold values from -6 to 6
- mu_block: int32 [64], P(('grp', 'pair', 'orb')), parts along dimension 0, may hold values from 0 to 31, as said below
- nu_block: int32 [64], P(('grp', 'pair', 'orb')), parts along dimension 0, may hold values from 0 to 31
- counts: int32 [32], P(('grp', 'pair', 'orb')), parts along dimension 0, may hold values from 1 to 2
- coeff: bfloat16 [4096, 512], P(('grp', 'pair', 'orb')), parts along dimension 0, may hold values from -0.125 to 0.125
Outputs:
- transformed: float32 [1024, 8, 512], P(('grp', 'orb'), 'pair'), parts along dimension 0
There are 2 independent parts, one for each index of `grp`. A program takes and returns all parts, laid end to end along the dimension named above; each array names one. Nothing has to cross between parts.
Inputs may be any that keep to these rules, and one draw needn't show every extreme that they name: mu_block and nu_block together name distinct pairs of shell blocks. `counts`: slots of a device beyond its count hold arbitrary values, which must be ignored.
All inputs are finite; a program needn't handle non-finite values.
Results may differ from a plain program's by a relative error of at most 0.0029.
Values may be sent and summed in bfloat16 or wider, within the bound.
No kernel may reach another device: no remote copies, remote signals or barrier semaphores. Data moves between devices by JAX's collectives and lax.ppermute only.
A program may use at most 64 MiB of HBM per device.

v0:
```python
import jax
import jax.numpy as jnp
from jax import lax
from jax.sharding import PartitionSpec as P

SB = 64


def second_quarter(tiles, nu_ids, coeff_blocks):
    count = tiles.shape[0]
    square = tiles.reshape(count, tiles.shape[1], SB, SB)
    rows = coeff_blocks[nu_ids]
    half = jnp.einsum("rkmn,rni->rmki", square, rows, preferred_element_type=jnp.float32)
    return half.astype(jnp.bfloat16)


def body(integrals, mu_block, nu_block, counts, coeff):
    slots_dev = integrals.shape[0]
    coeff_full = lax.all_gather(coeff, ("pair", "orb"), axis=0, tiled=True)
    orbitals = coeff_full.shape[1]
    shells = coeff_full.shape[0] // SB
    coeff_blocks = coeff_full.reshape(shells, SB, orbitals)
    keep = (jnp.arange(slots_dev, dtype=jnp.int32) < counts[0]).astype(jnp.bfloat16)
    masked = integrals * keep[:, None, None]
    mu_all, nu_all = (
        lax.all_gather(mu_block, "pair", axis=0, tiled=True),
        lax.all_gather(nu_block, "pair", axis=0, tiled=True),
    )
    arrived = lax.all_to_all(masked, "pair", split_axis=1, concat_axis=0, tiled=True)
    moved = second_quarter(arrived, nu_all, coeff_blocks)
    received = moved.shape[0]
    columns = moved.shape[2]
    rows_a = coeff_blocks[mu_all].reshape(received * SB, orbitals)
    flat = moved.reshape(received * SB, columns, orbitals)
    return lax.psum_scatter(
        jnp.einsum("ra,rki->aki", rows_a, flat, preferred_element_type=jnp.float32),
        "orb",
        scatter_dimension=0,
        tiled=True,
    )


def solution(mesh):
    placed = (
        P(("grp", "pair", "orb"), None, None),
        P(("grp", "pair", "orb")),
        P(("grp", "pair", "orb")),
        P(("grp", "pair", "orb")),
        P(("grp", "pair", "orb"), None),
    )
    return jax.shard_map(
        body, mesh=mesh, in_specs=placed, out_specs=P(("grp", "orb"), "pair", None), check_vma=False
    )
```

profile of v0, /device:TPU:0, one launch (start us, length us, event | category | flops | bytes accessed | tf_op | source)
XLA Modules:
  0.0 100.8 jit_solution(13691886423708310397)
XLA Ops:
  6.5 0.0 all-gather.2.cloned.1.call-start
  6.5 0.7 all-gather.2.cloned.1.call-update
  7.9 1.2 %dynamic-slice = u32[1]{0:T(128)} dynamic-slice(u32[32]{0:T(128)} %constant.10, u32[]{:T(128)S(6)} %add.10), dynamic_slice_sizes={1} | dynamic-slice | bytes 12
  9.8 0.9 dynamic-update-slice
  10.7 0.8 dynamic-update-slice.1
  11.5 1.7 %copy_multiply_fusion = bf16[2,8,4096]{2,0,1:T(2,128)(2,1)} fusion(bf16[2,8,4096]{2,1,0:T(8,128)(2,1)} %param.5, bf16[2]{0:T(256)(128)(2,1)S(1)} %compare_convert_fusion), kind=kLoop, calls=%fused_computation.9 | loop fusion | flops 65536 | bytes 262148 | tf_op jit(solution)/shard_map/mul | solution.py:24
  13.2 6.3 %all-to-all-start = ((bf16[2,8,4096]{2,0,1:T(2,128)(2,1)}), bf16[2,8,4096]{2,0,1:T(2,128)(2,1)S(1)}, u32[]{:S(2)}, u32[]{:S(2)}) async-start(bf16[2,8,4096]{2,0,1:T(2,128)(2,1)} %copy_multiply_fusion), calls=%async_computation | async-start | bytes 262144 | tf_op jit(solution)/shard_map/all_to_all | solution.py:29
  19.6 0.0 reduce-scatter.2.cloned.1.call-start
  19.6 10.0 %all-reduce.2 = (s32[8]{0:T(128)S(1)}, s32[8]{0:T(128)S(1)}) all-reduce(s32[8]{0:T(128)S(1)} %dynamic-update-slice.1, s32[8]{0:T(128)S(1)} %dynamic-update-slice), channel_id=1, replica_groups=mesh['grp'=2,'pair'=4,'orb'=4] {'pair'}, use_global_device_ids=true, to_apply=%add.1 | all-reduce | flops 16 | bytes 128
  29.6 0.0 all-to-all-done
  29.6 0.1 copy.19
  29.7 0.2 reshape.15
  30.0 24.7 %all-gather.2.cloned.1.call-done = bf16[2048,512]{1,0:T(8,128)(2,1)} async-done(((bf16[128,512]{1,0:T(8,128)(2,1)}), bf16[2048,512]{1,0:T(8,128)(2,1)}) %all-gather.2.cloned.1.call-update) | async-done | bytes 2097168 | tf_op jit(solution)/shard_map/all_gather | solution.py:19
  54.7 2.2 %gather_fusion = bf16[8,64,512]{2,1,0:T(8,128)(2,1)S(1)} fusion(bf16[32,64,512]{2,1,0:T(8,128)(2,1)} %bitcast.24, s32[1024]{0:T(1024)S(1)} %pad_clamp_fusion.1), kind=kCustom, calls=%fused_computation | custom fusion | bytes 1048608 | tf_op jit(solution)/shard_map/gather | solution.py:33
  56.9 2.2 %gather_fusion.1 = bf16[8,64,512]{2,1,0:T(8,128)(2,1)S(1)} fusion(bf16[32,64,512]{2,1,0:T(8,128)(2,1)} %bitcast.25, s32[1024]{0:T(1024)S(1)} %pad_clamp_fusion), kind=kCustom, calls=%fused_computation.1 | custom fusion | bytes 1048608 | tf_op jit(solution)/shard_map/gather | solution.py:12
  59.0 2.3 %convolution_bitcast_fusion = f32[512,2,512]{2,0,1:T(8,128)} fusion(bf16[8,64,512]{2,1,0:T(8,128)(2,1)S(1)} %gather_fusion.1, bf16[8,64,512]{2,1,0:T(8,128)(2,1)S(1)} %gather_fusion, bf16[8,2,64,64]{3,2,1,0:T(8,128)(2,1)S(1)} %reshape.15), kind=kOutput, calls=%fused_computation.2 | convolution fusion | flops 604504064 | bytes 3276800 | tf_op jit(solution)/shard_map/ra,rki->aki/dot_general | solution.py:36
  61.3 0.0 reduce-scatter.2.cloned.1.call-update
  61.4 30.4 %reduce-scatter.2.cloned.1.call-done = f32[128,2,512]{2,0,1:T(8,128)} async-done(((f32[512,2,512]{2,0,1:T(8,128)}), f32[128,2,512]{2,0,1:T(8,128)}) %reduce-scatter.2.cloned.1.call-update) | async-done | bytes 524304 | tf_op jit(solution)/shard_map/reduce_scatter | solution.py:35
  91.7 2.2 %copy.12 = f32[128,2,512]{2,1,0:T(2,128)} copy(f32[128,2,512]{2,0,1:T(8,128)} %reduce-scatter.2.cloned.1.call-done) | data formatting | bytes 1048576 | tf_op jit(solution)/shard_map/reduce_scatter | solution.py:35
  (6 shorter events, 0.0 us)
Async XLA Ops:
  6.5 48.2 %all-gather.2.cloned.1.call-start = ((), (), s32[]{:S(2)}) async-start(), calls=%async_computation.2 | async-start | bytes 2228224 | tf_op jit(solution)/shard_map/all_gather | solution.py:19
  13.2 16.3 %all-to-all-start = ((bf16[2,8,4096]{2,0,1:T(2,128)(2,1)}), bf16[2,8,4096]{2,0,1:T(2,128)(2,1)S(1)}, u32[]{:S(2)}, u32[]{:S(2)}) async-start(bf16[2,8,4096]{2,0,1:T(2,128)(2,1)} %copy_multiply_fusion), calls=%async_computation | async-start | bytes 262144 | tf_op jit(solution)/shard_map/all_to_all | solution.py:29
  19.6 72.2 %reduce-scatter.2.cloned.1.call-start = ((), (), s32[]{:S(2)}) async-start(), calls=%async_computation.3 | async-start | bytes 2621440 | tf_op jit(solution)/shard_map/reduce_scatter | solution.py:35
Sparse Core Ops, SparseCore 0:
  9.5 45.1 all-gather.1
  61.5 30.2 reduce-scatter.1
where the time goes:
time: 101 us
  waiting for transfers between devices  55.8 us (55%)
  between operations  14.7 us (15%)
  blocking collectives  10 us (10%)
  local copies, waits for them, and re-layouts  9.87 us (10%)
  starting transfers between devices  6.32 us (6%)
  matrix products  2.29 us (2%)
  other arithmetic  1.76 us (2%)
    reduce_scatter x1, waiting for transfers between devices, body(): lax.psum_scatter(jnp.einsum('ra,rki->aki', rows_a, flat, preferred_elemen...  30.4 us
    all_gather x1, waiting for transfers between devices, body(): coeff_full = lax.all_gather(coeff, ('pair', 'orb'), axis=0, tiled=True)  24.7 us
    unnamed x1, blocking collectives  10 us
    all_to_all x1, starting transfers between devices, body(): lax.all_to_all(masked, 'pair', split_axis=1, concat_axis=0, tiled=True)  6.32 us
    unnamed x5, local copies, waits for them, and re-layouts  2.94 us
    dot_general x1, matrix products, body(): jnp.einsum('ra,rki->aki', rows_a, flat, preferred_element_type=jnp.float32)  2.29 us
    reduce_scatter x1, local copies, waits for them, and re-layouts, body(): lax.psum_scatter(jnp.einsum('ra,rki->aki', rows_a, flat, preferred_elemen...  2.24 us
    gather x1, local copies, waits for them, and re-layouts, second_quarter(): rows = coeff_blocks[nu_ids]  2.17 us
  transfers between devices with their start and end apart: 3, of which 2 were waited for; matrix products, arithmetic and copies ran while one was open for 5% of the time, Pallas kernels for 0%

commit v1 on v0

v1 whole, which is shorter than its diff:
```python
import functools

import jax
import jax.numpy as jnp
from jax import lax
from jax.experimental import pallas as pl
from jax.experimental.pallas import tpu as pltpu
from jax.sharding import PartitionSpec as P

SB = 64
LANES = 128
CHUNK = 16


def transform_kernel(c_rows, x_devs, n_c, n_x, *refs):
    where, mu, nu, keep = refs[:4]
    c_in, x_in = refs[4 : 4 + n_c], refs[4 + n_c : 4 + n_c + n_x]
    out, c_all, x_all, half, left, sems = refs[4 + n_c + n_x :]
    copies = []
    for q, piece in enumerate(c_in):
        rows = pl.ds(pl.multiple_of(where[q] * c_rows, c_rows), c_rows)
        copies.append(pltpu.make_async_copy(piece, c_all.at[rows], sems.at[q]))
    for q, piece in enumerate(x_in):
        place = pl.ds(where[n_c + q] * x_devs, x_devs)
        copies.append(pltpu.make_async_copy(piece, x_all.at[place], sems.at[n_c + q]))
    for copy in copies:
        copy.start()
    for copy in copies:
        copy.wait()

    mine = pl.ds(pl.multiple_of(where[n_c + n_x] * LANES, LANES), LANES)
    lane = lax.broadcasted_iota(jnp.int32, (2 * SB, LANES), 1)
    devices = x_all.shape[0]
    chunks = devices // CHUNK

    def rows_of(block):
        return pl.ds(pl.multiple_of(block * SB, SB), SB)

    def chunk_step(chunk, carry):
        for d in range(CHUNK):
            device = chunk * CHUNK + d
            first, second = 2 * device, 2 * device + 1
            tile = x_all[device]
            one = jnp.where(lane < SB * keep[first], tile, jnp.zeros_like(tile))
            two = jnp.where(lane >= LANES - SB * keep[second], tile, jnp.zeros_like(tile))
            one = jnp.where(lane < SB, one, jnp.zeros_like(tile))
            two = jnp.where(lane >= SB, two, jnp.zeros_like(tile))
            rows = jnp.concatenate([c_all[rows_of(nu[first])], c_all[rows_of(nu[second])]], 0)
            stacked = jnp.concatenate([one[:SB], two[:SB], one[SB:], two[SB:]], 0)
            moved = jnp.dot(stacked, rows, preferred_element_type=jnp.float32)
            moved = moved.astype(jnp.bfloat16)
            at = pl.ds(d * 2 * SB, 2 * SB)
            half[0, at] = moved[: 2 * SB]
            half[1, at] = moved[2 * SB :]
            left[at, :] = jnp.concatenate([c_all[rows_of(mu[first]), mine], c_all[rows_of(mu[second]), mine]], 0)
        for k in range(2):
            part = lax.dot_general(
                left[...], half[k], (((0,), (0,)), ((), ())), preferred_element_type=jnp.float32
            )
            for j in range(part.shape[1] // LANES):
                at = pl.ds(2 * j + k, part.shape[0], stride=2 * (part.shape[1] // LANES))
                value = part[:, j * LANES : (j + 1) * LANES]
                if chunks == 1:
                    out[at, :] = value
                else:
                    out[at, :] = jnp.where(chunk == 0, value, value + out[at, :])
        return carry

    if chunks == 1:
        chunk_step(0, 0)
    else:
        out[...] = jnp.zeros_like(out)
        lax.fori_loop(0, chunks, chunk_step, 0)


def transform(c_pieces, c_at, x_pieces, x_at, mine, mu, nu, keep):
    c_rows, orbitals = c_pieces[0].shape
    x_devs = x_pieces[0].shape[0]
    n_c, n_x = len(c_pieces), len(x_pieces)
    devices = x_devs * n_x
    where = jnp.stack(c_at + x_at + [mine]).astype(jnp.int32)
    smem = pl.BlockSpec(memory_space=pltpu.SMEM)
    hbm = pl.BlockSpec(memory_space=pl.ANY)
    wide = CHUNK * 2 * SB
    out = pl.pallas_call(
        functools.partial(transform_kernel, c_rows, x_devs, n_c, n_x),
        out_shape=jax.ShapeDtypeStruct((2 * orbitals // 4 // LANES * orbitals, LANES), jnp.float32),
        in_specs=[smem] * 4 + [hbm] * (n_c + n_x),
        out_specs=pl.BlockSpec(memory_space=pltpu.VMEM),
        scratch_shapes=[
            pltpu.VMEM((c_rows * n_c, orbitals), jnp.bfloat16),
            pltpu.VMEM((devices, LANES, LANES), jnp.bfloat16),
            pltpu.VMEM((2, wide, orbitals), jnp.bfloat16),
            pltpu.VMEM((wide, LANES), jnp.bfloat16),
            pltpu.SemaphoreType.DMA((n_c + n_x,)),
        ],
        compiler_params=pltpu.CompilerParams(vmem_limit_bytes=40 << 20),
        name="transform",
    )(where, mu, nu, keep, *c_pieces, *x_pieces)
    return out


def shift(array, axis, size, step):
    return lax.ppermute(array, axis, [(i, (i + step) % size) for i in range(size)])


def flip(array, axis, size, bit):
    return lax.ppermute(array, axis, [(i, i ^ bit) for i in range(size)])


def body(n_pair, n_orb, integrals, mu_block, nu_block, counts, coeff):
    p, o = lax.axis_index("pair"), lax.axis_index("orb")
    slots = integrals.shape[0]
    columns = integrals.shape[1] // n_pair
    everyone = ("pair", "orb")

    tiles = integrals.reshape(slots, n_pair, columns, SB, SB).transpose(1, 2, 3, 0, 4)
    tiles = tiles.reshape(n_pair, columns * SB, slots * SB)
    kept = (jnp.arange(slots, dtype=jnp.int32) < counts[0]).astype(jnp.int32)
    index = jnp.stack([jnp.where(kept > 0, mu_block, 0), jnp.where(kept > 0, nu_block, 0), kept])
    index = index.reshape(1, 3 * slots)

    arrived = None
    if n_pair * n_orb <= 16:
        lines = [coeff] + [shift(coeff, "pair", n_pair, s) for s in range(1, n_pair)]
        c_pieces, c_at = [], []
        for s, line in enumerate(lines):
            source = (p - s) % n_pair
            across = flip(line, "orb", n_orb, 2)
            for far, piece in ((0, line), (2, across)):
                c_pieces += [piece, flip(piece, "orb", n_orb, 1)]
                c_at += [source * n_orb + (o ^ far), source * n_orb + (o ^ far ^ 1)]
        line = lax.all_to_all(tiles, "pair", split_axis=0, concat_axis=0, tiled=True)
        across = flip(line, "orb", n_orb, 2)
        x_pieces = [line, flip(line, "orb", n_orb, 1), across, flip(across, "orb", n_orb, 1)]
        x_at = [o, o ^ 1, o ^ 2, o ^ 3]
        spread = jnp.broadcast_to(index, (n_pair * n_orb, 3 * slots))
        table = lax.all_to_all(spread, everyone, split_axis=0, concat_axis=0, tiled=True)
    else:
        c_pieces, c_at = [lax.all_gather(coeff, everyone, axis=0, tiled=True)], [p * 0]
        line = lax.all_to_all(tiles, "pair", split_axis=0, concat_axis=0, tiled=True)
        whole = lax.all_gather(line, "orb", axis=0, tiled=True)
        x_pieces, x_at = [whole], [p * 0]
        table = lax.all_gather(index, everyone, axis=0, tiled=True)
    table = table.reshape(n_pair, n_orb, 3, slots).transpose(2, 1, 0, 3).reshape(3, -1)
    out = transform(c_pieces, c_at, x_pieces, x_at, o, table[0], table[1], table[2])
    orbitals = coeff.shape[1]
    out = out.reshape(orbitals // n_orb, orbitals // LANES, columns, LANES)
    return out.transpose(0, 2, 1, 3).reshape(orbitals // n_orb, columns, orbitals)


def solution(mesh):
    placed = (
        P(("grp", "pair", "orb"), None, None),
        P(("grp", "pair", "orb")),
        P(("grp", "pair", "orb")),
        P(("grp", "pair", "orb")),
        P(("grp", "pair", "orb"), None),
    )
    return jax.shard_map(
        functools.partial(body, mesh.shape["pair"], mesh.shape["orb"]),
        mesh=mesh,
        in_specs=placed,
        out_specs=P(("grp", "orb"), "pair", None),
        check_vma=False,
    )
```

time: 101 us -> 48.9 us (0.48)
  waiting for transfers between devices: 55.8 us -> 12.5 us
  starting transfers between devices: 6.32 us -> 23.9 us
  between operations: 14.7 us -> 0.86 us
  blocking collectives: 10 us -> 0 us
  Pallas kernels: 0 us -> 7.47 us
  local copies, waits for them, and re-layouts: 9.87 us -> 3.85 us
  matrix products: 2.29 us -> 0 us
  other arithmetic: 1.76 us -> 0.02 us
    reduce_scatter x1 -> x0, waiting for transfers between devices: 30.4 us -> none  [body(): lax.psum_scatter(jnp.einsum('ra,rki->aki', rows_a, flat, preferred_elemen...]
    all_gather x1 -> x0, waiting for transfers between devices: 24.7 us -> none  [body(): coeff_full = lax.all_gather(coeff, ('pair', 'orb'), axis=0, tiled=True)]
    ppermute x0 -> x18, starting transfers between devices: none -> 14.4 us  [the longest x3 7.86 us: shift(): lax.ppermute(array, axis, [(i, (i + step) % size) for i in range(size)])]
    unnamed x1 -> x0, blocking collectives: 10 us -> none
    pallas_call x0 -> x1, Pallas kernels: none -> 7.47 us  [transform(): pl.pallas_call(functools.partial(transform_kernel, c_rows, x_devs, n_c, n...]
    ppermute x0 -> x18, waiting for transfers between devices: none -> 6.38 us  [the longest x15 6.37 us: flip(): return lax.ppermute(array, axis, [(i, i ^ bit) for i in range(size)])]
    all_to_all x1 -> x2, waiting for transfers between devices: 0.01 us -> 6.15 us  [the longest x1 6.14 us: body(): lax.all_to_all(spread, everyone, split_axis=0, concat_axis=0, tiled=True)]
    gather x2 -> x0, local copies, waits for them, and re-layouts: 4.34 us -> none  [the longest x1 2.17 us: second_quarter(): rows = coeff_blocks[nu_ids]]
  transfers between devices with their start and end apart: 3 -> 20, of which waited for: 2 -> 6; matrix products, arithmetic and copies ran while one was open for 5% -> 8% of each run, Pallas kernels for 0% -> 0%
where the time goes in v1:
time: 48.9 us; the launch traced here: 48.6 us
  starting transfers between devices  23.9 us (49%)
  waiting for transfers between devices  12.5 us (26%)
  Pallas kernels  7.47 us (15%)
  local copies, waits for them, and re-layouts  3.85 us (8%)
  between operations  0.86 us (2%)
    ppermute x3, starting transfers between devices, shift(): lax.ppermute(array, axis, [(i, (i + step) % size) for i in range(size)])  7.86 us
    pallas_call x1, Pallas kernels, transform(): pl.pallas_call(functools.partial(transform_kernel, c_rows, x_devs, n_c, n...  7.47 us
    ppermute x15, starting transfers between devices, flip(): return lax.ppermute(array, axis, [(i, i ^ bit) for i in range(size)])  6.58 us
    ppermute x15, waiting for transfers between devices, flip(): return lax.ppermute(array, axis, [(i, i ^ bit) for i in range(size)])  6.37 us
    all_to_all x1, waiting for transfers between devices, body(): lax.all_to_all(spread, everyone, split_axis=0, concat_axis=0, tiled=True)  6.14 us
    all_to_all x1, starting transfers between devices, body(): lax.all_to_all(spread, everyone, split_axis=0, concat_axis=0, tiled=True)  6.14 us
    all_to_all x1, starting transfers between devices, body(): lax.all_to_all(tiles, 'pair', split_axis=0, concat_axis=0, tiled=True)  3.33 us
    reshape x2, local copies, waits for them, and re-layouts, body(): integrals.reshape(slots, n_pair, columns, SB, SB).transpose(1, 2, 3, 0, 4)  1.45 us
  transfers between devices with their start and end apart: 20, of which 6 were waited for; matrix products, arithmetic and copies ran while one was open for 8% of the time, Pallas kernels for 0%

profile of v1, /device:TPU:0, one launch (start us, length us, event | category | flops | bytes accessed | tf_op | source)
XLA Modules:
  0.0 48.6 jit_solution(5430460116009438341)
XLA Ops:
  0.0 4.0 %collective-permute-start.7 = (bf16[128,512]{1,0:T(8,128)(2,1)}, bf16[128,512]{1,0:T(8,128)(2,1)S(1)}, u32[]{:S(2)}, u32[]{:S(2)}) collective-permute-start(bf16[128,512]{1,0:T(8,128)(2,1)} %refs_4_.1), channel_id=1, source_target_pairs={{0,8},{4,12},{8,0},{12,4},{1,9},{5,13},{9,1},{13,5},{2,10},{6,14},... | collective-permute-start | bytes 393224 | tf_op jit(solution)/shard_map/ppermute | solution.py:104
  4.0 1.6 %collective-permute-start.3 = (bf16[128,512]{1,0:T(8,128)(2,1)}, bf16[128,512]{1,0:T(8,128)(2,1)S(1)}, u32[]{:S(2)}, u32[]{:S(2)}) collective-permute-start(bf16[128,512]{1,0:T(8,128)(2,1)} %refs_4_.1), channel_id=1, source_target_pairs={{0,4},{4,8},{8,12},{12,0},{1,5},{5,9},{9,13},{13,1},{2,6},{6,10},{... | collective-permute-start | bytes 393224 | tf_op jit(solution)/shard_map/ppermute | solution.py:104
  5.6 1.5 %collective-permute-start.1 = (bf16[128,512]{1,0:T(8,128)(2,1)}, bf16[128,512]{1,0:T(8,128)(2,1)S(1)}, u32[]{:S(2)}, u32[]{:S(2)}) collective-permute-start(bf16[128,512]{1,0:T(8,128)(2,1)} %refs_4_.1), channel_id=1, source_target_pairs={{0,2},{1,3},{2,0},{3,1},{4,6},{5,7},{6,4},{7,5},{8,10},{9,11},{10,... | collective-permute-start | bytes 393224 | tf_op jit(solution)/shard_map/ppermute | solution.py:108
  7.1 0.0 collective-permute-start
  7.1 2.2 %collective-permute-start.11 = (bf16[128,512]{1,0:T(8,128)(2,1)}, bf16[128,512]{1,0:T(8,128)(2,1)S(1)}, u32[]{:S(2)}, u32[]{:S(2)}) collective-permute-start(bf16[128,512]{1,0:T(8,128)(2,1)} %refs_4_.1), channel_id=1, source_target_pairs={{0,12},{4,0},{8,4},{12,8},{1,13},{5,1},{9,5},{13,9},{2,14},{6,2},{... | collective-permute-start | bytes 393224 | tf_op jit(solution)/shard_map/ppermute | solution.py:104
  9.4 1.2 %reshape.43 = bf16[2,4,2,64,64]{4,3,2,1,0:T(8,128)(2,1)S(1)} reshape(bf16[2,8,4096]{2,1,0:T(8,128)(2,1)} %param.5) | data formatting | bytes 262144 | tf_op jit(solution)/shard_map/reshape | solution.py:117
  10.5 0.3 copy.23
  10.8 0.8 %reshape.44 = bf16[4,128,128]{2,1,0:T(8,128)(2,1)} reshape(bf16[4,2,64,2,64]{4,3,2,1,0:T(2,128)(2,1)S(1)} %bitcast.38) | data formatting | bytes 262144 | tf_op jit(solution)/shard_map/reshape | solution.py:118
  11.6 3.3 %all-to-all-start.1 = ((bf16[4,128,128]{2,1,0:T(8,128)(2,1)}), bf16[4,128,128]{2,1,0:T(8,128)(2,1)S(1)}, u32[]{:S(2)}, u32[]{:S(2)}) async-start(bf16[4,128,128]{2,1,0:T(8,128)(2,1)} %reshape.44), calls=%async_computation.1 | async-start | bytes 262144 | tf_op jit(solution)/shard_map/all_to_all | solution.py:133
  15.6 0.0 copy-start.1
  15.6 0.0 copy-start.2
  15.6 0.0 collective-permute-done.7.refs_12_
  15.6 0.6 %collective-permute-start.9 = (bf16[128,512]{1,0:T(8,128)(2,1)S(1)}, bf16[128,512]{1,0:T(8,128)(2,1)S(1)}, u32[]{:S(2)}, u32[]{:S(2)}) collective-permute-start(bf16[128,512]{1,0:T(8,128)(2,1)S(1)} %collective-permute-done.7.refs_12_), channel_id=1, source_target_pairs={{0,2},{1,3},{2,0},{3,1},{4,6},{5,7},{6,4},{7,5},{8,10},{9,11},{10,... | collective-permute-start | bytes 393224 | tf_op jit(solution)/shard_map/ppermute | solution.py:108
  16.2 0.0 collective-permute-done.3.refs_8_
  16.2 0.0 collective-permute-start.8
  16.3 0.0 collective-permute-done.1.refs_6_
  16.3 1.6 %collective-permute-start.5 = (bf16[128,512]{1,0:T(8,128)(2,1)S(1)}, bf16[128,512]{1,0:T(8,128)(2,1)S(1)}, u32[]{:S(2)}, u32[]{:S(2)}) collective-permute-start(bf16[128,512]{1,0:T(8,128)(2,1)S(1)} %collective-permute-done.3.refs_8_), channel_id=1, source_target_pairs={{0,2},{1,3},{2,0},{3,1},{4,6},{5,7},{6,4},{7,5},{8,10},{9,11},{10,... | collective-permute-start | bytes 393224 | tf_op jit(solution)/shard_map/ppermute | solution.py:108
  17.8 0.0 copy-done.1
  17.8 0.0 copy-done.2
  17.8 0.0 collective-permute-done.refs_5_
  17.8 0.2 collective-permute-start.4
  18.1 0.0 collective-permute-done.11.refs_16_
  18.1 0.5 %collective-permute-start.13 = (bf16[128,512]{1,0:T(8,128)(2,1)S(1)}, bf16[128,512]{1,0:T(8,128)(2,1)S(1)}, u32[]{:S(2)}, u32[]{:S(2)}) collective-permute-start(bf16[128,512]{1,0:T(8,128)(2,1)S(1)} %collective-permute-done.11.refs_16_), channel_id=1, source_target_pairs={{0,2},{1,3},{2,0},{3,1},{4,6},{5,7},{6,4},{7,5},{8,10},{9,11},{10,... | collective-permute-start | bytes 393224 | tf_op jit(solution)/shard_map/ppermute | solution.py:108
  18.6 3.4 %collective-permute-done.9.refs_14_ = bf16[128,512]{1,0:T(8,128)(2,1)S(1)} collective-permute-done((bf16[128,512]{1,0:T(8,128)(2,1)S(1)}, bf16[128,512]{1,0:T(8,128)(2,1)S(1)}, u32[]{:S(2)}, u32[]{:S(2)}) %collective-permute-start.9) | collective-permute-done | bytes 131104 | tf_op jit(solution)/shard_map/ppermute | solution.py:108
  22.0 0.0 collective-permute-start.12
  22.0 0.0 collective-permute-done.8.refs_13_
  22.0 0.5 %collective-permute-start.2 = (bf16[128,512]{1,0:T(8,128)(2,1)S(1)}, bf16[128,512]{1,0:T(8,128)(2,1)S(1)}, u32[]{:S(2)}, u32[]{:S(2)}) collective-permute-start(bf16[128,512]{1,0:T(8,128)(2,1)S(1)} %collective-permute-done.1.refs_6_), channel_id=1, source_target_pairs={{0,1},{1,0},{2,3},{3,2},{4,5},{5,4},{6,7},{7,6},{8,9},{9,8},{10,11... | collective-permute-start | bytes 393224 | tf_op jit(solution)/shard_map/ppermute | solution.py:108
  22.6 0.0 all-to-all-done.1.refs_20_
  22.6 2.3 %collective-permute-done.5.refs_10_ = bf16[128,512]{1,0:T(8,128)(2,1)S(1)} collective-permute-done((bf16[128,512]{1,0:T(8,128)(2,1)S(1)}, bf16[128,512]{1,0:T(8,128)(2,1)S(1)}, u32[]{:S(2)}, u32[]{:S(2)}) %collective-permute-start.5) | collective-permute-done | bytes 131104 | tf_op jit(solution)/shard_map/ppermute | solution.py:108
  24.9 0.5 %collective-permute-start.16 = (bf16[4,128,128]{2,1,0:T(8,128)(2,1)S(1)}, bf16[4,128,128]{2,1,0:T(8,128)(2,1)S(1)}, u32[]{:S(2)}, u32[]{:S(2)}) collective-permute-start(bf16[4,128,128]{2,1,0:T(8,128)(2,1)S(1)} %all-to-all-done.1.refs_20_), channel_id=1, source_target_pairs={{0,2},{1,3},{2,0},{3,1},{4,6},{5,7},{6,4},{7,5},{8,10},{9,11},{10,... | collective-permute-start | bytes 393224 | tf_op jit(solution)/shard_map/ppermute | solution.py:108
  25.4 0.1 broadcast_in_dim.10
  25.5 0.6 %broadcast_in_dim.11 = s32[16,1,6]{2,1,0:T(1,128)} broadcast(s32[6]{0:T(128)S(1)} %broadcast_in_dim.10), dimensions={2} | broadcast | bytes 408 | tf_op jit(solution)/shard_map/broadcast_in_dim | solution.py:137
  26.1 6.1 %all-to-all-start = ((s32[16,1,6]{2,1,0:T(1,128)}), s32[16,1,6]{2,1,0:T(1,128)S(1)}, u32[]{:S(2)}, u32[]{:S(2)}) async-start(s32[16,1,6]{2,1,0:T(1,128)} %broadcast_in_dim.11), calls=%async_computation | async-start | bytes 16384 | tf_op jit(solution)/shard_map/all_to_all | solution.py:138
  32.3 0.0 copy-start
  32.3 0.1 stack.94.refs_0_
  32.4 6.1 %all-to-all-done = s32[16,1,6]{2,1,0:T(1,128)S(1)} async-done(((s32[16,1,6]{2,1,0:T(1,128)}), s32[16,1,6]{2,1,0:T(1,128)S(1)}, u32[]{:S(2)}, u32[]{:S(2)}) %all-to-all-start) | async-done | bytes 416 | tf_op jit(solution)/shard_map/all_to_all | solution.py:138
  38.6 0.1 copy.16
  38.7 0.1 reshape.42
  38.7 0.0 collective-permute-done.4.refs_9_
  38.7 0.0 collective-permute-start.15
  38.8 0.0 collective-permute-done.2.refs_7_
  38.8 0.5 %collective-permute-start.10 = (bf16[128,512]{1,0:T(8,128)(2,1)S(1)}, bf16[128,512]{1,0:T(8,128)(2,1)S(1)}, u32[]{:S(2)}, u32[]{:S(2)}) collective-permute-start(bf16[128,512]{1,0:T(8,128)(2,1)S(1)} %collective-permute-done.9.refs_14_), channel_id=1, source_target_pairs={{0,1},{1,0},{2,3},{3,2},{4,5},{5,4},{6,7},{7,6},{8,9},{9,8},{10,11... | collective-permute-start | bytes 393224 | tf_op jit(solution)/shard_map/ppermute | solution.py:108
  39.3 0.0 collective-permute-done.13.refs_18_
  39.3 0.1 collective-permute-start.6
  39.4 0.0 collective-permute-done.12.refs_17_
  39.4 0.4 collective-permute-start.14
  39.8 0.0 collective-permute-done.16.refs_22_
  39.8 0.1 collective-permute-start.17
  39.9 0.1 copy.19
  40.0 0.1 squeeze.15.refs_3_
  40.1 0.1 copy.18
  40.2 0.1 squeeze.14.refs_2_
  40.3 0.1 copy.17
  40.4 0.1 squeeze.13.refs_1_
  40.5 0.0 collective-permute-done.15.refs_21_
  40.5 0.0 collective-permute-done.10.refs_15_
  40.5 0.1 collective-permute-done.6.refs_11_
  40.6 0.2 collective-permute-done.14.refs_19_
  40.8 0.3 collective-permute-done.17.refs_23_
  41.2 0.0 copy-done
  41.2 7.5 %transform.1 = f32[1024,128]{1,0:T(8,128)} custom-call(s32[21]{0:T(128)S(1)} %stack.94.refs_0_, s32[32]{0:T(128)S(1)} %squeeze.13.refs_1_, s32[32]{0:T(128)S(1)} %squeeze.14.refs_2_, s32[32]{0:T(128)S(1)} %squeeze.15.refs_3_, bf16[128,512]{1,0:T(8,128)(2,1)S(1)} %copy-done, bf16[128,512]{1,0:T(8,128)(2,1)S(1)} %collective-permute-done.refs_5_, ...), custom_call_target="tpu_custom_call" | custom-call | tf_op jit(solution)/shard_map/transform/pallas_call | solution.py:85
  (4 shorter events, 0.0 us)
Async XLA Ops:
  0.0 15.6 %collective-permute-start.7 = (bf16[128,512]{1,0:T(8,128)(2,1)}, bf16[128,512]{1,0:T(8,128)(2,1)S(1)}, u32[]{:S(2)}, u32[]{:S(2)}) collective-permute-start(bf16[128,512]{1,0:T(8,128)(2,1)} %refs_4_.1), channel_id=1, source_target_pairs={{0,8},{4,12},{8,0},{12,4},{1,9},{5,13},{9,1},{13,5},{2,10},{6,14},... | collective-permute-start | bytes 393224 | tf_op jit(solution)/shard_map/ppermute | solution.py:104
  4.0 12.2 %collective-permute-start.3 = (bf16[128,512]{1,0:T(8,128)(2,1)}, bf16[128,512]{1,0:T(8,128)(2,1)S(1)}, u32[]{:S(2)}, u32[]{:S(2)}) collective-permute-start(bf16[128,512]{1,0:T(8,128)(2,1)} %refs_4_.1), channel_id=1, source_target_pairs={{0,4},{4,8},{8,12},{12,0},{1,5},{5,9},{9,13},{13,1},{2,6},{6,10},{... | collective-permute-start | bytes 393224 | tf_op jit(solution)/shard_map/ppermute | solution.py:104
  5.6 10.6 %collective-permute-start.1 = (bf16[128,512]{1,0:T(8,128)(2,1)}, bf16[128,512]{1,0:T(8,128)(2,1)S(1)}, u32[]{:S(2)}, u32[]{:S(2)}) collective-permute-start(bf16[128,512]{1,0:T(8,128)(2,1)} %refs_4_.1), channel_id=1, source_target_pairs={{0,2},{1,3},{2,0},{3,1},{4,6},{5,7},{6,4},{7,5},{8,10},{9,11},{10,... | collective-permute-start | bytes 393224 | tf_op jit(solution)/shard_map/ppermute | solution.py:108
  7.1 10.7 %collective-permute-start = (bf16[128,512]{1,0:T(8,128)(2,1)}, bf16[128,512]{1,0:T(8,128)(2,1)S(1)}, u32[]{:S(2)}, u32[]{:S(2)}) collective-permute-start(bf16[128,512]{1,0:T(8,128)(2,1)} %refs_4_.1), channel_id=1, source_target_pairs={{0,1},{1,0},{2,3},{3,2},{4,5},{5,4},{6,7},{7,6},{8,9},{9,8},{10,11... | collective-permute-start | bytes 393224 | tf_op jit(solution)/shard_map/ppermute | solution.py:108
  7.1 11.0 %collective-permute-start.11 = (bf16[128,512]{1,0:T(8,128)(2,1)}, bf16[128,512]{1,0:T(8,128)(2,1)S(1)}, u32[]{:S(2)}, u32[]{:S(2)}) collective-permute-start(bf16[128,512]{1,0:T(8,128)(2,1)} %refs_4_.1), channel_id=1, source_target_pairs={{0,12},{4,0},{8,4},{12,8},{1,13},{5,1},{9,5},{13,9},{2,14},{6,2},{... | collective-permute-start | bytes 393224 | tf_op jit(solution)/shard_map/ppermute | solution.py:104
  11.6 10.9 %all-to-all-start.1 = ((bf16[4,128,128]{2,1,0:T(8,128)(2,1)}), bf16[4,128,128]{2,1,0:T(8,128)(2,1)S(1)}, u32[]{:S(2)}, u32[]{:S(2)}) async-start(bf16[4,128,128]{2,1,0:T(8,128)(2,1)} %reshape.44), calls=%async_computation.1 | async-start | bytes 262144 | tf_op jit(solution)/shard_map/all_to_all | solution.py:133
  15.6 2.2 %copy-start.1 = (s32[2]{0:T(128)S(1)}, s32[2]{0:T(128)}, u32[]{:S(2)}) copy-start(s32[2]{0:T(128)} %param.6) | copy-start | bytes 28
  15.6 2.2 %copy-start.2 = (s32[2]{0:T(128)S(1)}, s32[2]{0:T(128)}, u32[]{:S(2)}) copy-start(s32[2]{0:T(128)} %param.7) | copy-start | bytes 28
  15.6 6.4 %collective-permute-start.9 = (bf16[128,512]{1,0:T(8,128)(2,1)S(1)}, bf16[128,512]{1,0:T(8,128)(2,1)S(1)}, u32[]{:S(2)}, u32[]{:S(2)}) collective-permute-start(bf16[128,512]{1,0:T(8,128)(2,1)S(1)} %collective-permute-done.7.refs_12_), channel_id=1, source_target_pairs={{0,2},{1,3},{2,0},{3,1},{4,6},{5,7},{6,4},{7,5},{8,10},{9,11},{10,... | collective-permute-start | bytes 393224 | tf_op jit(solution)/shard_map/ppermute | solution.py:108
  16.2 5.8 %collective-permute-start.8 = (bf16[128,512]{1,0:T(8,128)(2,1)S(1)}, bf16[128,512]{1,0:T(8,128)(2,1)S(1)}, u32[]{:S(2)}, u32[]{:S(2)}) collective-permute-start(bf16[128,512]{1,0:T(8,128)(2,1)S(1)} %collective-permute-done.7.refs_12_), channel_id=1, source_target_pairs={{0,1},{1,0},{2,3},{3,2},{4,5},{5,4},{6,7},{7,6},{8,9},{9,8},{10,11... | collective-permute-start | bytes 393224 | tf_op jit(solution)/shard_map/ppermute | solution.py:108
  16.3 8.6 %collective-permute-start.5 = (bf16[128,512]{1,0:T(8,128)(2,1)S(1)}, bf16[128,512]{1,0:T(8,128)(2,1)S(1)}, u32[]{:S(2)}, u32[]{:S(2)}) collective-permute-start(bf16[128,512]{1,0:T(8,128)(2,1)S(1)} %collective-permute-done.3.refs_8_), channel_id=1, source_target_pairs={{0,2},{1,3},{2,0},{3,1},{4,6},{5,7},{6,4},{7,5},{8,10},{9,11},{10,... | collective-permute-start | bytes 393224 | tf_op jit(solution)/shard_map/ppermute | solution.py:108
  17.8 20.9 %collective-permute-start.4 = (bf16[128,512]{1,0:T(8,128)(2,1)S(1)}, bf16[128,512]{1,0:T(8,128)(2,1)S(1)}, u32[]{:S(2)}, u32[]{:S(2)}) collective-permute-start(bf16[128,512]{1,0:T(8,128)(2,1)S(1)} %collective-permute-done.3.refs_8_), channel_id=1, source_target_pairs={{0,1},{1,0},{2,3},{3,2},{4,5},{5,4},{6,7},{7,6},{8,9},{9,8},{10,11... | collective-permute-start | bytes 393224 | tf_op jit(solution)/shard_map/ppermute | solution.py:108
  18.1 21.2 %collective-permute-start.13 = (bf16[128,512]{1,0:T(8,128)(2,1)S(1)}, bf16[128,512]{1,0:T(8,128)(2,1)S(1)}, u32[]{:S(2)}, u32[]{:S(2)}) collective-permute-start(bf16[128,512]{1,0:T(8,128)(2,1)S(1)} %collective-permute-done.11.refs_16_), channel_id=1, source_target_pairs={{0,2},{1,3},{2,0},{3,1},{4,6},{5,7},{6,4},{7,5},{8,10},{9,11},{10,... | collective-permute-start | bytes 393224 | tf_op jit(solution)/shard_map/ppermute | solution.py:108
  22.0 17.3 %collective-permute-start.12 = (bf16[128,512]{1,0:T(8,128)(2,1)S(1)}, bf16[128,512]{1,0:T(8,128)(2,1)S(1)}, u32[]{:S(2)}, u32[]{:S(2)}) collective-permute-start(bf16[128,512]{1,0:T(8,128)(2,1)S(1)} %collective-permute-done.11.refs_16_), channel_id=1, source_target_pairs={{0,1},{1,0},{2,3},{3,2},{4,5},{5,4},{6,7},{7,6},{8,9},{9,8},{10,11... | collective-permute-start | bytes 393224 | tf_op jit(solution)/shard_map/ppermute | solution.py:108
  22.0 16.7 %collective-permute-start.2 = (bf16[128,512]{1,0:T(8,128)(2,1)S(1)}, bf16[128,512]{1,0:T(8,128)(2,1)S(1)}, u32[]{:S(2)}, u32[]{:S(2)}) collective-permute-start(bf16[128,512]{1,0:T(8,128)(2,1)S(1)} %collective-permute-done.1.refs_6_), channel_id=1, source_target_pairs={{0,1},{1,0},{2,3},{3,2},{4,5},{5,4},{6,7},{7,6},{8,9},{9,8},{10,11... | collective-permute-start | bytes 393224 | tf_op jit(solution)/shard_map/ppermute | solution.py:108
  24.9 15.0 %collective-permute-start.16 = (bf16[4,128,128]{2,1,0:T(8,128)(2,1)S(1)}, bf16[4,128,128]{2,1,0:T(8,128)(2,1)S(1)}, u32[]{:S(2)}, u32[]{:S(2)}) collective-permute-start(bf16[4,128,128]{2,1,0:T(8,128)(2,1)S(1)} %all-to-all-done.1.refs_20_), channel_id=1, source_target_pairs={{0,2},{1,3},{2,0},{3,1},{4,6},{5,7},{6,4},{7,5},{8,10},{9,11},{10,... | collective-permute-start | bytes 393224 | tf_op jit(solution)/shard_map/ppermute | solution.py:108
  26.1 12.5 %all-to-all-start = ((s32[16,1,6]{2,1,0:T(1,128)}), s32[16,1,6]{2,1,0:T(1,128)S(1)}, u32[]{:S(2)}, u32[]{:S(2)}) async-start(s32[16,1,6]{2,1,0:T(1,128)} %broadcast_in_dim.11), calls=%async_computation | async-start | bytes 16384 | tf_op jit(solution)/shard_map/all_to_all | solution.py:138
  32.3 8.9 %copy-start = (bf16[128,512]{1,0:T(8,128)(2,1)S(1)}, bf16[128,512]{1,0:T(8,128)(2,1)}, u32[]{:S(2)}) copy-start(bf16[128,512]{1,0:T(8,128)(2,1)} %refs_4_.1) | copy-start | bytes 393220
  38.7 1.8 %collective-permute-start.15 = (bf16[4,128,128]{2,1,0:T(8,128)(2,1)S(1)}, bf16[4,128,128]{2,1,0:T(8,128)(2,1)S(1)}, u32[]{:S(2)}, u32[]{:S(2)}) collective-permute-start(bf16[4,128,128]{2,1,0:T(8,128)(2,1)S(1)} %all-to-all-done.1.refs_20_), channel_id=1, source_target_pairs={{0,1},{1,0},{2,3},{3,2},{4,5},{5,4},{6,7},{7,6},{8,9},{9,8},{10,11... | collective-permute-start | bytes 393224 | tf_op jit(solution)/shard_map/ppermute | solution.py:108
  38.8 1.7 %collective-permute-start.10 = (bf16[128,512]{1,0:T(8,128)(2,1)S(1)}, bf16[128,512]{1,0:T(8,128)(2,1)S(1)}, u32[]{:S(2)}, u32[]{:S(2)}) collective-permute-start(bf16[128,512]{1,0:T(8,128)(2,1)S(1)} %collective-permute-done.9.refs_14_), channel_id=1, source_target_pairs={{0,1},{1,0},{2,3},{3,2},{4,5},{5,4},{6,7},{7,6},{8,9},{9,8},{10,11... | collective-permute-start | bytes 393224 | tf_op jit(solution)/shard_map/ppermute | solution.py:108
  39.3 1.3 %collective-permute-start.6 = (bf16[128,512]{1,0:T(8,128)(2,1)S(1)}, bf16[128,512]{1,0:T(8,128)(2,1)S(1)}, u32[]{:S(2)}, u32[]{:S(2)}) collective-permute-start(bf16[128,512]{1,0:T(8,128)(2,1)S(1)} %collective-permute-done.5.refs_10_), channel_id=1, source_target_pairs={{0,1},{1,0},{2,3},{3,2},{4,5},{5,4},{6,7},{7,6},{8,9},{9,8},{10,11... | collective-permute-start | bytes 393224 | tf_op jit(solution)/shard_map/ppermute | solution.py:108
  39.4 1.4 %collective-permute-start.14 = (bf16[128,512]{1,0:T(8,128)(2,1)S(1)}, bf16[128,512]{1,0:T(8,128)(2,1)S(1)}, u32[]{:S(2)}, u32[]{:S(2)}) collective-permute-start(bf16[128,512]{1,0:T(8,128)(2,1)S(1)} %collective-permute-done.13.refs_18_), channel_id=1, source_target_pairs={{0,1},{1,0},{2,3},{3,2},{4,5},{5,4},{6,7},{7,6},{8,9},{9,8},{10,11... | collective-permute-start | bytes 393224 | tf_op jit(solution)/shard_map/ppermute | solution.py:108
  39.8 1.3 %collective-permute-start.17 = (bf16[4,128,128]{2,1,0:T(8,128)(2,1)S(1)}, bf16[4,128,128]{2,1,0:T(8,128)(2,1)S(1)}, u32[]{:S(2)}, u32[]{:S(2)}) collective-permute-start(bf16[4,128,128]{2,1,0:T(8,128)(2,1)S(1)} %collective-permute-done.16.refs_22_), channel_id=1, source_target_pairs={{0,1},{1,0},{2,3},{3,2},{4,5},{5,4},{6,7},{7,6},{8,9},{9,8},{10,11... | collective-permute-start | bytes 393224 | tf_op jit(solution)/shard_map/ppermute | solution.py:108

commit v2 on v0

v2 whole, which is shorter than its diff:
```python
import functools

import jax
import jax.numpy as jnp
from jax import lax
from jax.experimental import pallas as pl
from jax.experimental.pallas import tpu as pltpu
from jax.sharding import PartitionSpec as P

SB = 64
LANES = 128
TAG = 16
CHUNK = 16


def pack_kernel(n_pair, integrals, mu, nu, counts, coeff, *refs):
    outs, spread, woven = refs[:n_pair], refs[n_pair], refs[n_pair + 1]
    p = lax.axis_index("pair")
    slots, kets, flat = integrals.shape
    wide = flat // LANES
    columns = kets // n_pair
    rows, orbitals = coeff.shape
    blocks = orbitals // LANES
    for t in range(slots):
        for j in range(wide):
            at = pl.ds((t * wide + j) * kets, kets)
            spread[at, :] = integrals[t, :, j * LANES : (j + 1) * LANES].astype(jnp.float32)
    lane = lax.broadcasted_iota(jnp.int32, (wide, LANES), 1)
    low, kept = lane < SB, lane < SB * counts[0]
    lane = lax.broadcasted_iota(jnp.int32, (TAG, LANES), 1)
    tag = jnp.zeros((TAG, LANES), jnp.int32)
    for t in range(slots):
        tag = jnp.where((lane == 2 * t) & (t < counts[0]), mu[t], tag)
        tag = jnp.where((lane == 2 * t + 1) & (t < counts[0]), nu[t], tag)
    tag = tag.astype(jnp.float32).astype(jnp.bfloat16)
    for s in range(n_pair):
        dest = lax.rem(p + s, n_pair)
        for k in range(columns):
            column = dest * columns + k
            one = spread[pl.ds(column, wide, stride=kets), :]
            two = spread[pl.ds(wide * kets + column, wide, stride=kets), :]
            even = jnp.where(low, one, pltpu.roll(two, SB, axis=1))
            odd = jnp.where(low, pltpu.roll(one, SB, axis=1), two)
            start = (s * columns + k) * SB
            woven[pl.ds(start, wide, stride=2), :] = jnp.where(kept, even, 0.0)
            woven[pl.ds(start + 1, wide, stride=2), :] = jnp.where(kept, odd, 0.0)
        for j in range(blocks):
            outs[s][pl.ds(j * rows, rows), :] = coeff[:, j * LANES : (j + 1) * LANES]
        tile = woven[pl.ds(s * columns * SB, columns * SB), :]
        outs[s][pl.ds(blocks * rows, columns * SB), :] = tile.astype(jnp.bfloat16)
        outs[s][pl.ds(blocks * rows + columns * SB, TAG), :] = tag


def pack(n_pair, integrals, mu, nu, counts, coeff):
    slots, kets, flat = integrals.shape
    rows, orbitals = coeff.shape
    total = orbitals // LANES * rows + kets // n_pair * SB + TAG
    smem = pl.BlockSpec(memory_space=pltpu.SMEM)
    vmem = pl.BlockSpec(memory_space=pltpu.VMEM)
    return pl.pallas_call(
        functools.partial(pack_kernel, n_pair),
        out_shape=[jax.ShapeDtypeStruct((total, LANES), jnp.bfloat16)] * n_pair,
        in_specs=[vmem, smem, smem, smem, vmem],
        out_specs=[vmem] * n_pair,
        scratch_shapes=[
            pltpu.VMEM((slots * kets * flat // LANES, LANES), jnp.float32),
            pltpu.VMEM((kets * SB, LANES), jnp.float32),
        ],
        compiler_params=pltpu.CompilerParams(vmem_limit_bytes=16 << 20),
        name="pack",
    )(integrals, mu, nu, counts, coeff)


def transform_kernel(n_pair, n_orb, steps, sides, n_in, *refs):
    pieces = refs[:n_in]
    out, c_all, x_all, tags, codes, index, half, left, sems = refs[n_in:]
    p, o = lax.axis_index("pair"), lax.axis_index("orb")
    devices = x_all.shape[0]
    orbitals = c_all.shape[1]
    blocks = orbitals // LANES
    first_copies, copies = [], []
    if steps:
        rows = c_all.shape[0] // devices
        tile_at = blocks * rows
        for q, piece in enumerate(pieces):
            source = lax.rem(p + n_pair - steps[q], n_pair) * n_orb + (o ^ sides[q])
            place = pl.ds(pl.multiple_of(source * rows, rows), rows)
            for j in range(blocks):
                copies.append(
                    pltpu.make_async_copy(
                        piece.at[pl.ds(j * rows, rows), :],
                        c_all.at[place, pl.ds(j * LANES, LANES)],
                        sems.at[q, j],
                    )
                )
            copies.append(
                pltpu.make_async_copy(piece.at[pl.ds(tile_at, 2 * SB), :], x_all.at[q], sems.at[q, blocks])
            )
            first_copies.append(
                pltpu.make_async_copy(piece.at[pl.ds(tile_at + 2 * SB, TAG), :], tags.at[q], sems.at[q, blocks + 1])
            )
    else:
        whole, coeff = pieces
        copies = [
            pltpu.make_async_copy(coeff, c_all, sems.at[0, 0]),
            pltpu.make_async_copy(whole.at[:, pl.ds(0, 2 * SB), :], x_all, sems.at[0, 1]),
        ]
        first_copies = [pltpu.make_async_copy(whole.at[:, pl.ds(2 * SB, TAG), :], tags, sems.at[0, 2])]
    for copy in first_copies + copies:
        copy.start()
    for copy in first_copies:
        copy.wait()
    codes[...] = tags[:, 0, :].astype(jnp.float32).astype(jnp.int32)
    to_scalars = pltpu.make_async_copy(codes, index, sems.at[0, blocks + 2])
    to_scalars.start()
    to_scalars.wait()
    for copy in copies:
        copy.wait()

    mine = pl.ds(pl.multiple_of(o * LANES, LANES), LANES)
    low = lax.broadcasted_iota(jnp.int32, (2 * SB, LANES), 1) < SB
    chunks = devices // CHUNK

    def rows_of(block):
        return pl.ds(pl.multiple_of(block * SB, SB), SB)

    def chunk_step(chunk, carry):
        for d in range(CHUNK):
            device = chunk * CHUNK + d
            tile = x_all[device]
            one = jnp.where(low, tile, jnp.zeros_like(tile))
            two = jnp.where(low, jnp.zeros_like(tile), tile)
            mu_one, nu_one, mu_two, nu_two = (index[device, n] for n in range(4))
            rows = jnp.concatenate([c_all[rows_of(nu_one)], c_all[rows_of(nu_two)]], 0)
            stacked = jnp.concatenate([one[:SB], two[:SB], one[SB:], two[SB:]], 0)
            moved = jnp.dot(stacked, rows, preferred_element_type=jnp.float32)
            moved = moved.astype(jnp.bfloat16)
            at = pl.ds(d * 2 * SB, 2 * SB)
            half[at, :orbitals] = moved[: 2 * SB]
            half[at, orbitals:] = moved[2 * SB :]
            left[at, :] = jnp.concatenate([c_all[rows_of(mu_one), mine], c_all[rows_of(mu_two), mine]], 0)
        part = lax.dot_general(
            left[...], half[...], (((0,), (0,)), ((), ())), preferred_element_type=jnp.float32
        )
        for k in range(2):
            for j in range(blocks):
                at = pl.ds(2 * j + k, LANES, stride=2 * blocks)
                begin = k * orbitals + j * LANES
                value = part[:, begin : begin + LANES]
                out[at, :] = value if chunks == 1 else out[at, :] + value
        return carry

    if chunks == 1:
        chunk_step(0, 0)
    else:
        out[...] = jnp.zeros_like(out)
        lax.fori_loop(0, chunks, chunk_step, 0)


def transform(n_pair, n_orb, steps, sides, pieces, rows_all, orbitals):
    devices = n_pair * n_orb
    wide = CHUNK * 2 * SB
    return pl.pallas_call(
        functools.partial(transform_kernel, n_pair, n_orb, steps, sides, len(pieces)),
        out_shape=jax.ShapeDtypeStruct((2 * orbitals // LANES * LANES, LANES), jnp.float32),
        in_specs=[pl.BlockSpec(memory_space=pl.ANY)] * len(pieces),
        out_specs=pl.BlockSpec(memory_space=pltpu.VMEM),
        scratch_shapes=[
            pltpu.VMEM((rows_all, orbitals), jnp.bfloat16),
            pltpu.VMEM((devices, 2 * SB, LANES), jnp.bfloat16),
            pltpu.VMEM((devices, TAG, LANES), jnp.bfloat16),
            pltpu.VMEM((devices, LANES), jnp.int32),
            pltpu.SMEM((devices, LANES), jnp.int32),
            pltpu.VMEM((wide, 2 * orbitals), jnp.bfloat16),
            pltpu.VMEM((wide, LANES), jnp.bfloat16),
            pltpu.SemaphoreType.DMA((len(pieces), orbitals // LANES + 3)),
        ],
        compiler_params=pltpu.CompilerParams(vmem_limit_bytes=40 << 20),
        name="transform",
    )(*pieces)


def shift(array, axis, size, step):
    return lax.ppermute(array, axis, [(i, (i + step) % size) for i in range(size)])


def flip(array, axis, size, bit):
    return lax.ppermute(array, axis, [(i, i ^ bit) for i in range(size)])


def body(n_pair, n_orb, integrals, mu_block, nu_block, counts, coeff):
    slots, kets, flat = integrals.shape
    columns = kets // n_pair
    orbitals = coeff.shape[1]
    everyone = ("pair", "orb")
    if n_pair * n_orb <= 16:
        packed = pack(n_pair, integrals, mu_block, nu_block, counts, coeff)
        pieces, steps, sides = [], [], []
        for s in range(n_pair):
            line = shift(packed[s], "pair", n_pair, s) if s else packed[0]
            across = flip(line, "orb", n_orb, 2)
            pieces += [line, flip(line, "orb", n_orb, 1), across, flip(across, "orb", n_orb, 1)]
            steps += [s] * 4
            sides += [0, 1, 2, 3]
    else:
        kept = jnp.arange(slots, dtype=jnp.int32) < counts[0]
        tiles = jnp.where(kept[:, None, None], integrals, jnp.zeros_like(integrals))
        tiles = tiles.reshape(slots, n_pair, columns, SB, SB).transpose(1, 2, 3, 0, 4)
        tiles = tiles.reshape(n_pair, columns * SB, slots * SB)
        tag = jnp.where(kept[:, None], jnp.stack([mu_block, nu_block], 1), 0).reshape(-1)
        tag = jnp.zeros((n_pair, TAG, LANES), jnp.bfloat16).at[:, :, : 2 * slots].set(tag.astype(jnp.bfloat16))
        packed = jnp.concatenate([tiles, tag], 1)
        line = lax.all_to_all(packed, "pair", split_axis=0, concat_axis=0, tiled=True)
        pieces = [lax.all_gather(line, "orb", axis=0, tiled=True), lax.all_gather(coeff, everyone, axis=0, tiled=True)]
        steps, sides = None, None
    out = transform(n_pair, n_orb, steps, sides, pieces, coeff.shape[0] * n_pair * n_orb, orbitals)
    out = out.reshape(orbitals // n_orb, orbitals // LANES, columns, LANES)
    return out.transpose(0, 2, 1, 3).reshape(orbitals // n_orb, columns, orbitals)


def solution(mesh):
    placed = (
        P(("grp", "pair", "orb"), None, None),
        P(("grp", "pair", "orb")),
        P(("grp", "pair", "orb")),
        P(("grp", "pair", "orb")),
        P(("grp", "pair", "orb"), None),
    )
    return jax.shard_map(
        functools.partial(body, mesh.shape["pair"], mesh.shape["orb"]),
        mesh=mesh,
        in_specs=placed,
        out_specs=P(("grp", "orb"), "pair", None),
        check_vma=False,
    )
```

time: 101 us -> 38.5 us (0.38)
  the two profiles are of different devices: /device:TPU:0 before, /device:TPU:11 now
where the time goes in v2:
time: 38.5 us; the launch traced here: 38.3 us
  starting transfers between devices  15 us (39%)
  waiting for transfers between devices  14.2 us (37%)
  Pallas kernels  6.58 us (17%)
  local copies, waits for them, and re-layouts  1.81 us (5%)
  between operations  0.74 us (2%)
    ppermute x12, starting transfers between devices, flip(): return lax.ppermute(array, axis, [(i, i ^ bit) for i in range(size)])  11.2 us
    ppermute x3, waiting for transfers between devices, shift(): lax.ppermute(array, axis, [(i, (i + step) % size) for i in range(size)])  9.27 us
    pallas_call x1, Pallas kernels, transform(): pl.pallas_call(functools.partial(transform_kernel, n_pair, n_orb, steps,...  5.81 us
    ppermute x12, waiting for transfers between devices, flip(): return lax.ppermute(array, axis, [(i, i ^ bit) for i in range(size)])  4.94 us
    ppermute x3, starting transfers between devices, shift(): lax.ppermute(array, axis, [(i, (i + step) % size) for i in range(size)])  3.83 us
    unnamed x8, local copies, waits for them, and re-layouts  1.81 us
    pallas_call x1, Pallas kernels, pack(): pl.pallas_call(functools.partial(pack_kernel, n_pair), out_shape=[jax.Sha...  0.77 us
  transfers between devices with their start and end apart: 15, of which 5 were waited for; matrix products, arithmetic and copies ran while one was open for 0% of the time, Pallas kernels for 0%

profile of v2, /device:TPU:11, one launch (start us, length us, event | category | flops | bytes accessed | tf_op | source)
XLA Modules:
  0.0 38.3 jit_solution(15520261306136659873)
XLA Ops:
  0.0 0.0 copy-start.3
  0.0 0.0 copy-start.2
  0.7 0.0 copy-done.3
  0.7 0.0 copy-done.2
  0.7 0.0 copy-start
  0.7 0.9 %copy-done = bf16[2,8,4096]{2,1,0:T(8,128)(2,1)S(1)} copy-done((bf16[2,8,4096]{2,1,0:T(8,128)(2,1)S(1)}, bf16[2,8,4096]{2,1,0:T(8,128)(2,1)}, u32[]{:S(2)}) %copy-start) | copy-done | bytes 131096
  1.6 0.0 copy-start.1
  1.6 0.9 %copy-done.1 = bf16[128,512]{1,0:T(8,128)(2,1)S(1)} copy-done((bf16[128,512]{1,0:T(8,128)(2,1)S(1)}, bf16[128,512]{1,0:T(8,128)(2,1)}, u32[]{:S(2)}) %copy-start.1) | copy-done | bytes 131096
  2.5 0.8 %pack.1 = (bf16[656,128]{1,0:T(8,128)(2,1)S(1)}, bf16[656,128]{1,0:T(8,128)(2,1)S(1)}, bf16[656,128]{1,0:T(8,128)(2,1)S(1)}, bf16[656,128]{1,0:T(8,128)(2,1)S(1)}) custom-call(bf16[2,8,4096]{2,1,0:T(8,128)(2,1)S(1)} %copy-done, s32[2]{0:T(128)S(1)} %copy-done.2, s32[2]{0:T(128)S(1)} %copy-done.3, s32[1]{0:T(128)S(6)} %copy.7.counts, ...), custom_call_target="tpu_custom_call" | custom-call | tf_op jit(solution)/shard_map/pack/pallas_call | solution.py:60
  3.3 1.3 %collective-permute-start.3 = (bf16[656,128]{1,0:T(8,128)(2,1)S(1)}, bf16[656,128]{1,0:T(8,128)(2,1)S(1)}, u32[]{:S(2)}, u32[]{:S(2)}) collective-permute-start(bf16[656,128]{1,0:T(8,128)(2,1)S(1)} %get-tuple-element.10), channel_id=1, source_target_pairs={{0,4},{4,8},{8,12},{12,0},{1,5},{5,9},{9,13},{13,1},{2,6},{6,10},{... | collective-permute-start | bytes 503816 | tf_op jit(solution)/shard_map/ppermute | solution.py:184
  4.6 1.1 %collective-permute-start.7 = (bf16[656,128]{1,0:T(8,128)(2,1)S(1)}, bf16[656,128]{1,0:T(8,128)(2,1)S(1)}, u32[]{:S(2)}, u32[]{:S(2)}) collective-permute-start(bf16[656,128]{1,0:T(8,128)(2,1)S(1)} %get-tuple-element.11), channel_id=1, source_target_pairs={{0,8},{4,12},{8,0},{12,4},{1,9},{5,13},{9,1},{13,5},{2,10},{6,14},... | collective-permute-start | bytes 503816 | tf_op jit(solution)/shard_map/ppermute | solution.py:184
  5.7 1.4 %collective-permute-start.11 = (bf16[656,128]{1,0:T(8,128)(2,1)S(1)}, bf16[656,128]{1,0:T(8,128)(2,1)S(1)}, u32[]{:S(2)}, u32[]{:S(2)}) collective-permute-start(bf16[656,128]{1,0:T(8,128)(2,1)S(1)} %get-tuple-element.12), channel_id=1, source_target_pairs={{0,12},{4,0},{8,4},{12,8},{1,13},{5,1},{9,5},{13,9},{2,14},{6,2},{... | collective-permute-start | bytes 503816 | tf_op jit(solution)/shard_map/ppermute | solution.py:184
  7.1 0.3 collective-permute-start.1
  7.4 1.8 %collective-permute-start = (bf16[656,128]{1,0:T(8,128)(2,1)S(1)}, bf16[656,128]{1,0:T(8,128)(2,1)S(1)}, u32[]{:S(2)}, u32[]{:S(2)}) collective-permute-start(bf16[656,128]{1,0:T(8,128)(2,1)S(1)} %get-tuple-element.9.refs_0_), channel_id=1, source_target_pairs={{0,1},{1,0},{2,3},{3,2},{4,5},{5,4},{6,7},{7,6},{8,9},{9,8},{10,11... | collective-permute-start | bytes 503816 | tf_op jit(solution)/shard_map/ppermute | solution.py:188
  9.2 0.0 collective-permute-done.3.refs_4_
  9.2 1.2 %collective-permute-start.5 = (bf16[656,128]{1,0:T(8,128)(2,1)S(1)}, bf16[656,128]{1,0:T(8,128)(2,1)S(1)}, u32[]{:S(2)}, u32[]{:S(2)}) collective-permute-start(bf16[656,128]{1,0:T(8,128)(2,1)S(1)} %collective-permute-done.3.refs_4_), channel_id=1, source_target_pairs={{0,2},{1,3},{2,0},{3,1},{4,6},{5,7},{6,4},{7,5},{8,10},{9,11},{10,... | collective-permute-start | bytes 503816 | tf_op jit(solution)/shard_map/ppermute | solution.py:188
  10.4 8.0 %collective-permute-done.7.refs_8_ = bf16[656,128]{1,0:T(8,128)(2,1)S(1)} collective-permute-done((bf16[656,128]{1,0:T(8,128)(2,1)S(1)}, bf16[656,128]{1,0:T(8,128)(2,1)S(1)}, u32[]{:S(2)}, u32[]{:S(2)}) %collective-permute-start.7) | collective-permute-done | bytes 167968 | tf_op jit(solution)/shard_map/ppermute | solution.py:184
  18.4 1.5 %collective-permute-start.4 = (bf16[656,128]{1,0:T(8,128)(2,1)S(1)}, bf16[656,128]{1,0:T(8,128)(2,1)S(1)}, u32[]{:S(2)}, u32[]{:S(2)}) collective-permute-start(bf16[656,128]{1,0:T(8,128)(2,1)S(1)} %collective-permute-done.3.refs_4_), channel_id=1, source_target_pairs={{0,1},{1,0},{2,3},{3,2},{4,5},{5,4},{6,7},{7,6},{8,9},{9,8},{10,11... | collective-permute-start | bytes 503816 | tf_op jit(solution)/shard_map/ppermute | solution.py:188
  19.9 1.3 %collective-permute-done.11.refs_12_ = bf16[656,128]{1,0:T(8,128)(2,1)S(1)} collective-permute-done((bf16[656,128]{1,0:T(8,128)(2,1)S(1)}, bf16[656,128]{1,0:T(8,128)(2,1)S(1)}, u32[]{:S(2)}, u32[]{:S(2)}) %collective-permute-start.11) | collective-permute-done | bytes 167968 | tf_op jit(solution)/shard_map/ppermute | solution.py:184
  21.2 0.3 collective-permute-start.9
  21.5 0.0 collective-permute-done.1.refs_2_
  21.5 0.8 %collective-permute-start.8 = (bf16[656,128]{1,0:T(8,128)(2,1)S(1)}, bf16[656,128]{1,0:T(8,128)(2,1)S(1)}, u32[]{:S(2)}, u32[]{:S(2)}) collective-permute-start(bf16[656,128]{1,0:T(8,128)(2,1)S(1)} %collective-permute-done.7.refs_8_), channel_id=1, source_target_pairs={{0,1},{1,0},{2,3},{3,2},{4,5},{5,4},{6,7},{7,6},{8,9},{9,8},{10,11... | collective-permute-start | bytes 503816 | tf_op jit(solution)/shard_map/ppermute | solution.py:188
  22.2 0.0 collective-permute-done.refs_1_
  22.2 1.2 %collective-permute-start.13 = (bf16[656,128]{1,0:T(8,128)(2,1)S(1)}, bf16[656,128]{1,0:T(8,128)(2,1)S(1)}, u32[]{:S(2)}, u32[]{:S(2)}) collective-permute-start(bf16[656,128]{1,0:T(8,128)(2,1)S(1)} %collective-permute-done.11.refs_12_), channel_id=1, source_target_pairs={{0,2},{1,3},{2,0},{3,1},{4,6},{5,7},{6,4},{7,5},{8,10},{9,11},{10,... | collective-permute-start | bytes 503816 | tf_op jit(solution)/shard_map/ppermute | solution.py:188
  23.4 0.0 collective-permute-done.5.refs_6_
  23.4 0.3 collective-permute-start.12
  23.8 0.0 collective-permute-done.4.refs_5_
  23.8 0.2 collective-permute-start.2
  24.0 2.6 %collective-permute-done.9.refs_10_ = bf16[656,128]{1,0:T(8,128)(2,1)S(1)} collective-permute-done((bf16[656,128]{1,0:T(8,128)(2,1)S(1)}, bf16[656,128]{1,0:T(8,128)(2,1)S(1)}, u32[]{:S(2)}, u32[]{:S(2)}) %collective-permute-start.9) | collective-permute-done | bytes 167968 | tf_op jit(solution)/shard_map/ppermute | solution.py:188
  26.6 2.3 %collective-permute-start.6 = (bf16[656,128]{1,0:T(8,128)(2,1)S(1)}, bf16[656,128]{1,0:T(8,128)(2,1)S(1)}, u32[]{:S(2)}, u32[]{:S(2)}) collective-permute-start(bf16[656,128]{1,0:T(8,128)(2,1)S(1)} %collective-permute-done.5.refs_6_), channel_id=1, source_target_pairs={{0,1},{1,0},{2,3},{3,2},{4,5},{5,4},{6,7},{7,6},{8,9},{9,8},{10,11... | collective-permute-start | bytes 503816 | tf_op jit(solution)/shard_map/ppermute | solution.py:188
  28.8 0.0 collective-permute-done.8.refs_9_
  28.8 0.0 collective-permute-start.10
  28.8 1.3 %collective-permute-done.13.refs_14_ = bf16[656,128]{1,0:T(8,128)(2,1)S(1)} collective-permute-done((bf16[656,128]{1,0:T(8,128)(2,1)S(1)}, bf16[656,128]{1,0:T(8,128)(2,1)S(1)}, u32[]{:S(2)}, u32[]{:S(2)}) %collective-permute-start.13) | collective-permute-done | bytes 167968 | tf_op jit(solution)/shard_map/ppermute | solution.py:188
  30.2 1.3 %collective-permute-start.14 = (bf16[656,128]{1,0:T(8,128)(2,1)S(1)}, bf16[656,128]{1,0:T(8,128)(2,1)S(1)}, u32[]{:S(2)}, u32[]{:S(2)}) collective-permute-start(bf16[656,128]{1,0:T(8,128)(2,1)S(1)} %collective-permute-done.13.refs_14_), channel_id=1, source_target_pairs={{0,1},{1,0},{2,3},{3,2},{4,5},{5,4},{6,7},{7,6},{8,9},{9,8},{10,11... | collective-permute-start | bytes 503816 | tf_op jit(solution)/shard_map/ppermute | solution.py:188
  31.5 0.0 collective-permute-done.12.refs_13_
  31.5 0.0 collective-permute-done.2.refs_3_
  31.5 0.0 collective-permute-done.6.refs_7_
  31.5 0.0 collective-permute-done.10.refs_11_
  31.5 1.0 %collective-permute-done.14.refs_15_ = bf16[656,128]{1,0:T(8,128)(2,1)S(1)} collective-permute-done((bf16[656,128]{1,0:T(8,128)(2,1)S(1)}, bf16[656,128]{1,0:T(8,128)(2,1)S(1)}, u32[]{:S(2)}, u32[]{:S(2)}) %collective-permute-start.14) | collective-permute-done | bytes 167968 | tf_op jit(solution)/shard_map/ppermute | solution.py:188
  32.5 5.8 %transform.1 = f32[1024,128]{1,0:T(8,128)} custom-call(bf16[656,128]{1,0:T(8,128)(2,1)S(1)} %get-tuple-element.9.refs_0_, bf16[656,128]{1,0:T(8,128)(2,1)S(1)} %collective-permute-done.refs_1_, bf16[656,128]{1,0:T(8,128)(2,1)S(1)} %collective-permute-done.1.refs_2_, bf16[656,128]{1,0:T(8,128)(2,1)S(1)} %collective-permute-done.2.refs_3_, ...), custom_call_target="tpu_custom_call" | custom-call | tf_op jit(solution)/shard_map/transform/pallas_call | solution.py:163
Async XLA Ops:
  0.0 0.7 %copy-start.3 = (s32[2]{0:T(128)S(1)}, s32[2]{0:T(128)}, u32[]{:S(2)}) copy-start(s32[2]{0:T(128)} %nu.1) | copy-start | bytes 28
  0.0 0.7 %copy-start.2 = (s32[2]{0:T(128)S(1)}, s32[2]{0:T(128)}, u32[]{:S(2)}) copy-start(s32[2]{0:T(128)} %mu.1) | copy-start | bytes 28
  0.7 0.9 %copy-start = (bf16[2,8,4096]{2,1,0:T(8,128)(2,1)S(1)}, bf16[2,8,4096]{2,1,0:T(8,128)(2,1)}, u32[]{:S(2)}) copy-start(bf16[2,8,4096]{2,1,0:T(8,128)(2,1)} %integrals.1) | copy-start | bytes 393220
  1.6 0.9 %copy-start.1 = (bf16[128,512]{1,0:T(8,128)(2,1)S(1)}, bf16[128,512]{1,0:T(8,128)(2,1)}, u32[]{:S(2)}) copy-start(bf16[128,512]{1,0:T(8,128)(2,1)} %coeff.1) | copy-start | bytes 393220
  3.3 5.9 %collective-permute-start.3 = (bf16[656,128]{1,0:T(8,128)(2,1)S(1)}, bf16[656,128]{1,0:T(8,128)(2,1)S(1)}, u32[]{:S(2)}, u32[]{:S(2)}) collective-permute-start(bf16[656,128]{1,0:T(8,128)(2,1)S(1)} %get-tuple-element.10), channel_id=1, source_target_pairs={{0,4},{4,8},{8,12},{12,0},{1,5},{5,9},{9,13},{13,1},{2,6},{6,10},{... | collective-permute-start | bytes 503816 | tf_op jit(solution)/shard_map/ppermute | solution.py:184
  4.6 13.8 %collective-permute-start.7 = (bf16[656,128]{1,0:T(8,128)(2,1)S(1)}, bf16[656,128]{1,0:T(8,128)(2,1)S(1)}, u32[]{:S(2)}, u32[]{:S(2)}) collective-permute-start(bf16[656,128]{1,0:T(8,128)(2,1)S(1)} %get-tuple-element.11), channel_id=1, source_target_pairs={{0,8},{4,12},{8,0},{12,4},{1,9},{5,13},{9,1},{13,5},{2,10},{6,14},... | collective-permute-start | bytes 503816 | tf_op jit(solution)/shard_map/ppermute | solution.py:184
  5.7 15.5 %collective-permute-start.11 = (bf16[656,128]{1,0:T(8,128)(2,1)S(1)}, bf16[656,128]{1,0:T(8,128)(2,1)S(1)}, u32[]{:S(2)}, u32[]{:S(2)}) collective-permute-start(bf16[656,128]{1,0:T(8,128)(2,1)S(1)} %get-tuple-element.12), channel_id=1, source_target_pairs={{0,12},{4,0},{8,4},{12,8},{1,13},{5,1},{9,5},{13,9},{2,14},{6,2},{... | collective-permute-start | bytes 503816 | tf_op jit(solution)/shard_map/ppermute | solution.py:184
  7.1 14.3 %collective-permute-start.1 = (bf16[656,128]{1,0:T(8,128)(2,1)S(1)}, bf16[656,128]{1,0:T(8,128)(2,1)S(1)}, u32[]{:S(2)}, u32[]{:S(2)}) collective-permute-start(bf16[656,128]{1,0:T(8,128)(2,1)S(1)} %get-tuple-element.9.refs_0_), channel_id=1, source_target_pairs={{0,2},{1,3},{2,0},{3,1},{4,6},{5,7},{6,4},{7,5},{8,10},{9,11},{10,... | collective-permute-start | bytes 503816 | tf_op jit(solution)/shard_map/ppermute | solution.py:188
  7.4 14.9 %collective-permute-start = (bf16[656,128]{1,0:T(8,128)(2,1)S(1)}, bf16[656,128]{1,0:T(8,128)(2,1)S(1)}, u32[]{:S(2)}, u32[]{:S(2)}) collective-permute-start(bf16[656,128]{1,0:T(8,128)(2,1)S(1)} %get-tuple-element.9.refs_0_), channel_id=1, source_target_pairs={{0,1},{1,0},{2,3},{3,2},{4,5},{5,4},{6,7},{7,6},{8,9},{9,8},{10,11... | collective-permute-start | bytes 503816 | tf_op jit(solution)/shard_map/ppermute | solution.py:188
  9.2 14.3 %collective-permute-start.5 = (bf16[656,128]{1,0:T(8,128)(2,1)S(1)}, bf16[656,128]{1,0:T(8,128)(2,1)S(1)}, u32[]{:S(2)}, u32[]{:S(2)}) collective-permute-start(bf16[656,128]{1,0:T(8,128)(2,1)S(1)} %collective-permute-done.3.refs_4_), channel_id=1, source_target_pairs={{0,2},{1,3},{2,0},{3,1},{4,6},{5,7},{6,4},{7,5},{8,10},{9,11},{10,... | collective-permute-start | bytes 503816 | tf_op jit(solution)/shard_map/ppermute | solution.py:188
  18.4 5.4 %collective-permute-start.4 = (bf16[656,128]{1,0:T(8,128)(2,1)S(1)}, bf16[656,128]{1,0:T(8,128)(2,1)S(1)}, u32[]{:S(2)}, u32[]{:S(2)}) collective-permute-start(bf16[656,128]{1,0:T(8,128)(2,1)S(1)} %collective-permute-done.3.refs_4_), channel_id=1, source_target_pairs={{0,1},{1,0},{2,3},{3,2},{4,5},{5,4},{6,7},{7,6},{8,9},{9,8},{10,11... | collective-permute-start | bytes 503816 | tf_op jit(solution)/shard_map/ppermute | solution.py:188
  21.2 5.4 %collective-permute-start.9 = (bf16[656,128]{1,0:T(8,128)(2,1)S(1)}, bf16[656,128]{1,0:T(8,128)(2,1)S(1)}, u32[]{:S(2)}, u32[]{:S(2)}) collective-permute-start(bf16[656,128]{1,0:T(8,128)(2,1)S(1)} %collective-permute-done.7.refs_8_), channel_id=1, source_target_pairs={{0,2},{1,3},{2,0},{3,1},{4,6},{5,7},{6,4},{7,5},{8,10},{9,11},{10,... | collective-permute-start | bytes 503816 | tf_op jit(solution)/shard_map/ppermute | solution.py:188
  21.5 7.4 %collective-permute-start.8 = (bf16[656,128]{1,0:T(8,128)(2,1)S(1)}, bf16[656,128]{1,0:T(8,128)(2,1)S(1)}, u32[]{:S(2)}, u32[]{:S(2)}) collective-permute-start(bf16[656,128]{1,0:T(8,128)(2,1)S(1)} %collective-permute-done.7.refs_8_), channel_id=1, source_target_pairs={{0,1},{1,0},{2,3},{3,2},{4,5},{5,4},{6,7},{7,6},{8,9},{9,8},{10,11... | collective-permute-start | bytes 503816 | tf_op jit(solution)/shard_map/ppermute | solution.py:188
  22.2 7.9 %collective-permute-start.13 = (bf16[656,128]{1,0:T(8,128)(2,1)S(1)}, bf16[656,128]{1,0:T(8,128)(2,1)S(1)}, u32[]{:S(2)}, u32[]{:S(2)}) collective-permute-start(bf16[656,128]{1,0:T(8,128)(2,1)S(1)} %collective-permute-done.11.refs_12_), channel_id=1, source_target_pairs={{0,2},{1,3},{2,0},{3,1},{4,6},{5,7},{6,4},{7,5},{8,10},{9,11},{10,... | collective-permute-start | bytes 503816 | tf_op jit(solution)/shard_map/ppermute | solution.py:188
  23.4 8.1 %collective-permute-start.12 = (bf16[656,128]{1,0:T(8,128)(2,1)S(1)}, bf16[656,128]{1,0:T(8,128)(2,1)S(1)}, u32[]{:S(2)}, u32[]{:S(2)}) collective-permute-start(bf16[656,128]{1,0:T(8,128)(2,1)S(1)} %collective-permute-done.11.refs_12_), channel_id=1, source_target_pairs={{0,1},{1,0},{2,3},{3,2},{4,5},{5,4},{6,7},{7,6},{8,9},{9,8},{10,11... | collective-permute-start | bytes 503816 | tf_op jit(solution)/shard_map/ppermute | solution.py:188
  23.8 7.7 %collective-permute-start.2 = (bf16[656,128]{1,0:T(8,128)(2,1)S(1)}, bf16[656,128]{1,0:T(8,128)(2,1)S(1)}, u32[]{:S(2)}, u32[]{:S(2)}) collective-permute-start(bf16[656,128]{1,0:T(8,128)(2,1)S(1)} %collective-permute-done.1.refs_2_), channel_id=1, source_target_pairs={{0,1},{1,0},{2,3},{3,2},{4,5},{5,4},{6,7},{7,6},{8,9},{9,8},{10,11... | collective-permute-start | bytes 503816 | tf_op jit(solution)/shard_map/ppermute | solution.py:188
  26.6 4.9 %collective-permute-start.6 = (bf16[656,128]{1,0:T(8,128)(2,1)S(1)}, bf16[656,128]{1,0:T(8,128)(2,1)S(1)}, u32[]{:S(2)}, u32[]{:S(2)}) collective-permute-start(bf16[656,128]{1,0:T(8,128)(2,1)S(1)} %collective-permute-done.5.refs_6_), channel_id=1, source_target_pairs={{0,1},{1,0},{2,3},{3,2},{4,5},{5,4},{6,7},{7,6},{8,9},{9,8},{10,11... | collective-permute-start | bytes 503816 | tf_op jit(solution)/shard_map/ppermute | solution.py:188
  28.8 2.7 %collective-permute-start.10 = (bf16[656,128]{1,0:T(8,128)(2,1)S(1)}, bf16[656,128]{1,0:T(8,128)(2,1)S(1)}, u32[]{:S(2)}, u32[]{:S(2)}) collective-permute-start(bf16[656,128]{1,0:T(8,128)(2,1)S(1)} %collective-permute-done.9.refs_10_), channel_id=1, source_target_pairs={{0,1},{1,0},{2,3},{3,2},{4,5},{5,4},{6,7},{7,6},{8,9},{9,8},{10,11... | collective-permute-start | bytes 503816 | tf_op jit(solution)/shard_map/ppermute | solution.py:188
  30.2 2.4 %collective-permute-start.14 = (bf16[656,128]{1,0:T(8,128)(2,1)S(1)}, bf16[656,128]{1,0:T(8,128)(2,1)S(1)}, u32[]{:S(2)}, u32[]{:S(2)}) collective-permute-start(bf16[656,128]{1,0:T(8,128)(2,1)S(1)} %collective-permute-done.13.refs_14_), channel_id=1, source_target_pairs={{0,1},{1,0},{2,3},{3,2},{4,5},{5,4},{6,7},{7,6},{8,9},{9,8},{10,11... | collective-permute-start | bytes 503816 | tf_op jit(solution)/shard_map/ppermute | solution.py:188

commit v3 on v2

v3 whole, which is shorter than its diff:
```python
import functools

import jax
import jax.numpy as jnp
from jax import lax
from jax.experimental import pallas as pl
from jax.experimental.pallas import tpu as pltpu
from jax.sharding import PartitionSpec as P

SB = 64
LANES = 128
GROUP = 16
CHUNK = 16


def pack_kernel(n_pair, integrals, mu, nu, counts, coeff, *refs):
    outs = refs[:n_pair]
    tiles, shard, mu_in, nu_in, spread, woven, sems = refs[n_pair:]
    copies = [
        pltpu.make_async_copy(source, target, sems.at[n])
        for n, (source, target) in enumerate(
            ((integrals, tiles), (coeff, shard), (mu, mu_in), (nu, nu_in))
        )
    ]
    for copy in copies:
        copy.start()
    p = lax.axis_index("pair")
    slots, kets, flat = tiles.shape
    wide = flat // LANES
    columns = kets // n_pair
    rows, orbitals = shard.shape
    blocks = orbitals // LANES
    copies[0].wait()
    for t in range(slots):
        for j in range(wide):
            at = pl.ds((t * wide + j) * kets, kets)
            spread[at, :] = tiles[t, :, j * LANES : (j + 1) * LANES].astype(jnp.float32)
    for copy in copies[2:]:
        copy.wait()
    count = counts[0]
    lane = lax.broadcasted_iota(jnp.int32, (wide, LANES), 1)
    low, kept = lane < SB, lane < SB * count
    lane = lax.broadcasted_iota(jnp.int32, (GROUP, LANES), 1)
    tag = jnp.zeros((GROUP, LANES), jnp.int32)
    for t in range(slots):
        tag = jnp.where((lane == 2 * t) & (t < count), mu_in[t], tag)
        tag = jnp.where((lane == 2 * t + 1) & (t < count), nu_in[t], tag)
    tag = tag.astype(jnp.float32).astype(jnp.bfloat16)
    tile_at = rows // GROUP * blocks
    for s in range(n_pair):
        dest = lax.rem(p + s, n_pair)
        for k in range(columns):
            column = dest * columns + k
            one = spread[pl.ds(column, wide, stride=kets), :]
            two = spread[pl.ds(wide * kets + column, wide, stride=kets), :]
            even = jnp.where(low, one, pltpu.roll(two, SB, axis=1))
            odd = jnp.where(low, pltpu.roll(one, SB, axis=1), two)
            begin = (s * columns + k) * SB
            woven[pl.ds(begin, wide, stride=2), :] = jnp.where(kept, even, 0.0)
            woven[pl.ds(begin + 1, wide, stride=2), :] = jnp.where(kept, odd, 0.0)
        tiled = columns * SB // GROUP
        for g in range(tiled):
            rows_at = pl.ds((s * tiled + g) * GROUP, GROUP)
            outs[s][tile_at + g] = woven[rows_at, :].astype(jnp.bfloat16)
        outs[s][tile_at + tiled] = tag
    copies[1].wait()
    for g in range(rows // GROUP):
        for j in range(blocks):
            group = shard[g * GROUP : (g + 1) * GROUP, j * LANES : (j + 1) * LANES]
            for s in range(n_pair):
                outs[s][g * blocks + j] = group


def pack(n_pair, integrals, mu, nu, counts, coeff):
    slots, kets, flat = integrals.shape
    rows, orbitals = coeff.shape
    groups = rows // GROUP * (orbitals // LANES) + kets // n_pair * SB // GROUP + 1
    hbm = pl.BlockSpec(memory_space=pltpu.HBM)
    return pl.pallas_call(
        functools.partial(pack_kernel, n_pair),
        out_shape=[jax.ShapeDtypeStruct((groups, GROUP, LANES), jnp.bfloat16)] * n_pair,
        in_specs=[hbm, hbm, hbm, pl.BlockSpec(memory_space=pltpu.SMEM), hbm],
        out_specs=[pl.BlockSpec(memory_space=pltpu.VMEM)] * n_pair,
        scratch_shapes=[
            pltpu.VMEM(integrals.shape, jnp.bfloat16),
            pltpu.VMEM(coeff.shape, jnp.bfloat16),
            pltpu.SMEM(mu.shape, jnp.int32),
            pltpu.SMEM(nu.shape, jnp.int32),
            pltpu.VMEM((slots * kets * flat // LANES, LANES), jnp.float32),
            pltpu.VMEM((kets * SB, LANES), jnp.float32),
            pltpu.SemaphoreType.DMA((4,)),
        ],
        compiler_params=pltpu.CompilerParams(vmem_limit_bytes=60 << 20),
        name="pack",
    )(integrals, mu, nu, counts, coeff)


def transform_kernel(n_pair, n_orb, steps, sides, blocks, n_in, *refs):
    pieces = refs[:n_in]
    out, *held = refs[n_in:-6]
    codes, index, half, left, sems, tag_sem = refs[-6:]
    p, o = lax.axis_index("pair"), lax.axis_index("orb")
    devices = codes.shape[0]
    orbitals = blocks * LANES
    tiled = 2 * SB // GROUP
    in_block = SB // GROUP * blocks
    if steps:
        (together,) = held
        per = together.shape[0] // devices
        copies = []
        for q, piece in enumerate(pieces):
            source = lax.rem(p + n_pair - steps[q], n_pair) * n_orb + (o ^ sides[q])
            copies.append(pltpu.make_async_copy(piece, together.at[pl.ds(source * per, per)], sems.at[q]))
        tiles, spacing, tile_at = together, per, per - tiled - 1
        coeffs, per_dev = together, tile_at // in_block

        def block_at(block):
            return lax.div(block, per_dev) * per + lax.rem(block, per_dev) * in_block
    else:
        tiles, coeffs = held
        spacing, tile_at = tiled + 1, 0
        copies = [pltpu.make_async_copy(piece, target, sems.at[q]) for q, (piece, target) in enumerate(zip(pieces, held))]

        def block_at(block):
            return block * in_block

    for copy in copies:
        copy.start()
    for copy in copies:
        copy.wait()
    for d in range(devices):
        codes[d : d + 1, :] = tiles[d * spacing + tile_at + tiled][:1].astype(jnp.float32).astype(jnp.int32)
    to_scalars = pltpu.make_async_copy(codes, index, tag_sem)
    to_scalars.start()
    to_scalars.wait()

    low = lax.broadcasted_iota(jnp.int32, (SB, LANES), 1) < SB
    chunks = devices // CHUNK

    def block_rows(block):
        at = block_at(block)
        return jnp.concatenate(
            [
                jnp.concatenate([coeffs[at + g * blocks + j] for j in range(blocks)], 1)
                for g in range(SB // GROUP)
            ],
            0,
        )

    def block_mine(block):
        at = block_at(block) + o
        return jnp.concatenate([coeffs[at + g * blocks] for g in range(SB // GROUP)], 0)

    def chunk_step(chunk, carry):
        for d in range(CHUNK):
            device = chunk * CHUNK + d
            at = device * spacing + tile_at
            stacked = []
            for k in range(2):
                begin = at + k * (SB // GROUP)
                tile = jnp.concatenate([tiles[begin + g] for g in range(SB // GROUP)], 0)
                stacked += [jnp.where(low, tile, jnp.zeros_like(tile)), jnp.where(low, jnp.zeros_like(tile), tile)]
            mu_one, nu_one, mu_two, nu_two = (index[device, n] for n in range(4))
            rows = jnp.concatenate([block_rows(nu_one), block_rows(nu_two)], 0)
            moved = jnp.dot(jnp.concatenate(stacked, 0), rows, preferred_element_type=jnp.float32)
            moved = moved.astype(jnp.bfloat16)
            at = pl.ds(d * 2 * SB, 2 * SB)
            half[at, :orbitals] = moved[: 2 * SB]
            half[at, orbitals:] = moved[2 * SB :]
            left[at, :] = jnp.concatenate([block_mine(mu_one), block_mine(mu_two)], 0)
        part = lax.dot_general(
            left[...], half[...], (((0,), (0,)), ((), ())), preferred_element_type=jnp.float32
        )
        for k in range(2):
            for j in range(blocks):
                at = pl.ds(2 * j + k, LANES, stride=2 * blocks)
                begin = k * orbitals + j * LANES
                value = part[:, begin : begin + LANES]
                out[at, :] = value if chunks == 1 else out[at, :] + value
        return carry

    if chunks == 1:
        chunk_step(0, 0)
    else:
        out[...] = jnp.zeros_like(out)
        lax.fori_loop(0, chunks, chunk_step, 0)


def transform(n_pair, n_orb, steps, sides, pieces, orbitals):
    devices = n_pair * n_orb
    wide = CHUNK * 2 * SB
    if steps:
        held = [(sum(piece.shape[0] for piece in pieces), GROUP, LANES)]
    else:
        held = [piece.shape for piece in pieces]
    return pl.pallas_call(
        functools.partial(transform_kernel, n_pair, n_orb, steps, sides, orbitals // LANES, len(pieces)),
        out_shape=jax.ShapeDtypeStruct((2 * orbitals // LANES * LANES, LANES), jnp.float32),
        in_specs=[pl.BlockSpec(memory_space=pl.ANY)] * len(pieces),
        out_specs=pl.BlockSpec(memory_space=pltpu.VMEM),
        scratch_shapes=[pltpu.VMEM(shape, jnp.bfloat16) for shape in held]
        + [
            pltpu.VMEM((devices, LANES), jnp.int32),
            pltpu.SMEM((devices, LANES), jnp.int32),
            pltpu.VMEM((wide, 2 * orbitals), jnp.bfloat16),
            pltpu.VMEM((wide, LANES), jnp.bfloat16),
            pltpu.SemaphoreType.DMA((len(pieces),)),
            pltpu.SemaphoreType.DMA,
        ],
        compiler_params=pltpu.CompilerParams(vmem_limit_bytes=40 << 20),
        name="transform",
    )(*pieces)


def shift(array, axis, size, step):
    return lax.ppermute(array, axis, [(i, (i + step) % size) for i in range(size)])


def flip(array, axis, size, bit):
    return lax.ppermute(array, axis, [(i, i ^ bit) for i in range(size)])


def body(n_pair, n_orb, integrals, mu_block, nu_block, counts, coeff):
    slots, kets, flat = integrals.shape
    columns = kets // n_pair
    orbitals = coeff.shape[1]
    everyone = ("pair", "orb")
    if n_pair * n_orb == CHUNK and n_pair == 4:
        packed = pack(n_pair, integrals, mu_block, nu_block, counts, coeff)
        first = shift(packed[1], "pair", n_pair, 1)
        third = shift(packed[3], "pair", n_pair, 3)
        held_back, first = lax.optimization_barrier((packed[2], first))
        second = shift(held_back, "pair", n_pair, 2)
        pieces, steps, sides = [], [], []
        for s, line in enumerate([packed[0], first, second, third]):
            across = flip(line, "orb", n_orb, 2)
            pieces += [line, flip(line, "orb", n_orb, 1), across, flip(across, "orb", n_orb, 1)]
            steps += [s] * 4
            sides += [0, 1, 2, 3]
    else:
        kept = jnp.arange(slots, dtype=jnp.int32) < counts[0]
        tiles = jnp.where(kept[:, None, None], integrals, jnp.zeros_like(integrals))
        tiles = tiles.reshape(slots, n_pair, columns, SB, SB).transpose(1, 2, 3, 0, 4)
        tiles = tiles.reshape(n_pair, columns * SB, slots * SB)
        tag = jnp.where(kept[:, None], jnp.stack([mu_block, nu_block], 1), 0).reshape(-1)
        tag = jnp.zeros((n_pair, GROUP, LANES), jnp.bfloat16).at[:, :, : 2 * slots].set(tag.astype(jnp.bfloat16))
        packed = jnp.concatenate([tiles, tag], 1)
        line = lax.all_to_all(packed, "pair", split_axis=0, concat_axis=0, tiled=True)
        whole = lax.all_gather(line, "orb", axis=0, tiled=True)
        rows = lax.all_gather(coeff, everyone, axis=0, tiled=True)
        rows = rows.reshape(rows.shape[0] // GROUP, GROUP, orbitals // LANES, LANES).transpose(0, 2, 1, 3)
        pieces = [whole.reshape(-1, GROUP, LANES), rows.reshape(-1, GROUP, LANES)]
        steps, sides = None, None
    out = transform(n_pair, n_orb, steps, sides, pieces, orbitals)
    out = out.reshape(orbitals // n_orb, orbitals // LANES, columns, LANES)
    return out.transpose(0, 2, 1, 3).reshape(orbitals // n_orb, columns, orbitals)


def solution(mesh):
    placed = (
        P(("grp", "pair", "orb"), None, None),
        P(("grp", "pair", "orb")),
        P(("grp", "pair", "orb")),
        P(("grp", "pair", "orb")),
        P(("grp", "pair", "orb"), None),
    )
    return jax.shard_map(
        functools.partial(body, mesh.shape["pair"], mesh.shape["orb"]),
        mesh=mesh,
        in_specs=placed,
        out_specs=P(("grp", "orb"), "pair", None),
        check_vma=False,
    )
```

time: 38.5 us -> 40.3 us (1.047)
  the two profiles are of different devices: /device:TPU:11 before, /device:TPU:0 now
where the time goes in v3:
time: 40.3 us; the launch traced here: 40.2 us
  starting transfers between devices  17.4 us (43%)
  waiting for transfers between devices  11.7 us (29%)
  Pallas kernels  9.43 us (23%)
  local copies, waits for them, and re-layouts  0.92 us (2%)
  between operations  0.7 us (2%)
    ppermute x12, starting transfers between devices, flip(): return lax.ppermute(array, axis, [(i, i ^ bit) for i in range(size)])  11.5 us
    pallas_call x1, Pallas kernels, transform(): pl.pallas_call(functools.partial(transform_kernel, n_pair, n_orb, steps,...  7.4 us
    ppermute x12, waiting for transfers between devices, flip(): return lax.ppermute(array, axis, [(i, i ^ bit) for i in range(size)])  6.22 us
    ppermute x3, starting transfers between devices, shift(): lax.ppermute(array, axis, [(i, (i + step) % size) for i in range(size)])  5.92 us
    ppermute x3, waiting for transfers between devices, shift(): lax.ppermute(array, axis, [(i, (i + step) % size) for i in range(size)])  5.5 us
    pallas_call x1, Pallas kernels, pack(): pl.pallas_call(functools.partial(pack_kernel, n_pair), out_shape=[jax.Sha...  2.03 us
    unnamed x2, local copies, waits for them, and re-layouts  0.92 us
  transfers between devices with their start and end apart: 15, of which 5 were waited for; matrix products, arithmetic and copies ran while one was open for 0% of the time, Pallas kernels for 0%

profile of v3, /device:TPU:0, one launch (start us, length us, event | category | flops | bytes accessed | tf_op | source)
XLA Modules:
  0.0 40.2 jit_solution(11304354602997631441)
XLA Ops:
  0.7 2.0 %pack.1 = (bf16[41,16,128]{2,1,0:T(8,128)(2,1)}, bf16[41,16,128]{2,1,0:T(8,128)(2,1)}, bf16[41,16,128]{2,1,0:T(8,128)(2,1)}, bf16[41,16,128]{2,1,0:T(8,128)(2,1)}) custom-call(bf16[2,8,4096]{2,1,0:T(8,128)(2,1)} %integrals.1, s32[2]{0:T(128)} %mu.1, s32[2]{0:T(128)} %nu.1, s32[1]{0:T(128)S(6)} %copy.7.counts, bf16[128,512]{1,0:T(8,128)(2,1)} %coeff.1), custom_call_target="tpu_custom_call" | custom-call | tf_op jit(solution)/shard_map/pack/pallas_call | solution.py:79
  2.7 3.1 %collective-permute-start.3 = (bf16[41,16,128]{2,1,0:T(8,128)(2,1)}, bf16[41,16,128]{2,1,0:T(8,128)(2,1)S(1)}, u32[]{:S(2)}, u32[]{:S(2)}) collective-permute-start(bf16[41,16,128]{2,1,0:T(8,128)(2,1)} %get-tuple-element.13), channel_id=1, source_target_pairs={{0,4},{4,8},{8,12},{12,0},{1,5},{5,9},{9,13},{13,1},{2,6},{6,10},{... | collective-permute-start | bytes 503816 | tf_op jit(solution)/shard_map/ppermute | solution.py:216
  5.8 1.5 %collective-permute-start.1 = (bf16[41,16,128]{2,1,0:T(8,128)(2,1)}, bf16[41,16,128]{2,1,0:T(8,128)(2,1)S(1)}, u32[]{:S(2)}, u32[]{:S(2)}) collective-permute-start(bf16[41,16,128]{2,1,0:T(8,128)(2,1)} %get-tuple-element.11.refs_0_), channel_id=1, source_target_pairs={{0,2},{1,3},{2,0},{3,1},{4,6},{5,7},{6,4},{7,5},{8,10},{9,11},{10,... | collective-permute-start | bytes 503816 | tf_op jit(solution)/shard_map/ppermute | solution.py:220
  7.3 0.0 collective-permute-start
  7.3 2.2 %collective-permute-start.11 = (bf16[41,16,128]{2,1,0:T(8,128)(2,1)}, bf16[41,16,128]{2,1,0:T(8,128)(2,1)S(1)}, u32[]{:S(2)}, u32[]{:S(2)}) collective-permute-start(bf16[41,16,128]{2,1,0:T(8,128)(2,1)} %get-tuple-element.16), channel_id=1, source_target_pairs={{0,12},{4,0},{8,4},{12,8},{1,13},{5,1},{9,5},{13,9},{2,14},{6,2},{... | collective-permute-start | bytes 503816 | tf_op jit(solution)/shard_map/ppermute | solution.py:216
  9.5 2.9 %collective-permute-done.3.refs_4_ = bf16[41,16,128]{2,1,0:T(8,128)(2,1)S(1)} collective-permute-done((bf16[41,16,128]{2,1,0:T(8,128)(2,1)}, bf16[41,16,128]{2,1,0:T(8,128)(2,1)S(1)}, u32[]{:S(2)}, u32[]{:S(2)}) %collective-permute-start.3) | collective-permute-done | bytes 167968 | tf_op jit(solution)/shard_map/ppermute | solution.py:216
  12.4 0.6 %collective-permute-start.7 = (bf16[41,16,128]{2,1,0:T(8,128)(2,1)}, bf16[41,16,128]{2,1,0:T(8,128)(2,1)S(1)}, u32[]{:S(2)}, u32[]{:S(2)}) collective-permute-start(bf16[41,16,128]{2,1,0:T(8,128)(2,1)} %get-tuple-element.15), channel_id=1, source_target_pairs={{0,8},{4,12},{8,0},{12,4},{1,9},{5,13},{9,1},{13,5},{2,10},{6,14},... | collective-permute-start | bytes 503816 | tf_op jit(solution)/shard_map/ppermute | solution.py:216
  13.0 6.9 %collective-permute-start.5 = (bf16[41,16,128]{2,1,0:T(8,128)(2,1)S(1)}, bf16[41,16,128]{2,1,0:T(8,128)(2,1)S(1)}, u32[]{:S(2)}, u32[]{:S(2)}) collective-permute-start(bf16[41,16,128]{2,1,0:T(8,128)(2,1)S(1)} %collective-permute-done.3.refs_4_), channel_id=1, source_target_pairs={{0,2},{1,3},{2,0},{3,1},{4,6},{5,7},{6,4},{7,5},{8,10},{9,11},{10,... | collective-permute-start | bytes 503816 | tf_op jit(solution)/shard_map/ppermute | solution.py:220
  19.9 0.0 collective-permute-done.11.refs_12_
  19.9 0.0 collective-permute-start.4
  19.9 0.0 collective-permute-done.1.refs_2_
  19.9 0.1 collective-permute-start.13
  20.0 0.0 collective-permute-done.refs_1_
  20.0 0.5 %collective-permute-start.12 = (bf16[41,16,128]{2,1,0:T(8,128)(2,1)S(1)}, bf16[41,16,128]{2,1,0:T(8,128)(2,1)S(1)}, u32[]{:S(2)}, u32[]{:S(2)}) collective-permute-start(bf16[41,16,128]{2,1,0:T(8,128)(2,1)S(1)} %collective-permute-done.11.refs_12_), channel_id=1, source_target_pairs={{0,1},{1,0},{2,3},{3,2},{4,5},{5,4},{6,7},{7,6},{8,9},{9,8},{10,11... | collective-permute-start | bytes 503816 | tf_op jit(solution)/shard_map/ppermute | solution.py:220
  20.5 2.6 %collective-permute-done.7.refs_8_ = bf16[41,16,128]{2,1,0:T(8,128)(2,1)S(1)} collective-permute-done((bf16[41,16,128]{2,1,0:T(8,128)(2,1)}, bf16[41,16,128]{2,1,0:T(8,128)(2,1)S(1)}, u32[]{:S(2)}, u32[]{:S(2)}) %collective-permute-start.7) | collective-permute-done | bytes 167968 | tf_op jit(solution)/shard_map/ppermute | solution.py:216
  23.1 1.5 %collective-permute-start.9 = (bf16[41,16,128]{2,1,0:T(8,128)(2,1)S(1)}, bf16[41,16,128]{2,1,0:T(8,128)(2,1)S(1)}, u32[]{:S(2)}, u32[]{:S(2)}) collective-permute-start(bf16[41,16,128]{2,1,0:T(8,128)(2,1)S(1)} %collective-permute-done.7.refs_8_), channel_id=1, source_target_pairs={{0,2},{1,3},{2,0},{3,1},{4,6},{5,7},{6,4},{7,5},{8,10},{9,11},{10,... | collective-permute-start | bytes 503816 | tf_op jit(solution)/shard_map/ppermute | solution.py:220
  24.6 0.0 collective-permute-done.5.refs_6_
  24.6 0.0 collective-permute-start.2
  24.6 0.0 collective-permute-done.4.refs_5_
  24.6 0.5 %collective-permute-start.8 = (bf16[41,16,128]{2,1,0:T(8,128)(2,1)S(1)}, bf16[41,16,128]{2,1,0:T(8,128)(2,1)S(1)}, u32[]{:S(2)}, u32[]{:S(2)}) collective-permute-start(bf16[41,16,128]{2,1,0:T(8,128)(2,1)S(1)} %collective-permute-done.7.refs_8_), channel_id=1, source_target_pairs={{0,1},{1,0},{2,3},{3,2},{4,5},{5,4},{6,7},{7,6},{8,9},{9,8},{10,11... | collective-permute-start | bytes 503816 | tf_op jit(solution)/shard_map/ppermute | solution.py:220
  25.1 2.9 %collective-permute-done.13.refs_14_ = bf16[41,16,128]{2,1,0:T(8,128)(2,1)S(1)} collective-permute-done((bf16[41,16,128]{2,1,0:T(8,128)(2,1)S(1)}, bf16[41,16,128]{2,1,0:T(8,128)(2,1)S(1)}, u32[]{:S(2)}, u32[]{:S(2)}) %collective-permute-start.13) | collective-permute-done | bytes 167968 | tf_op jit(solution)/shard_map/ppermute | solution.py:220
  28.0 0.0 collective-permute-start.6
  28.0 0.0 collective-permute-done.12.refs_13_
  28.0 0.5 %collective-permute-start.14 = (bf16[41,16,128]{2,1,0:T(8,128)(2,1)S(1)}, bf16[41,16,128]{2,1,0:T(8,128)(2,1)S(1)}, u32[]{:S(2)}, u32[]{:S(2)}) collective-permute-start(bf16[41,16,128]{2,1,0:T(8,128)(2,1)S(1)} %collective-permute-done.13.refs_14_), channel_id=1, source_target_pairs={{0,1},{1,0},{2,3},{3,2},{4,5},{5,4},{6,7},{7,6},{8,9},{9,8},{10,11... | collective-permute-start | bytes 503816 | tf_op jit(solution)/shard_map/ppermute | solution.py:220
  28.5 1.9 %collective-permute-done.9.refs_10_ = bf16[41,16,128]{2,1,0:T(8,128)(2,1)S(1)} collective-permute-done((bf16[41,16,128]{2,1,0:T(8,128)(2,1)S(1)}, bf16[41,16,128]{2,1,0:T(8,128)(2,1)S(1)}, u32[]{:S(2)}, u32[]{:S(2)}) %collective-permute-start.9) | collective-permute-done | bytes 167968 | tf_op jit(solution)/shard_map/ppermute | solution.py:220
  30.4 0.0 collective-permute-start.10
  30.5 0.0 collective-permute-done.2.refs_3_
  30.5 0.0 collective-permute-done.8.refs_9_
  30.5 0.0 collective-permute-done.6.refs_7_
  30.5 0.0 collective-permute-done.14.refs_15_
  30.5 1.4 %collective-permute-done.10.refs_11_ = bf16[41,16,128]{2,1,0:T(8,128)(2,1)S(1)} collective-permute-done((bf16[41,16,128]{2,1,0:T(8,128)(2,1)S(1)}, bf16[41,16,128]{2,1,0:T(8,128)(2,1)S(1)}, u32[]{:S(2)}, u32[]{:S(2)}) %collective-permute-start.10) | collective-permute-done | bytes 167968 | tf_op jit(solution)/shard_map/ppermute | solution.py:220
  31.8 0.0 copy-start
  31.9 0.9 %copy-done = bf16[41,16,128]{2,1,0:T(8,128)(2,1)S(1)} copy-done((bf16[41,16,128]{2,1,0:T(8,128)(2,1)S(1)}, bf16[41,16,128]{2,1,0:T(8,128)(2,1)}, u32[]{:S(2)}) %copy-start) | copy-done | bytes 167960
  32.8 7.4 %transform.1 = f32[1024,128]{1,0:T(8,128)} custom-call(bf16[41,16,128]{2,1,0:T(8,128)(2,1)S(1)} %copy-done, bf16[41,16,128]{2,1,0:T(8,128)(2,1)S(1)} %collective-permute-done.refs_1_, bf16[41,16,128]{2,1,0:T(8,128)(2,1)S(1)} %collective-permute-done.1.refs_2_, bf16[41,16,128]{2,1,0:T(8,128)(2,1)S(1)} %collective-permute-done.2.refs_3_, ...), custom_call_target="tpu_custom_call" | custom-call | tf_op jit(solution)/shard_map/transform/pallas_call | solution.py:196
Async XLA Ops:
  2.7 9.7 %collective-permute-start.3 = (bf16[41,16,128]{2,1,0:T(8,128)(2,1)}, bf16[41,16,128]{2,1,0:T(8,128)(2,1)S(1)}, u32[]{:S(2)}, u32[]{:S(2)}) collective-permute-start(bf16[41,16,128]{2,1,0:T(8,128)(2,1)} %get-tuple-element.13), channel_id=1, source_target_pairs={{0,4},{4,8},{8,12},{12,0},{1,5},{5,9},{9,13},{13,1},{2,6},{6,10},{... | collective-permute-start | bytes 503816 | tf_op jit(solution)/shard_map/ppermute | solution.py:216
  5.8 14.1 %collective-permute-start.1 = (bf16[41,16,128]{2,1,0:T(8,128)(2,1)}, bf16[41,16,128]{2,1,0:T(8,128)(2,1)S(1)}, u32[]{:S(2)}, u32[]{:S(2)}) collective-permute-start(bf16[41,16,128]{2,1,0:T(8,128)(2,1)} %get-tuple-element.11.refs_0_), channel_id=1, source_target_pairs={{0,2},{1,3},{2,0},{3,1},{4,6},{5,7},{6,4},{7,5},{8,10},{9,11},{10,... | collective-permute-start | bytes 503816 | tf_op jit(solution)/shard_map/ppermute | solution.py:220
  7.3 12.7 %collective-permute-start = (bf16[41,16,128]{2,1,0:T(8,128)(2,1)}, bf16[41,16,128]{2,1,0:T(8,128)(2,1)S(1)}, u32[]{:S(2)}, u32[]{:S(2)}) collective-permute-start(bf16[41,16,128]{2,1,0:T(8,128)(2,1)} %get-tuple-element.11.refs_0_), channel_id=1, source_target_pairs={{0,1},{1,0},{2,3},{3,2},{4,5},{5,4},{6,7},{7,6},{8,9},{9,8},{10,11... | collective-permute-start | bytes 503816 | tf_op jit(solution)/shard_map/ppermute | solution.py:220
  7.3 12.6 %collective-permute-start.11 = (bf16[41,16,128]{2,1,0:T(8,128)(2,1)}, bf16[41,16,128]{2,1,0:T(8,128)(2,1)S(1)}, u32[]{:S(2)}, u32[]{:S(2)}) collective-permute-start(bf16[41,16,128]{2,1,0:T(8,128)(2,1)} %get-tuple-element.16), channel_id=1, source_target_pairs={{0,12},{4,0},{8,4},{12,8},{1,13},{5,1},{9,5},{13,9},{2,14},{6,2},{... | collective-permute-start | bytes 503816 | tf_op jit(solution)/shard_map/ppermute | solution.py:216
  12.4 10.7 %collective-permute-start.7 = (bf16[41,16,128]{2,1,0:T(8,128)(2,1)}, bf16[41,16,128]{2,1,0:T(8,128)(2,1)S(1)}, u32[]{:S(2)}, u32[]{:S(2)}) collective-permute-start(bf16[41,16,128]{2,1,0:T(8,128)(2,1)} %get-tuple-element.15), channel_id=1, source_target_pairs={{0,8},{4,12},{8,0},{12,4},{1,9},{5,13},{9,1},{13,5},{2,10},{6,14},... | collective-permute-start | bytes 503816 | tf_op jit(solution)/shard_map/ppermute | solution.py:216
  13.0 11.6 %collective-permute-start.5 = (bf16[41,16,128]{2,1,0:T(8,128)(2,1)S(1)}, bf16[41,16,128]{2,1,0:T(8,128)(2,1)S(1)}, u32[]{:S(2)}, u32[]{:S(2)}) collective-permute-start(bf16[41,16,128]{2,1,0:T(8,128)(2,1)S(1)} %collective-permute-done.3.refs_4_), channel_id=1, source_target_pairs={{0,2},{1,3},{2,0},{3,1},{4,6},{5,7},{6,4},{7,5},{8,10},{9,11},{10,... | collective-permute-start | bytes 503816 | tf_op jit(solution)/shard_map/ppermute | solution.py:220
  19.9 4.7 %collective-permute-start.4 = (bf16[41,16,128]{2,1,0:T(8,128)(2,1)S(1)}, bf16[41,16,128]{2,1,0:T(8,128)(2,1)S(1)}, u32[]{:S(2)}, u32[]{:S(2)}) collective-permute-start(bf16[41,16,128]{2,1,0:T(8,128)(2,1)S(1)} %collective-permute-done.3.refs_4_), channel_id=1, source_target_pairs={{0,1},{1,0},{2,3},{3,2},{4,5},{5,4},{6,7},{7,6},{8,9},{9,8},{10,11... | collective-permute-start | bytes 503816 | tf_op jit(solution)/shard_map/ppermute | solution.py:220
  19.9 8.1 %collective-permute-start.13 = (bf16[41,16,128]{2,1,0:T(8,128)(2,1)S(1)}, bf16[41,16,128]{2,1,0:T(8,128)(2,1)S(1)}, u32[]{:S(2)}, u32[]{:S(2)}) collective-permute-start(bf16[41,16,128]{2,1,0:T(8,128)(2,1)S(1)} %collective-permute-done.11.refs_12_), channel_id=1, source_target_pairs={{0,2},{1,3},{2,0},{3,1},{4,6},{5,7},{6,4},{7,5},{8,10},{9,11},{10,... | collective-permute-start | bytes 503816 | tf_op jit(solution)/shard_map/ppermute | solution.py:220
  20.0 8.0 %collective-permute-start.12 = (bf16[41,16,128]{2,1,0:T(8,128)(2,1)S(1)}, bf16[41,16,128]{2,1,0:T(8,128)(2,1)S(1)}, u32[]{:S(2)}, u32[]{:S(2)}) collective-permute-start(bf16[41,16,128]{2,1,0:T(8,128)(2,1)S(1)} %collective-permute-done.11.refs_12_), channel_id=1, source_target_pairs={{0,1},{1,0},{2,3},{3,2},{4,5},{5,4},{6,7},{7,6},{8,9},{9,8},{10,11... | collective-permute-start | bytes 503816 | tf_op jit(solution)/shard_map/ppermute | solution.py:220
  23.1 7.4 %collective-permute-start.9 = (bf16[41,16,128]{2,1,0:T(8,128)(2,1)S(1)}, bf16[41,16,128]{2,1,0:T(8,128)(2,1)S(1)}, u32[]{:S(2)}, u32[]{:S(2)}) collective-permute-start(bf16[41,16,128]{2,1,0:T(8,128)(2,1)S(1)} %collective-permute-done.7.refs_8_), channel_id=1, source_target_pairs={{0,2},{1,3},{2,0},{3,1},{4,6},{5,7},{6,4},{7,5},{8,10},{9,11},{10,... | collective-permute-start | bytes 503816 | tf_op jit(solution)/shard_map/ppermute | solution.py:220
  24.6 5.9 %collective-permute-start.2 = (bf16[41,16,128]{2,1,0:T(8,128)(2,1)S(1)}, bf16[41,16,128]{2,1,0:T(8,128)(2,1)S(1)}, u32[]{:S(2)}, u32[]{:S(2)}) collective-permute-start(bf16[41,16,128]{2,1,0:T(8,128)(2,1)S(1)} %collective-permute-done.1.refs_2_), channel_id=1, source_target_pairs={{0,1},{1,0},{2,3},{3,2},{4,5},{5,4},{6,7},{7,6},{8,9},{9,8},{10,11... | collective-permute-start | bytes 503816 | tf_op jit(solution)/shard_map/ppermute | solution.py:220
  24.6 5.9 %collective-permute-start.8 = (bf16[41,16,128]{2,1,0:T(8,128)(2,1)S(1)}, bf16[41,16,128]{2,1,0:T(8,128)(2,1)S(1)}, u32[]{:S(2)}, u32[]{:S(2)}) collective-permute-start(bf16[41,16,128]{2,1,0:T(8,128)(2,1)S(1)} %collective-permute-done.7.refs_8_), channel_id=1, source_target_pairs={{0,1},{1,0},{2,3},{3,2},{4,5},{5,4},{6,7},{7,6},{8,9},{9,8},{10,11... | collective-permute-start | bytes 503816 | tf_op jit(solution)/shard_map/ppermute | solution.py:220
  28.0 2.4 %collective-permute-start.6 = (bf16[41,16,128]{2,1,0:T(8,128)(2,1)S(1)}, bf16[41,16,128]{2,1,0:T(8,128)(2,1)S(1)}, u32[]{:S(2)}, u32[]{:S(2)}) collective-permute-start(bf16[41,16,128]{2,1,0:T(8,128)(2,1)S(1)} %collective-permute-done.5.refs_6_), channel_id=1, source_target_pairs={{0,1},{1,0},{2,3},{3,2},{4,5},{5,4},{6,7},{7,6},{8,9},{9,8},{10,11... | collective-permute-start | bytes 503816 | tf_op jit(solution)/shard_map/ppermute | solution.py:220
  28.0 2.4 %collective-permute-start.14 = (bf16[41,16,128]{2,1,0:T(8,128)(2,1)S(1)}, bf16[41,16,128]{2,1,0:T(8,128)(2,1)S(1)}, u32[]{:S(2)}, u32[]{:S(2)}) collective-permute-start(bf16[41,16,128]{2,1,0:T(8,128)(2,1)S(1)} %collective-permute-done.13.refs_14_), channel_id=1, source_target_pairs={{0,1},{1,0},{2,3},{3,2},{4,5},{5,4},{6,7},{7,6},{8,9},{9,8},{10,11... | collective-permute-start | bytes 503816 | tf_op jit(solution)/shard_map/ppermute | solution.py:220
  30.4 1.4 %collective-permute-start.10 = (bf16[41,16,128]{2,1,0:T(8,128)(2,1)S(1)}, bf16[41,16,128]{2,1,0:T(8,128)(2,1)S(1)}, u32[]{:S(2)}, u32[]{:S(2)}) collective-permute-start(bf16[41,16,128]{2,1,0:T(8,128)(2,1)S(1)} %collective-permute-done.9.refs_10_), channel_id=1, source_target_pairs={{0,1},{1,0},{2,3},{3,2},{4,5},{5,4},{6,7},{7,6},{8,9},{9,8},{10,11... | collective-permute-start | bytes 503816 | tf_op jit(solution)/shard_map/ppermute | solution.py:220
  31.8 0.9 %copy-start = (bf16[41,16,128]{2,1,0:T(8,128)(2,1)S(1)}, bf16[41,16,128]{2,1,0:T(8,128)(2,1)}, u32[]{:S(2)}) copy-start(bf16[41,16,128]{2,1,0:T(8,128)(2,1)} %get-tuple-element.11.refs_0_) | copy-start | bytes 503812

commit v4 on v3

v4 whole, which is shorter than its diff:
```python
import functools

import jax
import jax.numpy as jnp
from jax import lax
from jax.experimental import pallas as pl
from jax.experimental.pallas import tpu as pltpu
from jax.sharding import PartitionSpec as P

SB = 64
LANES = 128
GROUP = 16
CHUNK = 16


def pack_kernel(n_pair, integrals, mu, nu, counts, out, tiles, mu_in, nu_in, spread, woven, sems):
    copies = [
        pltpu.make_async_copy(source, target, sems.at[n])
        for n, (source, target) in enumerate(((integrals, tiles), (mu, mu_in), (nu, nu_in)))
    ]
    for copy in copies:
        copy.start()
    slots, kets, flat = tiles.shape
    wide = flat // LANES
    columns = kets // n_pair
    for copy in copies[1:]:
        copy.wait()
    count = counts[0]
    lane = lax.broadcasted_iota(jnp.int32, (wide, LANES), 1)
    low, kept = lane < SB, lane < SB * count
    lane = lax.broadcasted_iota(jnp.int32, (GROUP, LANES), 1)
    tag = jnp.zeros((GROUP, LANES), jnp.int32)
    for t in range(slots):
        tag = jnp.where((lane == 2 * t) & (t < count), mu_in[t], tag)
        tag = jnp.where((lane == 2 * t + 1) & (t < count), nu_in[t], tag)
    tag = tag.astype(jnp.float32).astype(jnp.bfloat16)
    copies[0].wait()
    for t in range(slots):
        for j in range(wide):
            at = pl.ds((t * wide + j) * kets, kets)
            spread[at, :] = tiles[t, :, j * LANES : (j + 1) * LANES].astype(jnp.float32)
    tiled = columns * SB // GROUP
    for dest in range(n_pair):
        for k in range(columns):
            column = dest * columns + k
            one = spread[pl.ds(column, wide, stride=kets), :]
            two = spread[pl.ds(wide * kets + column, wide, stride=kets), :]
            even = jnp.where(low, one, pltpu.roll(two, SB, axis=1))
            odd = jnp.where(low, pltpu.roll(one, SB, axis=1), two)
            begin = column * SB
            woven[pl.ds(begin, wide, stride=2), :] = jnp.where(kept, even, 0.0)
            woven[pl.ds(begin + 1, wide, stride=2), :] = jnp.where(kept, odd, 0.0)
        for g in range(tiled):
            rows_at = pl.ds((dest * tiled + g) * GROUP, GROUP)
            out[dest, g] = woven[rows_at, :].astype(jnp.bfloat16)
        out[dest, tiled] = tag


def pack(n_pair, integrals, mu, nu, counts):
    slots, kets, flat = integrals.shape
    groups = kets // n_pair * SB // GROUP + 1
    hbm, smem = pl.BlockSpec(memory_space=pltpu.HBM), pl.BlockSpec(memory_space=pltpu.SMEM)
    return pl.pallas_call(
        functools.partial(pack_kernel, n_pair),
        out_shape=jax.ShapeDtypeStruct((n_pair, groups, GROUP, LANES), jnp.bfloat16),
        in_specs=[hbm, hbm, hbm, smem],
        out_specs=pl.BlockSpec(memory_space=pltpu.VMEM),
        scratch_shapes=[
            pltpu.VMEM(integrals.shape, jnp.bfloat16),
            pltpu.SMEM(mu.shape, jnp.int32),
            pltpu.SMEM(nu.shape, jnp.int32),
            pltpu.VMEM((slots * kets * flat // LANES, LANES), jnp.float32),
            pltpu.VMEM((kets * SB, LANES), jnp.float32),
            pltpu.SemaphoreType.DMA((3,)),
        ],
        compiler_params=pltpu.CompilerParams(vmem_limit_bytes=60 << 20),
        name="pack",
    )(integrals, mu, nu, counts)


def transform_kernel(source_of, n_c, n_x, *refs):
    c_in, x_in = refs[:n_c], refs[n_c : n_c + n_x]
    out, c_all, x_all, tags, codes, index, half, left, sems = refs[n_c + n_x :]
    o = lax.axis_index("orb")
    devices = codes.shape[0]
    orbitals = c_all.shape[1]
    blocks = orbitals // LANES
    tiled = 2 * SB // GROUP
    early, late = [], []
    per = devices // n_x
    for q, piece in enumerate(x_in):
        place = pl.ds(q * per, per)
        early.append(pltpu.make_async_copy(piece.at[:, tiled], tags.at[place], sems.at[q]))
        late.append(pltpu.make_async_copy(piece.at[:, pl.ds(0, tiled)], x_all.at[place], sems.at[n_x + q]))
    for q, piece in enumerate(c_in):
        rows = c_all.shape[0] // n_c
        place = pl.ds(pl.multiple_of(source_of(q) * rows, rows), rows)
        late.append(pltpu.make_async_copy(piece, c_all.at[place], sems.at[2 * n_x + q]))
    for copy in early + late:
        copy.start()
    for copy in early:
        copy.wait()
    codes[...] = tags[:, 0, :].astype(jnp.float32).astype(jnp.int32)
    to_scalars = pltpu.make_async_copy(codes, index, sems.at[2 * n_x + n_c])
    to_scalars.start()
    to_scalars.wait()
    for copy in late:
        copy.wait()

    mine = pl.ds(pl.multiple_of(o * LANES, LANES), LANES)
    low = lax.broadcasted_iota(jnp.int32, (SB, LANES), 1) < SB
    chunks = devices // CHUNK

    def rows_of(block):
        return pl.ds(pl.multiple_of(block * SB, SB), SB)

    def chunk_step(chunk, carry):
        for d in range(CHUNK):
            device = chunk * CHUNK + d
            stacked = []
            for k in range(2):
                tile = jnp.concatenate([x_all[device, k * (tiled // 2) + g] for g in range(tiled // 2)], 0)
                stacked += [jnp.where(low, tile, jnp.zeros_like(tile)), jnp.where(low, jnp.zeros_like(tile), tile)]
            mu_one, nu_one, mu_two, nu_two = (index[device, n] for n in range(4))
            rows = jnp.concatenate([c_all[rows_of(nu_one)], c_all[rows_of(nu_two)]], 0)
            moved = jnp.dot(jnp.concatenate(stacked, 0), rows, preferred_element_type=jnp.float32)
            moved = moved.astype(jnp.bfloat16)
            at = pl.ds(d * 2 * SB, 2 * SB)
            half[at, :orbitals] = moved[: 2 * SB]
            half[at, orbitals:] = moved[2 * SB :]
            left[at, :] = jnp.concatenate([c_all[rows_of(mu_one), mine], c_all[rows_of(mu_two), mine]], 0)
        part = lax.dot_general(
            left[...], half[...], (((0,), (0,)), ((), ())), preferred_element_type=jnp.float32
        )
        for k in range(2):
            for j in range(blocks):
                at = pl.ds(2 * j + k, LANES, stride=2 * blocks)
                begin = k * orbitals + j * LANES
                value = part[:, begin : begin + LANES]
                out[at, :] = value if chunks == 1 else out[at, :] + value
        return carry

    if chunks == 1:
        chunk_step(0, 0)
    else:
        out[...] = jnp.zeros_like(out)
        lax.fori_loop(0, chunks, chunk_step, 0)


def transform(source_of, c_pieces, x_pieces):
    orbitals = c_pieces[0].shape[1]
    devices = sum(piece.shape[0] for piece in x_pieces)
    n_c, n_x = len(c_pieces), len(x_pieces)
    wide = CHUNK * 2 * SB
    return pl.pallas_call(
        functools.partial(transform_kernel, source_of, n_c, n_x),
        out_shape=jax.ShapeDtypeStruct((2 * orbitals // LANES * LANES, LANES), jnp.float32),
        in_specs=[pl.BlockSpec(memory_space=pl.ANY)] * (n_c + n_x),
        out_specs=pl.BlockSpec(memory_space=pltpu.VMEM),
        scratch_shapes=[
            pltpu.VMEM((c_pieces[0].shape[0] * n_c, orbitals), jnp.bfloat16),
            pltpu.VMEM((devices, 2 * SB // GROUP, GROUP, LANES), jnp.bfloat16),
            pltpu.VMEM((devices, GROUP, LANES), jnp.bfloat16),
            pltpu.VMEM((devices, LANES), jnp.int32),
            pltpu.SMEM((devices, LANES), jnp.int32),
            pltpu.VMEM((wide, 2 * orbitals), jnp.bfloat16),
            pltpu.VMEM((wide, LANES), jnp.bfloat16),
            pltpu.SemaphoreType.DMA((n_c + 2 * n_x + 1,)),
        ],
        compiler_params=pltpu.CompilerParams(vmem_limit_bytes=40 << 20),
        name="transform",
    )(*c_pieces, *x_pieces)


def flip(array, axis, size, bit):
    return lax.ppermute(array, axis, [(i, i ^ bit) for i in range(size)])


def around(n_pair, n_orb, core, step):
    length = 2 * n_pair
    far = n_orb // 2
    stops = [p * n_orb + core for p in range(n_pair)] + [p * n_orb + far + core for p in reversed(range(n_pair))]
    return [(stops[r], stops[(r + step) % length]) for r in range(length)]


def ring_source(n_pair, n_orb, step, flipped):
    p, o = lax.axis_index("pair"), lax.axis_index("orb")
    length = 2 * n_pair
    column = lax.div(o, 2)
    place = jnp.where(column == 0, p, length - 1 - p)
    place = lax.rem(place + length - step, length)
    second = (place >= n_pair).astype(jnp.int32)
    source = jnp.where(second == 1, length - 1 - place, place)
    return source * n_orb + 2 * second + (lax.rem(o, 2) ^ flipped)


def body(n_pair, n_orb, integrals, mu_block, nu_block, counts, coeff):
    slots, kets, flat = integrals.shape
    columns = kets // n_pair
    orbitals = coeff.shape[1]
    everyone = ("pair", "orb")
    if n_orb == 4 and n_pair <= 4:
        forward = around(n_pair, n_orb, 0, 1) + around(n_pair, n_orb, 1, 1)
        backward = [(b, a) for a, b in forward]
        held = {0: coeff}
        for step in range(1, n_pair + 1):
            held[step] = lax.ppermute(held[step - 1], everyone, forward)
            if step < n_pair:
                held[-step] = lax.ppermute(held[1 - step], everyone, backward)
        packed = pack(n_pair, integrals, mu_block, nu_block, counts)
        line = lax.all_to_all(packed, "pair", split_axis=0, concat_axis=0, tiled=True)
        across = flip(line, "orb", n_orb, 2)
        x_pieces = [line, flip(line, "orb", n_orb, 1), across, flip(across, "orb", n_orb, 1)]
        c_pieces, came = [], []
        for step, piece in held.items():
            c_pieces += [piece, flip(piece, "orb", n_orb, 1)]
            came += [(step % (2 * n_pair), 0), (step % (2 * n_pair), 1)]

        def source_of(q):
            return ring_source(n_pair, n_orb, *came[q])
    else:
        kept = jnp.arange(slots, dtype=jnp.int32) < counts[0]
        tiles = jnp.where(kept[:, None, None], integrals, jnp.zeros_like(integrals))
        tiles = tiles.reshape(slots, n_pair, columns, SB, SB).transpose(1, 2, 3, 0, 4)
        tiles = tiles.reshape(n_pair, columns * SB, slots * SB)
        tag = jnp.where(kept[:, None], jnp.stack([mu_block, nu_block], 1), 0).reshape(-1)
        tag = jnp.zeros((n_pair, GROUP, LANES), jnp.bfloat16).at[:, :, : 2 * slots].set(tag.astype(jnp.bfloat16))
        packed = jnp.concatenate([tiles, tag], 1).reshape(n_pair, -1, GROUP, LANES)
        line = lax.all_to_all(packed, "pair", split_axis=0, concat_axis=0, tiled=True)
        x_pieces = [lax.all_gather(line, "orb", axis=0, tiled=True)]
        c_pieces = [lax.all_gather(coeff, everyone, axis=0, tiled=True)]

        def source_of(q):
            return q
    out = transform(source_of, c_pieces, x_pieces)
    out = out.reshape(orbitals // n_orb, orbitals // LANES, columns, LANES)
    return out.transpose(0, 2, 1, 3).reshape(orbitals // n_orb, columns, orbitals)


def solution(mesh):
    placed = (
        P(("grp", "pair", "orb"), None, None),
        P(("grp", "pair", "orb")),
        P(("grp", "pair", "orb")),
        P(("grp", "pair", "orb")),
        P(("grp", "pair", "orb"), None),
    )
    return jax.shard_map(
        functools.partial(body, mesh.shape["pair"], mesh.shape["orb"]),
        mesh=mesh,
        in_specs=placed,
        out_specs=P(("grp", "orb"), "pair", None),
        check_vma=False,
    )
```

time: 40.3 us -> 39.1 us (0.970)
  waiting for transfers between devices: 11.7 us -> 14.1 us
  starting transfers between devices: 17.4 us -> 15.2 us
  local copies, waits for them, and re-layouts: 0.92 us -> 0.01 us
  Pallas kernels: 9.43 us -> 8.85 us
    ppermute x12 -> x11, starting transfers between devices: 11.5 us -> 1.1 us  [flip(): return lax.ppermute(array, axis, [(i, i ^ bit) for i in range(size)])]
    all_to_all x0 -> x1, starting transfers between devices: none -> 4.93 us  [body(): lax.all_to_all(packed, 'pair', split_axis=0, concat_axis=0, tiled=True)]
    all_to_all x0 -> x1, waiting for transfers between devices: none -> 4.02 us  [body(): lax.all_to_all(packed, 'pair', split_axis=0, concat_axis=0, tiled=True)]
    ppermute x3 -> x7, starting transfers between devices: 5.92 us -> 9.16 us  [the longest x4 6.91 us: body(): held[step] = lax.ppermute(held[step - 1], everyone, forward)]
    ppermute x12 -> x11, waiting for transfers between devices: 6.22 us -> 3.56 us  [flip(): return lax.ppermute(array, axis, [(i, i ^ bit) for i in range(size)])]
    ppermute x3 -> x7, waiting for transfers between devices: 5.5 us -> 6.54 us  [the longest x4 4.51 us: body(): held[step] = lax.ppermute(held[step - 1], everyone, forward)]
    unnamed x2, local copies, waits for them, and re-layouts: 0.92 us -> 0.01 us
    pallas_call x2, Pallas kernels: 9.43 us -> 8.85 us  [the longest x1 7.07 us: transform(): pl.pallas_call(functools.partial(transform_kernel, source_of, n_c, n_x),...]
  transfers between devices with their start and end apart: 15 -> 19, of which waited for: 5 -> 8; matrix products, arithmetic and copies ran while one was open for 0% -> 0% of each run, Pallas kernels for 0% -> 5%
where the time goes in v4:
time: 39.1 us; the launch traced here: 38.9 us
  starting transfers between devices  15.2 us (39%)
  waiting for transfers between devices  14.1 us (36%)
  Pallas kernels  8.85 us (23%)
  between operations  0.71 us (2%)
    pallas_call x1, Pallas kernels, transform(): pl.pallas_call(functools.partial(transform_kernel, source_of, n_c, n_x),...  7.07 us
    ppermute x4, starting transfers between devices, body(): held[step] = lax.ppermute(held[step - 1], everyone, forward)  6.91 us
    all_to_all x1, starting transfers between devices, body(): lax.all_to_all(packed, 'pair', split_axis=0, concat_axis=0, tiled=True)  4.93 us
    ppermute x4, waiting for transfers between devices, body(): held[step] = lax.ppermute(held[step - 1], everyone, forward)  4.51 us
    all_to_all x1, waiting for transfers between devices, body(): lax.all_to_all(packed, 'pair', split_axis=0, concat_axis=0, tiled=True)  4.02 us
    ppermute x11, waiting for transfers between devices, flip(): return lax.ppermute(array, axis, [(i, i ^ bit) for i in range(size)])  3.56 us
    ppermute x3, starting transfers between devices, body(): held[-step] = lax.ppermute(held[1 - step], everyone, backward)  2.25 us
    ppermute x3, waiting for transfers between devices, body(): held[-step] = lax.ppermute(held[1 - step], everyone, backward)  2.03 us
  transfers between devices with their start and end apart: 19, of which 8 were waited for; matrix products, arithmetic and copies ran while one was open for 0% of the time, Pallas kernels for 5%

profile of v4, /device:TPU:0, one launch (start us, length us, event | category | flops | bytes accessed | tf_op | source)
XLA Modules:
  0.0 38.9 jit_solution(18307640208230367043)
XLA Ops:
  0.0 3.0 %collective-permute-start.1 = (bf16[128,512]{1,0:T(8,128)(2,1)}, bf16[128,512]{1,0:T(8,128)(2,1)S(1)}, u32[]{:S(2)}, u32[]{:S(2)}) collective-permute-start(bf16[128,512]{1,0:T(8,128)(2,1)} %refs_0_.1), channel_id=1, source_target_pairs={{0,4},{4,8},{8,12},{12,14},{14,10},{10,6},{6,2},{2,0},{1,5},{5,9},... | collective-permute-start | bytes 393224 | tf_op jit(solution)/shard_map/ppermute | solution.py:207
  3.0 0.0 collective-permute-start.3
  3.0 3.6 %collective-permute-done.1.refs_2_ = bf16[128,512]{1,0:T(8,128)(2,1)S(1)} collective-permute-done((bf16[128,512]{1,0:T(8,128)(2,1)}, bf16[128,512]{1,0:T(8,128)(2,1)S(1)}, u32[]{:S(2)}, u32[]{:S(2)}) %collective-permute-start.1) | collective-permute-done | bytes 131104 | tf_op jit(solution)/shard_map/ppermute | solution.py:207
  6.6 1.8 %collective-permute-start.5 = (bf16[128,512]{1,0:T(8,128)(2,1)S(1)}, bf16[128,512]{1,0:T(8,128)(2,1)S(1)}, u32[]{:S(2)}, u32[]{:S(2)}) collective-permute-start(bf16[128,512]{1,0:T(8,128)(2,1)S(1)} %collective-permute-done.1.refs_2_), channel_id=1, source_target_pairs={{0,4},{4,8},{8,12},{12,14},{14,10},{10,6},{6,2},{2,0},{1,5},{5,9},... | collective-permute-start | bytes 393224 | tf_op jit(solution)/shard_map/ppermute | solution.py:207
  9.1 1.8 %pack.1 = bf16[4,9,16,128]{3,2,1,0:T(8,128)(2,1)} custom-call(bf16[2,8,4096]{2,1,0:T(8,128)(2,1)} %integrals.1, s32[2]{0:T(128)} %mu.1, s32[2]{0:T(128)} %nu.1, s32[1]{0:T(128)S(6)} %copy.7.counts), custom_call_target="tpu_custom_call" | custom-call | tf_op jit(solution)/shard_map/pack/pallas_call | solution.py:63
  10.9 0.0 copy-start
  10.9 4.9 %all-to-all-start = ((bf16[4,9,16,128]{3,2,1,0:T(8,128)(2,1)}), bf16[4,9,16,128]{3,2,1,0:T(8,128)(2,1)S(1)}, u32[]{:S(2)}, u32[]{:S(2)}) async-start(bf16[4,9,16,128]{3,2,1,0:T(8,128)(2,1)} %pack.1), calls=%async_computation | async-start | bytes 294912 | tf_op jit(solution)/shard_map/all_to_all | solution.py:211
  15.9 0.0 copy-done
  15.9 0.0 collective-permute-start
  15.9 0.5 %collective-permute-start.2 = (bf16[128,512]{1,0:T(8,128)(2,1)S(1)}, bf16[128,512]{1,0:T(8,128)(2,1)S(1)}, u32[]{:S(2)}, u32[]{:S(2)}) collective-permute-start(bf16[128,512]{1,0:T(8,128)(2,1)S(1)} %collective-permute-done.1.refs_2_), channel_id=1, source_target_pairs={{0,1},{1,0},{2,3},{3,2},{4,5},{5,4},{6,7},{7,6},{8,9},{9,8},{10,11... | collective-permute-start | bytes 393224 | tf_op jit(solution)/shard_map/ppermute | solution.py:176
  16.4 0.0 collective-permute-done.3.refs_4_
  16.4 0.5 %collective-permute-start.7 = (bf16[128,512]{1,0:T(8,128)(2,1)S(1)}, bf16[128,512]{1,0:T(8,128)(2,1)S(1)}, u32[]{:S(2)}, u32[]{:S(2)}) collective-permute-start(bf16[128,512]{1,0:T(8,128)(2,1)S(1)} %collective-permute-done.3.refs_4_), channel_id=1, source_target_pairs={{4,0},{8,4},{12,8},{14,12},{10,14},{6,10},{2,6},{0,2},{5,1},{9,5},... | collective-permute-start | bytes 393224 | tf_op jit(solution)/shard_map/ppermute | solution.py:209
  16.8 0.0 collective-permute-start.4
  16.8 0.0 collective-permute-done.5.refs_6_
  16.8 1.6 %collective-permute-start.9 = (bf16[128,512]{1,0:T(8,128)(2,1)S(1)}, bf16[128,512]{1,0:T(8,128)(2,1)S(1)}, u32[]{:S(2)}, u32[]{:S(2)}) collective-permute-start(bf16[128,512]{1,0:T(8,128)(2,1)S(1)} %collective-permute-done.5.refs_6_), channel_id=1, source_target_pairs={{0,4},{4,8},{8,12},{12,14},{14,10},{10,6},{6,2},{2,0},{1,5},{5,9},... | collective-permute-start | bytes 393224 | tf_op jit(solution)/shard_map/ppermute | solution.py:207
  18.5 0.0 collective-permute-done.refs_1_
  18.5 4.0 %all-to-all-done.refs_16_ = bf16[4,9,16,128]{3,2,1,0:T(8,128)(2,1)S(1)} async-done(((bf16[4,9,16,128]{3,2,1,0:T(8,128)(2,1)}), bf16[4,9,16,128]{3,2,1,0:T(8,128)(2,1)S(1)}, u32[]{:S(2)}, u32[]{:S(2)}) %all-to-all-start) | async-done | bytes 147488 | tf_op jit(solution)/shard_map/all_to_all | solution.py:211
  22.5 0.0 collective-permute-start.16
  22.5 0.0 collective-permute-done.2.refs_3_
  22.5 0.0 collective-permute-start.15
  22.5 0.7 %collective-permute-done.7.refs_8_ = bf16[128,512]{1,0:T(8,128)(2,1)S(1)} collective-permute-done((bf16[128,512]{1,0:T(8,128)(2,1)S(1)}, bf16[128,512]{1,0:T(8,128)(2,1)S(1)}, u32[]{:S(2)}, u32[]{:S(2)}) %collective-permute-start.7) | collective-permute-done | bytes 131104 | tf_op jit(solution)/shard_map/ppermute | solution.py:209
  23.2 0.0 collective-permute-start.6
  23.2 0.0 collective-permute-done.4.refs_5_
  23.2 1.8 %collective-permute-start.11 = (bf16[128,512]{1,0:T(8,128)(2,1)S(1)}, bf16[128,512]{1,0:T(8,128)(2,1)S(1)}, u32[]{:S(2)}, u32[]{:S(2)}) collective-permute-start(bf16[128,512]{1,0:T(8,128)(2,1)S(1)} %collective-permute-done.7.refs_8_), channel_id=1, source_target_pairs={{4,0},{8,4},{12,8},{14,12},{10,14},{6,10},{2,6},{0,2},{5,1},{9,5},... | collective-permute-start | bytes 393224 | tf_op jit(solution)/shard_map/ppermute | solution.py:209
  25.0 0.0 collective-permute-done.9.refs_10_
  25.0 0.4 %collective-permute-start.13 = (bf16[128,512]{1,0:T(8,128)(2,1)S(1)}, bf16[128,512]{1,0:T(8,128)(2,1)S(1)}, u32[]{:S(2)}, u32[]{:S(2)}) collective-permute-start(bf16[128,512]{1,0:T(8,128)(2,1)S(1)} %collective-permute-done.9.refs_10_), channel_id=1, source_target_pairs={{0,4},{4,8},{8,12},{12,14},{14,10},{10,6},{6,2},{2,0},{1,5},{5,9},... | collective-permute-start | bytes 393224 | tf_op jit(solution)/shard_map/ppermute | solution.py:207
  25.5 2.2 %collective-permute-done.16.refs_18_ = bf16[4,9,16,128]{3,2,1,0:T(8,128)(2,1)S(1)} collective-permute-done((bf16[4,9,16,128]{3,2,1,0:T(8,128)(2,1)S(1)}, bf16[4,9,16,128]{3,2,1,0:T(8,128)(2,1)S(1)}, u32[]{:S(2)}, u32[]{:S(2)}) %collective-permute-start.16) | collective-permute-done | bytes 147488 | tf_op jit(solution)/shard_map/ppermute | solution.py:176
  27.7 0.0 collective-permute-start.17
  27.7 0.0 collective-permute-done.15.refs_17_
  27.7 0.5 %collective-permute-start.8 = (bf16[128,512]{1,0:T(8,128)(2,1)S(1)}, bf16[128,512]{1,0:T(8,128)(2,1)S(1)}, u32[]{:S(2)}, u32[]{:S(2)}) collective-permute-start(bf16[128,512]{1,0:T(8,128)(2,1)S(1)} %collective-permute-done.7.refs_8_), channel_id=1, source_target_pairs={{0,1},{1,0},{2,3},{3,2},{4,5},{5,4},{6,7},{7,6},{8,9},{9,8},{10,11... | collective-permute-start | bytes 393224 | tf_op jit(solution)/shard_map/ppermute | solution.py:176
  28.2 0.0 collective-permute-done.6.refs_7_
  28.2 0.1 collective-permute-start.10
  28.3 1.3 %collective-permute-done.11.refs_12_ = bf16[128,512]{1,0:T(8,128)(2,1)S(1)} collective-permute-done((bf16[128,512]{1,0:T(8,128)(2,1)S(1)}, bf16[128,512]{1,0:T(8,128)(2,1)S(1)}, u32[]{:S(2)}, u32[]{:S(2)}) %collective-permute-start.11) | collective-permute-done | bytes 131104 | tf_op jit(solution)/shard_map/ppermute | solution.py:209
  29.6 0.0 collective-permute-start.12
  29.6 0.9 %collective-permute-done.13.refs_14_ = bf16[128,512]{1,0:T(8,128)(2,1)S(1)} collective-permute-done((bf16[128,512]{1,0:T(8,128)(2,1)S(1)}, bf16[128,512]{1,0:T(8,128)(2,1)S(1)}, u32[]{:S(2)}, u32[]{:S(2)}) %collective-permute-start.13) | collective-permute-done | bytes 131104 | tf_op jit(solution)/shard_map/ppermute | solution.py:207
  30.4 0.0 collective-permute-start.14
  30.5 0.0 collective-permute-done.8.refs_9_
  30.5 0.0 collective-permute-done.17.refs_19_
  30.5 0.0 collective-permute-done.10.refs_11_
  30.5 0.4 %collective-permute-done.12.refs_13_ = bf16[128,512]{1,0:T(8,128)(2,1)S(1)} collective-permute-done((bf16[128,512]{1,0:T(8,128)(2,1)S(1)}, bf16[128,512]{1,0:T(8,128)(2,1)S(1)}, u32[]{:S(2)}, u32[]{:S(2)}) %collective-permute-start.12) | collective-permute-done | bytes 131104 | tf_op jit(solution)/shard_map/ppermute | solution.py:176
  30.9 0.9 %collective-permute-done.14.refs_15_ = bf16[128,512]{1,0:T(8,128)(2,1)S(1)} collective-permute-done((bf16[128,512]{1,0:T(8,128)(2,1)S(1)}, bf16[128,512]{1,0:T(8,128)(2,1)S(1)}, u32[]{:S(2)}, u32[]{:S(2)}) %collective-permute-start.14) | collective-permute-done | bytes 131104 | tf_op jit(solution)/shard_map/ppermute | solution.py:176
  31.8 7.1 %transform.1 = f32[1024,128]{1,0:T(8,128)} custom-call(bf16[128,512]{1,0:T(8,128)(2,1)S(1)} %copy-done, bf16[128,512]{1,0:T(8,128)(2,1)S(1)} %collective-permute-done.refs_1_, bf16[128,512]{1,0:T(8,128)(2,1)S(1)} %collective-permute-done.1.refs_2_, bf16[128,512]{1,0:T(8,128)(2,1)S(1)} %collective-permute-done.2.refs_3_, ...), custom_call_target="tpu_custom_call" | custom-call | tf_op jit(solution)/shard_map/transform/pallas_call | solution.py:155
Async XLA Ops:
  0.0 6.6 %collective-permute-start.1 = (bf16[128,512]{1,0:T(8,128)(2,1)}, bf16[128,512]{1,0:T(8,128)(2,1)S(1)}, u32[]{:S(2)}, u32[]{:S(2)}) collective-permute-start(bf16[128,512]{1,0:T(8,128)(2,1)} %refs_0_.1), channel_id=1, source_target_pairs={{0,4},{4,8},{8,12},{12,14},{14,10},{10,6},{6,2},{2,0},{1,5},{5,9},... | collective-permute-start | bytes 393224 | tf_op jit(solution)/shard_map/ppermute | solution.py:207
  3.0 13.3 %collective-permute-start.3 = (bf16[128,512]{1,0:T(8,128)(2,1)}, bf16[128,512]{1,0:T(8,128)(2,1)S(1)}, u32[]{:S(2)}, u32[]{:S(2)}) collective-permute-start(bf16[128,512]{1,0:T(8,128)(2,1)} %refs_0_.1), channel_id=1, source_target_pairs={{4,0},{8,4},{12,8},{14,12},{10,14},{6,10},{2,6},{0,2},{5,1},{9,5},... | collective-permute-start | bytes 393224 | tf_op jit(solution)/shard_map/ppermute | solution.py:209
  6.6 10.2 %collective-permute-start.5 = (bf16[128,512]{1,0:T(8,128)(2,1)S(1)}, bf16[128,512]{1,0:T(8,128)(2,1)S(1)}, u32[]{:S(2)}, u32[]{:S(2)}) collective-permute-start(bf16[128,512]{1,0:T(8,128)(2,1)S(1)} %collective-permute-done.1.refs_2_), channel_id=1, source_target_pairs={{0,4},{4,8},{8,12},{12,14},{14,10},{10,6},{6,2},{2,0},{1,5},{5,9},... | collective-permute-start | bytes 393224 | tf_op jit(solution)/shard_map/ppermute | solution.py:207
  10.9 4.9 %copy-start = (bf16[128,512]{1,0:T(8,128)(2,1)S(1)}, bf16[128,512]{1,0:T(8,128)(2,1)}, u32[]{:S(2)}) copy-start(bf16[128,512]{1,0:T(8,128)(2,1)} %refs_0_.1) | copy-start | bytes 393220
  10.9 11.6 %all-to-all-start = ((bf16[4,9,16,128]{3,2,1,0:T(8,128)(2,1)}), bf16[4,9,16,128]{3,2,1,0:T(8,128)(2,1)S(1)}, u32[]{:S(2)}, u32[]{:S(2)}) async-start(bf16[4,9,16,128]{3,2,1,0:T(8,128)(2,1)} %pack.1), calls=%async_computation | async-start | bytes 294912 | tf_op jit(solution)/shard_map/all_to_all | solution.py:211
  15.9 2.6 %collective-permute-start = (bf16[128,512]{1,0:T(8,128)(2,1)S(1)}, bf16[128,512]{1,0:T(8,128)(2,1)S(1)}, u32[]{:S(2)}, u32[]{:S(2)}) collective-permute-start(bf16[128,512]{1,0:T(8,128)(2,1)S(1)} %copy-done), channel_id=1, source_target_pairs={{0,1},{1,0},{2,3},{3,2},{4,5},{5,4},{6,7},{7,6},{8,9},{9,8},{10,11... | collective-permute-start | bytes 393224 | tf_op jit(solution)/shard_map/ppermute | solution.py:176
  15.9 6.6 %collective-permute-start.2 = (bf16[128,512]{1,0:T(8,128)(2,1)S(1)}, bf16[128,512]{1,0:T(8,128)(2,1)S(1)}, u32[]{:S(2)}, u32[]{:S(2)}) collective-permute-start(bf16[128,512]{1,0:T(8,128)(2,1)S(1)} %collective-permute-done.1.refs_2_), channel_id=1, source_target_pairs={{0,1},{1,0},{2,3},{3,2},{4,5},{5,4},{6,7},{7,6},{8,9},{9,8},{10,11... | collective-permute-start | bytes 393224 | tf_op jit(solution)/shard_map/ppermute | solution.py:176
  16.4 6.9 %collective-permute-start.7 = (bf16[128,512]{1,0:T(8,128)(2,1)S(1)}, bf16[128,512]{1,0:T(8,128)(2,1)S(1)}, u32[]{:S(2)}, u32[]{:S(2)}) collective-permute-start(bf16[128,512]{1,0:T(8,128)(2,1)S(1)} %collective-permute-done.3.refs_4_), channel_id=1, source_target_pairs={{4,0},{8,4},{12,8},{14,12},{10,14},{6,10},{2,6},{0,2},{5,1},{9,5},... | collective-permute-start | bytes 393224 | tf_op jit(solution)/shard_map/ppermute | solution.py:209
  16.8 6.4 %collective-permute-start.4 = (bf16[128,512]{1,0:T(8,128)(2,1)S(1)}, bf16[128,512]{1,0:T(8,128)(2,1)S(1)}, u32[]{:S(2)}, u32[]{:S(2)}) collective-permute-start(bf16[128,512]{1,0:T(8,128)(2,1)S(1)} %collective-permute-done.3.refs_4_), channel_id=1, source_target_pairs={{0,1},{1,0},{2,3},{3,2},{4,5},{5,4},{6,7},{7,6},{8,9},{9,8},{10,11... | collective-permute-start | bytes 393224 | tf_op jit(solution)/shard_map/ppermute | solution.py:176
  16.8 8.2 %collective-permute-start.9 = (bf16[128,512]{1,0:T(8,128)(2,1)S(1)}, bf16[128,512]{1,0:T(8,128)(2,1)S(1)}, u32[]{:S(2)}, u32[]{:S(2)}) collective-permute-start(bf16[128,512]{1,0:T(8,128)(2,1)S(1)} %collective-permute-done.5.refs_6_), channel_id=1, source_target_pairs={{0,4},{4,8},{8,12},{12,14},{14,10},{10,6},{6,2},{2,0},{1,5},{5,9},... | collective-permute-start | bytes 393224 | tf_op jit(solution)/shard_map/ppermute | solution.py:207
  22.5 5.2 %collective-permute-start.16 = (bf16[4,9,16,128]{3,2,1,0:T(8,128)(2,1)S(1)}, bf16[4,9,16,128]{3,2,1,0:T(8,128)(2,1)S(1)}, u32[]{:S(2)}, u32[]{:S(2)}) collective-permute-start(bf16[4,9,16,128]{3,2,1,0:T(8,128)(2,1)S(1)} %all-to-all-done.refs_16_), channel_id=1, source_target_pairs={{0,2},{1,3},{2,0},{3,1},{4,6},{5,7},{6,4},{7,5},{8,10},{9,11},{10,... | collective-permute-start | bytes 442376 | tf_op jit(solution)/shard_map/ppermute | solution.py:176
  22.5 5.2 %collective-permute-start.15 = (bf16[4,9,16,128]{3,2,1,0:T(8,128)(2,1)S(1)}, bf16[4,9,16,128]{3,2,1,0:T(8,128)(2,1)S(1)}, u32[]{:S(2)}, u32[]{:S(2)}) collective-permute-start(bf16[4,9,16,128]{3,2,1,0:T(8,128)(2,1)S(1)} %all-to-all-done.refs_16_), channel_id=1, source_target_pairs={{0,1},{1,0},{2,3},{3,2},{4,5},{5,4},{6,7},{7,6},{8,9},{9,8},{10,11... | collective-permute-start | bytes 442376 | tf_op jit(solution)/shard_map/ppermute | solution.py:176
  23.2 4.9 %collective-permute-start.6 = (bf16[128,512]{1,0:T(8,128)(2,1)S(1)}, bf16[128,512]{1,0:T(8,128)(2,1)S(1)}, u32[]{:S(2)}, u32[]{:S(2)}) collective-permute-start(bf16[128,512]{1,0:T(8,128)(2,1)S(1)} %collective-permute-done.5.refs_6_), channel_id=1, source_target_pairs={{0,1},{1,0},{2,3},{3,2},{4,5},{5,4},{6,7},{7,6},{8,9},{9,8},{10,11... | collective-permute-start | bytes 393224 | tf_op jit(solution)/shard_map/ppermute | solution.py:176
  23.2 6.3 %collective-permute-start.11 = (bf16[128,512]{1,0:T(8,128)(2,1)S(1)}, bf16[128,512]{1,0:T(8,128)(2,1)S(1)}, u32[]{:S(2)}, u32[]{:S(2)}) collective-permute-start(bf16[128,512]{1,0:T(8,128)(2,1)S(1)} %collective-permute-done.7.refs_8_), channel_id=1, source_target_pairs={{4,0},{8,4},{12,8},{14,12},{10,14},{6,10},{2,6},{0,2},{5,1},{9,5},... | collective-permute-start | bytes 393224 | tf_op jit(solution)/shard_map/ppermute | solution.py:209
  25.0 5.4 %collective-permute-start.13 = (bf16[128,512]{1,0:T(8,128)(2,1)S(1)}, bf16[128,512]{1,0:T(8,128)(2,1)S(1)}, u32[]{:S(2)}, u32[]{:S(2)}) collective-permute-start(bf16[128,512]{1,0:T(8,128)(2,1)S(1)} %collective-permute-done.9.refs_10_), channel_id=1, source_target_pairs={{0,4},{4,8},{8,12},{12,14},{14,10},{10,6},{6,2},{2,0},{1,5},{5,9},... | collective-permute-start | bytes 393224 | tf_op jit(solution)/shard_map/ppermute | solution.py:207
  27.7 2.8 %collective-permute-start.17 = (bf16[4,9,16,128]{3,2,1,0:T(8,128)(2,1)S(1)}, bf16[4,9,16,128]{3,2,1,0:T(8,128)(2,1)S(1)}, u32[]{:S(2)}, u32[]{:S(2)}) collective-permute-start(bf16[4,9,16,128]{3,2,1,0:T(8,128)(2,1)S(1)} %collective-permute-done.16.refs_18_), channel_id=1, source_target_pairs={{0,1},{1,0},{2,3},{3,2},{4,5},{5,4},{6,7},{7,6},{8,9},{9,8},{10,11... | collective-permute-start | bytes 442376 | tf_op jit(solution)/shard_map/ppermute | solution.py:176
  27.7 2.8 %collective-permute-start.8 = (bf16[128,512]{1,0:T(8,128)(2,1)S(1)}, bf16[128,512]{1,0:T(8,128)(2,1)S(1)}, u32[]{:S(2)}, u32[]{:S(2)}) collective-permute-start(bf16[128,512]{1,0:T(8,128)(2,1)S(1)} %collective-permute-done.7.refs_8_), channel_id=1, source_target_pairs={{0,1},{1,0},{2,3},{3,2},{4,5},{5,4},{6,7},{7,6},{8,9},{9,8},{10,11... | collective-permute-start | bytes 393224 | tf_op jit(solution)/shard_map/ppermute | solution.py:176
  28.2 2.3 %collective-permute-start.10 = (bf16[128,512]{1,0:T(8,128)(2,1)S(1)}, bf16[128,512]{1,0:T(8,128)(2,1)S(1)}, u32[]{:S(2)}, u32[]{:S(2)}) collective-permute-start(bf16[128,512]{1,0:T(8,128)(2,1)S(1)} %collective-permute-done.9.refs_10_), channel_id=1, source_target_pairs={{0,1},{1,0},{2,3},{3,2},{4,5},{5,4},{6,7},{7,6},{8,9},{9,8},{10,11... | collective-permute-start | bytes 393224 | tf_op jit(solution)/shard_map/ppermute | solution.py:176
  29.6 1.3 %collective-permute-start.12 = (bf16[128,512]{1,0:T(8,128)(2,1)S(1)}, bf16[128,512]{1,0:T(8,128)(2,1)S(1)}, u32[]{:S(2)}, u32[]{:S(2)}) collective-permute-start(bf16[128,512]{1,0:T(8,128)(2,1)S(1)} %collective-permute-done.11.refs_12_), channel_id=1, source_target_pairs={{0,1},{1,0},{2,3},{3,2},{4,5},{5,4},{6,7},{7,6},{8,9},{9,8},{10,11... | collective-permute-start | bytes 393224 | tf_op jit(solution)/shard_map/ppermute | solution.py:176
  30.4 1.3 %collective-permute-start.14 = (bf16[128,512]{1,0:T(8,128)(2,1)S(1)}, bf16[128,512]{1,0:T(8,128)(2,1)S(1)}, u32[]{:S(2)}, u32[]{:S(2)}) collective-permute-start(bf16[128,512]{1,0:T(8,128)(2,1)S(1)} %collective-permute-done.13.refs_14_), channel_id=1, source_target_pairs={{0,1},{1,0},{2,3},{3,2},{4,5},{5,4},{6,7},{7,6},{8,9},{9,8},{10,11... | collective-permute-start | bytes 393224 | tf_op jit(solution)/shard_map/ppermute | solution.py:176

commit v5 on v4

--- a/solution.py
+++ b/solution.py
@@ -9,11 +9,14 @@
 
 SB = 64
 LANES = 128
-GROUP = 16
+TAG = 16
 CHUNK = 16
 
 
-def pack_kernel(n_pair, integrals, mu, nu, counts, out, tiles, mu_in, nu_in, spread, woven, sems):
+def pack_kernel(n_pair, integrals, mu, nu, counts, *refs):
+    outs = refs[:n_pair]
+    tiles, mu_in, nu_in, spread, woven, sems = refs[n_pair:]
+    p = lax.axis_index("pair")
     copies = [
         pltpu.make_async_copy(source, target, sems.at[n])
         for n, (source, target) in enumerate(((integrals, tiles), (mu, mu_in), (nu, nu_in)))
@@ -28,8 +31,8 @@
     count = counts[0]
     lane = lax.broadcasted_iota(jnp.int32, (wide, LANES), 1)
     low, kept = lane < SB, lane < SB * count
-    lane = lax.broadcasted_iota(jnp.int32, (GROUP, LANES), 1)
-    tag = jnp.zeros((GROUP, LANES), jnp.int32)
+    lane = lax.broadcasted_iota(jnp.int32, (TAG, LANES), 1)
+    tag = jnp.zeros((TAG, LANES), jnp.int32)
     for t in range(slots):
         tag = jnp.where((lane == 2 * t) & (t < count), mu_in[t], tag)
         tag = jnp.where((lane == 2 * t + 1) & (t < count), nu_in[t], tag)
@@ -39,32 +42,31 @@
         for j in range(wide):
             at = pl.ds((t * wide + j) * kets, kets)
             spread[at, :] = tiles[t, :, j * LANES : (j + 1) * LANES].astype(jnp.float32)
-    tiled = columns * SB // GROUP
-    for dest in range(n_pair):
+    for s in range(n_pair):
+        dest = lax.rem(p + s, n_pair)
         for k in range(columns):
             column = dest * columns + k
             one = spread[pl.ds(column, wide, stride=kets), :]
             two = spread[pl.ds(wide * kets + column, wide, stride=kets), :]
             even = jnp.where(low, one, pltpu.roll(two, SB, axis=1))
             odd = jnp.where(low, pltpu.roll(one, SB, axis=1), two)
-            begin = column * SB
+            begin = (s * columns + k) * SB
             woven[pl.ds(begin, wide, stride=2), :] = jnp.where(kept, even, 0.0)
             woven[pl.ds(begin + 1, wide, stride=2), :] = jnp.where(kept, odd, 0.0)
-        for g in range(tiled):
-            rows_at = pl.ds((dest * tiled + g) * GROUP, GROUP)
-            out[dest, g] = woven[rows_at, :].astype(jnp.bfloat16)
-        out[dest, tiled] = tag
+        rows = columns * SB
+        outs[s][0, :rows] = woven[pl.ds(s * rows, rows), :].astype(jnp.bfloat16)
+        outs[s][0, rows:] = tag
 
 
 def pack(n_pair, integrals, mu, nu, counts):
     slots, kets, flat = integrals.shape
-    groups = kets // n_pair * SB // GROUP + 1
+    rows = kets // n_pair * SB + TAG
     hbm, smem = pl.BlockSpec(memory_space=pltpu.HBM), pl.BlockSpec(memory_space=pltpu.SMEM)
     return pl.pallas_call(
         functools.partial(pack_kernel, n_pair),
-        out_shape=jax.ShapeDtypeStruct((n_pair, groups, GROUP, LANES), jnp.bfloat16),
+        out_shape=[jax.ShapeDtypeStruct((1, rows, LANES), jnp.bfloat16)] * n_pair,
         in_specs=[hbm, hbm, hbm, smem],
-        out_specs=pl.BlockSpec(memory_space=pltpu.VMEM),
+        out_specs=[pl.BlockSpec(memory_space=pltpu.VMEM)] * n_pair,
         scratch_shapes=[
             pltpu.VMEM(integrals.shape, jnp.bfloat16),
             pltpu.SMEM(mu.shape, jnp.int32),
@@ -85,13 +87,12 @@
     devices = codes.shape[0]
     orbitals = c_all.shape[1]
     blocks = orbitals // LANES
-    tiled = 2 * SB // GROUP
     early, late = [], []
     per = devices // n_x
     for q, piece in enumerate(x_in):
         place = pl.ds(q * per, per)
-        early.append(pltpu.make_async_copy(piece.at[:, tiled], tags.at[place], sems.at[q]))
-        late.append(pltpu.make_async_copy(piece.at[:, pl.ds(0, tiled)], x_all.at[place], sems.at[n_x + q]))
+        early.append(pltpu.make_async_copy(piece.at[:, pl.ds(2 * SB, TAG)], tags.at[place], sems.at[q]))
+        late.append(pltpu.make_async_copy(piece.at[:, pl.ds(0, 2 * SB)], x_all.at[place], sems.at[n_x + q]))
     for q, piece in enumerate(c_in):
         rows = c_all.shape[0] // n_c
         place = pl.ds(pl.multiple_of(source_of(q) * rows, rows), rows)
@@ -119,7 +120,7 @@
             device = chunk * CHUNK + d
             stacked = []
             for k in range(2):
-                tile = jnp.concatenate([x_all[device, k * (tiled // 2) + g] for g in range(tiled // 2)], 0)
+                tile = x_all[device, k * SB : (k + 1) * SB, :]
                 stacked += [jnp.where(low, tile, jnp.zeros_like(tile)), jnp.where(low, jnp.zeros_like(tile), tile)]
             mu_one, nu_one, mu_two, nu_two = (index[device, n] for n in range(4))
             rows = jnp.concatenate([c_all[rows_of(nu_one)], c_all[rows_of(nu_two)]], 0)
@@ -159,8 +160,8 @@
         out_specs=pl.BlockSpec(memory_space=pltpu.VMEM),
         scratch_shapes=[
             pltpu.VMEM((c_pieces[0].shape[0] * n_c, orbitals), jnp.bfloat16),
-            pltpu.VMEM((devices, 2 * SB // GROUP, GROUP, LANES), jnp.bfloat16),
-            pltpu.VMEM((devices, GROUP, LANES), jnp.bfloat16),
+            pltpu.VMEM((devices, 2 * SB, LANES), jnp.bfloat16),
+            pltpu.VMEM((devices, TAG, LANES), jnp.bfloat16),
             pltpu.VMEM((devices, LANES), jnp.int32),
             pltpu.SMEM((devices, LANES), jnp.int32),
             pltpu.VMEM((wide, 2 * orbitals), jnp.bfloat16),
@@ -172,26 +173,30 @@
     )(*c_pieces, *x_pieces)
 
 
+def shift(array, axis, size, step):
+    return lax.ppermute(array, axis, [(i, (i + step) % size) for i in range(size)])
+
+
 def flip(array, axis, size, bit):
     return lax.ppermute(array, axis, [(i, i ^ bit) for i in range(size)])
 
 
-def around(n_pair, n_orb, core, step):
+def around(n_pair, n_orb):
     length = 2 * n_pair
-    far = n_orb // 2
-    stops = [p * n_orb + core for p in range(n_pair)] + [p * n_orb + far + core for p in reversed(range(n_pair))]
-    return [(stops[r], stops[(r + step) % length]) for r in range(length)]
+    ups = [p * n_orb for p in range(n_pair)]
+    stops = ups + [stop + n_orb // 2 for stop in reversed(ups)]
+    ring = [(stops[r], stops[(r + 1) % length]) for r in range(length)]
+    return ring + [(b + 1, a + 1) for a, b in ring]
 
 
 def ring_source(n_pair, n_orb, step, flipped):
     p, o = lax.axis_index("pair"), lax.axis_index("orb")
     length = 2 * n_pair
-    column = lax.div(o, 2)
-    place = jnp.where(column == 0, p, length - 1 - p)
-    place = lax.rem(place + length - step, length)
-    second = (place >= n_pair).astype(jnp.int32)
-    source = jnp.where(second == 1, length - 1 - place, place)
-    return source * n_orb + 2 * second + (lax.rem(o, 2) ^ flipped)
+    core = lax.rem(o, 2) ^ flipped
+    place = jnp.where(o < 2, p, length - 1 - p)
+    place = lax.rem(place + jnp.where(core == 0, length - step, length + step), length)
+    down = place >= n_pair
+    return jnp.where(down, (length - 1 - place) * n_orb + 2, place * n_orb) + core
 
 
 def body(n_pair, n_orb, integrals, mu_block, nu_block, counts, coeff):
@@ -200,7 +205,7 @@
     orbitals = coeff.shape[1]
     everyone = ("pair", "orb")
     if n_orb == 4 and n_pair <= 4:
-        forward = around(n_pair, n_orb, 0, 1) + around(n_pair, n_orb, 1, 1)
+        forward = around(n_pair, n_orb)
         backward = [(b, a) for a, b in forward]
         held = {0: coeff}
         for step in range(1, n_pair + 1):
@@ -208,13 +213,13 @@
             if step < n_pair:
                 held[-step] = lax.ppermute(held[1 - step], everyone, backward)
         packed = pack(n_pair, integrals, mu_block, nu_block, counts)
-        line = lax.all_to_all(packed, "pair", split_axis=0, concat_axis=0, tiled=True)
+        line = jnp.concatenate([packed[0]] + [shift(packed[s], "pair", n_pair, s) for s in range(1, n_pair)], 0)
         across = flip(line, "orb", n_orb, 2)
         x_pieces = [line, flip(line, "orb", n_orb, 1), across, flip(across, "orb", n_orb, 1)]
         c_pieces, came = [], []
         for step, piece in held.items():
             c_pieces += [piece, flip(piece, "orb", n_orb, 1)]
-            came += [(step % (2 * n_pair), 0), (step % (2 * n_pair), 1)]
+            came += [(step, 0), (step, 1)]
 
         def source_of(q):
             return ring_source(n_pair, n_orb, *came[q])
@@ -224,8 +229,8 @@
         tiles = tiles.reshape(slots, n_pair, columns, SB, SB).transpose(1, 2, 3, 0, 4)
         tiles = tiles.reshape(n_pair, columns * SB, slots * SB)
         tag = jnp.where(kept[:, None], jnp.stack([mu_block, nu_block], 1), 0).reshape(-1)
-        tag = jnp.zeros((n_pair, GROUP, LANES), jnp.bfloat16).at[:, :, : 2 * slots].set(tag.astype(jnp.bfloat16))
-        packed = jnp.concatenate([tiles, tag], 1).reshape(n_pair, -1, GROUP, LANES)
+        tag = jnp.zeros((n_pair, TAG, LANES), jnp.bfloat16).at[:, :, : 2 * slots].set(tag.astype(jnp.bfloat16))
+        packed = jnp.concatenate([tiles, tag], 1)
         line = lax.all_to_all(packed, "pair", split_axis=0, concat_axis=0, tiled=True)
         x_pieces = [lax.all_gather(line, "orb", axis=0, tiled=True)]
         c_pieces = [lax.all_gather(coeff, everyone, axis=0, tiled=True)]

time: 39.1 us -> 37.3 us (0.954)
  waiting for transfers between devices: 14.1 us -> 9.44 us
  starting transfers between devices: 15.2 us -> 17.4 us
  local copies, waits for them, and re-layouts: 0.01 us -> 0.84 us
    ppermute x0 -> x3, starting transfers between devices: none -> 6.01 us  [shift(): lax.ppermute(array, axis, [(i, (i + step) % size) for i in range(size)])]
    all_to_all x1 -> x0, starting transfers between devices: 4.93 us -> none  [body(): lax.all_to_all(packed, 'pair', split_axis=0, concat_axis=0, tiled=True)]
    all_to_all x1 -> x0, waiting for transfers between devices: 4.02 us -> none  [body(): lax.all_to_all(packed, 'pair', split_axis=0, concat_axis=0, tiled=True)]
    ppermute x4, waiting for transfers between devices: 4.51 us -> 2.42 us  [body(): held[step] = lax.ppermute(held[step - 1], everyone, forward)]
    ppermute x11, starting transfers between devices: 1.1 us -> 2.91 us  [flip(): return lax.ppermute(array, axis, [(i, i ^ bit) for i in range(size)])]
    ppermute x3, waiting for transfers between devices: 2.03 us -> 3.38 us  [body(): held[-step] = lax.ppermute(held[1 - step], everyone, backward)]
    ppermute x4, starting transfers between devices: 6.91 us -> 6 us  [body(): held[step] = lax.ppermute(held[step - 1], everyone, forward)]
    ppermute x0 -> x3, waiting for transfers between devices: none -> 0.88 us  [shift(): lax.ppermute(array, axis, [(i, (i + step) % size) for i in range(size)])]
  transfers between devices with their start and end apart: 19 -> 21, of which waited for: 8 -> 8; matrix products, arithmetic and copies ran while one was open for 0% -> 2% of each run, Pallas kernels for 5% -> 5%
where the time goes in v5:
time: 37.3 us; the launch traced here: 37.1 us
  starting transfers between devices  17.4 us (47%)
  waiting for transfers between devices  9.44 us (25%)
  Pallas kernels  8.79 us (24%)
  local copies, waits for them, and re-layouts  0.84 us (2%)
  between operations  0.71 us (2%)
    pallas_call x1, Pallas kernels, transform(): pl.pallas_call(functools.partial(transform_kernel, source_of, n_c, n_x),...  7.07 us
    ppermute x3, starting transfers between devices, shift(): lax.ppermute(array, axis, [(i, (i + step) % size) for i in range(size)])  6.01 us
    ppermute x4, starting transfers between devices, body(): held[step] = lax.ppermute(held[step - 1], everyone, forward)  6 us
    ppermute x3, waiting for transfers between devices, body(): held[-step] = lax.ppermute(held[1 - step], everyone, backward)  3.38 us
    ppermute x11, starting transfers between devices, flip(): return lax.ppermute(array, axis, [(i, i ^ bit) for i in range(size)])  2.91 us
    ppermute x11, waiting for transfers between devices, flip(): return lax.ppermute(array, axis, [(i, i ^ bit) for i in range(size)])  2.76 us
    ppermute x3, starting transfers between devices, body(): held[-step] = lax.ppermute(held[1 - step], everyone, backward)  2.46 us
    ppermute x4, waiting for transfers between devices, body(): held[step] = lax.ppermute(held[step - 1], everyone, forward)  2.42 us
  transfers between devices with their start and end apart: 21, of which 8 were waited for; matrix products, arithmetic and copies ran while one was open for 2% of the time, Pallas kernels for 5%

profile of v5, /device:TPU:0, one launch (start us, length us, event | category | flops | bytes accessed | tf_op | source)
XLA Modules:
  0.0 37.1 jit_solution(4093054035363411875)
XLA Ops:
  0.0 3.0 %collective-permute-start.1 = (bf16[128,512]{1,0:T(8,128)(2,1)}, bf16[128,512]{1,0:T(8,128)(2,1)S(1)}, u32[]{:S(2)}, u32[]{:S(2)}) collective-permute-start(bf16[128,512]{1,0:T(8,128)(2,1)} %refs_0_.1), channel_id=1, source_target_pairs={{0,4},{4,8},{8,12},{12,14},{14,10},{10,6},{6,2},{2,0},{5,1},{9,5},... | collective-permute-start | bytes 393224 | tf_op jit(solution)/shard_map/ppermute | solution.py:212
  3.0 0.0 collective-permute-start.3
  3.7 1.7 %pack.1 = (bf16[1,144,128]{2,1,0:T(8,128)(2,1)}, bf16[1,144,128]{2,1,0:T(8,128)(2,1)}, bf16[1,144,128]{2,1,0:T(8,128)(2,1)}, bf16[1,144,128]{2,1,0:T(8,128)(2,1)}) custom-call(bf16[2,8,4096]{2,1,0:T(8,128)(2,1)} %integrals.1, s32[2]{0:T(128)} %mu.1, s32[2]{0:T(128)} %nu.1, s32[1]{0:T(128)S(6)} %copy.10.counts), custom_call_target="tpu_custom_call" | custom-call | tf_op jit(solution)/shard_map/pack/pallas_call | solution.py:65
  5.4 2.1 %collective-permute-start.15 = (bf16[1,144,128]{2,1,0:T(8,128)(2,1)}, bf16[1,144,128]{2,1,0:T(8,128)(2,1)S(1)}, u32[]{:S(2)}, u32[]{:S(2)}) collective-permute-start(bf16[1,144,128]{2,1,0:T(8,128)(2,1)} %get-tuple-element.10), channel_id=1, source_target_pairs={{0,4},{4,8},{8,12},{12,0},{1,5},{5,9},{9,13},{13,1},{2,6},{6,10},{... | collective-permute-start | bytes 110600 | tf_op jit(solution)/shard_map/ppermute | solution.py:177
  7.5 2.6 %collective-permute-start.16 = (bf16[1,144,128]{2,1,0:T(8,128)(2,1)}, bf16[1,144,128]{2,1,0:T(8,128)(2,1)S(1)}, u32[]{:S(2)}, u32[]{:S(2)}) collective-permute-start(bf16[1,144,128]{2,1,0:T(8,128)(2,1)} %get-tuple-element.11), channel_id=1, source_target_pairs={{0,8},{4,12},{8,0},{12,4},{1,9},{5,13},{9,1},{13,5},{2,10},{6,14},... | collective-permute-start | bytes 110600 | tf_op jit(solution)/shard_map/ppermute | solution.py:177
  10.1 1.3 %collective-permute-start.17 = (bf16[1,144,128]{2,1,0:T(8,128)(2,1)}, bf16[1,144,128]{2,1,0:T(8,128)(2,1)S(1)}, u32[]{:S(2)}, u32[]{:S(2)}) collective-permute-start(bf16[1,144,128]{2,1,0:T(8,128)(2,1)} %get-tuple-element.12), channel_id=1, source_target_pairs={{0,12},{4,0},{8,4},{12,8},{1,13},{5,1},{9,5},{13,9},{2,14},{6,2},{... | collective-permute-start | bytes 110600 | tf_op jit(solution)/shard_map/ppermute | solution.py:177
  11.4 0.0 copy-start
  11.4 0.8 %constant_dynamic-update-slice_fusion.3 = bf16[4,144,128]{2,1,0:T(8,128)(2,1)S(1)} fusion(bf16[1,144,128]{2,1,0:T(8,128)(2,1)} %get-tuple-element.9), kind=kLoop, calls=%fused_computation.3 | loop fusion | bytes 73728
  12.2 0.0 collective-permute-done.15
  12.2 0.5 %collective-permute-done.16 = bf16[1,144,128]{2,1,0:T(8,128)(2,1)S(1)} collective-permute-done((bf16[1,144,128]{2,1,0:T(8,128)(2,1)}, bf16[1,144,128]{2,1,0:T(8,128)(2,1)S(1)}, u32[]{:S(2)}, u32[]{:S(2)}) %collective-permute-start.16) | collective-permute-done | bytes 36896 | tf_op jit(solution)/shard_map/ppermute | solution.py:177
  12.8 0.0 collective-permute-done.1.refs_2_
  12.8 1.4 %collective-permute-start.5 = (bf16[128,512]{1,0:T(8,128)(2,1)S(1)}, bf16[128,512]{1,0:T(8,128)(2,1)S(1)}, u32[]{:S(2)}, u32[]{:S(2)}) collective-permute-start(bf16[128,512]{1,0:T(8,128)(2,1)S(1)} %collective-permute-done.1.refs_2_), channel_id=1, source_target_pairs={{0,4},{4,8},{8,12},{12,14},{14,10},{10,6},{6,2},{2,0},{5,1},{9,5},... | collective-permute-start | bytes 393224 | tf_op jit(solution)/shard_map/ppermute | solution.py:212
  14.2 0.3 collective-permute-done.17
  14.6 1.2 %collective-permute-start.19 = (bf16[4,144,128]{2,1,0:T(8,128)(2,1)S(1)}, bf16[4,144,128]{2,1,0:T(8,128)(2,1)S(1)}, u32[]{:S(2)}, u32[]{:S(2)}) collective-permute-start(bf16[4,144,128]{2,1,0:T(8,128)(2,1)S(1)} %constant_dynamic-update-slice_fusion.refs_16_), channel_id=1, source_target_pairs={{0,2},{1,3},{2,0},{3,1},{4,6},{5,7},{6,4},{7,5},{8,10},{9,11},{10,... | collective-permute-start | bytes 442376 | tf_op jit(solution)/shard_map/ppermute | solution.py:181
  15.8 0.0 collective-permute-start.18
  15.8 0.0 copy-done
  15.8 0.5 %collective-permute-start = (bf16[128,512]{1,0:T(8,128)(2,1)S(1)}, bf16[128,512]{1,0:T(8,128)(2,1)S(1)}, u32[]{:S(2)}, u32[]{:S(2)}) collective-permute-start(bf16[128,512]{1,0:T(8,128)(2,1)S(1)} %copy-done), channel_id=1, source_target_pairs={{0,1},{1,0},{2,3},{3,2},{4,5},{5,4},{6,7},{7,6},{8,9},{9,8},{10,11... | collective-permute-start | bytes 393224 | tf_op jit(solution)/shard_map/ppermute | solution.py:181
  16.3 0.0 collective-permute-done.3.refs_4_
  16.3 0.9 %collective-permute-start.7 = (bf16[128,512]{1,0:T(8,128)(2,1)S(1)}, bf16[128,512]{1,0:T(8,128)(2,1)S(1)}, u32[]{:S(2)}, u32[]{:S(2)}) collective-permute-start(bf16[128,512]{1,0:T(8,128)(2,1)S(1)} %collective-permute-done.3.refs_4_), channel_id=1, source_target_pairs={{4,0},{8,4},{12,8},{14,12},{10,14},{6,10},{2,6},{0,2},{1,5},{5,9},... | collective-permute-start | bytes 393224 | tf_op jit(solution)/shard_map/ppermute | solution.py:214
  17.2 0.9 %collective-permute-done.5.refs_6_ = bf16[128,512]{1,0:T(8,128)(2,1)S(1)} collective-permute-done((bf16[128,512]{1,0:T(8,128)(2,1)S(1)}, bf16[128,512]{1,0:T(8,128)(2,1)S(1)}, u32[]{:S(2)}, u32[]{:S(2)}) %collective-permute-start.5) | collective-permute-done | bytes 131104 | tf_op jit(solution)/shard_map/ppermute | solution.py:212
  18.1 1.1 %collective-permute-start.9 = (bf16[128,512]{1,0:T(8,128)(2,1)S(1)}, bf16[128,512]{1,0:T(8,128)(2,1)S(1)}, u32[]{:S(2)}, u32[]{:S(2)}) collective-permute-start(bf16[128,512]{1,0:T(8,128)(2,1)S(1)} %collective-permute-done.5.refs_6_), channel_id=1, source_target_pairs={{0,4},{4,8},{8,12},{12,14},{14,10},{10,6},{6,2},{2,0},{5,1},{9,5},... | collective-permute-start | bytes 393224 | tf_op jit(solution)/shard_map/ppermute | solution.py:212
  19.2 1.4 %collective-permute-done.19.refs_18_ = bf16[4,144,128]{2,1,0:T(8,128)(2,1)S(1)} collective-permute-done((bf16[4,144,128]{2,1,0:T(8,128)(2,1)S(1)}, bf16[4,144,128]{2,1,0:T(8,128)(2,1)S(1)}, u32[]{:S(2)}, u32[]{:S(2)}) %collective-permute-start.19) | collective-permute-done | bytes 147488 | tf_op jit(solution)/shard_map/ppermute | solution.py:181
  20.6 0.0 collective-permute-start.20
  20.6 0.0 collective-permute-done.refs_1_
  20.6 0.5 %collective-permute-start.2 = (bf16[128,512]{1,0:T(8,128)(2,1)S(1)}, bf16[128,512]{1,0:T(8,128)(2,1)S(1)}, u32[]{:S(2)}, u32[]{:S(2)}) collective-permute-start(bf16[128,512]{1,0:T(8,128)(2,1)S(1)} %collective-permute-done.1.refs_2_), channel_id=1, source_target_pairs={{0,1},{1,0},{2,3},{3,2},{4,5},{5,4},{6,7},{7,6},{8,9},{9,8},{10,11... | collective-permute-start | bytes 393224 | tf_op jit(solution)/shard_map/ppermute | solution.py:181
  21.1 0.0 collective-permute-done.18.refs_17_
  21.1 0.1 collective-permute-start.4
  21.2 1.0 %collective-permute-done.7.refs_8_ = bf16[128,512]{1,0:T(8,128)(2,1)S(1)} collective-permute-done((bf16[128,512]{1,0:T(8,128)(2,1)S(1)}, bf16[128,512]{1,0:T(8,128)(2,1)S(1)}, u32[]{:S(2)}, u32[]{:S(2)}) %collective-permute-start.7) | collective-permute-done | bytes 131104 | tf_op jit(solution)/shard_map/ppermute | solution.py:214
  22.2 1.6 %collective-permute-start.11 = (bf16[128,512]{1,0:T(8,128)(2,1)S(1)}, bf16[128,512]{1,0:T(8,128)(2,1)S(1)}, u32[]{:S(2)}, u32[]{:S(2)}) collective-permute-start(bf16[128,512]{1,0:T(8,128)(2,1)S(1)} %collective-permute-done.7.refs_8_), channel_id=1, source_target_pairs={{4,0},{8,4},{12,8},{14,12},{10,14},{6,10},{2,6},{0,2},{1,5},{5,9},... | collective-permute-start | bytes 393224 | tf_op jit(solution)/shard_map/ppermute | solution.py:214
  23.8 0.0 collective-permute-done.9.refs_10_
  23.8 0.4 %collective-permute-start.13 = (bf16[128,512]{1,0:T(8,128)(2,1)S(1)}, bf16[128,512]{1,0:T(8,128)(2,1)S(1)}, u32[]{:S(2)}, u32[]{:S(2)}) collective-permute-start(bf16[128,512]{1,0:T(8,128)(2,1)S(1)} %collective-permute-done.9.refs_10_), channel_id=1, source_target_pairs={{0,4},{4,8},{8,12},{12,14},{14,10},{10,6},{6,2},{2,0},{5,1},{9,5},... | collective-permute-start | bytes 393224 | tf_op jit(solution)/shard_map/ppermute | solution.py:212
  24.2 0.0 collective-permute-done.2.refs_3_
  24.2 0.0 collective-permute-start.6
  24.2 0.0 collective-permute-done.4.refs_5_
  24.2 0.5 %collective-permute-start.8 = (bf16[128,512]{1,0:T(8,128)(2,1)S(1)}, bf16[128,512]{1,0:T(8,128)(2,1)S(1)}, u32[]{:S(2)}, u32[]{:S(2)}) collective-permute-start(bf16[128,512]{1,0:T(8,128)(2,1)S(1)} %collective-permute-done.7.refs_8_), channel_id=1, source_target_pairs={{0,1},{1,0},{2,3},{3,2},{4,5},{5,4},{6,7},{7,6},{8,9},{9,8},{10,11... | collective-permute-start | bytes 393224 | tf_op jit(solution)/shard_map/ppermute | solution.py:181
  24.7 0.0 collective-permute-done.20.refs_19_
  24.7 0.1 collective-permute-start.10
  24.8 2.4 %collective-permute-done.11.refs_12_ = bf16[128,512]{1,0:T(8,128)(2,1)S(1)} collective-permute-done((bf16[128,512]{1,0:T(8,128)(2,1)S(1)}, bf16[128,512]{1,0:T(8,128)(2,1)S(1)}, u32[]{:S(2)}, u32[]{:S(2)}) %collective-permute-start.11) | collective-permute-done | bytes 131104 | tf_op jit(solution)/shard_map/ppermute | solution.py:214
  27.2 0.0 collective-permute-start.12
  27.2 1.5 %collective-permute-done.13.refs_14_ = bf16[128,512]{1,0:T(8,128)(2,1)S(1)} collective-permute-done((bf16[128,512]{1,0:T(8,128)(2,1)S(1)}, bf16[128,512]{1,0:T(8,128)(2,1)S(1)}, u32[]{:S(2)}, u32[]{:S(2)}) %collective-permute-start.13) | collective-permute-done | bytes 131104 | tf_op jit(solution)/shard_map/ppermute | solution.py:212
  28.7 0.0 collective-permute-start.14
  28.7 0.0 collective-permute-done.6.refs_7_
  28.7 0.0 collective-permute-done.8.refs_9_
  28.7 0.0 collective-permute-done.10.refs_11_
  28.8 0.0 collective-permute-done.12.refs_13_
  28.8 1.3 %collective-permute-done.14.refs_15_ = bf16[128,512]{1,0:T(8,128)(2,1)S(1)} collective-permute-done((bf16[128,512]{1,0:T(8,128)(2,1)S(1)}, bf16[128,512]{1,0:T(8,128)(2,1)S(1)}, u32[]{:S(2)}, u32[]{:S(2)}) %collective-permute-start.14) | collective-permute-done | bytes 131104 | tf_op jit(solution)/shard_map/ppermute | solution.py:181
  30.1 7.1 %transform.1 = f32[1024,128]{1,0:T(8,128)} custom-call(bf16[128,512]{1,0:T(8,128)(2,1)S(1)} %copy-done, bf16[128,512]{1,0:T(8,128)(2,1)S(1)} %collective-permute-done.refs_1_, bf16[128,512]{1,0:T(8,128)(2,1)S(1)} %collective-permute-done.1.refs_2_, bf16[128,512]{1,0:T(8,128)(2,1)S(1)} %collective-permute-done.2.refs_3_, ...), custom_call_target="tpu_custom_call" | custom-call | tf_op jit(solution)/shard_map/transform/pallas_call | solution.py:156
  (3 shorter events, 0.0 us)
Async XLA Ops:
  0.0 12.8 %collective-permute-start.1 = (bf16[128,512]{1,0:T(8,128)(2,1)}, bf16[128,512]{1,0:T(8,128)(2,1)S(1)}, u32[]{:S(2)}, u32[]{:S(2)}) collective-permute-start(bf16[128,512]{1,0:T(8,128)(2,1)} %refs_0_.1), channel_id=1, source_target_pairs={{0,4},{4,8},{8,12},{12,14},{14,10},{10,6},{6,2},{2,0},{5,1},{9,5},... | collective-permute-start | bytes 393224 | tf_op jit(solution)/shard_map/ppermute | solution.py:212
  3.0 13.3 %collective-permute-start.3 = (bf16[128,512]{1,0:T(8,128)(2,1)}, bf16[128,512]{1,0:T(8,128)(2,1)S(1)}, u32[]{:S(2)}, u32[]{:S(2)}) collective-permute-start(bf16[128,512]{1,0:T(8,128)(2,1)} %refs_0_.1), channel_id=1, source_target_pairs={{4,0},{8,4},{12,8},{14,12},{10,14},{6,10},{2,6},{0,2},{1,5},{5,9},... | collective-permute-start | bytes 393224 | tf_op jit(solution)/shard_map/ppermute | solution.py:214
  5.4 6.8 %collective-permute-start.15 = (bf16[1,144,128]{2,1,0:T(8,128)(2,1)}, bf16[1,144,128]{2,1,0:T(8,128)(2,1)S(1)}, u32[]{:S(2)}, u32[]{:S(2)}) collective-permute-start(bf16[1,144,128]{2,1,0:T(8,128)(2,1)} %get-tuple-element.10), channel_id=1, source_target_pairs={{0,4},{4,8},{8,12},{12,0},{1,5},{5,9},{9,13},{13,1},{2,6},{6,10},{... | collective-permute-start | bytes 110600 | tf_op jit(solution)/shard_map/ppermute | solution.py:177
  7.5 5.3 %collective-permute-start.16 = (bf16[1,144,128]{2,1,0:T(8,128)(2,1)}, bf16[1,144,128]{2,1,0:T(8,128)(2,1)S(1)}, u32[]{:S(2)}, u32[]{:S(2)}) collective-permute-start(bf16[1,144,128]{2,1,0:T(8,128)(2,1)} %get-tuple-element.11), channel_id=1, source_target_pairs={{0,8},{4,12},{8,0},{12,4},{1,9},{5,13},{9,1},{13,5},{2,10},{6,14},... | collective-permute-start | bytes 110600 | tf_op jit(solution)/shard_map/ppermute | solution.py:177
  10.1 4.5 %collective-permute-start.17 = (bf16[1,144,128]{2,1,0:T(8,128)(2,1)}, bf16[1,144,128]{2,1,0:T(8,128)(2,1)S(1)}, u32[]{:S(2)}, u32[]{:S(2)}) collective-permute-start(bf16[1,144,128]{2,1,0:T(8,128)(2,1)} %get-tuple-element.12), channel_id=1, source_target_pairs={{0,12},{4,0},{8,4},{12,8},{1,13},{5,1},{9,5},{13,9},{2,14},{6,2},{... | collective-permute-start | bytes 110600 | tf_op jit(solution)/shard_map/ppermute | solution.py:177
  11.4 4.4 %copy-start = (bf16[128,512]{1,0:T(8,128)(2,1)S(1)}, bf16[128,512]{1,0:T(8,128)(2,1)}, u32[]{:S(2)}) copy-start(bf16[128,512]{1,0:T(8,128)(2,1)} %refs_0_.1) | copy-start | bytes 393220
  12.8 5.3 %collective-permute-start.5 = (bf16[128,512]{1,0:T(8,128)(2,1)S(1)}, bf16[128,512]{1,0:T(8,128)(2,1)S(1)}, u32[]{:S(2)}, u32[]{:S(2)}) collective-permute-start(bf16[128,512]{1,0:T(8,128)(2,1)S(1)} %collective-permute-done.1.refs_2_), channel_id=1, source_target_pairs={{0,4},{4,8},{8,12},{12,14},{14,10},{10,6},{6,2},{2,0},{5,1},{9,5},... | collective-permute-start | bytes 393224 | tf_op jit(solution)/shard_map/ppermute | solution.py:212
  14.6 6.0 %collective-permute-start.19 = (bf16[4,144,128]{2,1,0:T(8,128)(2,1)S(1)}, bf16[4,144,128]{2,1,0:T(8,128)(2,1)S(1)}, u32[]{:S(2)}, u32[]{:S(2)}) collective-permute-start(bf16[4,144,128]{2,1,0:T(8,128)(2,1)S(1)} %constant_dynamic-update-slice_fusion.refs_16_), channel_id=1, source_target_pairs={{0,2},{1,3},{2,0},{3,1},{4,6},{5,7},{6,4},{7,5},{8,10},{9,11},{10,... | collective-permute-start | bytes 442376 | tf_op jit(solution)/shard_map/ppermute | solution.py:181
  15.8 5.3 %collective-permute-start.18 = (bf16[4,144,128]{2,1,0:T(8,128)(2,1)S(1)}, bf16[4,144,128]{2,1,0:T(8,128)(2,1)S(1)}, u32[]{:S(2)}, u32[]{:S(2)}) collective-permute-start(bf16[4,144,128]{2,1,0:T(8,128)(2,1)S(1)} %constant_dynamic-update-slice_fusion.refs_16_), channel_id=1, source_target_pairs={{0,1},{1,0},{2,3},{3,2},{4,5},{5,4},{6,7},{7,6},{8,9},{9,8},{10,11... | collective-permute-start | bytes 442376 | tf_op jit(solution)/shard_map/ppermute | solution.py:181
  15.8 4.8 %collective-permute-start = (bf16[128,512]{1,0:T(8,128)(2,1)S(1)}, bf16[128,512]{1,0:T(8,128)(2,1)S(1)}, u32[]{:S(2)}, u32[]{:S(2)}) collective-permute-start(bf16[128,512]{1,0:T(8,128)(2,1)S(1)} %copy-done), channel_id=1, source_target_pairs={{0,1},{1,0},{2,3},{3,2},{4,5},{5,4},{6,7},{7,6},{8,9},{9,8},{10,11... | collective-permute-start | bytes 393224 | tf_op jit(solution)/shard_map/ppermute | solution.py:181
  16.3 5.8 %collective-permute-start.7 = (bf16[128,512]{1,0:T(8,128)(2,1)S(1)}, bf16[128,512]{1,0:T(8,128)(2,1)S(1)}, u32[]{:S(2)}, u32[]{:S(2)}) collective-permute-start(bf16[128,512]{1,0:T(8,128)(2,1)S(1)} %collective-permute-done.3.refs_4_), channel_id=1, source_target_pairs={{4,0},{8,4},{12,8},{14,12},{10,14},{6,10},{2,6},{0,2},{1,5},{5,9},... | collective-permute-start | bytes 393224 | tf_op jit(solution)/shard_map/ppermute | solution.py:214
  18.1 5.7 %collective-permute-start.9 = (bf16[128,512]{1,0:T(8,128)(2,1)S(1)}, bf16[128,512]{1,0:T(8,128)(2,1)S(1)}, u32[]{:S(2)}, u32[]{:S(2)}) collective-permute-start(bf16[128,512]{1,0:T(8,128)(2,1)S(1)} %collective-permute-done.5.refs_6_), channel_id=1, source_target_pairs={{0,4},{4,8},{8,12},{12,14},{14,10},{10,6},{6,2},{2,0},{5,1},{9,5},... | collective-permute-start | bytes 393224 | tf_op jit(solution)/shard_map/ppermute | solution.py:212
  20.6 4.1 %collective-permute-start.20 = (bf16[4,144,128]{2,1,0:T(8,128)(2,1)S(1)}, bf16[4,144,128]{2,1,0:T(8,128)(2,1)S(1)}, u32[]{:S(2)}, u32[]{:S(2)}) collective-permute-start(bf16[4,144,128]{2,1,0:T(8,128)(2,1)S(1)} %collective-permute-done.19.refs_18_), channel_id=1, source_target_pairs={{0,1},{1,0},{2,3},{3,2},{4,5},{5,4},{6,7},{7,6},{8,9},{9,8},{10,11... | collective-permute-start | bytes 442376 | tf_op jit(solution)/shard_map/ppermute | solution.py:181
  20.6 3.6 %collective-permute-start.2 = (bf16[128,512]{1,0:T(8,128)(2,1)S(1)}, bf16[128,512]{1,0:T(8,128)(2,1)S(1)}, u32[]{:S(2)}, u32[]{:S(2)}) collective-permute-start(bf16[128,512]{1,0:T(8,128)(2,1)S(1)} %collective-permute-done.1.refs_2_), channel_id=1, source_target_pairs={{0,1},{1,0},{2,3},{3,2},{4,5},{5,4},{6,7},{7,6},{8,9},{9,8},{10,11... | collective-permute-start | bytes 393224 | tf_op jit(solution)/shard_map/ppermute | solution.py:181
  21.1 3.1 %collective-permute-start.4 = (bf16[128,512]{1,0:T(8,128)(2,1)S(1)}, bf16[128,512]{1,0:T(8,128)(2,1)S(1)}, u32[]{:S(2)}, u32[]{:S(2)}) collective-permute-start(bf16[128,512]{1,0:T(8,128)(2,1)S(1)} %collective-permute-done.3.refs_4_), channel_id=1, source_target_pairs={{0,1},{1,0},{2,3},{3,2},{4,5},{5,4},{6,7},{7,6},{8,9},{9,8},{10,11... | collective-permute-start | bytes 393224 | tf_op jit(solution)/shard_map/ppermute | solution.py:181
  22.2 5.0 %collective-permute-start.11 = (bf16[128,512]{1,0:T(8,128)(2,1)S(1)}, bf16[128,512]{1,0:T(8,128)(2,1)S(1)}, u32[]{:S(2)}, u32[]{:S(2)}) collective-permute-start(bf16[128,512]{1,0:T(8,128)(2,1)S(1)} %collective-permute-done.7.refs_8_), channel_id=1, source_target_pairs={{4,0},{8,4},{12,8},{14,12},{10,14},{6,10},{2,6},{0,2},{1,5},{5,9},... | collective-permute-start | bytes 393224 | tf_op jit(solution)/shard_map/ppermute | solution.py:214
  23.8 5.0 %collective-permute-start.13 = (bf16[128,512]{1,0:T(8,128)(2,1)S(1)}, bf16[128,512]{1,0:T(8,128)(2,1)S(1)}, u32[]{:S(2)}, u32[]{:S(2)}) collective-permute-start(bf16[128,512]{1,0:T(8,128)(2,1)S(1)} %collective-permute-done.9.refs_10_), channel_id=1, source_target_pairs={{0,4},{4,8},{8,12},{12,14},{14,10},{10,6},{6,2},{2,0},{5,1},{9,5},... | collective-permute-start | bytes 393224 | tf_op jit(solution)/shard_map/ppermute | solution.py:212
  24.2 4.5 %collective-permute-start.6 = (bf16[128,512]{1,0:T(8,128)(2,1)S(1)}, bf16[128,512]{1,0:T(8,128)(2,1)S(1)}, u32[]{:S(2)}, u32[]{:S(2)}) collective-permute-start(bf16[128,512]{1,0:T(8,128)(2,1)S(1)} %collective-permute-done.5.refs_6_), channel_id=1, source_target_pairs={{0,1},{1,0},{2,3},{3,2},{4,5},{5,4},{6,7},{7,6},{8,9},{9,8},{10,11... | collective-permute-start | bytes 393224 | tf_op jit(solution)/shard_map/ppermute | solution.py:181
  24.2 4.5 %collective-permute-start.8 = (bf16[128,512]{1,0:T(8,128)(2,1)S(1)}, bf16[128,512]{1,0:T(8,128)(2,1)S(1)}, u32[]{:S(2)}, u32[]{:S(2)}) collective-permute-start(bf16[128,512]{1,0:T(8,128)(2,1)S(1)} %collective-permute-done.7.refs_8_), channel_id=1, source_target_pairs={{0,1},{1,0},{2,3},{3,2},{4,5},{5,4},{6,7},{7,6},{8,9},{9,8},{10,11... | collective-permute-start | bytes 393224 | tf_op jit(solution)/shard_map/ppermute | solution.py:181
  24.7 4.0 %collective-permute-start.10 = (bf16[128,512]{1,0:T(8,128)(2,1)S(1)}, bf16[128,512]{1,0:T(8,128)(2,1)S(1)}, u32[]{:S(2)}, u32[]{:S(2)}) collective-permute-start(bf16[128,512]{1,0:T(8,128)(2,1)S(1)} %collective-permute-done.9.refs_10_), channel_id=1, source_target_pairs={{0,1},{1,0},{2,3},{3,2},{4,5},{5,4},{6,7},{7,6},{8,9},{9,8},{10,11... | collective-permute-start | bytes 393224 | tf_op jit(solution)/shard_map/ppermute | solution.py:181
  27.2 1.6 %collective-permute-start.12 = (bf16[128,512]{1,0:T(8,128)(2,1)S(1)}, bf16[128,512]{1,0:T(8,128)(2,1)S(1)}, u32[]{:S(2)}, u32[]{:S(2)}) collective-permute-start(bf16[128,512]{1,0:T(8,128)(2,1)S(1)} %collective-permute-done.11.refs_12_), channel_id=1, source_target_pairs={{0,1},{1,0},{2,3},{3,2},{4,5},{5,4},{6,7},{7,6},{8,9},{9,8},{10,11... | collective-permute-start | bytes 393224 | tf_op jit(solution)/shard_map/ppermute | solution.py:181
  28.7 1.3 %collective-permute-start.14 = (bf16[128,512]{1,0:T(8,128)(2,1)S(1)}, bf16[128,512]{1,0:T(8,128)(2,1)S(1)}, u32[]{:S(2)}, u32[]{:S(2)}) collective-permute-start(bf16[128,512]{1,0:T(8,128)(2,1)S(1)} %collective-permute-done.13.refs_14_), channel_id=1, source_target_pairs={{0,1},{1,0},{2,3},{3,2},{4,5},{5,4},{6,7},{7,6},{8,9},{9,8},{10,11... | collective-permute-start | bytes 393224 | tf_op jit(solution)/shard_map/ppermute | solution.py:181

commit v6 on v5

--- a/solution.py
+++ b/solution.py
@@ -80,33 +80,27 @@
     )(integrals, mu, nu, counts)
 
 
-def transform_kernel(source_of, n_c, n_x, *refs):
+def transform_kernel(place_of, n_c, n_x, *refs):
     c_in, x_in = refs[:n_c], refs[n_c : n_c + n_x]
-    out, c_all, x_all, tags, codes, index, half, left, sems = refs[n_c + n_x :]
+    out, c_all, codes, index, half, left, sem = refs[n_c + n_x :]
     o = lax.axis_index("orb")
     devices = codes.shape[0]
-    orbitals = c_all.shape[1]
+    orbitals = c_in[0].shape[1]
     blocks = orbitals // LANES
-    early, late = [], []
     per = devices // n_x
     for q, piece in enumerate(x_in):
-        place = pl.ds(q * per, per)
-        early.append(pltpu.make_async_copy(piece.at[:, pl.ds(2 * SB, TAG)], tags.at[place], sems.at[q]))
-        late.append(pltpu.make_async_copy(piece.at[:, pl.ds(0, 2 * SB)], x_all.at[place], sems.at[n_x + q]))
-    for q, piece in enumerate(c_in):
-        rows = c_all.shape[0] // n_c
-        place = pl.ds(pl.multiple_of(source_of(q) * rows, rows), rows)
-        late.append(pltpu.make_async_copy(piece, c_all.at[place], sems.at[2 * n_x + q]))
-    for copy in early + late:
-        copy.start()
-    for copy in early:
-        copy.wait()
-    codes[...] = tags[:, 0, :].astype(jnp.float32).astype(jnp.int32)
-    to_scalars = pltpu.make_async_copy(codes, index, sems.at[2 * n_x + n_c])
+        tag = piece[:, 2 * SB :, :][:, 0, :]
+        codes[q * per : (q + 1) * per, :] = tag.astype(jnp.float32).astype(jnp.int32)
+    to_scalars = pltpu.make_async_copy(codes, index, sem)
     to_scalars.start()
+    if n_c == 1:
+        (c_all,) = c_in
+    else:
+        for q, piece in enumerate(c_in):
+            for at, row in place_of(q):
+                rows = c_all.shape[0] // devices
+                c_all[pl.ds(pl.multiple_of(row * rows, rows), rows), :] = piece[at * rows : (at + 1) * rows, :]
     to_scalars.wait()
-    for copy in late:
-        copy.wait()
 
     mine = pl.ds(pl.multiple_of(o * LANES, LANES), LANES)
     low = lax.broadcasted_iota(jnp.int32, (SB, LANES), 1) < SB
@@ -120,7 +114,8 @@
             device = chunk * CHUNK + d
             stacked = []
             for k in range(2):
-                tile = x_all[device, k * SB : (k + 1) * SB, :]
+                piece, at = (x_in[d // per], d % per) if chunks == 1 else (x_in[0], device)
+                tile = piece[at, k * SB : (k + 1) * SB, :]
                 stacked += [jnp.where(low, tile, jnp.zeros_like(tile)), jnp.where(low, jnp.zeros_like(tile), tile)]
             mu_one, nu_one, mu_two, nu_two = (index[device, n] for n in range(4))
             rows = jnp.concatenate([c_all[rows_of(nu_one)], c_all[rows_of(nu_two)]], 0)
@@ -148,29 +143,32 @@
         lax.fori_loop(0, chunks, chunk_step, 0)
 
 
-def transform(source_of, c_pieces, x_pieces):
+def transform(place_of, c_pieces, x_pieces):
     orbitals = c_pieces[0].shape[1]
     devices = sum(piece.shape[0] for piece in x_pieces)
     n_c, n_x = len(c_pieces), len(x_pieces)
     wide = CHUNK * 2 * SB
+    joined = sum(piece.shape[0] for piece in c_pieces) if n_c > 1 else TAG
     return pl.pallas_call(
-        functools.partial(transform_kernel, source_of, n_c, n_x),
+        functools.partial(transform_kernel, place_of, n_c, n_x),
         out_shape=jax.ShapeDtypeStruct((2 * orbitals // LANES * LANES, LANES), jnp.float32),
-        in_specs=[pl.BlockSpec(memory_space=pl.ANY)] * (n_c + n_x),
+        in_specs=[pl.BlockSpec(memory_space=pltpu.VMEM)] * (n_c + n_x),
         out_specs=pl.BlockSpec(memory_space=pltpu.VMEM),
         scratch_shapes=[
-            pltpu.VMEM((c_pieces[0].shape[0] * n_c, orbitals), jnp.bfloat16),
-            pltpu.VMEM((devices, 2 * SB, LANES), jnp.bfloat16),
-            pltpu.VMEM((devices, TAG, LANES), jnp.bfloat16),
+            pltpu.VMEM((joined, orbitals), jnp.bfloat16),
             pltpu.VMEM((devices, LANES), jnp.int32),
             pltpu.SMEM((devices, LANES), jnp.int32),
             pltpu.VMEM((wide, 2 * orbitals), jnp.bfloat16),
             pltpu.VMEM((wide, LANES), jnp.bfloat16),
-            pltpu.SemaphoreType.DMA((n_c + 2 * n_x + 1,)),
+            pltpu.SemaphoreType.DMA,
         ],
         compiler_params=pltpu.CompilerParams(vmem_limit_bytes=40 << 20),
         name="transform",
     )(*c_pieces, *x_pieces)
+
+
+def together(*arrays):
+    return lax.optimization_barrier(arrays)
 
 
 def shift(array, axis, size, step):
@@ -196,7 +194,7 @@
     place = jnp.where(o < 2, p, length - 1 - p)
     place = lax.rem(place + jnp.where(core == 0, length - step, length + step), length)
     down = place >= n_pair
-    return jnp.where(down, (length - 1 - place) * n_orb + 2, place * n_orb) + core
+    return jnp.where(down, (length - 1 - place) * n_orb + 2, place * n_orb), core
 
 
 def body(n_pair, n_orb, integrals, mu_block, nu_block, counts, coeff):
@@ -204,25 +202,35 @@
     columns = kets // n_pair
     orbitals = coeff.shape[1]
     everyone = ("pair", "orb")
-    if n_orb == 4 and n_pair <= 4:
-        forward = around(n_pair, n_orb)
-        backward = [(b, a) for a, b in forward]
-        held = {0: coeff}
-        for step in range(1, n_pair + 1):
-            held[step] = lax.ppermute(held[step - 1], everyone, forward)
-            if step < n_pair:
-                held[-step] = lax.ppermute(held[1 - step], everyone, backward)
-        packed = pack(n_pair, integrals, mu_block, nu_block, counts)
-        line = jnp.concatenate([packed[0]] + [shift(packed[s], "pair", n_pair, s) for s in range(1, n_pair)], 0)
+    if n_orb == 4 and n_pair == 4:
+        ring = around(n_pair, n_orb)
+        swapped = flip(coeff, "orb", n_orb, 1)
+        half = coeff.shape[0]
+        start = jnp.concatenate([coeff, swapped], 0)
+        first = lax.ppermute(start, everyone, ring)
+        first, packed = together(first, pack(n_pair, integrals, mu_block, nu_block, counts))
+        second = lax.ppermute(first, everyone, ring)
+        moved = [shift(packed[s], "pair", n_pair, s) for s in (1, 2)]
+        second, moved, last = together(second, moved, packed[3])
+        third = lax.ppermute(second, everyone, ring)
+        moved.append(shift(last, "pair", n_pair, 3))
+        third, moved = together(third, moved)
+        fourth = lax.ppermute(third[:half], everyone, ring)
+        line = jnp.concatenate([packed[0]] + moved, 0)
         across = flip(line, "orb", n_orb, 2)
         x_pieces = [line, flip(line, "orb", n_orb, 1), across, flip(across, "orb", n_orb, 1)]
-        c_pieces, came = [], []
-        for step, piece in held.items():
-            c_pieces += [piece, flip(piece, "orb", n_orb, 1)]
-            came += [(step, 0), (step, 1)]
-
-        def source_of(q):
-            return ring_source(n_pair, n_orb, *came[q])
+        held = [start, first, second, third, fourth]
+        c_pieces, came = [coeff, swapped], [(0, 0, 0), (0, 0, 1)]
+        for step in range(1, n_pair + 1):
+            c_pieces += [held[step], flip(held[step], "orb", n_orb, 1)]
+            came += [(step, 0, 0), (step, 1, 0)]
+
+        def place_of(q):
+            step, flipped, other = came[q]
+            chip, core = ring_source(n_pair, n_orb, step, flipped)
+            if 0 < step < n_pair:
+                return [(0, chip + core), (1, chip + 1 - core)]
+            return [(0, chip + (core ^ other))]
     else:
         kept = jnp.arange(slots, dtype=jnp.int32) < counts[0]
         tiles = jnp.where(kept[:, None, None], integrals, jnp.zeros_like(integrals))
@@ -235,9 +243,8 @@
         x_pieces = [lax.all_gather(line, "orb", axis=0, tiled=True)]
         c_pieces = [lax.all_gather(coeff, everyone, axis=0, tiled=True)]
 
-        def source_of(q):
-            return q
-    out = transform(source_of, c_pieces, x_pieces)
+        place_of = None
+    out = transform(place_of, c_pieces, x_pieces)
     out = out.reshape(orbitals // n_orb, orbitals // LANES, columns, LANES)
     return out.transpose(0, 2, 1, 3).reshape(orbitals // n_orb, columns, orbitals)
 

time: 37.3 us -> 39 us (1.046)
  waiting for transfers between devices: 9.44 us -> 14 us
  Pallas kernels: 8.79 us -> 5.24 us
  other arithmetic: 0 us -> 0.92 us
    ppermute x3, waiting for transfers between devices: 0.88 us -> 4.56 us  [shift(): lax.ppermute(array, axis, [(i, (i + step) % size) for i in range(size)])]
    pallas_call x1, Pallas kernels: 7.07 us -> 3.52 us  [transform(): pl.pallas_call(functools.partial(transform_kernel, place_of, n_c, n_x), o...]
    ppermute x11 -> x8, waiting for transfers between devices: 2.76 us -> 5.43 us  [flip(): return lax.ppermute(array, axis, [(i, i ^ bit) for i in range(size)])]
    ppermute x7 -> x4, waiting for transfers between devices: 5.8 us -> 3.98 us  [the longest x1 1.89 us: body(): first = lax.ppermute(start, everyone, ring)]
    ppermute x7 -> x4, starting transfers between devices: 8.45 us -> 7.13 us  [the longest x1 2.99 us: body(): first = lax.ppermute(start, everyone, ring)]
    ppermute x11 -> x8, starting transfers between devices: 2.91 us -> 3.86 us  [flip(): return lax.ppermute(array, axis, [(i, i ^ bit) for i in range(size)])]
    concatenate x0 -> x1, other arithmetic: none -> 0.92 us  [body(): start = jnp.concatenate([coeff, swapped], 0)]
  transfers between devices with their start and end apart: 21 -> 15, of which waited for: 8 -> 9; matrix products, arithmetic and copies ran while one was open for 2% -> 2% of each run, Pallas kernels for 5% -> 4%
where the time goes in v6:
time: 39 us; the launch traced here: 38.8 us
  starting transfers between devices  17.2 us (44%)
  waiting for transfers between devices  14 us (36%)
  Pallas kernels  5.24 us (13%)
  other arithmetic  0.92 us (2%)
  local copies, waits for them, and re-layouts  0.82 us (2%)
  between operations  0.7 us (2%)
    ppermute x3, starting transfers between devices, shift(): lax.ppermute(array, axis, [(i, (i + step) % size) for i in range(size)])  6.18 us
    ppermute x8, waiting for transfers between devices, flip(): return lax.ppermute(array, axis, [(i, i ^ bit) for i in range(size)])  5.43 us
    ppermute x3, waiting for transfers between devices, shift(): lax.ppermute(array, axis, [(i, (i + step) % size) for i in range(size)])  4.56 us
    ppermute x8, starting transfers between devices, flip(): return lax.ppermute(array, axis, [(i, i ^ bit) for i in range(size)])  3.86 us
    pallas_call x1, Pallas kernels, transform(): pl.pallas_call(functools.partial(transform_kernel, place_of, n_c, n_x), o...  3.52 us
    ppermute x1, starting transfers between devices, body(): first = lax.ppermute(start, everyone, ring)  2.99 us
    ppermute x1, starting transfers between devices, body(): second = lax.ppermute(first, everyone, ring)  2.11 us
    ppermute x1, waiting for transfers between devices, body(): first = lax.ppermute(start, everyone, ring)  1.89 us
  transfers between devices with their start and end apart: 15, of which 9 were waited for; matrix products, arithmetic and copies ran while one was open for 2% of the time, Pallas kernels for 4%

profile of v6, /device:TPU:0, one launch (start us, length us, event | category | flops | bytes accessed | tf_op | source)
XLA Modules:
  0.0 38.8 jit_solution(17925803842967315119)
XLA Ops:
  0.0 0.5 %collective-permute-start = (bf16[128,512]{1,0:T(8,128)(2,1)}, bf16[128,512]{1,0:T(8,128)(2,1)S(1)}, u32[]{:S(2)}, u32[]{:S(2)}) collective-permute-start(bf16[128,512]{1,0:T(8,128)(2,1)} %refs_0_.1), channel_id=1, source_target_pairs={{0,1},{1,0},{2,3},{3,2},{4,5},{5,4},{6,7},{7,6},{8,9},{9,8},{10,11... | collective-permute-start | bytes 393224 | tf_op jit(solution)/shard_map/ppermute | solution.py:179
  0.5 1.2 %collective-permute-done.refs_1_ = bf16[128,512]{1,0:T(8,128)(2,1)S(1)} collective-permute-done((bf16[128,512]{1,0:T(8,128)(2,1)}, bf16[128,512]{1,0:T(8,128)(2,1)S(1)}, u32[]{:S(2)}, u32[]{:S(2)}) %collective-permute-start) | collective-permute-done | bytes 131104 | tf_op jit(solution)/shard_map/ppermute | solution.py:179
  1.7 0.9 %pad_maximum_fusion = bf16[256,512]{1,0:T(8,128)(2,1)S(1)} fusion(bf16[128,512]{1,0:T(8,128)(2,1)S(1)} %collective-permute-done.refs_1_, bf16[128,512]{1,0:T(8,128)(2,1)} %refs_0_.1), kind=kLoop, calls=%fused_computation | loop fusion | flops 524288 | bytes 524288 | tf_op jit(solution)/shard_map/concatenate | solution.py:209
  2.6 3.0 %collective-permute-start.1 = (bf16[256,512]{1,0:T(8,128)(2,1)S(1)}, bf16[256,512]{1,0:T(8,128)(2,1)S(1)}, u32[]{:S(2)}, u32[]{:S(2)}) collective-permute-start(bf16[256,512]{1,0:T(8,128)(2,1)S(1)} %pad_maximum_fusion), channel_id=1, source_target_pairs={{0,4},{4,8},{8,12},{12,14},{14,10},{10,6},{6,2},{2,0},{5,1},{9,5},... | collective-permute-start | bytes 786440 | tf_op jit(solution)/shard_map/ppermute | solution.py:210
  6.2 1.7 %pack.1 = (bf16[1,144,128]{2,1,0:T(8,128)(2,1)}, bf16[1,144,128]{2,1,0:T(8,128)(2,1)}, bf16[1,144,128]{2,1,0:T(8,128)(2,1)}, bf16[1,144,128]{2,1,0:T(8,128)(2,1)}) custom-call(bf16[2,8,4096]{2,1,0:T(8,128)(2,1)} %integrals.1, s32[2]{0:T(128)} %mu.1, s32[2]{0:T(128)} %nu.1, s32[1]{0:T(128)S(6)} %copy.10.counts), custom_call_target="tpu_custom_call" | custom-call | tf_op jit(solution)/shard_map/pack/pallas_call | solution.py:65
  7.9 1.9 %collective-permute-done.1.refs_2_ = bf16[256,512]{1,0:T(8,128)(2,1)S(1)} collective-permute-done((bf16[256,512]{1,0:T(8,128)(2,1)S(1)}, bf16[256,512]{1,0:T(8,128)(2,1)S(1)}, u32[]{:S(2)}, u32[]{:S(2)}) %collective-permute-start.1) | collective-permute-done | bytes 262176 | tf_op jit(solution)/shard_map/ppermute | solution.py:210
  9.8 2.1 %collective-permute-start.3 = (bf16[256,512]{1,0:T(8,128)(2,1)S(1)}, bf16[256,512]{1,0:T(8,128)(2,1)S(1)}, u32[]{:S(2)}, u32[]{:S(2)}) collective-permute-start(bf16[256,512]{1,0:T(8,128)(2,1)S(1)} %collective-permute-done.1.refs_2_), channel_id=1, source_target_pairs={{0,4},{4,8},{8,12},{12,14},{14,10},{10,6},{6,2},{2,0},{5,1},{9,5},... | collective-permute-start | bytes 786440 | tf_op jit(solution)/shard_map/ppermute | solution.py:212
  11.9 1.6 %collective-permute-start.4 = (bf16[1,144,128]{2,1,0:T(8,128)(2,1)}, bf16[1,144,128]{2,1,0:T(8,128)(2,1)S(1)}, u32[]{:S(2)}, u32[]{:S(2)}) collective-permute-start(bf16[1,144,128]{2,1,0:T(8,128)(2,1)} %get-tuple-element.27), channel_id=1, source_target_pairs={{0,4},{4,8},{8,12},{12,0},{1,5},{5,9},{9,13},{13,1},{2,6},{6,10},{... | collective-permute-start | bytes 110600 | tf_op jit(solution)/shard_map/ppermute | solution.py:175
  13.5 2.5 %collective-permute-start.5 = (bf16[1,144,128]{2,1,0:T(8,128)(2,1)}, bf16[1,144,128]{2,1,0:T(8,128)(2,1)S(1)}, u32[]{:S(2)}, u32[]{:S(2)}) collective-permute-start(bf16[1,144,128]{2,1,0:T(8,128)(2,1)} %get-tuple-element.28), channel_id=1, source_target_pairs={{0,8},{4,12},{8,0},{12,4},{1,9},{5,13},{9,1},{13,5},{2,10},{6,14},... | collective-permute-start | bytes 110600 | tf_op jit(solution)/shard_map/ppermute | solution.py:175
  16.0 2.3 %collective-permute-done.4 = bf16[1,144,128]{2,1,0:T(8,128)(2,1)S(1)} collective-permute-done((bf16[1,144,128]{2,1,0:T(8,128)(2,1)}, bf16[1,144,128]{2,1,0:T(8,128)(2,1)S(1)}, u32[]{:S(2)}, u32[]{:S(2)}) %collective-permute-start.4) | collective-permute-done | bytes 36896 | tf_op jit(solution)/shard_map/ppermute | solution.py:175
  18.3 0.4 %collective-permute-done.5 = bf16[1,144,128]{2,1,0:T(8,128)(2,1)S(1)} collective-permute-done((bf16[1,144,128]{2,1,0:T(8,128)(2,1)}, bf16[1,144,128]{2,1,0:T(8,128)(2,1)S(1)}, u32[]{:S(2)}, u32[]{:S(2)}) %collective-permute-start.5) | collective-permute-done | bytes 36896 | tf_op jit(solution)/shard_map/ppermute | solution.py:175
  18.7 0.0 collective-permute-done.3.refs_4_
  18.7 1.5 %collective-permute-start.7 = (bf16[256,512]{1,0:T(8,128)(2,1)S(1)}, bf16[256,512]{1,0:T(8,128)(2,1)S(1)}, u32[]{:S(2)}, u32[]{:S(2)}) collective-permute-start(bf16[256,512]{1,0:T(8,128)(2,1)S(1)} %collective-permute-done.3.refs_4_), channel_id=1, source_target_pairs={{0,4},{4,8},{8,12},{12,14},{14,10},{10,6},{6,2},{2,0},{5,1},{9,5},... | collective-permute-start | bytes 786440 | tf_op jit(solution)/shard_map/ppermute | solution.py:215
  20.2 0.0 collective-permute-start.2
  20.2 2.1 %collective-permute-start.8 = (bf16[1,144,128]{2,1,0:T(8,128)(2,1)}, bf16[1,144,128]{2,1,0:T(8,128)(2,1)S(1)}, u32[]{:S(2)}, u32[]{:S(2)}) collective-permute-start(bf16[1,144,128]{2,1,0:T(8,128)(2,1)} %get-tuple-element.33), channel_id=1, source_target_pairs={{0,12},{4,0},{8,4},{12,8},{1,13},{5,1},{9,5},{13,9},{2,14},{6,2},{... | collective-permute-start | bytes 110600 | tf_op jit(solution)/shard_map/ppermute | solution.py:175
  22.3 0.8 %constant_dynamic-update-slice_fusion.3 = bf16[4,144,128]{2,1,0:T(8,128)(2,1)S(1)} fusion(bf16[1,144,128]{2,1,0:T(8,128)(2,1)} %get-tuple-element.35), kind=kLoop, calls=%fused_computation.4 | loop fusion | bytes 73728
  23.0 1.9 %collective-permute-done.8 = bf16[1,144,128]{2,1,0:T(8,128)(2,1)S(1)} collective-permute-done((bf16[1,144,128]{2,1,0:T(8,128)(2,1)}, bf16[1,144,128]{2,1,0:T(8,128)(2,1)S(1)}, u32[]{:S(2)}, u32[]{:S(2)}) %collective-permute-start.8) | collective-permute-done | bytes 36896 | tf_op jit(solution)/shard_map/ppermute | solution.py:175
  24.9 1.0 %collective-permute-done.7.refs_6_ = bf16[256,512]{1,0:T(8,128)(2,1)S(1)} collective-permute-done((bf16[256,512]{1,0:T(8,128)(2,1)S(1)}, bf16[256,512]{1,0:T(8,128)(2,1)S(1)}, u32[]{:S(2)}, u32[]{:S(2)}) %collective-permute-start.7) | collective-permute-done | bytes 262176 | tf_op jit(solution)/shard_map/ppermute | solution.py:215
  26.0 0.0 copy-start
  26.0 2.9 %collective-permute-start.13 = (bf16[4,144,128]{2,1,0:T(8,128)(2,1)S(1)}, bf16[4,144,128]{2,1,0:T(8,128)(2,1)S(1)}, u32[]{:S(2)}, u32[]{:S(2)}) collective-permute-start(bf16[4,144,128]{2,1,0:T(8,128)(2,1)S(1)} %constant_dynamic-update-slice_fusion.refs_10_), channel_id=1, source_target_pairs={{0,2},{1,3},{2,0},{3,1},{4,6},{5,7},{6,4},{7,5},{8,10},{9,11},{10,... | collective-permute-start | bytes 442376 | tf_op jit(solution)/shard_map/ppermute | solution.py:179
  28.9 0.0 collective-permute-start.6
  28.9 0.5 %collective-permute-start.10 = (bf16[128,512]{1,0:T(8,128)(2,1)S(1)}, bf16[128,512]{1,0:T(8,128)(2,1)S(1)}, u32[]{:S(2)}, u32[]{:S(2)}) collective-permute-start(bf16[128,512]{1,0:T(8,128)(2,1)S(1)} %slice.3), channel_id=1, source_target_pairs={{0,4},{4,8},{8,12},{12,14},{14,10},{10,6},{6,2},{2,0},{5,1},{9,5},... | collective-permute-start | bytes 393224 | tf_op jit(solution)/shard_map/ppermute | solution.py:218
  29.5 0.1 collective-permute-start.9
  29.5 0.0 collective-permute-done.2.refs_3_
  29.6 0.4 %collective-permute-start.12 = (bf16[4,144,128]{2,1,0:T(8,128)(2,1)S(1)}, bf16[4,144,128]{2,1,0:T(8,128)(2,1)S(1)}, u32[]{:S(2)}, u32[]{:S(2)}) collective-permute-start(bf16[4,144,128]{2,1,0:T(8,128)(2,1)S(1)} %constant_dynamic-update-slice_fusion.refs_10_), channel_id=1, source_target_pairs={{0,1},{1,0},{2,3},{3,2},{4,5},{5,4},{6,7},{7,6},{8,9},{9,8},{10,11... | collective-permute-start | bytes 442376 | tf_op jit(solution)/shard_map/ppermute | solution.py:179
  30.0 2.9 %collective-permute-done.13.refs_12_ = bf16[4,144,128]{2,1,0:T(8,128)(2,1)S(1)} collective-permute-done((bf16[4,144,128]{2,1,0:T(8,128)(2,1)S(1)}, bf16[4,144,128]{2,1,0:T(8,128)(2,1)S(1)}, u32[]{:S(2)}, u32[]{:S(2)}) %collective-permute-start.13) | collective-permute-done | bytes 147488 | tf_op jit(solution)/shard_map/ppermute | solution.py:179
  32.9 0.0 collective-permute-start.14
  32.9 1.1 %collective-permute-done.10.refs_8_ = bf16[128,512]{1,0:T(8,128)(2,1)S(1)} collective-permute-done((bf16[128,512]{1,0:T(8,128)(2,1)S(1)}, bf16[128,512]{1,0:T(8,128)(2,1)S(1)}, u32[]{:S(2)}, u32[]{:S(2)}) %collective-permute-start.10) | collective-permute-done | bytes 131104 | tf_op jit(solution)/shard_map/ppermute | solution.py:218
  33.9 0.0 collective-permute-start.11
  33.9 0.0 collective-permute-done.6.refs_5_
  33.9 0.0 collective-permute-done.12.refs_11_
  33.9 1.3 %collective-permute-done.11.refs_9_ = bf16[128,512]{1,0:T(8,128)(2,1)S(1)} collective-permute-done((bf16[128,512]{1,0:T(8,128)(2,1)S(1)}, bf16[128,512]{1,0:T(8,128)(2,1)S(1)}, u32[]{:S(2)}, u32[]{:S(2)}) %collective-permute-start.11) | collective-permute-done | bytes 131104 | tf_op jit(solution)/shard_map/ppermute | solution.py:179
  35.3 0.0 collective-permute-done.9.refs_7_
  35.3 0.0 collective-permute-done.14.refs_13_
  35.3 0.0 copy-done
  35.3 3.5 %transform.1 = f32[1024,128]{1,0:T(8,128)} custom-call(bf16[128,512]{1,0:T(8,128)(2,1)S(1)} %copy-done, bf16[128,512]{1,0:T(8,128)(2,1)S(1)} %collective-permute-done.refs_1_, bf16[256,512]{1,0:T(8,128)(2,1)S(1)} %collective-permute-done.1.refs_2_, bf16[256,512]{1,0:T(8,128)(2,1)S(1)} %collective-permute-done.2.refs_3_, ...), custom_call_target="tpu_custom_call" | custom-call | tf_op jit(solution)/shard_map/transform/pallas_call | solution.py:152
  (4 shorter events, 0.0 us)
Async XLA Ops:
  0.0 1.6 %collective-permute-start = (bf16[128,512]{1,0:T(8,128)(2,1)}, bf16[128,512]{1,0:T(8,128)(2,1)S(1)}, u32[]{:S(2)}, u32[]{:S(2)}) collective-permute-start(bf16[128,512]{1,0:T(8,128)(2,1)} %refs_0_.1), channel_id=1, source_target_pairs={{0,1},{1,0},{2,3},{3,2},{4,5},{5,4},{6,7},{7,6},{8,9},{9,8},{10,11... | collective-permute-start | bytes 393224 | tf_op jit(solution)/shard_map/ppermute | solution.py:179
  2.6 7.3 %collective-permute-start.1 = (bf16[256,512]{1,0:T(8,128)(2,1)S(1)}, bf16[256,512]{1,0:T(8,128)(2,1)S(1)}, u32[]{:S(2)}, u32[]{:S(2)}) collective-permute-start(bf16[256,512]{1,0:T(8,128)(2,1)S(1)} %pad_maximum_fusion), channel_id=1, source_target_pairs={{0,4},{4,8},{8,12},{12,14},{14,10},{10,6},{6,2},{2,0},{5,1},{9,5},... | collective-permute-start | bytes 786440 | tf_op jit(solution)/shard_map/ppermute | solution.py:210
  9.8 8.8 %collective-permute-start.3 = (bf16[256,512]{1,0:T(8,128)(2,1)S(1)}, bf16[256,512]{1,0:T(8,128)(2,1)S(1)}, u32[]{:S(2)}, u32[]{:S(2)}) collective-permute-start(bf16[256,512]{1,0:T(8,128)(2,1)S(1)} %collective-permute-done.1.refs_2_), channel_id=1, source_target_pairs={{0,4},{4,8},{8,12},{12,14},{14,10},{10,6},{6,2},{2,0},{5,1},{9,5},... | collective-permute-start | bytes 786440 | tf_op jit(solution)/shard_map/ppermute | solution.py:212
  11.9 6.3 %collective-permute-start.4 = (bf16[1,144,128]{2,1,0:T(8,128)(2,1)}, bf16[1,144,128]{2,1,0:T(8,128)(2,1)S(1)}, u32[]{:S(2)}, u32[]{:S(2)}) collective-permute-start(bf16[1,144,128]{2,1,0:T(8,128)(2,1)} %get-tuple-element.27), channel_id=1, source_target_pairs={{0,4},{4,8},{8,12},{12,0},{1,5},{5,9},{9,13},{13,1},{2,6},{6,10},{... | collective-permute-start | bytes 110600 | tf_op jit(solution)/shard_map/ppermute | solution.py:175
  13.5 5.1 %collective-permute-start.5 = (bf16[1,144,128]{2,1,0:T(8,128)(2,1)}, bf16[1,144,128]{2,1,0:T(8,128)(2,1)S(1)}, u32[]{:S(2)}, u32[]{:S(2)}) collective-permute-start(bf16[1,144,128]{2,1,0:T(8,128)(2,1)} %get-tuple-element.28), channel_id=1, source_target_pairs={{0,8},{4,12},{8,0},{12,4},{1,9},{5,13},{9,1},{13,5},{2,10},{6,14},... | collective-permute-start | bytes 110600 | tf_op jit(solution)/shard_map/ppermute | solution.py:175
  18.7 7.3 %collective-permute-start.7 = (bf16[256,512]{1,0:T(8,128)(2,1)S(1)}, bf16[256,512]{1,0:T(8,128)(2,1)S(1)}, u32[]{:S(2)}, u32[]{:S(2)}) collective-permute-start(bf16[256,512]{1,0:T(8,128)(2,1)S(1)} %collective-permute-done.3.refs_4_), channel_id=1, source_target_pairs={{0,4},{4,8},{8,12},{12,14},{14,10},{10,6},{6,2},{2,0},{5,1},{9,5},... | collective-permute-start | bytes 786440 | tf_op jit(solution)/shard_map/ppermute | solution.py:215
  20.2 9.4 %collective-permute-start.2 = (bf16[256,512]{1,0:T(8,128)(2,1)S(1)}, bf16[256,512]{1,0:T(8,128)(2,1)S(1)}, u32[]{:S(2)}, u32[]{:S(2)}) collective-permute-start(bf16[256,512]{1,0:T(8,128)(2,1)S(1)} %collective-permute-done.1.refs_2_), channel_id=1, source_target_pairs={{0,1},{1,0},{2,3},{3,2},{4,5},{5,4},{6,7},{7,6},{8,9},{9,8},{10,11... | collective-permute-start | bytes 786440 | tf_op jit(solution)/shard_map/ppermute | solution.py:179
  20.2 4.8 %collective-permute-start.8 = (bf16[1,144,128]{2,1,0:T(8,128)(2,1)}, bf16[1,144,128]{2,1,0:T(8,128)(2,1)S(1)}, u32[]{:S(2)}, u32[]{:S(2)}) collective-permute-start(bf16[1,144,128]{2,1,0:T(8,128)(2,1)} %get-tuple-element.33), channel_id=1, source_target_pairs={{0,12},{4,0},{8,4},{12,8},{1,13},{5,1},{9,5},{13,9},{2,14},{6,2},{... | collective-permute-start | bytes 110600 | tf_op jit(solution)/shard_map/ppermute | solution.py:175
  26.0 9.3 %copy-start = (bf16[128,512]{1,0:T(8,128)(2,1)S(1)}, bf16[128,512]{1,0:T(8,128)(2,1)}, u32[]{:S(2)}) copy-start(bf16[128,512]{1,0:T(8,128)(2,1)} %refs_0_.1) | copy-start | bytes 393220
  26.0 6.8 %collective-permute-start.13 = (bf16[4,144,128]{2,1,0:T(8,128)(2,1)S(1)}, bf16[4,144,128]{2,1,0:T(8,128)(2,1)S(1)}, u32[]{:S(2)}, u32[]{:S(2)}) collective-permute-start(bf16[4,144,128]{2,1,0:T(8,128)(2,1)S(1)} %constant_dynamic-update-slice_fusion.refs_10_), channel_id=1, source_target_pairs={{0,2},{1,3},{2,0},{3,1},{4,6},{5,7},{6,4},{7,5},{8,10},{9,11},{10,... | collective-permute-start | bytes 442376 | tf_op jit(solution)/shard_map/ppermute | solution.py:179
  28.9 5.0 %collective-permute-start.6 = (bf16[256,512]{1,0:T(8,128)(2,1)S(1)}, bf16[256,512]{1,0:T(8,128)(2,1)S(1)}, u32[]{:S(2)}, u32[]{:S(2)}) collective-permute-start(bf16[256,512]{1,0:T(8,128)(2,1)S(1)} %collective-permute-done.3.refs_4_), channel_id=1, source_target_pairs={{0,1},{1,0},{2,3},{3,2},{4,5},{5,4},{6,7},{7,6},{8,9},{9,8},{10,11... | collective-permute-start | bytes 786440 | tf_op jit(solution)/shard_map/ppermute | solution.py:179
  28.9 5.0 %collective-permute-start.10 = (bf16[128,512]{1,0:T(8,128)(2,1)S(1)}, bf16[128,512]{1,0:T(8,128)(2,1)S(1)}, u32[]{:S(2)}, u32[]{:S(2)}) collective-permute-start(bf16[128,512]{1,0:T(8,128)(2,1)S(1)} %slice.3), channel_id=1, source_target_pairs={{0,4},{4,8},{8,12},{12,14},{14,10},{10,6},{6,2},{2,0},{5,1},{9,5},... | collective-permute-start | bytes 393224 | tf_op jit(solution)/shard_map/ppermute | solution.py:218
  29.5 5.8 %collective-permute-start.9 = (bf16[256,512]{1,0:T(8,128)(2,1)S(1)}, bf16[256,512]{1,0:T(8,128)(2,1)S(1)}, u32[]{:S(2)}, u32[]{:S(2)}) collective-permute-start(bf16[256,512]{1,0:T(8,128)(2,1)S(1)} %collective-permute-done.7.refs_6_), channel_id=1, source_target_pairs={{0,1},{1,0},{2,3},{3,2},{4,5},{5,4},{6,7},{7,6},{8,9},{9,8},{10,11... | collective-permute-start | bytes 786440 | tf_op jit(solution)/shard_map/ppermute | solution.py:179
  29.6 4.4 %collective-permute-start.12 = (bf16[4,144,128]{2,1,0:T(8,128)(2,1)S(1)}, bf16[4,144,128]{2,1,0:T(8,128)(2,1)S(1)}, u32[]{:S(2)}, u32[]{:S(2)}) collective-permute-start(bf16[4,144,128]{2,1,0:T(8,128)(2,1)S(1)} %constant_dynamic-update-slice_fusion.refs_10_), channel_id=1, source_target_pairs={{0,1},{1,0},{2,3},{3,2},{4,5},{5,4},{6,7},{7,6},{8,9},{9,8},{10,11... | collective-permute-start | bytes 442376 | tf_op jit(solution)/shard_map/ppermute | solution.py:179
  32.9 2.4 %collective-permute-start.14 = (bf16[4,144,128]{2,1,0:T(8,128)(2,1)S(1)}, bf16[4,144,128]{2,1,0:T(8,128)(2,1)S(1)}, u32[]{:S(2)}, u32[]{:S(2)}) collective-permute-start(bf16[4,144,128]{2,1,0:T(8,128)(2,1)S(1)} %collective-permute-done.13.refs_12_), channel_id=1, source_target_pairs={{0,1},{1,0},{2,3},{3,2},{4,5},{5,4},{6,7},{7,6},{8,9},{9,8},{10,11... | collective-permute-start | bytes 442376 | tf_op jit(solution)/shard_map/ppermute | solution.py:179
  33.9 1.3 %collective-permute-start.11 = (bf16[128,512]{1,0:T(8,128)(2,1)S(1)}, bf16[128,512]{1,0:T(8,128)(2,1)S(1)}, u32[]{:S(2)}, u32[]{:S(2)}) collective-permute-start(bf16[128,512]{1,0:T(8,128)(2,1)S(1)} %collective-permute-done.10.refs_8_), channel_id=1, source_target_pairs={{0,1},{1,0},{2,3},{3,2},{4,5},{5,4},{6,7},{7,6},{8,9},{9,8},{10,11... | collective-permute-start | bytes 393224 | tf_op jit(solution)/shard_map/ppermute | solution.py:179

commit v7 on v6

--- a/solution.py
+++ b/solution.py
@@ -64,7 +64,7 @@
     hbm, smem = pl.BlockSpec(memory_space=pltpu.HBM), pl.BlockSpec(memory_space=pltpu.SMEM)
     return pl.pallas_call(
         functools.partial(pack_kernel, n_pair),
-        out_shape=[jax.ShapeDtypeStruct((1, rows, LANES), jnp.bfloat16)] * n_pair,
+        out_shape=[pltpu.VMEM((1, rows, LANES), jnp.bfloat16)] * n_pair,
         in_specs=[hbm, hbm, hbm, smem],
         out_specs=[pl.BlockSpec(memory_space=pltpu.VMEM)] * n_pair,
         scratch_shapes=[
@@ -75,7 +75,7 @@
             pltpu.VMEM((kets * SB, LANES), jnp.float32),
             pltpu.SemaphoreType.DMA((3,)),
         ],
-        compiler_params=pltpu.CompilerParams(vmem_limit_bytes=60 << 20),
+        compiler_params=pltpu.CompilerParams(vmem_limit_bytes=56 << 20),
         name="pack",
     )(integrals, mu, nu, counts)
 
@@ -184,17 +184,16 @@
     ups = [p * n_orb for p in range(n_pair)]
     stops = ups + [stop + n_orb // 2 for stop in reversed(ups)]
     ring = [(stops[r], stops[(r + 1) % length]) for r in range(length)]
-    return ring + [(b + 1, a + 1) for a, b in ring]
+    return ring + [(a + 1, b + 1) for a, b in ring]
 
 
 def ring_source(n_pair, n_orb, step, flipped):
     p, o = lax.axis_index("pair"), lax.axis_index("orb")
     length = 2 * n_pair
-    core = lax.rem(o, 2) ^ flipped
     place = jnp.where(o < 2, p, length - 1 - p)
-    place = lax.rem(place + jnp.where(core == 0, length - step, length + step), length)
+    place = lax.rem(place + length - step, length)
     down = place >= n_pair
-    return jnp.where(down, (length - 1 - place) * n_orb + 2, place * n_orb), core
+    return jnp.where(down, (length - 1 - place) * n_orb + 2, place * n_orb) + (lax.rem(o, 2) ^ flipped)
 
 
 def body(n_pair, n_orb, integrals, mu_block, nu_block, counts, coeff):
@@ -204,33 +203,32 @@
     everyone = ("pair", "orb")
     if n_orb == 4 and n_pair == 4:
         ring = around(n_pair, n_orb)
-        swapped = flip(coeff, "orb", n_orb, 1)
-        half = coeff.shape[0]
-        start = jnp.concatenate([coeff, swapped], 0)
-        first = lax.ppermute(start, everyone, ring)
-        first, packed = together(first, pack(n_pair, integrals, mu_block, nu_block, counts))
-        second = lax.ppermute(first, everyone, ring)
-        moved = [shift(packed[s], "pair", n_pair, s) for s in (1, 2)]
-        second, moved, last = together(second, moved, packed[3])
-        third = lax.ppermute(second, everyone, ring)
-        moved.append(shift(last, "pair", n_pair, 3))
-        third, moved = together(third, moved)
-        fourth = lax.ppermute(third[:half], everyone, ring)
-        line = jnp.concatenate([packed[0]] + moved, 0)
+        back = [(b, a) for a, b in ring]
+        held = {0: coeff}
+        held[1] = lax.ppermute(held[0], everyone, ring)
+        held[-1] = lax.ppermute(held[0], everyone, back)
+        packed = pack(n_pair, integrals, mu_block, nu_block, counts)
+        held[1], packed = together(held[1], packed)
+        held[2] = lax.ppermute(held[1], everyone, ring)
+        held[-2] = lax.ppermute(held[-1], everyone, back)
+        moved = {1: shift(packed[1], "pair", n_pair, 1)}
+        held[2], later = together(held[2], packed[3])
+        moved[3] = shift(later, "pair", n_pair, 3)
+        held[3] = lax.ppermute(held[2], everyone, ring)
+        held[-3] = lax.ppermute(held[-2], everyone, back)
+        held[2], later = together(held[2], packed[2])
+        moved[2] = shift(later, "pair", n_pair, 2)
+        held[4] = lax.ppermute(held[3], everyone, ring)
+        line = jnp.concatenate([packed[0]] + [moved[s] for s in range(1, n_pair)], 0)
         across = flip(line, "orb", n_orb, 2)
         x_pieces = [line, flip(line, "orb", n_orb, 1), across, flip(across, "orb", n_orb, 1)]
-        held = [start, first, second, third, fourth]
-        c_pieces, came = [coeff, swapped], [(0, 0, 0), (0, 0, 1)]
-        for step in range(1, n_pair + 1):
-            c_pieces += [held[step], flip(held[step], "orb", n_orb, 1)]
-            came += [(step, 0, 0), (step, 1, 0)]
+        c_pieces, came = [], []
+        for step, piece in held.items():
+            c_pieces += [piece, flip(piece, "orb", n_orb, 1)]
+            came += [(step, 0), (step, 1)]
 
         def place_of(q):
-            step, flipped, other = came[q]
-            chip, core = ring_source(n_pair, n_orb, step, flipped)
-            if 0 < step < n_pair:
-                return [(0, chip + core), (1, chip + 1 - core)]
-            return [(0, chip + (core ^ other))]
+            return [(0, ring_source(n_pair, n_orb, *came[q]))]
     else:
         kept = jnp.arange(slots, dtype=jnp.int32) < counts[0]
         tiles = jnp.where(kept[:, None, None], integrals, jnp.zeros_like(integrals))

time: 39 us -> 38.6 us (0.990)
  waiting for transfers between devices: 14 us -> 20 us
  starting transfers between devices: 17.2 us -> 13.1 us
  other arithmetic: 0.92 us -> 0 us
  local copies, waits for them, and re-layouts: 0.82 us -> 0.04 us
  Pallas kernels: 5.24 us -> 4.61 us
    ppermute x3, waiting for transfers between devices: 4.56 us -> 9.4 us  [shift(): lax.ppermute(array, axis, [(i, (i + step) % size) for i in range(size)])]
    ppermute x4 -> x7, waiting for transfers between devices: 3.98 us -> 8.74 us  [the longest x1 2.27 us: body(): held[3] = lax.ppermute(held[2], everyone, ring)]
    ppermute x8 -> x11, waiting for transfers between devices: 5.43 us -> 1.9 us  [flip(): return lax.ppermute(array, axis, [(i, i ^ bit) for i in range(size)])]
    ppermute x3, starting transfers between devices: 6.18 us -> 4.17 us  [shift(): lax.ppermute(array, axis, [(i, (i + step) % size) for i in range(size)])]
    ppermute x4 -> x7, starting transfers between devices: 7.13 us -> 5.23 us  [the longest x1 3.02 us: body(): held[1] = lax.ppermute(held[0], everyone, ring)]
    concatenate x1 -> x0, other arithmetic: 0.92 us -> none  [body(): start = jnp.concatenate([coeff, swapped], 0)]
    unnamed x5, local copies, waits for them, and re-layouts: 0.8 us -> 0.03 us
    pallas_call x1, Pallas kernels: 1.72 us -> 1.11 us  [pack(): pl.pallas_call(functools.partial(pack_kernel, n_pair), out_shape=[pltpu.V...]
  transfers between devices with their start and end apart: 15 -> 21, of which waited for: 9 -> 10; matrix products, arithmetic and copies ran while one was open for 2% -> 0% of each run, Pallas kernels for 4% -> 3%
where the time goes in v7:
time: 38.6 us; the launch traced here: 38.5 us
  waiting for transfers between devices  20 us (52%)
  starting transfers between devices  13.1 us (34%)
  Pallas kernels  4.61 us (12%)
  between operations  0.73 us (2%)
    ppermute x3, waiting for transfers between devices, shift(): lax.ppermute(array, axis, [(i, (i + step) % size) for i in range(size)])  9.4 us
    ppermute x3, starting transfers between devices, shift(): lax.ppermute(array, axis, [(i, (i + step) % size) for i in range(size)])  4.17 us
    ppermute x11, starting transfers between devices, flip(): return lax.ppermute(array, axis, [(i, i ^ bit) for i in range(size)])  3.68 us
    pallas_call x1, Pallas kernels, transform(): pl.pallas_call(functools.partial(transform_kernel, place_of, n_c, n_x), o...  3.5 us
    ppermute x1, starting transfers between devices, body(): held[1] = lax.ppermute(held[0], everyone, ring)  3.02 us
    ppermute x1, waiting for transfers between devices, body(): held[3] = lax.ppermute(held[2], everyone, ring)  2.27 us
    ppermute x1, waiting for transfers between devices, body(): held[-3] = lax.ppermute(held[-2], everyone, back)  2.1 us
    ppermute x1, waiting for transfers between devices, body(): held[1] = lax.ppermute(held[0], everyone, ring)  1.91 us
  transfers between devices with their start and end apart: 21, of which 10 were waited for; matrix products, arithmetic and copies ran while one was open for 0% of the time, Pallas kernels for 3%

profile of v7, /device:TPU:0, one launch (start us, length us, event | category | flops | bytes accessed | tf_op | source)
XLA Modules:
  0.0 38.5 jit_solution(12860922526089910480)
XLA Ops:
  0.0 0.0 copy-start
  0.0 3.0 %collective-permute-start.1 = (bf16[128,512]{1,0:T(8,128)(2,1)}, bf16[128,512]{1,0:T(8,128)(2,1)S(1)}, u32[]{:S(2)}, u32[]{:S(2)}) collective-permute-start(bf16[128,512]{1,0:T(8,128)(2,1)} %refs_0_.1), channel_id=1, source_target_pairs={{0,4},{4,8},{8,12},{12,14},{14,10},{10,6},{6,2},{2,0},{1,5},{5,9},... | collective-permute-start | bytes 393224 | tf_op jit(solution)/shard_map/ppermute | solution.py:208
  3.0 0.0 collective-permute-start.3
  3.7 1.1 %pack.1 = (bf16[1,144,128]{2,1,0:T(8,128)(2,1)S(1)}, bf16[1,144,128]{2,1,0:T(8,128)(2,1)S(1)}, bf16[1,144,128]{2,1,0:T(8,128)(2,1)S(1)}, bf16[1,144,128]{2,1,0:T(8,128)(2,1)S(1)}) custom-call(bf16[2,8,4096]{2,1,0:T(8,128)(2,1)} %integrals.1, s32[2]{0:T(128)} %mu.1, s32[2]{0:T(128)} %nu.1, s32[1]{0:T(128)S(6)} %copy.10.counts), custom_call_target="tpu_custom_call" | custom-call | tf_op jit(solution)/shard_map/pack/pallas_call | solution.py:65
  4.8 1.9 %collective-permute-done.1.refs_2_ = bf16[128,512]{1,0:T(8,128)(2,1)S(1)} collective-permute-done((bf16[128,512]{1,0:T(8,128)(2,1)}, bf16[128,512]{1,0:T(8,128)(2,1)S(1)}, u32[]{:S(2)}, u32[]{:S(2)}) %collective-permute-start.1) | collective-permute-done | bytes 131104 | tf_op jit(solution)/shard_map/ppermute | solution.py:208
  6.7 1.8 %collective-permute-start.5 = (bf16[128,512]{1,0:T(8,128)(2,1)S(1)}, bf16[128,512]{1,0:T(8,128)(2,1)S(1)}, u32[]{:S(2)}, u32[]{:S(2)}) collective-permute-start(bf16[128,512]{1,0:T(8,128)(2,1)S(1)} %collective-permute-done.1.refs_2_), channel_id=1, source_target_pairs={{0,4},{4,8},{8,12},{12,14},{14,10},{10,6},{6,2},{2,0},{1,5},{5,9},... | collective-permute-start | bytes 393224 | tf_op jit(solution)/shard_map/ppermute | solution.py:212
  8.5 0.0 copy-done
  8.5 0.0 collective-permute-start
  8.5 0.5 %collective-permute-start.2 = (bf16[128,512]{1,0:T(8,128)(2,1)S(1)}, bf16[128,512]{1,0:T(8,128)(2,1)S(1)}, u32[]{:S(2)}, u32[]{:S(2)}) collective-permute-start(bf16[128,512]{1,0:T(8,128)(2,1)S(1)} %collective-permute-done.1.refs_2_), channel_id=1, source_target_pairs={{0,1},{1,0},{2,3},{3,2},{4,5},{5,4},{6,7},{7,6},{8,9},{9,8},{10,11... | collective-permute-start | bytes 393224 | tf_op jit(solution)/shard_map/ppermute | solution.py:179
  9.0 1.6 %collective-permute-start.15 = (bf16[1,144,128]{2,1,0:T(8,128)(2,1)S(1)}, bf16[1,144,128]{2,1,0:T(8,128)(2,1)S(1)}, u32[]{:S(2)}, u32[]{:S(2)}) collective-permute-start(bf16[1,144,128]{2,1,0:T(8,128)(2,1)S(1)} %get-tuple-element.28), channel_id=1, source_target_pairs={{0,4},{4,8},{8,12},{12,0},{1,5},{5,9},{9,13},{13,1},{2,6},{6,10},{... | collective-permute-start | bytes 110600 | tf_op jit(solution)/shard_map/ppermute | solution.py:175
  10.6 0.0 collective-permute-done.3.refs_4_
  10.6 0.4 collective-permute-start.7
  10.9 0.7 %collective-permute-done.5.refs_6_ = bf16[128,512]{1,0:T(8,128)(2,1)S(1)} collective-permute-done((bf16[128,512]{1,0:T(8,128)(2,1)S(1)}, bf16[128,512]{1,0:T(8,128)(2,1)S(1)}, u32[]{:S(2)}, u32[]{:S(2)}) %collective-permute-start.5) | collective-permute-done | bytes 131104 | tf_op jit(solution)/shard_map/ppermute | solution.py:212
  11.7 0.0 collective-permute-start.4
  11.7 3.2 %collective-permute-done.15 = bf16[1,144,128]{2,1,0:T(8,128)(2,1)S(1)} collective-permute-done((bf16[1,144,128]{2,1,0:T(8,128)(2,1)S(1)}, bf16[1,144,128]{2,1,0:T(8,128)(2,1)S(1)}, u32[]{:S(2)}, u32[]{:S(2)}) %collective-permute-start.15) | collective-permute-done | bytes 36896 | tf_op jit(solution)/shard_map/ppermute | solution.py:175
  14.9 0.6 %collective-permute-start.16 = (bf16[1,144,128]{2,1,0:T(8,128)(2,1)S(1)}, bf16[1,144,128]{2,1,0:T(8,128)(2,1)S(1)}, u32[]{:S(2)}, u32[]{:S(2)}) collective-permute-start(bf16[1,144,128]{2,1,0:T(8,128)(2,1)S(1)} %get-tuple-element.29), channel_id=1, source_target_pairs={{0,8},{4,12},{8,0},{12,4},{1,9},{5,13},{9,1},{13,5},{2,10},{6,14},... | collective-permute-start | bytes 110600 | tf_op jit(solution)/shard_map/ppermute | solution.py:175
  15.5 4.2 %collective-permute-done.16 = bf16[1,144,128]{2,1,0:T(8,128)(2,1)S(1)} collective-permute-done((bf16[1,144,128]{2,1,0:T(8,128)(2,1)S(1)}, bf16[1,144,128]{2,1,0:T(8,128)(2,1)S(1)}, u32[]{:S(2)}, u32[]{:S(2)}) %collective-permute-start.16) | collective-permute-done | bytes 36896 | tf_op jit(solution)/shard_map/ppermute | solution.py:175
  19.7 1.9 %collective-permute-start.17 = (bf16[1,144,128]{2,1,0:T(8,128)(2,1)S(1)}, bf16[1,144,128]{2,1,0:T(8,128)(2,1)S(1)}, u32[]{:S(2)}, u32[]{:S(2)}) collective-permute-start(bf16[1,144,128]{2,1,0:T(8,128)(2,1)S(1)} %get-tuple-element.30), channel_id=1, source_target_pairs={{0,12},{4,0},{8,4},{12,8},{1,13},{5,1},{9,5},{13,9},{2,14},{6,2},{... | collective-permute-start | bytes 110600 | tf_op jit(solution)/shard_map/ppermute | solution.py:175
  21.7 2.0 %collective-permute-done.17 = bf16[1,144,128]{2,1,0:T(8,128)(2,1)S(1)} collective-permute-done((bf16[1,144,128]{2,1,0:T(8,128)(2,1)S(1)}, bf16[1,144,128]{2,1,0:T(8,128)(2,1)S(1)}, u32[]{:S(2)}, u32[]{:S(2)}) %collective-permute-start.17) | collective-permute-done | bytes 36896 | tf_op jit(solution)/shard_map/ppermute | solution.py:175
  23.7 0.0 collective-permute-start.9
  23.7 0.0 collective-permute-done.refs_1_
  23.7 2.1 %collective-permute-start.19 = (bf16[4,144,128]{2,1,0:T(8,128)(2,1)S(1)}, bf16[4,144,128]{2,1,0:T(8,128)(2,1)S(1)}, u32[]{:S(2)}, u32[]{:S(2)}) collective-permute-start(bf16[4,144,128]{2,1,0:T(8,128)(2,1)S(1)} %constant_dynamic-update-slice_fusion.refs_16_), channel_id=1, source_target_pairs={{0,2},{1,3},{2,0},{3,1},{4,6},{5,7},{6,4},{7,5},{8,10},{9,11},{10,... | collective-permute-start | bytes 442376 | tf_op jit(solution)/shard_map/ppermute | solution.py:179
  25.8 0.0 collective-permute-done.7.refs_8_
  25.8 0.1 collective-permute-start.11
  25.9 0.0 collective-permute-done.4.refs_5_
  25.9 0.0 collective-permute-start.8
  25.9 0.0 collective-permute-done.2.refs_3_
  25.9 0.5 %collective-permute-start.6 = (bf16[128,512]{1,0:T(8,128)(2,1)S(1)}, bf16[128,512]{1,0:T(8,128)(2,1)S(1)}, u32[]{:S(2)}, u32[]{:S(2)}) collective-permute-start(bf16[128,512]{1,0:T(8,128)(2,1)S(1)} %collective-permute-done.5.refs_6_), channel_id=1, source_target_pairs={{0,1},{1,0},{2,3},{3,2},{4,5},{5,4},{6,7},{7,6},{8,9},{9,8},{10,11... | collective-permute-start | bytes 393224 | tf_op jit(solution)/shard_map/ppermute | solution.py:179
  26.4 2.3 %collective-permute-done.9.refs_10_ = bf16[128,512]{1,0:T(8,128)(2,1)S(1)} collective-permute-done((bf16[128,512]{1,0:T(8,128)(2,1)S(1)}, bf16[128,512]{1,0:T(8,128)(2,1)S(1)}, u32[]{:S(2)}, u32[]{:S(2)}) %collective-permute-start.9) | collective-permute-done | bytes 131104 | tf_op jit(solution)/shard_map/ppermute | solution.py:217
  28.7 0.0 collective-permute-start.13
  28.7 2.1 %collective-permute-done.11.refs_12_ = bf16[128,512]{1,0:T(8,128)(2,1)S(1)} collective-permute-done((bf16[128,512]{1,0:T(8,128)(2,1)S(1)}, bf16[128,512]{1,0:T(8,128)(2,1)S(1)}, u32[]{:S(2)}, u32[]{:S(2)}) %collective-permute-start.11) | collective-permute-done | bytes 131104 | tf_op jit(solution)/shard_map/ppermute | solution.py:218
  30.8 0.0 collective-permute-start.18
  30.8 0.6 %collective-permute-done.19.refs_18_ = bf16[4,144,128]{2,1,0:T(8,128)(2,1)S(1)} collective-permute-done((bf16[4,144,128]{2,1,0:T(8,128)(2,1)S(1)}, bf16[4,144,128]{2,1,0:T(8,128)(2,1)S(1)}, u32[]{:S(2)}, u32[]{:S(2)}) %collective-permute-start.19) | collective-permute-done | bytes 147488 | tf_op jit(solution)/shard_map/ppermute | solution.py:179
  31.4 0.0 collective-permute-start.20
  31.4 0.0 collective-permute-done.8.refs_9_
  31.4 0.5 %collective-permute-start.12 = (bf16[128,512]{1,0:T(8,128)(2,1)S(1)}, bf16[128,512]{1,0:T(8,128)(2,1)S(1)}, u32[]{:S(2)}, u32[]{:S(2)}) collective-permute-start(bf16[128,512]{1,0:T(8,128)(2,1)S(1)} %collective-permute-done.11.refs_12_), channel_id=1, source_target_pairs={{0,1},{1,0},{2,3},{3,2},{4,5},{5,4},{6,7},{7,6},{8,9},{9,8},{10,11... | collective-permute-start | bytes 393224 | tf_op jit(solution)/shard_map/ppermute | solution.py:179
  31.9 0.0 collective-permute-done.6.refs_7_
  31.9 0.1 collective-permute-start.10
  31.9 1.7 %collective-permute-done.13.refs_14_ = bf16[128,512]{1,0:T(8,128)(2,1)S(1)} collective-permute-done((bf16[128,512]{1,0:T(8,128)(2,1)S(1)}, bf16[128,512]{1,0:T(8,128)(2,1)S(1)}, u32[]{:S(2)}, u32[]{:S(2)}) %collective-permute-start.13) | collective-permute-done | bytes 131104 | tf_op jit(solution)/shard_map/ppermute | solution.py:221
  33.6 0.0 collective-permute-start.14
  33.6 0.0 collective-permute-done.18.refs_17_
  33.6 0.0 collective-permute-done.12.refs_13_
  33.7 0.0 collective-permute-done.10.refs_11_
  33.7 0.0 collective-permute-done.20.refs_19_
  33.7 1.3 %collective-permute-done.14.refs_15_ = bf16[128,512]{1,0:T(8,128)(2,1)S(1)} collective-permute-done((bf16[128,512]{1,0:T(8,128)(2,1)S(1)}, bf16[128,512]{1,0:T(8,128)(2,1)S(1)}, u32[]{:S(2)}, u32[]{:S(2)}) %collective-permute-start.14) | collective-permute-done | bytes 131104 | tf_op jit(solution)/shard_map/ppermute | solution.py:179
  35.0 3.5 %transform.1 = f32[1024,128]{1,0:T(8,128)} custom-call(bf16[128,512]{1,0:T(8,128)(2,1)S(1)} %copy-done, bf16[128,512]{1,0:T(8,128)(2,1)S(1)} %collective-permute-done.refs_1_, bf16[128,512]{1,0:T(8,128)(2,1)S(1)} %collective-permute-done.1.refs_2_, bf16[128,512]{1,0:T(8,128)(2,1)S(1)} %collective-permute-done.2.refs_3_, ...), custom_call_target="tpu_custom_call" | custom-call | tf_op jit(solution)/shard_map/transform/pallas_call | solution.py:152
  (4 shorter events, 0.0 us)
Async XLA Ops:
  0.0 8.5 %copy-start = (bf16[128,512]{1,0:T(8,128)(2,1)S(1)}, bf16[128,512]{1,0:T(8,128)(2,1)}, u32[]{:S(2)}) copy-start(bf16[128,512]{1,0:T(8,128)(2,1)} %refs_0_.1) | copy-start | bytes 393220
  0.0 6.7 %collective-permute-start.1 = (bf16[128,512]{1,0:T(8,128)(2,1)}, bf16[128,512]{1,0:T(8,128)(2,1)S(1)}, u32[]{:S(2)}, u32[]{:S(2)}) collective-permute-start(bf16[128,512]{1,0:T(8,128)(2,1)} %refs_0_.1), channel_id=1, source_target_pairs={{0,4},{4,8},{8,12},{12,14},{14,10},{10,6},{6,2},{2,0},{1,5},{5,9},... | collective-permute-start | bytes 393224 | tf_op jit(solution)/shard_map/ppermute | solution.py:208
  3.0 7.5 %collective-permute-start.3 = (bf16[128,512]{1,0:T(8,128)(2,1)}, bf16[128,512]{1,0:T(8,128)(2,1)S(1)}, u32[]{:S(2)}, u32[]{:S(2)}) collective-permute-start(bf16[128,512]{1,0:T(8,128)(2,1)} %refs_0_.1), channel_id=1, source_target_pairs={{4,0},{8,4},{12,8},{14,12},{10,14},{6,10},{2,6},{0,2},{5,1},{9,5},... | collective-permute-start | bytes 393224 | tf_op jit(solution)/shard_map/ppermute | solution.py:209
  6.7 5.0 %collective-permute-start.5 = (bf16[128,512]{1,0:T(8,128)(2,1)S(1)}, bf16[128,512]{1,0:T(8,128)(2,1)S(1)}, u32[]{:S(2)}, u32[]{:S(2)}) collective-permute-start(bf16[128,512]{1,0:T(8,128)(2,1)S(1)} %collective-permute-done.1.refs_2_), channel_id=1, source_target_pairs={{0,4},{4,8},{8,12},{12,14},{14,10},{10,6},{6,2},{2,0},{1,5},{5,9},... | collective-permute-start | bytes 393224 | tf_op jit(solution)/shard_map/ppermute | solution.py:212
  8.5 15.2 %collective-permute-start = (bf16[128,512]{1,0:T(8,128)(2,1)S(1)}, bf16[128,512]{1,0:T(8,128)(2,1)S(1)}, u32[]{:S(2)}, u32[]{:S(2)}) collective-permute-start(bf16[128,512]{1,0:T(8,128)(2,1)S(1)} %copy-done), channel_id=1, source_target_pairs={{0,1},{1,0},{2,3},{3,2},{4,5},{5,4},{6,7},{7,6},{8,9},{9,8},{10,11... | collective-permute-start | bytes 393224 | tf_op jit(solution)/shard_map/ppermute | solution.py:179
  8.5 17.4 %collective-permute-start.2 = (bf16[128,512]{1,0:T(8,128)(2,1)S(1)}, bf16[128,512]{1,0:T(8,128)(2,1)S(1)}, u32[]{:S(2)}, u32[]{:S(2)}) collective-permute-start(bf16[128,512]{1,0:T(8,128)(2,1)S(1)} %collective-permute-done.1.refs_2_), channel_id=1, source_target_pairs={{0,1},{1,0},{2,3},{3,2},{4,5},{5,4},{6,7},{7,6},{8,9},{9,8},{10,11... | collective-permute-start | bytes 393224 | tf_op jit(solution)/shard_map/ppermute | solution.py:179
  9.0 5.9 %collective-permute-start.15 = (bf16[1,144,128]{2,1,0:T(8,128)(2,1)S(1)}, bf16[1,144,128]{2,1,0:T(8,128)(2,1)S(1)}, u32[]{:S(2)}, u32[]{:S(2)}) collective-permute-start(bf16[1,144,128]{2,1,0:T(8,128)(2,1)S(1)} %get-tuple-element.28), channel_id=1, source_target_pairs={{0,4},{4,8},{8,12},{12,0},{1,5},{5,9},{9,13},{13,1},{2,6},{6,10},{... | collective-permute-start | bytes 110600 | tf_op jit(solution)/shard_map/ppermute | solution.py:175
  10.6 15.2 %collective-permute-start.7 = (bf16[128,512]{1,0:T(8,128)(2,1)S(1)}, bf16[128,512]{1,0:T(8,128)(2,1)S(1)}, u32[]{:S(2)}, u32[]{:S(2)}) collective-permute-start(bf16[128,512]{1,0:T(8,128)(2,1)S(1)} %collective-permute-done.3.refs_4_), channel_id=1, source_target_pairs={{4,0},{8,4},{12,8},{14,12},{10,14},{6,10},{2,6},{0,2},{5,1},{9,5},... | collective-permute-start | bytes 393224 | tf_op jit(solution)/shard_map/ppermute | solution.py:213
  11.7 14.2 %collective-permute-start.4 = (bf16[128,512]{1,0:T(8,128)(2,1)S(1)}, bf16[128,512]{1,0:T(8,128)(2,1)S(1)}, u32[]{:S(2)}, u32[]{:S(2)}) collective-permute-start(bf16[128,512]{1,0:T(8,128)(2,1)S(1)} %collective-permute-done.3.refs_4_), channel_id=1, source_target_pairs={{0,1},{1,0},{2,3},{3,2},{4,5},{5,4},{6,7},{7,6},{8,9},{9,8},{10,11... | collective-permute-start | bytes 393224 | tf_op jit(solution)/shard_map/ppermute | solution.py:179
  14.9 4.9 %collective-permute-start.16 = (bf16[1,144,128]{2,1,0:T(8,128)(2,1)S(1)}, bf16[1,144,128]{2,1,0:T(8,128)(2,1)S(1)}, u32[]{:S(2)}, u32[]{:S(2)}) collective-permute-start(bf16[1,144,128]{2,1,0:T(8,128)(2,1)S(1)} %get-tuple-element.29), channel_id=1, source_target_pairs={{0,8},{4,12},{8,0},{12,4},{1,9},{5,13},{9,1},{13,5},{2,10},{6,14},... | collective-permute-start | bytes 110600 | tf_op jit(solution)/shard_map/ppermute | solution.py:175
  19.7 4.0 %collective-permute-start.17 = (bf16[1,144,128]{2,1,0:T(8,128)(2,1)S(1)}, bf16[1,144,128]{2,1,0:T(8,128)(2,1)S(1)}, u32[]{:S(2)}, u32[]{:S(2)}) collective-permute-start(bf16[1,144,128]{2,1,0:T(8,128)(2,1)S(1)} %get-tuple-element.30), channel_id=1, source_target_pairs={{0,12},{4,0},{8,4},{12,8},{1,13},{5,1},{9,5},{13,9},{2,14},{6,2},{... | collective-permute-start | bytes 110600 | tf_op jit(solution)/shard_map/ppermute | solution.py:175
  23.7 5.0 %collective-permute-start.9 = (bf16[128,512]{1,0:T(8,128)(2,1)S(1)}, bf16[128,512]{1,0:T(8,128)(2,1)S(1)}, u32[]{:S(2)}, u32[]{:S(2)}) collective-permute-start(bf16[128,512]{1,0:T(8,128)(2,1)S(1)} %collective-permute-done.5.refs_6_), channel_id=1, source_target_pairs={{0,4},{4,8},{8,12},{12,14},{14,10},{10,6},{6,2},{2,0},{1,5},{5,9},... | collective-permute-start | bytes 393224 | tf_op jit(solution)/shard_map/ppermute | solution.py:217
  23.7 7.6 %collective-permute-start.19 = (bf16[4,144,128]{2,1,0:T(8,128)(2,1)S(1)}, bf16[4,144,128]{2,1,0:T(8,128)(2,1)S(1)}, u32[]{:S(2)}, u32[]{:S(2)}) collective-permute-start(bf16[4,144,128]{2,1,0:T(8,128)(2,1)S(1)} %constant_dynamic-update-slice_fusion.refs_16_), channel_id=1, source_target_pairs={{0,2},{1,3},{2,0},{3,1},{4,6},{5,7},{6,4},{7,5},{8,10},{9,11},{10,... | collective-permute-start | bytes 442376 | tf_op jit(solution)/shard_map/ppermute | solution.py:179
  25.8 5.0 %collective-permute-start.11 = (bf16[128,512]{1,0:T(8,128)(2,1)S(1)}, bf16[128,512]{1,0:T(8,128)(2,1)S(1)}, u32[]{:S(2)}, u32[]{:S(2)}) collective-permute-start(bf16[128,512]{1,0:T(8,128)(2,1)S(1)} %collective-permute-done.7.refs_8_), channel_id=1, source_target_pairs={{4,0},{8,4},{12,8},{14,12},{10,14},{6,10},{2,6},{0,2},{5,1},{9,5},... | collective-permute-start | bytes 393224 | tf_op jit(solution)/shard_map/ppermute | solution.py:218
  25.9 5.5 %collective-permute-start.8 = (bf16[128,512]{1,0:T(8,128)(2,1)S(1)}, bf16[128,512]{1,0:T(8,128)(2,1)S(1)}, u32[]{:S(2)}, u32[]{:S(2)}) collective-permute-start(bf16[128,512]{1,0:T(8,128)(2,1)S(1)} %collective-permute-done.7.refs_8_), channel_id=1, source_target_pairs={{0,1},{1,0},{2,3},{3,2},{4,5},{5,4},{6,7},{7,6},{8,9},{9,8},{10,11... | collective-permute-start | bytes 393224 | tf_op jit(solution)/shard_map/ppermute | solution.py:179
  25.9 6.0 %collective-permute-start.6 = (bf16[128,512]{1,0:T(8,128)(2,1)S(1)}, bf16[128,512]{1,0:T(8,128)(2,1)S(1)}, u32[]{:S(2)}, u32[]{:S(2)}) collective-permute-start(bf16[128,512]{1,0:T(8,128)(2,1)S(1)} %collective-permute-done.5.refs_6_), channel_id=1, source_target_pairs={{0,1},{1,0},{2,3},{3,2},{4,5},{5,4},{6,7},{7,6},{8,9},{9,8},{10,11... | collective-permute-start | bytes 393224 | tf_op jit(solution)/shard_map/ppermute | solution.py:179
  28.7 5.0 %collective-permute-start.13 = (bf16[128,512]{1,0:T(8,128)(2,1)S(1)}, bf16[128,512]{1,0:T(8,128)(2,1)S(1)}, u32[]{:S(2)}, u32[]{:S(2)}) collective-permute-start(bf16[128,512]{1,0:T(8,128)(2,1)S(1)} %collective-permute-done.9.refs_10_), channel_id=1, source_target_pairs={{0,4},{4,8},{8,12},{12,14},{14,10},{10,6},{6,2},{2,0},{1,5},{5,9},... | collective-permute-start | bytes 393224 | tf_op jit(solution)/shard_map/ppermute | solution.py:221
  30.8 2.9 %collective-permute-start.18 = (bf16[4,144,128]{2,1,0:T(8,128)(2,1)S(1)}, bf16[4,144,128]{2,1,0:T(8,128)(2,1)S(1)}, u32[]{:S(2)}, u32[]{:S(2)}) collective-permute-start(bf16[4,144,128]{2,1,0:T(8,128)(2,1)S(1)} %constant_dynamic-update-slice_fusion.refs_16_), channel_id=1, source_target_pairs={{0,1},{1,0},{2,3},{3,2},{4,5},{5,4},{6,7},{7,6},{8,9},{9,8},{10,11... | collective-permute-start | bytes 442376 | tf_op jit(solution)/shard_map/ppermute | solution.py:179
  31.4 2.3 %collective-permute-start.20 = (bf16[4,144,128]{2,1,0:T(8,128)(2,1)S(1)}, bf16[4,144,128]{2,1,0:T(8,128)(2,1)S(1)}, u32[]{:S(2)}, u32[]{:S(2)}) collective-permute-start(bf16[4,144,128]{2,1,0:T(8,128)(2,1)S(1)} %collective-permute-done.19.refs_18_), channel_id=1, source_target_pairs={{0,1},{1,0},{2,3},{3,2},{4,5},{5,4},{6,7},{7,6},{8,9},{9,8},{10,11... | collective-permute-start | bytes 442376 | tf_op jit(solution)/shard_map/ppermute | solution.py:179
  31.4 2.3 %collective-permute-start.12 = (bf16[128,512]{1,0:T(8,128)(2,1)S(1)}, bf16[128,512]{1,0:T(8,128)(2,1)S(1)}, u32[]{:S(2)}, u32[]{:S(2)}) collective-permute-start(bf16[128,512]{1,0:T(8,128)(2,1)S(1)} %collective-permute-done.11.refs_12_), channel_id=1, source_target_pairs={{0,1},{1,0},{2,3},{3,2},{4,5},{5,4},{6,7},{7,6},{8,9},{9,8},{10,11... | collective-permute-start | bytes 393224 | tf_op jit(solution)/shard_map/ppermute | solution.py:179
  31.9 1.8 %collective-permute-start.10 = (bf16[128,512]{1,0:T(8,128)(2,1)S(1)}, bf16[128,512]{1,0:T(8,128)(2,1)S(1)}, u32[]{:S(2)}, u32[]{:S(2)}) collective-permute-start(bf16[128,512]{1,0:T(8,128)(2,1)S(1)} %collective-permute-done.9.refs_10_), channel_id=1, source_target_pairs={{0,1},{1,0},{2,3},{3,2},{4,5},{5,4},{6,7},{7,6},{8,9},{9,8},{10,11... | collective-permute-start | bytes 393224 | tf_op jit(solution)/shard_map/ppermute | solution.py:179
  33.6 1.3 %collective-permute-start.14 = (bf16[128,512]{1,0:T(8,128)(2,1)S(1)}, bf16[128,512]{1,0:T(8,128)(2,1)S(1)}, u32[]{:S(2)}, u32[]{:S(2)}) collective-permute-start(bf16[128,512]{1,0:T(8,128)(2,1)S(1)} %collective-permute-done.13.refs_14_), channel_id=1, source_target_pairs={{0,1},{1,0},{2,3},{3,2},{4,5},{5,4},{6,7},{7,6},{8,9},{9,8},{10,11... | collective-permute-start | bytes 393224 | tf_op jit(solution)/shard_map/ppermute | solution.py:179

commit v8 on v7

v8 whole, which is shorter than its diff:
```python
import functools

import jax
import jax.numpy as jnp
from jax import lax
from jax.experimental import pallas as pl
from jax.experimental.pallas import tpu as pltpu
from jax.sharding import PartitionSpec as P

SB = 64
LANES = 128
TAG = 16
CHUNK = 16


def pack_kernel(n_pair, integrals, mu, nu, counts, coeff, *refs):
    outs = refs[:n_pair]
    tiles, shard, mu_in, nu_in, spread, woven, sems = refs[n_pair:]
    p = lax.axis_index("pair")
    copies = [
        pltpu.make_async_copy(source, target, sems.at[n])
        for n, (source, target) in enumerate(((integrals, tiles), (mu, mu_in), (nu, nu_in), (coeff, shard)))
    ]
    for copy in copies:
        copy.start()
    slots, kets, flat = tiles.shape
    wide = flat // LANES
    columns = kets // n_pair
    held, orbitals = shard.shape
    for copy in copies[1:3]:
        copy.wait()
    count = counts[0]
    lane = lax.broadcasted_iota(jnp.int32, (wide, LANES), 1)
    low, kept = lane < SB, lane < SB * count
    lane = lax.broadcasted_iota(jnp.int32, (TAG, LANES), 1)
    tag = jnp.zeros((TAG, LANES), jnp.int32)
    for t in range(slots):
        tag = jnp.where((lane == 2 * t) & (t < count), mu_in[t], tag)
        tag = jnp.where((lane == 2 * t + 1) & (t < count), nu_in[t], tag)
    tag = tag.astype(jnp.float32).astype(jnp.bfloat16)
    copies[0].wait()
    for t in range(slots):
        for j in range(wide):
            at = pl.ds((t * wide + j) * kets, kets)
            spread[at, :] = tiles[t, :, j * LANES : (j + 1) * LANES].astype(jnp.float32)
    tile_at, rows = orbitals // LANES * held, columns * SB
    for s in range(n_pair):
        dest = p ^ s
        for k in range(columns):
            column = dest * columns + k
            one = spread[pl.ds(column, wide, stride=kets), :]
            two = spread[pl.ds(wide * kets + column, wide, stride=kets), :]
            even = jnp.where(low, one, pltpu.roll(two, SB, axis=1))
            odd = jnp.where(low, pltpu.roll(one, SB, axis=1), two)
            begin = (s * columns + k) * SB
            woven[pl.ds(begin, wide, stride=2), :] = jnp.where(kept, even, 0.0)
            woven[pl.ds(begin + 1, wide, stride=2), :] = jnp.where(kept, odd, 0.0)
        outs[s][tile_at : tile_at + rows] = woven[pl.ds(s * rows, rows), :].astype(jnp.bfloat16)
        outs[s][tile_at + rows :] = tag
    copies[3].wait()
    for j in range(orbitals // LANES):
        lanes = shard[:, j * LANES : (j + 1) * LANES]
        for s in range(n_pair):
            outs[s][j * held : (j + 1) * held] = lanes


def pack(n_pair, integrals, mu, nu, counts, coeff):
    slots, kets, flat = integrals.shape
    rows = coeff.shape[0] * coeff.shape[1] // LANES + kets // n_pair * SB + TAG
    hbm, smem = pl.BlockSpec(memory_space=pltpu.HBM), pl.BlockSpec(memory_space=pltpu.SMEM)
    return pl.pallas_call(
        functools.partial(pack_kernel, n_pair),
        out_shape=[pltpu.VMEM((rows, LANES), jnp.bfloat16)] * n_pair,
        in_specs=[hbm, hbm, hbm, smem, hbm],
        out_specs=[pl.BlockSpec(memory_space=pltpu.VMEM)] * n_pair,
        scratch_shapes=[
            pltpu.VMEM(integrals.shape, jnp.bfloat16),
            pltpu.VMEM(coeff.shape, jnp.bfloat16),
            pltpu.SMEM(mu.shape, jnp.int32),
            pltpu.SMEM(nu.shape, jnp.int32),
            pltpu.VMEM((slots * kets * flat // LANES, LANES), jnp.float32),
            pltpu.VMEM((kets * SB, LANES), jnp.float32),
            pltpu.SemaphoreType.DMA((4,)),
        ],
        compiler_params=pltpu.CompilerParams(vmem_limit_bytes=56 << 20),
        name="pack",
    )(integrals, mu, nu, counts, coeff)


def transform_kernel(came, n_orb, orbitals, n_in, *refs):
    pieces = refs[:n_in]
    out, c_all, codes, index, half, left, sem = refs[n_in:]
    p, o = lax.axis_index("pair"), lax.axis_index("orb")
    devices = codes.shape[0]
    blocks = orbitals // LANES
    tile_at = pieces[0].shape[-2] - TAG - 2 * SB
    if came:
        for q, piece in enumerate(pieces):
            codes[q : q + 1, :] = piece[tile_at + 2 * SB :][:1].astype(jnp.float32).astype(jnp.int32)
    else:
        codes[...] = pieces[0][:, 2 * SB :, :][:, 0, :].astype(jnp.float32).astype(jnp.int32)
    to_scalars = pltpu.make_async_copy(codes, index, sem)
    to_scalars.start()
    if came:
        rows = c_all.shape[0] // devices
        for q, piece in enumerate(pieces):
            source = (p ^ came[q][0]) * n_orb + (o ^ came[q][1])
            place = pl.ds(pl.multiple_of(source * rows, rows), rows)
            for j in range(blocks):
                c_all[place, j * LANES : (j + 1) * LANES] = piece[j * rows : (j + 1) * rows, :]
    else:
        c_all = pieces[1]
    to_scalars.wait()

    mine = pl.ds(pl.multiple_of(o * LANES, LANES), LANES)
    low = lax.broadcasted_iota(jnp.int32, (SB, LANES), 1) < SB
    chunks = devices // CHUNK

    def rows_of(block):
        return pl.ds(pl.multiple_of(block * SB, SB), SB)

    def chunk_step(chunk, carry):
        for d in range(CHUNK):
            device = chunk * CHUNK + d
            stacked = []
            for k in range(2):
                if came:
                    tile = pieces[d][tile_at + k * SB : tile_at + (k + 1) * SB, :]
                else:
                    tile = pieces[0][device, k * SB : (k + 1) * SB, :]
                stacked += [jnp.where(low, tile, jnp.zeros_like(tile)), jnp.where(low, jnp.zeros_like(tile), tile)]
            mu_one, nu_one, mu_two, nu_two = (index[device, n] for n in range(4))
            rows = jnp.concatenate([c_all[rows_of(nu_one)], c_all[rows_of(nu_two)]], 0)
            moved = jnp.dot(jnp.concatenate(stacked, 0), rows, preferred_element_type=jnp.float32)
            moved = moved.astype(jnp.bfloat16)
            at = pl.ds(d * 2 * SB, 2 * SB)
            half[at, :orbitals] = moved[: 2 * SB]
            half[at, orbitals:] = moved[2 * SB :]
            left[at, :] = jnp.concatenate([c_all[rows_of(mu_one), mine], c_all[rows_of(mu_two), mine]], 0)
        part = lax.dot_general(
            left[...], half[...], (((0,), (0,)), ((), ())), preferred_element_type=jnp.float32
        )
        for k in range(2):
            for j in range(blocks):
                at = pl.ds(2 * j + k, LANES, stride=2 * blocks)
                begin = k * orbitals + j * LANES
                value = part[:, begin : begin + LANES]
                out[at, :] = value if chunks == 1 else out[at, :] + value
        return carry

    if chunks == 1:
        chunk_step(0, 0)
    else:
        out[...] = jnp.zeros_like(out)
        lax.fori_loop(0, chunks, chunk_step, 0)


def transform(came, n_orb, devices, orbitals, pieces):
    wide = CHUNK * 2 * SB
    held = pieces[0].shape[0] - 2 * SB - TAG if came else TAG
    return pl.pallas_call(
        functools.partial(transform_kernel, came, n_orb, orbitals, len(pieces)),
        out_shape=jax.ShapeDtypeStruct((2 * orbitals // LANES * LANES, LANES), jnp.float32),
        in_specs=[pl.BlockSpec(memory_space=pltpu.VMEM)] * len(pieces),
        out_specs=pl.BlockSpec(memory_space=pltpu.VMEM),
        scratch_shapes=[
            pltpu.VMEM((held * LANES // orbitals * devices if came else TAG, orbitals), jnp.bfloat16),
            pltpu.VMEM((devices, LANES), jnp.int32),
            pltpu.SMEM((devices, LANES), jnp.int32),
            pltpu.VMEM((wide, 2 * orbitals), jnp.bfloat16),
            pltpu.VMEM((wide, LANES), jnp.bfloat16),
            pltpu.SemaphoreType.DMA,
        ],
        compiler_params=pltpu.CompilerParams(vmem_limit_bytes=40 << 20),
        name="transform",
    )(*pieces)


def flip(array, axis, size, bit):
    return lax.ppermute(array, axis, [(i, i ^ bit) for i in range(size)])


def body(n_pair, n_orb, integrals, mu_block, nu_block, counts, coeff):
    slots, kets, flat = integrals.shape
    columns = kets // n_pair
    orbitals = coeff.shape[1]
    if n_orb == 4 and n_pair == 4:
        packed = pack(n_pair, integrals, mu_block, nu_block, counts, coeff)
        pieces, came = [], []
        for s in range(n_pair):
            line = flip(packed[s], "pair", n_pair, s) if s else packed[0]
            across = flip(line, "orb", n_orb, 2)
            pieces += [line, flip(line, "orb", n_orb, 1), across, flip(across, "orb", n_orb, 1)]
            came += [(s, 0), (s, 1), (s, 2), (s, 3)]
    else:
        kept = jnp.arange(slots, dtype=jnp.int32) < counts[0]
        tiles = jnp.where(kept[:, None, None], integrals, jnp.zeros_like(integrals))
        tiles = tiles.reshape(slots, n_pair, columns, SB, SB).transpose(1, 2, 3, 0, 4)
        tiles = tiles.reshape(n_pair, columns * SB, slots * SB)
        tag = jnp.where(kept[:, None], jnp.stack([mu_block, nu_block], 1), 0).reshape(-1)
        tag = jnp.zeros((n_pair, TAG, LANES), jnp.bfloat16).at[:, :, : 2 * slots].set(tag.astype(jnp.bfloat16))
        packed = jnp.concatenate([tiles, tag], 1)
        line = lax.all_to_all(packed, "pair", split_axis=0, concat_axis=0, tiled=True)
        gathered = lax.all_gather(coeff, ("pair", "orb"), axis=0, tiled=True)
        pieces, came = [lax.all_gather(line, "orb", axis=0, tiled=True), gathered], None
    out = transform(came, n_orb, n_pair * n_orb, orbitals, pieces)
    out = out.reshape(orbitals // n_orb, orbitals // LANES, columns, LANES)
    return out.transpose(0, 2, 1, 3).reshape(orbitals // n_orb, columns, orbitals)


def solution(mesh):
    placed = (
        P(("grp", "pair", "orb"), None, None),
        P(("grp", "pair", "orb")),
        P(("grp", "pair", "orb")),
        P(("grp", "pair", "orb")),
        P(("grp", "pair", "orb"), None),
    )
    return jax.shard_map(
        functools.partial(body, mesh.shape["pair"], mesh.shape["orb"]),
        mesh=mesh,
        in_specs=placed,
        out_specs=P(("grp", "orb"), "pair", None),
        check_vma=False,
    )
```

time: 38.6 us -> 35.8 us (0.927)
  waiting for transfers between devices: 20 us -> 17.7 us
  starting transfers between devices: 13.1 us -> 12.4 us
    ppermute x10 -> x0, waiting for transfers between devices: 18.1 us -> none  [the longest x3 9.4 us: shift(): lax.ppermute(array, axis, [(i, (i + step) % size) for i in range(size)])]
    ppermute x11 -> x15, waiting for transfers between devices: 1.9 us -> 17.7 us  [flip(): return lax.ppermute(array, axis, [(i, i ^ bit) for i in range(size)])]
    ppermute x10 -> x0, starting transfers between devices: 9.39 us -> none  [the longest x3 4.17 us: shift(): lax.ppermute(array, axis, [(i, (i + step) % size) for i in range(size)])]
    ppermute x11 -> x15, starting transfers between devices: 3.68 us -> 12.4 us  [flip(): return lax.ppermute(array, axis, [(i, i ^ bit) for i in range(size)])]
  transfers between devices with their start and end apart: 21 -> 15, of which waited for: 10 -> 5; matrix products, arithmetic and copies ran while one was open for 0% -> 0% of each run, Pallas kernels for 3% -> 0%
where the time goes in v8:
time: 35.8 us; the launch traced here: 35.7 us
  waiting for transfers between devices  17.7 us (49%)
  starting transfers between devices  12.4 us (35%)
  Pallas kernels  4.9 us (14%)
  between operations  0.69 us (2%)
    ppermute x15, waiting for transfers between devices, flip(): return lax.ppermute(array, axis, [(i, i ^ bit) for i in range(size)])  17.7 us
    ppermute x15, starting transfers between devices, flip(): return lax.ppermute(array, axis, [(i, i ^ bit) for i in range(size)])  12.4 us
    pallas_call x1, Pallas kernels, transform(): pl.pallas_call(functools.partial(transform_kernel, came, n_orb, orbitals,...  3.71 us
    pallas_call x1, Pallas kernels, pack(): pl.pallas_call(functools.partial(pack_kernel, n_pair), out_shape=[pltpu.V...  1.19 us
  transfers between devices with their start and end apart: 15, of which 5 were waited for; matrix products, arithmetic and copies ran while one was open for 0% of the time, Pallas kernels for 0%

profile of v8, /device:TPU:0, one launch (start us, length us, event | category | flops | bytes accessed | tf_op | source)
XLA Modules:
  0.0 35.7 jit_solution(6464043304699442731)
XLA Ops:
  0.7 1.2 %pack.1 = (bf16[656,128]{1,0:T(8,128)(2,1)S(1)}, bf16[656,128]{1,0:T(8,128)(2,1)S(1)}, bf16[656,128]{1,0:T(8,128)(2,1)S(1)}, bf16[656,128]{1,0:T(8,128)(2,1)S(1)}) custom-call(bf16[2,8,4096]{2,1,0:T(8,128)(2,1)} %integrals.1, s32[2]{0:T(128)} %mu.1, s32[2]{0:T(128)} %nu.1, s32[1]{0:T(128)S(6)} %copy.7.counts, bf16[128,512]{1,0:T(8,128)(2,1)} %coeff.1), custom_call_target="tpu_custom_call" | custom-call | tf_op jit(solution)/shard_map/pack/pallas_call | solution.py:71
  1.9 3.1 %collective-permute-start.3 = (bf16[656,128]{1,0:T(8,128)(2,1)S(1)}, bf16[656,128]{1,0:T(8,128)(2,1)S(1)}, u32[]{:S(2)}, u32[]{:S(2)}) collective-permute-start(bf16[656,128]{1,0:T(8,128)(2,1)S(1)} %get-tuple-element.10), channel_id=1, source_target_pairs={{0,4},{4,0},{8,12},{12,8},{1,5},{5,1},{9,13},{13,9},{2,6},{6,2},{1... | collective-permute-start | bytes 503816 | tf_op jit(solution)/shard_map/ppermute | solution.py:180
  4.9 2.6 %collective-permute-start.7 = (bf16[656,128]{1,0:T(8,128)(2,1)S(1)}, bf16[656,128]{1,0:T(8,128)(2,1)S(1)}, u32[]{:S(2)}, u32[]{:S(2)}) collective-permute-start(bf16[656,128]{1,0:T(8,128)(2,1)S(1)} %get-tuple-element.11), channel_id=1, source_target_pairs={{0,8},{4,12},{8,0},{12,4},{1,9},{5,13},{9,1},{13,5},{2,10},{6,14},... | collective-permute-start | bytes 503816 | tf_op jit(solution)/shard_map/ppermute | solution.py:180
  7.5 0.0 collective-permute-start.11
  7.5 1.7 %collective-permute-start.1 = (bf16[656,128]{1,0:T(8,128)(2,1)S(1)}, bf16[656,128]{1,0:T(8,128)(2,1)S(1)}, u32[]{:S(2)}, u32[]{:S(2)}) collective-permute-start(bf16[656,128]{1,0:T(8,128)(2,1)S(1)} %get-tuple-element.9.refs_0_), channel_id=1, source_target_pairs={{0,2},{1,3},{2,0},{3,1},{4,6},{5,7},{6,4},{7,5},{8,10},{9,11},{10,... | collective-permute-start | bytes 503816 | tf_op jit(solution)/shard_map/ppermute | solution.py:180
  9.2 0.0 collective-permute-start
  9.2 2.6 %collective-permute-done.3.refs_4_ = bf16[656,128]{1,0:T(8,128)(2,1)S(1)} collective-permute-done((bf16[656,128]{1,0:T(8,128)(2,1)S(1)}, bf16[656,128]{1,0:T(8,128)(2,1)S(1)}, u32[]{:S(2)}, u32[]{:S(2)}) %collective-permute-start.3) | collective-permute-done | bytes 167968 | tf_op jit(solution)/shard_map/ppermute | solution.py:180
  11.8 1.7 %collective-permute-start.5 = (bf16[656,128]{1,0:T(8,128)(2,1)S(1)}, bf16[656,128]{1,0:T(8,128)(2,1)S(1)}, u32[]{:S(2)}, u32[]{:S(2)}) collective-permute-start(bf16[656,128]{1,0:T(8,128)(2,1)S(1)} %collective-permute-done.3.refs_4_), channel_id=1, source_target_pairs={{0,2},{1,3},{2,0},{3,1},{4,6},{5,7},{6,4},{7,5},{8,10},{9,11},{10,... | collective-permute-start | bytes 503816 | tf_op jit(solution)/shard_map/ppermute | solution.py:180
  13.5 6.7 %collective-permute-done.7.refs_8_ = bf16[656,128]{1,0:T(8,128)(2,1)S(1)} collective-permute-done((bf16[656,128]{1,0:T(8,128)(2,1)S(1)}, bf16[656,128]{1,0:T(8,128)(2,1)S(1)}, u32[]{:S(2)}, u32[]{:S(2)}) %collective-permute-start.7) | collective-permute-done | bytes 167968 | tf_op jit(solution)/shard_map/ppermute | solution.py:180
  20.3 0.0 collective-permute-start.4
  20.3 0.0 collective-permute-done.11.refs_12_
  20.3 1.5 %collective-permute-start.9 = (bf16[656,128]{1,0:T(8,128)(2,1)S(1)}, bf16[656,128]{1,0:T(8,128)(2,1)S(1)}, u32[]{:S(2)}, u32[]{:S(2)}) collective-permute-start(bf16[656,128]{1,0:T(8,128)(2,1)S(1)} %collective-permute-done.7.refs_8_), channel_id=1, source_target_pairs={{0,2},{1,3},{2,0},{3,1},{4,6},{5,7},{6,4},{7,5},{8,10},{9,11},{10,... | collective-permute-start | bytes 503816 | tf_op jit(solution)/shard_map/ppermute | solution.py:180
  21.8 0.0 collective-permute-done.1.refs_2_
  21.8 0.2 collective-permute-start.8
  22.0 0.0 collective-permute-done.refs_1_
  22.0 0.5 %collective-permute-start.13 = (bf16[656,128]{1,0:T(8,128)(2,1)S(1)}, bf16[656,128]{1,0:T(8,128)(2,1)S(1)}, u32[]{:S(2)}, u32[]{:S(2)}) collective-permute-start(bf16[656,128]{1,0:T(8,128)(2,1)S(1)} %collective-permute-done.11.refs_12_), channel_id=1, source_target_pairs={{0,2},{1,3},{2,0},{3,1},{4,6},{5,7},{6,4},{7,5},{8,10},{9,11},{10,... | collective-permute-start | bytes 503816 | tf_op jit(solution)/shard_map/ppermute | solution.py:180
  22.5 0.0 collective-permute-done.5.refs_6_
  22.5 0.0 collective-permute-start.12
  22.5 0.0 collective-permute-done.4.refs_5_
  22.5 0.5 %collective-permute-start.2 = (bf16[656,128]{1,0:T(8,128)(2,1)S(1)}, bf16[656,128]{1,0:T(8,128)(2,1)S(1)}, u32[]{:S(2)}, u32[]{:S(2)}) collective-permute-start(bf16[656,128]{1,0:T(8,128)(2,1)S(1)} %collective-permute-done.1.refs_2_), channel_id=1, source_target_pairs={{0,1},{1,0},{2,3},{3,2},{4,5},{5,4},{6,7},{7,6},{8,9},{9,8},{10,11... | collective-permute-start | bytes 503816 | tf_op jit(solution)/shard_map/ppermute | solution.py:180
  23.0 4.3 %collective-permute-done.9.refs_10_ = bf16[656,128]{1,0:T(8,128)(2,1)S(1)} collective-permute-done((bf16[656,128]{1,0:T(8,128)(2,1)S(1)}, bf16[656,128]{1,0:T(8,128)(2,1)S(1)}, u32[]{:S(2)}, u32[]{:S(2)}) %collective-permute-start.9) | collective-permute-done | bytes 167968 | tf_op jit(solution)/shard_map/ppermute | solution.py:180
  27.3 0.0 collective-permute-start.6
  27.3 0.0 collective-permute-done.8.refs_9_
  27.4 0.5 %collective-permute-start.10 = (bf16[656,128]{1,0:T(8,128)(2,1)S(1)}, bf16[656,128]{1,0:T(8,128)(2,1)S(1)}, u32[]{:S(2)}, u32[]{:S(2)}) collective-permute-start(bf16[656,128]{1,0:T(8,128)(2,1)S(1)} %collective-permute-done.9.refs_10_), channel_id=1, source_target_pairs={{0,1},{1,0},{2,3},{3,2},{4,5},{5,4},{6,7},{7,6},{8,9},{9,8},{10,11... | collective-permute-start | bytes 503816 | tf_op jit(solution)/shard_map/ppermute | solution.py:180
  27.9 2.7 %collective-permute-done.13.refs_14_ = bf16[656,128]{1,0:T(8,128)(2,1)S(1)} collective-permute-done((bf16[656,128]{1,0:T(8,128)(2,1)S(1)}, bf16[656,128]{1,0:T(8,128)(2,1)S(1)}, u32[]{:S(2)}, u32[]{:S(2)}) %collective-permute-start.13) | collective-permute-done | bytes 167968 | tf_op jit(solution)/shard_map/ppermute | solution.py:180
  30.6 0.0 collective-permute-start.14
  30.6 0.0 collective-permute-done.12.refs_13_
  30.6 0.0 collective-permute-done.2.refs_3_
  30.6 0.0 collective-permute-done.6.refs_7_
  30.6 0.0 collective-permute-done.10.refs_11_
  30.6 1.4 %collective-permute-done.14.refs_15_ = bf16[656,128]{1,0:T(8,128)(2,1)S(1)} collective-permute-done((bf16[656,128]{1,0:T(8,128)(2,1)S(1)}, bf16[656,128]{1,0:T(8,128)(2,1)S(1)}, u32[]{:S(2)}, u32[]{:S(2)}) %collective-permute-start.14) | collective-permute-done | bytes 167968 | tf_op jit(solution)/shard_map/ppermute | solution.py:180
  32.0 3.7 %transform.1 = f32[1024,128]{1,0:T(8,128)} custom-call(bf16[656,128]{1,0:T(8,128)(2,1)S(1)} %get-tuple-element.9.refs_0_, bf16[656,128]{1,0:T(8,128)(2,1)S(1)} %collective-permute-done.refs_1_, bf16[656,128]{1,0:T(8,128)(2,1)S(1)} %collective-permute-done.1.refs_2_, bf16[656,128]{1,0:T(8,128)(2,1)S(1)} %collective-permute-done.2.refs_3_, ...), custom_call_target="tpu_custom_call" | custom-call | tf_op jit(solution)/shard_map/transform/pallas_call | solution.py:161
Async XLA Ops:
  1.9 10.0 %collective-permute-start.3 = (bf16[656,128]{1,0:T(8,128)(2,1)S(1)}, bf16[656,128]{1,0:T(8,128)(2,1)S(1)}, u32[]{:S(2)}, u32[]{:S(2)}) collective-permute-start(bf16[656,128]{1,0:T(8,128)(2,1)S(1)} %get-tuple-element.10), channel_id=1, source_target_pairs={{0,4},{4,0},{8,12},{12,8},{1,5},{5,1},{9,13},{13,9},{2,6},{6,2},{1... | collective-permute-start | bytes 503816 | tf_op jit(solution)/shard_map/ppermute | solution.py:180
  4.9 15.3 %collective-permute-start.7 = (bf16[656,128]{1,0:T(8,128)(2,1)S(1)}, bf16[656,128]{1,0:T(8,128)(2,1)S(1)}, u32[]{:S(2)}, u32[]{:S(2)}) collective-permute-start(bf16[656,128]{1,0:T(8,128)(2,1)S(1)} %get-tuple-element.11), channel_id=1, source_target_pairs={{0,8},{4,12},{8,0},{12,4},{1,9},{5,13},{9,1},{13,5},{2,10},{6,14},... | collective-permute-start | bytes 503816 | tf_op jit(solution)/shard_map/ppermute | solution.py:180
  7.5 12.7 %collective-permute-start.11 = (bf16[656,128]{1,0:T(8,128)(2,1)S(1)}, bf16[656,128]{1,0:T(8,128)(2,1)S(1)}, u32[]{:S(2)}, u32[]{:S(2)}) collective-permute-start(bf16[656,128]{1,0:T(8,128)(2,1)S(1)} %get-tuple-element.12), channel_id=1, source_target_pairs={{0,12},{4,8},{8,4},{12,0},{1,13},{5,9},{9,5},{13,1},{2,14},{6,10},... | collective-permute-start | bytes 503816 | tf_op jit(solution)/shard_map/ppermute | solution.py:180
  7.5 14.2 %collective-permute-start.1 = (bf16[656,128]{1,0:T(8,128)(2,1)S(1)}, bf16[656,128]{1,0:T(8,128)(2,1)S(1)}, u32[]{:S(2)}, u32[]{:S(2)}) collective-permute-start(bf16[656,128]{1,0:T(8,128)(2,1)S(1)} %get-tuple-element.9.refs_0_), channel_id=1, source_target_pairs={{0,2},{1,3},{2,0},{3,1},{4,6},{5,7},{6,4},{7,5},{8,10},{9,11},{10,... | collective-permute-start | bytes 503816 | tf_op jit(solution)/shard_map/ppermute | solution.py:180
  9.2 12.7 %collective-permute-start = (bf16[656,128]{1,0:T(8,128)(2,1)S(1)}, bf16[656,128]{1,0:T(8,128)(2,1)S(1)}, u32[]{:S(2)}, u32[]{:S(2)}) collective-permute-start(bf16[656,128]{1,0:T(8,128)(2,1)S(1)} %get-tuple-element.9.refs_0_), channel_id=1, source_target_pairs={{0,1},{1,0},{2,3},{3,2},{4,5},{5,4},{6,7},{7,6},{8,9},{9,8},{10,11... | collective-permute-start | bytes 503816 | tf_op jit(solution)/shard_map/ppermute | solution.py:180
  11.8 10.7 %collective-permute-start.5 = (bf16[656,128]{1,0:T(8,128)(2,1)S(1)}, bf16[656,128]{1,0:T(8,128)(2,1)S(1)}, u32[]{:S(2)}, u32[]{:S(2)}) collective-permute-start(bf16[656,128]{1,0:T(8,128)(2,1)S(1)} %collective-permute-done.3.refs_4_), channel_id=1, source_target_pairs={{0,2},{1,3},{2,0},{3,1},{4,6},{5,7},{6,4},{7,5},{8,10},{9,11},{10,... | collective-permute-start | bytes 503816 | tf_op jit(solution)/shard_map/ppermute | solution.py:180
  20.3 2.3 %collective-permute-start.4 = (bf16[656,128]{1,0:T(8,128)(2,1)S(1)}, bf16[656,128]{1,0:T(8,128)(2,1)S(1)}, u32[]{:S(2)}, u32[]{:S(2)}) collective-permute-start(bf16[656,128]{1,0:T(8,128)(2,1)S(1)} %collective-permute-done.3.refs_4_), channel_id=1, source_target_pairs={{0,1},{1,0},{2,3},{3,2},{4,5},{5,4},{6,7},{7,6},{8,9},{9,8},{10,11... | collective-permute-start | bytes 503816 | tf_op jit(solution)/shard_map/ppermute | solution.py:180
  20.3 7.1 %collective-permute-start.9 = (bf16[656,128]{1,0:T(8,128)(2,1)S(1)}, bf16[656,128]{1,0:T(8,128)(2,1)S(1)}, u32[]{:S(2)}, u32[]{:S(2)}) collective-permute-start(bf16[656,128]{1,0:T(8,128)(2,1)S(1)} %collective-permute-done.7.refs_8_), channel_id=1, source_target_pairs={{0,2},{1,3},{2,0},{3,1},{4,6},{5,7},{6,4},{7,5},{8,10},{9,11},{10,... | collective-permute-start | bytes 503816 | tf_op jit(solution)/shard_map/ppermute | solution.py:180
  21.8 5.6 %collective-permute-start.8 = (bf16[656,128]{1,0:T(8,128)(2,1)S(1)}, bf16[656,128]{1,0:T(8,128)(2,1)S(1)}, u32[]{:S(2)}, u32[]{:S(2)}) collective-permute-start(bf16[656,128]{1,0:T(8,128)(2,1)S(1)} %collective-permute-done.7.refs_8_), channel_id=1, source_target_pairs={{0,1},{1,0},{2,3},{3,2},{4,5},{5,4},{6,7},{7,6},{8,9},{9,8},{10,11... | collective-permute-start | bytes 503816 | tf_op jit(solution)/shard_map/ppermute | solution.py:180
  22.0 8.6 %collective-permute-start.13 = (bf16[656,128]{1,0:T(8,128)(2,1)S(1)}, bf16[656,128]{1,0:T(8,128)(2,1)S(1)}, u32[]{:S(2)}, u32[]{:S(2)}) collective-permute-start(bf16[656,128]{1,0:T(8,128)(2,1)S(1)} %collective-permute-done.11.refs_12_), channel_id=1, source_target_pairs={{0,2},{1,3},{2,0},{3,1},{4,6},{5,7},{6,4},{7,5},{8,10},{9,11},{10,... | collective-permute-start | bytes 503816 | tf_op jit(solution)/shard_map/ppermute | solution.py:180
  22.5 8.0 %collective-permute-start.12 = (bf16[656,128]{1,0:T(8,128)(2,1)S(1)}, bf16[656,128]{1,0:T(8,128)(2,1)S(1)}, u32[]{:S(2)}, u32[]{:S(2)}) collective-permute-start(bf16[656,128]{1,0:T(8,128)(2,1)S(1)} %collective-permute-done.11.refs_12_), channel_id=1, source_target_pairs={{0,1},{1,0},{2,3},{3,2},{4,5},{5,4},{6,7},{7,6},{8,9},{9,8},{10,11... | collective-permute-start | bytes 503816 | tf_op jit(solution)/shard_map/ppermute | solution.py:180
  22.5 8.0 %collective-permute-start.2 = (bf16[656,128]{1,0:T(8,128)(2,1)S(1)}, bf16[656,128]{1,0:T(8,128)(2,1)S(1)}, u32[]{:S(2)}, u32[]{:S(2)}) collective-permute-start(bf16[656,128]{1,0:T(8,128)(2,1)S(1)} %collective-permute-done.1.refs_2_), channel_id=1, source_target_pairs={{0,1},{1,0},{2,3},{3,2},{4,5},{5,4},{6,7},{7,6},{8,9},{9,8},{10,11... | collective-permute-start | bytes 503816 | tf_op jit(solution)/shard_map/ppermute | solution.py:180
  27.3 3.2 %collective-permute-start.6 = (bf16[656,128]{1,0:T(8,128)(2,1)S(1)}, bf16[656,128]{1,0:T(8,128)(2,1)S(1)}, u32[]{:S(2)}, u32[]{:S(2)}) collective-permute-start(bf16[656,128]{1,0:T(8,128)(2,1)S(1)} %collective-permute-done.5.refs_6_), channel_id=1, source_target_pairs={{0,1},{1,0},{2,3},{3,2},{4,5},{5,4},{6,7},{7,6},{8,9},{9,8},{10,11... | collective-permute-start | bytes 503816 | tf_op jit(solution)/shard_map/ppermute | solution.py:180
  27.4 3.2 %collective-permute-start.10 = (bf16[656,128]{1,0:T(8,128)(2,1)S(1)}, bf16[656,128]{1,0:T(8,128)(2,1)S(1)}, u32[]{:S(2)}, u32[]{:S(2)}) collective-permute-start(bf16[656,128]{1,0:T(8,128)(2,1)S(1)} %collective-permute-done.9.refs_10_), channel_id=1, source_target_pairs={{0,1},{1,0},{2,3},{3,2},{4,5},{5,4},{6,7},{7,6},{8,9},{9,8},{10,11... | collective-permute-start | bytes 503816 | tf_op jit(solution)/shard_map/ppermute | solution.py:180
  30.6 1.4 %collective-permute-start.14 = (bf16[656,128]{1,0:T(8,128)(2,1)S(1)}, bf16[656,128]{1,0:T(8,128)(2,1)S(1)}, u32[]{:S(2)}, u32[]{:S(2)}) collective-permute-start(bf16[656,128]{1,0:T(8,128)(2,1)S(1)} %collective-permute-done.13.refs_14_), channel_id=1, source_target_pairs={{0,1},{1,0},{2,3},{3,2},{4,5},{5,4},{6,7},{7,6},{8,9},{9,8},{10,11... | collective-permute-start | bytes 503816 | tf_op jit(solution)/shard_map/ppermute | solution.py:180

commit v9 on v8

--- a/solution.py
+++ b/solution.py
@@ -185,13 +185,16 @@
     columns = kets // n_pair
     orbitals = coeff.shape[1]
     if n_orb == 4 and n_pair == 4:
-        packed = pack(n_pair, integrals, mu_block, nu_block, counts, coeff)
-        pieces, came = [], []
-        for s in range(n_pair):
-            line = flip(packed[s], "pair", n_pair, s) if s else packed[0]
-            across = flip(line, "orb", n_orb, 2)
-            pieces += [line, flip(line, "orb", n_orb, 1), across, flip(across, "orb", n_orb, 1)]
-            came += [(s, 0), (s, 1), (s, 2), (s, 3)]
+        packed = list(pack(n_pair, integrals, mu_block, nu_block, counts, coeff))
+        lines = packed[:1] + [flip(packed[s], "pair", n_pair, s) for s in range(1, n_pair)]
+        across = [flip(line, "orb", n_orb, 2) for line in lines[:3]]
+        last, across[1] = lax.optimization_barrier((lines[3], across[1]))
+        across.append(flip(last, "orb", n_orb, 2))
+        early = lax.optimization_barrier(tuple(lines[:3] + across[:3] + [last]))
+        pieces = list(early) + across[3:]
+        pieces += [flip(piece, "orb", n_orb, 1) for piece in pieces]
+        came = [(0, 0), (1, 0), (2, 0), (0, 2), (1, 2), (2, 2), (3, 0), (3, 2)]
+        came += [(s, side ^ 1) for s, side in came]
     else:
         kept = jnp.arange(slots, dtype=jnp.int32) < counts[0]
         tiles = jnp.where(kept[:, None, None], integrals, jnp.zeros_like(integrals))

time: 35.8 us -> 33.8 us (0.944)
  waiting for transfers between devices: 17.7 us -> 16.3 us
  starting transfers between devices: 12.4 us -> 11.8 us
    ppermute x15, waiting for transfers between devices: 17.7 us -> 16.3 us  [flip(): return lax.ppermute(array, axis, [(i, i ^ bit) for i in range(size)])]
    ppermute x15, starting transfers between devices: 12.4 us -> 11.8 us  [flip(): return lax.ppermute(array, axis, [(i, i ^ bit) for i in range(size)])]
  transfers between devices with their start and end apart: 15 -> 15, of which waited for: 5 -> 9; matrix products, arithmetic and copies ran while one was open for 0% -> 0% of each run, Pallas kernels for 0% -> 0%
where the time goes in v9:
time: 33.8 us; the launch traced here: 33.7 us
  waiting for transfers between devices  16.3 us (48%)
  starting transfers between devices  11.8 us (35%)
  Pallas kernels  4.89 us (14%)
  between operations  0.68 us (2%)
    ppermute x15, waiting for transfers between devices, flip(): return lax.ppermute(array, axis, [(i, i ^ bit) for i in range(size)])  16.3 us
    ppermute x15, starting transfers between devices, flip(): return lax.ppermute(array, axis, [(i, i ^ bit) for i in range(size)])  11.8 us
    pallas_call x1, Pallas kernels, transform(): pl.pallas_call(functools.partial(transform_kernel, came, n_orb, orbitals,...  3.7 us
    pallas_call x1, Pallas kernels, pack(): pl.pallas_call(functools.partial(pack_kernel, n_pair), out_shape=[pltpu.V...  1.19 us
  transfers between devices with their start and end apart: 15, of which 9 were waited for; matrix products, arithmetic and copies ran while one was open for 0% of the time, Pallas kernels for 0%

profile of v9, /device:TPU:0, one launch (start us, length us, event | category | flops | bytes accessed | tf_op | source)
XLA Modules:
  0.0 33.7 jit_solution(7090652002921867758)
XLA Ops:
  0.7 1.2 %pack.1 = (bf16[656,128]{1,0:T(8,128)(2,1)S(1)}, bf16[656,128]{1,0:T(8,128)(2,1)S(1)}, bf16[656,128]{1,0:T(8,128)(2,1)S(1)}, bf16[656,128]{1,0:T(8,128)(2,1)S(1)}) custom-call(bf16[2,8,4096]{2,1,0:T(8,128)(2,1)} %integrals.1, s32[2]{0:T(128)} %mu.1, s32[2]{0:T(128)} %nu.1, s32[1]{0:T(128)S(6)} %copy.7.counts, bf16[128,512]{1,0:T(8,128)(2,1)} %coeff.1), custom_call_target="tpu_custom_call" | custom-call | tf_op jit(solution)/shard_map/pack/pallas_call | solution.py:71
  1.9 3.1 %collective-permute-start = (bf16[656,128]{1,0:T(8,128)(2,1)S(1)}, bf16[656,128]{1,0:T(8,128)(2,1)S(1)}, u32[]{:S(2)}, u32[]{:S(2)}) collective-permute-start(bf16[656,128]{1,0:T(8,128)(2,1)S(1)} %get-tuple-element.19), channel_id=1, source_target_pairs={{0,4},{4,0},{8,12},{12,8},{1,5},{5,1},{9,13},{13,9},{2,6},{6,2},{1... | collective-permute-start | bytes 503816 | tf_op jit(solution)/shard_map/ppermute | solution.py:180
  4.9 2.6 %collective-permute-start.1 = (bf16[656,128]{1,0:T(8,128)(2,1)S(1)}, bf16[656,128]{1,0:T(8,128)(2,1)S(1)}, u32[]{:S(2)}, u32[]{:S(2)}) collective-permute-start(bf16[656,128]{1,0:T(8,128)(2,1)S(1)} %get-tuple-element.20), channel_id=1, source_target_pairs={{0,8},{4,12},{8,0},{12,4},{1,9},{5,13},{9,1},{13,5},{2,10},{6,14},... | collective-permute-start | bytes 503816 | tf_op jit(solution)/shard_map/ppermute | solution.py:180
  7.5 0.0 collective-permute-start.3
  7.5 4.3 %collective-permute-done.refs_1_ = bf16[656,128]{1,0:T(8,128)(2,1)S(1)} collective-permute-done((bf16[656,128]{1,0:T(8,128)(2,1)S(1)}, bf16[656,128]{1,0:T(8,128)(2,1)S(1)}, u32[]{:S(2)}, u32[]{:S(2)}) %collective-permute-start) | collective-permute-done | bytes 167968 | tf_op jit(solution)/shard_map/ppermute | solution.py:180
  11.8 1.7 %collective-permute-start.4 = (bf16[656,128]{1,0:T(8,128)(2,1)S(1)}, bf16[656,128]{1,0:T(8,128)(2,1)S(1)}, u32[]{:S(2)}, u32[]{:S(2)}) collective-permute-start(bf16[656,128]{1,0:T(8,128)(2,1)S(1)} %collective-permute-done.refs_1_), channel_id=1, source_target_pairs={{0,2},{1,3},{2,0},{3,1},{4,6},{5,7},{6,4},{7,5},{8,10},{9,11},{10,... | collective-permute-start | bytes 503816 | tf_op jit(solution)/shard_map/ppermute | solution.py:180
  13.5 0.3 collective-permute-start.2
  13.8 6.4 %collective-permute-done.1.refs_2_ = bf16[656,128]{1,0:T(8,128)(2,1)S(1)} collective-permute-done((bf16[656,128]{1,0:T(8,128)(2,1)S(1)}, bf16[656,128]{1,0:T(8,128)(2,1)S(1)}, u32[]{:S(2)}, u32[]{:S(2)}) %collective-permute-start.1) | collective-permute-done | bytes 167968 | tf_op jit(solution)/shard_map/ppermute | solution.py:180
  20.3 1.5 %collective-permute-start.5 = (bf16[656,128]{1,0:T(8,128)(2,1)S(1)}, bf16[656,128]{1,0:T(8,128)(2,1)S(1)}, u32[]{:S(2)}, u32[]{:S(2)}) collective-permute-start(bf16[656,128]{1,0:T(8,128)(2,1)S(1)} %collective-permute-done.1.refs_2_), channel_id=1, source_target_pairs={{0,2},{1,3},{2,0},{3,1},{4,6},{5,7},{6,4},{7,5},{8,10},{9,11},{10,... | collective-permute-start | bytes 503816 | tf_op jit(solution)/shard_map/ppermute | solution.py:180
  21.7 0.0 collective-permute-done.3.refs_6_
  21.7 0.0 collective-permute-done.4.refs_4_
  21.7 0.5 %collective-permute-start.6 = (bf16[656,128]{1,0:T(8,128)(2,1)S(1)}, bf16[656,128]{1,0:T(8,128)(2,1)S(1)}, u32[]{:S(2)}, u32[]{:S(2)}) collective-permute-start(bf16[656,128]{1,0:T(8,128)(2,1)S(1)} %collective-permute-done.3.refs_6_), channel_id=1, source_target_pairs={{0,2},{1,3},{2,0},{3,1},{4,6},{5,7},{6,4},{7,5},{8,10},{9,11},{10,... | collective-permute-start | bytes 503816 | tf_op jit(solution)/shard_map/ppermute | solution.py:180
  22.3 0.4 %collective-permute-done.2.refs_3_ = bf16[656,128]{1,0:T(8,128)(2,1)S(1)} collective-permute-done((bf16[656,128]{1,0:T(8,128)(2,1)S(1)}, bf16[656,128]{1,0:T(8,128)(2,1)S(1)}, u32[]{:S(2)}, u32[]{:S(2)}) %collective-permute-start.2) | collective-permute-done | bytes 167968 | tf_op jit(solution)/shard_map/ppermute | solution.py:180
  22.6 3.4 %collective-permute-done.5.refs_5_ = bf16[656,128]{1,0:T(8,128)(2,1)S(1)} collective-permute-done((bf16[656,128]{1,0:T(8,128)(2,1)S(1)}, bf16[656,128]{1,0:T(8,128)(2,1)S(1)}, u32[]{:S(2)}, u32[]{:S(2)}) %collective-permute-start.5) | collective-permute-done | bytes 167968 | tf_op jit(solution)/shard_map/ppermute | solution.py:180
  26.0 0.0 collective-permute-start.7
  26.0 0.5 %collective-permute-start.8 = (bf16[656,128]{1,0:T(8,128)(2,1)S(1)}, bf16[656,128]{1,0:T(8,128)(2,1)S(1)}, u32[]{:S(2)}, u32[]{:S(2)}) collective-permute-start(bf16[656,128]{1,0:T(8,128)(2,1)S(1)} %collective-permute-done.refs_1_), channel_id=1, source_target_pairs={{0,1},{1,0},{2,3},{3,2},{4,5},{5,4},{6,7},{7,6},{8,9},{9,8},{10,11... | collective-permute-start | bytes 503816 | tf_op jit(solution)/shard_map/ppermute | solution.py:180
  26.5 0.0 collective-permute-start.9
  26.5 0.5 %collective-permute-start.10 = (bf16[656,128]{1,0:T(8,128)(2,1)S(1)}, bf16[656,128]{1,0:T(8,128)(2,1)S(1)}, u32[]{:S(2)}, u32[]{:S(2)}) collective-permute-start(bf16[656,128]{1,0:T(8,128)(2,1)S(1)} %collective-permute-done.2.refs_3_), channel_id=1, source_target_pairs={{0,1},{1,0},{2,3},{3,2},{4,5},{5,4},{6,7},{7,6},{8,9},{9,8},{10,11... | collective-permute-start | bytes 503816 | tf_op jit(solution)/shard_map/ppermute | solution.py:180
  27.0 0.8 %collective-permute-done.6.refs_7_ = bf16[656,128]{1,0:T(8,128)(2,1)S(1)} collective-permute-done((bf16[656,128]{1,0:T(8,128)(2,1)S(1)}, bf16[656,128]{1,0:T(8,128)(2,1)S(1)}, u32[]{:S(2)}, u32[]{:S(2)}) %collective-permute-start.6) | collective-permute-done | bytes 167968 | tf_op jit(solution)/shard_map/ppermute | solution.py:180
  27.8 0.0 collective-permute-start.11
  27.8 0.0 collective-permute-done.7.refs_8_
  27.8 0.5 %collective-permute-start.12 = (bf16[656,128]{1,0:T(8,128)(2,1)S(1)}, bf16[656,128]{1,0:T(8,128)(2,1)S(1)}, u32[]{:S(2)}, u32[]{:S(2)}) collective-permute-start(bf16[656,128]{1,0:T(8,128)(2,1)S(1)} %collective-permute-done.5.refs_5_), channel_id=1, source_target_pairs={{0,1},{1,0},{2,3},{3,2},{4,5},{5,4},{6,7},{7,6},{8,9},{9,8},{10,11... | collective-permute-start | bytes 503816 | tf_op jit(solution)/shard_map/ppermute | solution.py:180
  28.3 0.0 collective-permute-done.8.refs_9_
  28.3 0.1 collective-permute-start.13
  28.4 0.0 collective-permute-done.9.refs_10_
  28.4 0.4 %collective-permute-start.14 = (bf16[656,128]{1,0:T(8,128)(2,1)S(1)}, bf16[656,128]{1,0:T(8,128)(2,1)S(1)}, u32[]{:S(2)}, u32[]{:S(2)}) collective-permute-start(bf16[656,128]{1,0:T(8,128)(2,1)S(1)} %collective-permute-done.6.refs_7_), channel_id=1, source_target_pairs={{0,1},{1,0},{2,3},{3,2},{4,5},{5,4},{6,7},{7,6},{8,9},{9,8},{10,11... | collective-permute-start | bytes 503816 | tf_op jit(solution)/shard_map/ppermute | solution.py:180
  28.8 0.0 collective-permute-done.10.refs_11_
  28.8 0.4 %collective-permute-done.11.refs_12_ = bf16[656,128]{1,0:T(8,128)(2,1)S(1)} collective-permute-done((bf16[656,128]{1,0:T(8,128)(2,1)S(1)}, bf16[656,128]{1,0:T(8,128)(2,1)S(1)}, u32[]{:S(2)}, u32[]{:S(2)}) %collective-permute-start.11) | collective-permute-done | bytes 167968 | tf_op jit(solution)/shard_map/ppermute | solution.py:180
  29.2 0.2 collective-permute-done.12.refs_13_
  29.5 0.3 collective-permute-done.13.refs_14_
  29.7 0.2 collective-permute-done.14.refs_15_
  30.0 3.7 %transform.1 = f32[1024,128]{1,0:T(8,128)} custom-call(bf16[656,128]{1,0:T(8,128)(2,1)S(1)} %get-tuple-element.24.refs_0_, bf16[656,128]{1,0:T(8,128)(2,1)S(1)} %collective-permute-done.refs_1_, bf16[656,128]{1,0:T(8,128)(2,1)S(1)} %collective-permute-done.1.refs_2_, bf16[656,128]{1,0:T(8,128)(2,1)S(1)} %collective-permute-done.2.refs_3_, ...), custom_call_target="tpu_custom_call" | custom-call | tf_op jit(solution)/shard_map/transform/pallas_call | solution.py:161
Async XLA Ops:
  1.9 10.0 %collective-permute-start = (bf16[656,128]{1,0:T(8,128)(2,1)S(1)}, bf16[656,128]{1,0:T(8,128)(2,1)S(1)}, u32[]{:S(2)}, u32[]{:S(2)}) collective-permute-start(bf16[656,128]{1,0:T(8,128)(2,1)S(1)} %get-tuple-element.19), channel_id=1, source_target_pairs={{0,4},{4,0},{8,12},{12,8},{1,5},{5,1},{9,13},{13,9},{2,6},{6,2},{1... | collective-permute-start | bytes 503816 | tf_op jit(solution)/shard_map/ppermute | solution.py:180
  4.9 15.3 %collective-permute-start.1 = (bf16[656,128]{1,0:T(8,128)(2,1)S(1)}, bf16[656,128]{1,0:T(8,128)(2,1)S(1)}, u32[]{:S(2)}, u32[]{:S(2)}) collective-permute-start(bf16[656,128]{1,0:T(8,128)(2,1)S(1)} %get-tuple-element.20), channel_id=1, source_target_pairs={{0,8},{4,12},{8,0},{12,4},{1,9},{5,13},{9,1},{13,5},{2,10},{6,14},... | collective-permute-start | bytes 503816 | tf_op jit(solution)/shard_map/ppermute | solution.py:180
  7.5 14.2 %collective-permute-start.3 = (bf16[656,128]{1,0:T(8,128)(2,1)S(1)}, bf16[656,128]{1,0:T(8,128)(2,1)S(1)}, u32[]{:S(2)}, u32[]{:S(2)}) collective-permute-start(bf16[656,128]{1,0:T(8,128)(2,1)S(1)} %get-tuple-element.21), channel_id=1, source_target_pairs={{0,12},{4,8},{8,4},{12,0},{1,13},{5,9},{9,5},{13,1},{2,14},{6,10},... | collective-permute-start | bytes 503816 | tf_op jit(solution)/shard_map/ppermute | solution.py:180
  11.8 9.9 %collective-permute-start.4 = (bf16[656,128]{1,0:T(8,128)(2,1)S(1)}, bf16[656,128]{1,0:T(8,128)(2,1)S(1)}, u32[]{:S(2)}, u32[]{:S(2)}) collective-permute-start(bf16[656,128]{1,0:T(8,128)(2,1)S(1)} %collective-permute-done.refs_1_), channel_id=1, source_target_pairs={{0,2},{1,3},{2,0},{3,1},{4,6},{5,7},{6,4},{7,5},{8,10},{9,11},{10,... | collective-permute-start | bytes 503816 | tf_op jit(solution)/shard_map/ppermute | solution.py:180
  13.5 9.1 %collective-permute-start.2 = (bf16[656,128]{1,0:T(8,128)(2,1)S(1)}, bf16[656,128]{1,0:T(8,128)(2,1)S(1)}, u32[]{:S(2)}, u32[]{:S(2)}) collective-permute-start(bf16[656,128]{1,0:T(8,128)(2,1)S(1)} %get-tuple-element.24.refs_0_), channel_id=1, source_target_pairs={{0,2},{1,3},{2,0},{3,1},{4,6},{5,7},{6,4},{7,5},{8,10},{9,11},{10,... | collective-permute-start | bytes 503816 | tf_op jit(solution)/shard_map/ppermute | solution.py:180
  20.3 5.8 %collective-permute-start.5 = (bf16[656,128]{1,0:T(8,128)(2,1)S(1)}, bf16[656,128]{1,0:T(8,128)(2,1)S(1)}, u32[]{:S(2)}, u32[]{:S(2)}) collective-permute-start(bf16[656,128]{1,0:T(8,128)(2,1)S(1)} %collective-permute-done.1.refs_2_), channel_id=1, source_target_pairs={{0,2},{1,3},{2,0},{3,1},{4,6},{5,7},{6,4},{7,5},{8,10},{9,11},{10,... | collective-permute-start | bytes 503816 | tf_op jit(solution)/shard_map/ppermute | solution.py:180
  21.7 6.1 %collective-permute-start.6 = (bf16[656,128]{1,0:T(8,128)(2,1)S(1)}, bf16[656,128]{1,0:T(8,128)(2,1)S(1)}, u32[]{:S(2)}, u32[]{:S(2)}) collective-permute-start(bf16[656,128]{1,0:T(8,128)(2,1)S(1)} %collective-permute-done.3.refs_6_), channel_id=1, source_target_pairs={{0,2},{1,3},{2,0},{3,1},{4,6},{5,7},{6,4},{7,5},{8,10},{9,11},{10,... | collective-permute-start | bytes 503816 | tf_op jit(solution)/shard_map/ppermute | solution.py:180
  26.0 1.8 %collective-permute-start.7 = (bf16[656,128]{1,0:T(8,128)(2,1)S(1)}, bf16[656,128]{1,0:T(8,128)(2,1)S(1)}, u32[]{:S(2)}, u32[]{:S(2)}) collective-permute-start(bf16[656,128]{1,0:T(8,128)(2,1)S(1)} %get-tuple-element.24.refs_0_), channel_id=1, source_target_pairs={{0,1},{1,0},{2,3},{3,2},{4,5},{5,4},{6,7},{7,6},{8,9},{9,8},{10,11... | collective-permute-start | bytes 503816 | tf_op jit(solution)/shard_map/ppermute | solution.py:180
  26.0 2.3 %collective-permute-start.8 = (bf16[656,128]{1,0:T(8,128)(2,1)S(1)}, bf16[656,128]{1,0:T(8,128)(2,1)S(1)}, u32[]{:S(2)}, u32[]{:S(2)}) collective-permute-start(bf16[656,128]{1,0:T(8,128)(2,1)S(1)} %collective-permute-done.refs_1_), channel_id=1, source_target_pairs={{0,1},{1,0},{2,3},{3,2},{4,5},{5,4},{6,7},{7,6},{8,9},{9,8},{10,11... | collective-permute-start | bytes 503816 | tf_op jit(solution)/shard_map/ppermute | solution.py:180
  26.5 1.9 %collective-permute-start.9 = (bf16[656,128]{1,0:T(8,128)(2,1)S(1)}, bf16[656,128]{1,0:T(8,128)(2,1)S(1)}, u32[]{:S(2)}, u32[]{:S(2)}) collective-permute-start(bf16[656,128]{1,0:T(8,128)(2,1)S(1)} %collective-permute-done.1.refs_2_), channel_id=1, source_target_pairs={{0,1},{1,0},{2,3},{3,2},{4,5},{5,4},{6,7},{7,6},{8,9},{9,8},{10,11... | collective-permute-start | bytes 503816 | tf_op jit(solution)/shard_map/ppermute | solution.py:180
  26.5 2.3 %collective-permute-start.10 = (bf16[656,128]{1,0:T(8,128)(2,1)S(1)}, bf16[656,128]{1,0:T(8,128)(2,1)S(1)}, u32[]{:S(2)}, u32[]{:S(2)}) collective-permute-start(bf16[656,128]{1,0:T(8,128)(2,1)S(1)} %collective-permute-done.2.refs_3_), channel_id=1, source_target_pairs={{0,1},{1,0},{2,3},{3,2},{4,5},{5,4},{6,7},{7,6},{8,9},{9,8},{10,11... | collective-permute-start | bytes 503816 | tf_op jit(solution)/shard_map/ppermute | solution.py:180
  27.8 1.4 %collective-permute-start.11 = (bf16[656,128]{1,0:T(8,128)(2,1)S(1)}, bf16[656,128]{1,0:T(8,128)(2,1)S(1)}, u32[]{:S(2)}, u32[]{:S(2)}) collective-permute-start(bf16[656,128]{1,0:T(8,128)(2,1)S(1)} %collective-permute-done.4.refs_4_), channel_id=1, source_target_pairs={{0,1},{1,0},{2,3},{3,2},{4,5},{5,4},{6,7},{7,6},{8,9},{9,8},{10,11... | collective-permute-start | bytes 503816 | tf_op jit(solution)/shard_map/ppermute | solution.py:180
  27.8 1.6 %collective-permute-start.12 = (bf16[656,128]{1,0:T(8,128)(2,1)S(1)}, bf16[656,128]{1,0:T(8,128)(2,1)S(1)}, u32[]{:S(2)}, u32[]{:S(2)}) collective-permute-start(bf16[656,128]{1,0:T(8,128)(2,1)S(1)} %collective-permute-done.5.refs_5_), channel_id=1, source_target_pairs={{0,1},{1,0},{2,3},{3,2},{4,5},{5,4},{6,7},{7,6},{8,9},{9,8},{10,11... | collective-permute-start | bytes 503816 | tf_op jit(solution)/shard_map/ppermute | solution.py:180
  28.3 1.4 %collective-permute-start.13 = (bf16[656,128]{1,0:T(8,128)(2,1)S(1)}, bf16[656,128]{1,0:T(8,128)(2,1)S(1)}, u32[]{:S(2)}, u32[]{:S(2)}) collective-permute-start(bf16[656,128]{1,0:T(8,128)(2,1)S(1)} %collective-permute-done.3.refs_6_), channel_id=1, source_target_pairs={{0,1},{1,0},{2,3},{3,2},{4,5},{5,4},{6,7},{7,6},{8,9},{9,8},{10,11... | collective-permute-start | bytes 503816 | tf_op jit(solution)/shard_map/ppermute | solution.py:180
  28.4 1.6 %collective-permute-start.14 = (bf16[656,128]{1,0:T(8,128)(2,1)S(1)}, bf16[656,128]{1,0:T(8,128)(2,1)S(1)}, u32[]{:S(2)}, u32[]{:S(2)}) collective-permute-start(bf16[656,128]{1,0:T(8,128)(2,1)S(1)} %collective-permute-done.6.refs_7_), channel_id=1, source_target_pairs={{0,1},{1,0},{2,3},{3,2},{4,5},{5,4},{6,7},{7,6},{8,9},{9,8},{10,11... | collective-permute-start | bytes 503816 | tf_op jit(solution)/shard_map/ppermute | solution.py:180

commit v10 on v9

--- a/solution.py
+++ b/solution.py
@@ -14,8 +14,11 @@
 
 
 def pack_kernel(n_pair, integrals, mu, nu, counts, coeff, *refs):
-    outs = refs[:n_pair]
-    tiles, shard, mu_in, nu_in, spread, woven, sems = refs[n_pair:]
+    own, one_off, two_off, tiles, shard, mu_in, nu_in, spread, woven, sems = refs
+    rows = shard.shape[0] * shard.shape[1] // LANES
+    reach = integrals.shape[1] // n_pair * SB + TAG
+    tile_spots = ((own, rows), (one_off, rows), (two_off, reach + rows), (two_off, 0))
+    shard_spots = ((own, 0), (one_off, 0), (two_off, reach))
     p = lax.axis_index("pair")
     copies = [
         pltpu.make_async_copy(source, target, sems.at[n])
@@ -43,7 +46,7 @@
         for j in range(wide):
             at = pl.ds((t * wide + j) * kets, kets)
             spread[at, :] = tiles[t, :, j * LANES : (j + 1) * LANES].astype(jnp.float32)
-    tile_at, rows = orbitals // LANES * held, columns * SB
+    rows = columns * SB
     for s in range(n_pair):
         dest = p ^ s
         for k in range(columns):
@@ -55,24 +58,26 @@
             begin = (s * columns + k) * SB
             woven[pl.ds(begin, wide, stride=2), :] = jnp.where(kept, even, 0.0)
             woven[pl.ds(begin + 1, wide, stride=2), :] = jnp.where(kept, odd, 0.0)
-        outs[s][tile_at : tile_at + rows] = woven[pl.ds(s * rows, rows), :].astype(jnp.bfloat16)
-        outs[s][tile_at + rows :] = tag
+        target, at = tile_spots[s]
+        target[at : at + rows] = woven[pl.ds(s * rows, rows), :].astype(jnp.bfloat16)
+        target[at + rows : at + rows + TAG] = tag
     copies[3].wait()
     for j in range(orbitals // LANES):
         lanes = shard[:, j * LANES : (j + 1) * LANES]
-        for s in range(n_pair):
-            outs[s][j * held : (j + 1) * held] = lanes
+        for target, at in shard_spots:
+            target[at + j * held : at + (j + 1) * held] = lanes
 
 
 def pack(n_pair, integrals, mu, nu, counts, coeff):
     slots, kets, flat = integrals.shape
-    rows = coeff.shape[0] * coeff.shape[1] // LANES + kets // n_pair * SB + TAG
+    reach = kets // n_pair * SB + TAG
+    rows = coeff.shape[0] * coeff.shape[1] // LANES + reach
     hbm, smem = pl.BlockSpec(memory_space=pltpu.HBM), pl.BlockSpec(memory_space=pltpu.SMEM)
     return pl.pallas_call(
         functools.partial(pack_kernel, n_pair),
-        out_shape=[pltpu.VMEM((rows, LANES), jnp.bfloat16)] * n_pair,
+        out_shape=[pltpu.VMEM((size, LANES), jnp.bfloat16) for size in (rows, rows, rows + reach)],
         in_specs=[hbm, hbm, hbm, smem, hbm],
-        out_specs=[pl.BlockSpec(memory_space=pltpu.VMEM)] * n_pair,
+        out_specs=[pl.BlockSpec(memory_space=pltpu.VMEM)] * 3,
         scratch_shapes=[
             pltpu.VMEM(integrals.shape, jnp.bfloat16),
             pltpu.VMEM(coeff.shape, jnp.bfloat16),
@@ -93,21 +98,22 @@
     p, o = lax.axis_index("pair"), lax.axis_index("orb")
     devices = codes.shape[0]
     blocks = orbitals // LANES
-    tile_at = pieces[0].shape[-2] - TAG - 2 * SB
     if came:
+        rows = c_all.shape[0] // devices
+        tile_at = [0 if ahead else blocks * rows for _, _, ahead in came]
         for q, piece in enumerate(pieces):
-            codes[q : q + 1, :] = piece[tile_at + 2 * SB :][:1].astype(jnp.float32).astype(jnp.int32)
+            codes[q : q + 1, :] = piece[tile_at[q] + 2 * SB : tile_at[q] + 2 * SB + TAG][:1].astype(jnp.float32).astype(jnp.int32)
     else:
         codes[...] = pieces[0][:, 2 * SB :, :][:, 0, :].astype(jnp.float32).astype(jnp.int32)
     to_scalars = pltpu.make_async_copy(codes, index, sem)
     to_scalars.start()
     if came:
-        rows = c_all.shape[0] // devices
         for q, piece in enumerate(pieces):
+            begin = 2 * SB + TAG if came[q][2] else 0
             source = (p ^ came[q][0]) * n_orb + (o ^ came[q][1])
             place = pl.ds(pl.multiple_of(source * rows, rows), rows)
             for j in range(blocks):
-                c_all[place, j * LANES : (j + 1) * LANES] = piece[j * rows : (j + 1) * rows, :]
+                c_all[place, j * LANES : (j + 1) * LANES] = piece[begin + j * rows : begin + (j + 1) * rows, :]
     else:
         c_all = pieces[1]
     to_scalars.wait()
@@ -125,7 +131,7 @@
             stacked = []
             for k in range(2):
                 if came:
-                    tile = pieces[d][tile_at + k * SB : tile_at + (k + 1) * SB, :]
+                    tile = pieces[d][tile_at[d] + k * SB : tile_at[d] + (k + 1) * SB, :]
                 else:
                     tile = pieces[0][device, k * SB : (k + 1) * SB, :]
                 stacked += [jnp.where(low, tile, jnp.zeros_like(tile)), jnp.where(low, jnp.zeros_like(tile), tile)]
@@ -185,16 +191,19 @@
     columns = kets // n_pair
     orbitals = coeff.shape[1]
     if n_orb == 4 and n_pair == 4:
-        packed = list(pack(n_pair, integrals, mu_block, nu_block, counts, coeff))
-        lines = packed[:1] + [flip(packed[s], "pair", n_pair, s) for s in range(1, n_pair)]
-        across = [flip(line, "orb", n_orb, 2) for line in lines[:3]]
-        last, across[1] = lax.optimization_barrier((lines[3], across[1]))
+        own, one_off, two_off = pack(n_pair, integrals, mu_block, nu_block, counts, coeff)
+        two = flip(two_off, "pair", n_pair, 2)
+        one = flip(one_off, "pair", n_pair, 1)
+        last = flip(two[: own.shape[0]], "pair", n_pair, 1)
+        lines = [own, one, two[two.shape[0] - own.shape[0] :]]
+        across = [flip(line, "orb", n_orb, 2) for line in lines]
+        last, across[1] = lax.optimization_barrier((last, across[1]))
         across.append(flip(last, "orb", n_orb, 2))
-        early = lax.optimization_barrier(tuple(lines[:3] + across[:3] + [last]))
+        early = lax.optimization_barrier(tuple(lines + across[:3] + [last]))
         pieces = list(early) + across[3:]
         pieces += [flip(piece, "orb", n_orb, 1) for piece in pieces]
-        came = [(0, 0), (1, 0), (2, 0), (0, 2), (1, 2), (2, 2), (3, 0), (3, 2)]
-        came += [(s, side ^ 1) for s, side in came]
+        came = [(0, 0, 0), (1, 0, 0), (2, 0, 0), (0, 2, 0), (1, 2, 0), (2, 2, 0), (3, 0, 1), (3, 2, 1)]
+        came += [(s, side ^ 1, ahead) for s, side, ahead in came]
     else:
         kept = jnp.arange(slots, dtype=jnp.int32) < counts[0]
         tiles = jnp.where(kept[:, None, None], integrals, jnp.zeros_like(integrals))

time: 33.8 us -> 36.1 us (1.068)
  starting transfers between devices: 11.8 us -> 14.9 us
  waiting for transfers between devices: 16.3 us -> 15.5 us
    ppermute x15, starting transfers between devices: 11.8 us -> 14.9 us  [flip(): return lax.ppermute(array, axis, [(i, i ^ bit) for i in range(size)])]
    ppermute x15, waiting for transfers between devices: 16.3 us -> 15.5 us  [flip(): return lax.ppermute(array, axis, [(i, i ^ bit) for i in range(size)])]
where the time goes in v10:
time: 36.1 us; the launch traced here: 35.9 us
  waiting for transfers between devices  15.5 us (43%)
  starting transfers between devices  14.9 us (41%)
  Pallas kernels  4.88 us (14%)
  between operations  0.68 us (2%)
    ppermute x15, waiting for transfers between devices, flip(): return lax.ppermute(array, axis, [(i, i ^ bit) for i in range(size)])  15.5 us
    ppermute x15, starting transfers between devices, flip(): return lax.ppermute(array, axis, [(i, i ^ bit) for i in range(size)])  14.9 us
    pallas_call x1, Pallas kernels, transform(): pl.pallas_call(functools.partial(transform_kernel, came, n_orb, orbitals,...  3.7 us
    pallas_call x1, Pallas kernels, pack(): pl.pallas_call(functools.partial(pack_kernel, n_pair), out_shape=[pltpu.V...  1.17 us
  transfers between devices with their start and end apart: 15, of which 9 were waited for; matrix products, arithmetic and copies ran while one was open for 0% of the time, Pallas kernels for 0%

profile of v10, /device:TPU:0, one launch (start us, length us, event | category | flops | bytes accessed | tf_op | source)
XLA Modules:
  0.0 35.9 jit_solution(3700321869800560282)
XLA Ops:
  0.7 1.2 %pack.1 = (bf16[656,128]{1,0:T(8,128)(2,1)S(1)}, bf16[656,128]{1,0:T(8,128)(2,1)S(1)}, bf16[800,128]{1,0:T(8,128)(2,1)S(1)}) custom-call(bf16[2,8,4096]{2,1,0:T(8,128)(2,1)} %integrals.1, s32[2]{0:T(128)} %mu.1, s32[2]{0:T(128)} %nu.1, s32[1]{0:T(128)S(6)} %copy.7.counts, bf16[128,512]{1,0:T(8,128)(2,1)} %coeff.1), custom_call_target="tpu_custom_call" | custom-call | tf_op jit(solution)/shard_map/pack/pallas_call | solution.py:76
  1.8 4.1 %collective-permute-start.1 = (bf16[800,128]{1,0:T(8,128)(2,1)S(1)}, bf16[800,128]{1,0:T(8,128)(2,1)S(1)}, u32[]{:S(2)}, u32[]{:S(2)}) collective-permute-start(bf16[800,128]{1,0:T(8,128)(2,1)S(1)} %get-tuple-element.19), channel_id=1, source_target_pairs={{0,8},{4,12},{8,0},{12,4},{1,9},{5,13},{9,1},{13,5},{2,10},{6,14},... | collective-permute-start | bytes 614408 | tf_op jit(solution)/shard_map/ppermute | solution.py:186
  5.9 1.6 %collective-permute-start = (bf16[656,128]{1,0:T(8,128)(2,1)S(1)}, bf16[656,128]{1,0:T(8,128)(2,1)S(1)}, u32[]{:S(2)}, u32[]{:S(2)}) collective-permute-start(bf16[656,128]{1,0:T(8,128)(2,1)S(1)} %get-tuple-element.18), channel_id=1, source_target_pairs={{0,4},{4,0},{8,12},{12,8},{1,5},{5,1},{9,13},{13,9},{2,6},{6,2},{1... | collective-permute-start | bytes 503816 | tf_op jit(solution)/shard_map/ppermute | solution.py:186
  7.5 6.4 %collective-permute-done.refs_1_ = bf16[656,128]{1,0:T(8,128)(2,1)S(1)} collective-permute-done((bf16[656,128]{1,0:T(8,128)(2,1)S(1)}, bf16[656,128]{1,0:T(8,128)(2,1)S(1)}, u32[]{:S(2)}, u32[]{:S(2)}) %collective-permute-start) | collective-permute-done | bytes 167968 | tf_op jit(solution)/shard_map/ppermute | solution.py:186
  13.9 1.5 %collective-permute-start.4 = (bf16[656,128]{1,0:T(8,128)(2,1)S(1)}, bf16[656,128]{1,0:T(8,128)(2,1)S(1)}, u32[]{:S(2)}, u32[]{:S(2)}) collective-permute-start(bf16[656,128]{1,0:T(8,128)(2,1)S(1)} %collective-permute-done.refs_1_), channel_id=1, source_target_pairs={{0,2},{1,3},{2,0},{3,1},{4,6},{5,7},{6,4},{7,5},{8,10},{9,11},{10,... | collective-permute-start | bytes 503816 | tf_op jit(solution)/shard_map/ppermute | solution.py:186
  15.4 0.0 collective-permute-done.1
  15.4 2.5 %collective-permute-start.3 = (bf16[656,128]{1,0:T(8,128)(2,1)S(1)}, bf16[656,128]{1,0:T(8,128)(2,1)S(1)}, u32[]{:S(2)}, u32[]{:S(2)}) collective-permute-start(bf16[656,128]{1,0:T(8,128)(2,1)S(1)} %get-tuple-element.29), channel_id=1, source_target_pairs={{0,4},{4,0},{8,12},{12,8},{1,5},{5,1},{9,13},{13,9},{2,6},{6,2},{1... | collective-permute-start | bytes 503816 | tf_op jit(solution)/shard_map/ppermute | solution.py:186
  18.0 0.5 %collective-permute-start.2 = (bf16[656,128]{1,0:T(8,128)(2,1)S(1)}, bf16[656,128]{1,0:T(8,128)(2,1)S(1)}, u32[]{:S(2)}, u32[]{:S(2)}) collective-permute-start(bf16[656,128]{1,0:T(8,128)(2,1)S(1)} %get-tuple-element.22.refs_0_), channel_id=1, source_target_pairs={{0,2},{1,3},{2,0},{3,1},{4,6},{5,7},{6,4},{7,5},{8,10},{9,11},{10,... | collective-permute-start | bytes 503816 | tf_op jit(solution)/shard_map/ppermute | solution.py:186
  18.5 1.5 %collective-permute-start.5 = (bf16[656,128]{1,0:T(8,128)(2,1)S(1)}, bf16[656,128]{1,0:T(8,128)(2,1)S(1)}, u32[]{:S(2)}, u32[]{:S(2)}) collective-permute-start(bf16[656,128]{1,0:T(8,128)(2,1)S(1)} %get-tuple-element.24.refs_2_), channel_id=1, source_target_pairs={{0,2},{1,3},{2,0},{3,1},{4,6},{5,7},{6,4},{7,5},{8,10},{9,11},{10,... | collective-permute-start | bytes 503816 | tf_op jit(solution)/shard_map/ppermute | solution.py:186
  20.0 0.0 collective-permute-done.4.refs_4_
  20.0 1.3 %collective-permute-done.3.refs_6_ = bf16[656,128]{1,0:T(8,128)(2,1)S(1)} collective-permute-done((bf16[656,128]{1,0:T(8,128)(2,1)S(1)}, bf16[656,128]{1,0:T(8,128)(2,1)S(1)}, u32[]{:S(2)}, u32[]{:S(2)}) %collective-permute-start.3) | collective-permute-done | bytes 167968 | tf_op jit(solution)/shard_map/ppermute | solution.py:186
  21.3 1.1 %collective-permute-start.6 = (bf16[656,128]{1,0:T(8,128)(2,1)S(1)}, bf16[656,128]{1,0:T(8,128)(2,1)S(1)}, u32[]{:S(2)}, u32[]{:S(2)}) collective-permute-start(bf16[656,128]{1,0:T(8,128)(2,1)S(1)} %collective-permute-done.3.refs_6_), channel_id=1, source_target_pairs={{0,2},{1,3},{2,0},{3,1},{4,6},{5,7},{6,4},{7,5},{8,10},{9,11},{10,... | collective-permute-start | bytes 503816 | tf_op jit(solution)/shard_map/ppermute | solution.py:186
  22.4 2.8 %collective-permute-done.2.refs_3_ = bf16[656,128]{1,0:T(8,128)(2,1)S(1)} collective-permute-done((bf16[656,128]{1,0:T(8,128)(2,1)S(1)}, bf16[656,128]{1,0:T(8,128)(2,1)S(1)}, u32[]{:S(2)}, u32[]{:S(2)}) %collective-permute-start.2) | collective-permute-done | bytes 167968 | tf_op jit(solution)/shard_map/ppermute | solution.py:186
  25.2 3.1 %collective-permute-done.5.refs_5_ = bf16[656,128]{1,0:T(8,128)(2,1)S(1)} collective-permute-done((bf16[656,128]{1,0:T(8,128)(2,1)S(1)}, bf16[656,128]{1,0:T(8,128)(2,1)S(1)}, u32[]{:S(2)}, u32[]{:S(2)}) %collective-permute-start.5) | collective-permute-done | bytes 167968 | tf_op jit(solution)/shard_map/ppermute | solution.py:186
  28.3 0.0 collective-permute-start.7
  28.3 0.5 %collective-permute-start.8 = (bf16[656,128]{1,0:T(8,128)(2,1)S(1)}, bf16[656,128]{1,0:T(8,128)(2,1)S(1)}, u32[]{:S(2)}, u32[]{:S(2)}) collective-permute-start(bf16[656,128]{1,0:T(8,128)(2,1)S(1)} %collective-permute-done.refs_1_), channel_id=1, source_target_pairs={{0,1},{1,0},{2,3},{3,2},{4,5},{5,4},{6,7},{7,6},{8,9},{9,8},{10,11... | collective-permute-start | bytes 503816 | tf_op jit(solution)/shard_map/ppermute | solution.py:186
  28.8 0.0 collective-permute-start.9
  28.8 0.5 %collective-permute-start.10 = (bf16[656,128]{1,0:T(8,128)(2,1)S(1)}, bf16[656,128]{1,0:T(8,128)(2,1)S(1)}, u32[]{:S(2)}, u32[]{:S(2)}) collective-permute-start(bf16[656,128]{1,0:T(8,128)(2,1)S(1)} %collective-permute-done.2.refs_3_), channel_id=1, source_target_pairs={{0,1},{1,0},{2,3},{3,2},{4,5},{5,4},{6,7},{7,6},{8,9},{9,8},{10,11... | collective-permute-start | bytes 503816 | tf_op jit(solution)/shard_map/ppermute | solution.py:186
  29.3 0.8 %collective-permute-done.6.refs_7_ = bf16[656,128]{1,0:T(8,128)(2,1)S(1)} collective-permute-done((bf16[656,128]{1,0:T(8,128)(2,1)S(1)}, bf16[656,128]{1,0:T(8,128)(2,1)S(1)}, u32[]{:S(2)}, u32[]{:S(2)}) %collective-permute-start.6) | collective-permute-done | bytes 167968 | tf_op jit(solution)/shard_map/ppermute | solution.py:186
  30.1 0.0 collective-permute-start.11
  30.1 0.0 collective-permute-done.7.refs_8_
  30.1 0.5 %collective-permute-start.12 = (bf16[656,128]{1,0:T(8,128)(2,1)S(1)}, bf16[656,128]{1,0:T(8,128)(2,1)S(1)}, u32[]{:S(2)}, u32[]{:S(2)}) collective-permute-start(bf16[656,128]{1,0:T(8,128)(2,1)S(1)} %collective-permute-done.5.refs_5_), channel_id=1, source_target_pairs={{0,1},{1,0},{2,3},{3,2},{4,5},{5,4},{6,7},{7,6},{8,9},{9,8},{10,11... | collective-permute-start | bytes 503816 | tf_op jit(solution)/shard_map/ppermute | solution.py:186
  30.6 0.0 collective-permute-done.8.refs_9_
  30.6 0.1 collective-permute-start.13
  30.7 0.0 collective-permute-done.9.refs_10_
  30.7 0.4 %collective-permute-start.14 = (bf16[656,128]{1,0:T(8,128)(2,1)S(1)}, bf16[656,128]{1,0:T(8,128)(2,1)S(1)}, u32[]{:S(2)}, u32[]{:S(2)}) collective-permute-start(bf16[656,128]{1,0:T(8,128)(2,1)S(1)} %collective-permute-done.6.refs_7_), channel_id=1, source_target_pairs={{0,1},{1,0},{2,3},{3,2},{4,5},{5,4},{6,7},{7,6},{8,9},{9,8},{10,11... | collective-permute-start | bytes 503816 | tf_op jit(solution)/shard_map/ppermute | solution.py:186
  31.1 0.0 collective-permute-done.10.refs_11_
  31.1 0.4 %collective-permute-done.11.refs_12_ = bf16[656,128]{1,0:T(8,128)(2,1)S(1)} collective-permute-done((bf16[656,128]{1,0:T(8,128)(2,1)S(1)}, bf16[656,128]{1,0:T(8,128)(2,1)S(1)}, u32[]{:S(2)}, u32[]{:S(2)}) %collective-permute-start.11) | collective-permute-done | bytes 167968 | tf_op jit(solution)/shard_map/ppermute | solution.py:186
  31.5 0.2 collective-permute-done.12.refs_13_
  31.7 0.3 collective-permute-done.13.refs_14_
  32.0 0.2 collective-permute-done.14.refs_15_
  32.2 3.7 %transform.1 = f32[1024,128]{1,0:T(8,128)} custom-call(bf16[656,128]{1,0:T(8,128)(2,1)S(1)} %get-tuple-element.22.refs_0_, bf16[656,128]{1,0:T(8,128)(2,1)S(1)} %collective-permute-done.refs_1_, bf16[656,128]{1,0:T(8,128)(2,1)S(1)} %get-tuple-element.24.refs_2_, bf16[656,128]{1,0:T(8,128)(2,1)S(1)} %collective-permute-done.2.refs_3_, ...), custom_call_target="tpu_custom_call" | custom-call | tf_op jit(solution)/shard_map/transform/pallas_call | solution.py:167
  (1 shorter events, 0.0 us)
Async XLA Ops:
  1.8 13.6 %collective-permute-start.1 = (bf16[800,128]{1,0:T(8,128)(2,1)S(1)}, bf16[800,128]{1,0:T(8,128)(2,1)S(1)}, u32[]{:S(2)}, u32[]{:S(2)}) collective-permute-start(bf16[800,128]{1,0:T(8,128)(2,1)S(1)} %get-tuple-element.19), channel_id=1, source_target_pairs={{0,8},{4,12},{8,0},{12,4},{1,9},{5,13},{9,1},{13,5},{2,10},{6,14},... | collective-permute-start | bytes 614408 | tf_op jit(solution)/shard_map/ppermute | solution.py:186
  5.9 8.0 %collective-permute-start = (bf16[656,128]{1,0:T(8,128)(2,1)S(1)}, bf16[656,128]{1,0:T(8,128)(2,1)S(1)}, u32[]{:S(2)}, u32[]{:S(2)}) collective-permute-start(bf16[656,128]{1,0:T(8,128)(2,1)S(1)} %get-tuple-element.18), channel_id=1, source_target_pairs={{0,4},{4,0},{8,12},{12,8},{1,5},{5,1},{9,13},{13,9},{2,6},{6,2},{1... | collective-permute-start | bytes 503816 | tf_op jit(solution)/shard_map/ppermute | solution.py:186
  13.9 6.1 %collective-permute-start.4 = (bf16[656,128]{1,0:T(8,128)(2,1)S(1)}, bf16[656,128]{1,0:T(8,128)(2,1)S(1)}, u32[]{:S(2)}, u32[]{:S(2)}) collective-permute-start(bf16[656,128]{1,0:T(8,128)(2,1)S(1)} %collective-permute-done.refs_1_), channel_id=1, source_target_pairs={{0,2},{1,3},{2,0},{3,1},{4,6},{5,7},{6,4},{7,5},{8,10},{9,11},{10,... | collective-permute-start | bytes 503816 | tf_op jit(solution)/shard_map/ppermute | solution.py:186
  15.4 5.9 %collective-permute-start.3 = (bf16[656,128]{1,0:T(8,128)(2,1)S(1)}, bf16[656,128]{1,0:T(8,128)(2,1)S(1)}, u32[]{:S(2)}, u32[]{:S(2)}) collective-permute-start(bf16[656,128]{1,0:T(8,128)(2,1)S(1)} %get-tuple-element.29), channel_id=1, source_target_pairs={{0,4},{4,0},{8,12},{12,8},{1,5},{5,1},{9,13},{13,9},{2,6},{6,2},{1... | collective-permute-start | bytes 503816 | tf_op jit(solution)/shard_map/ppermute | solution.py:186
  18.0 7.2 %collective-permute-start.2 = (bf16[656,128]{1,0:T(8,128)(2,1)S(1)}, bf16[656,128]{1,0:T(8,128)(2,1)S(1)}, u32[]{:S(2)}, u32[]{:S(2)}) collective-permute-start(bf16[656,128]{1,0:T(8,128)(2,1)S(1)} %get-tuple-element.22.refs_0_), channel_id=1, source_target_pairs={{0,2},{1,3},{2,0},{3,1},{4,6},{5,7},{6,4},{7,5},{8,10},{9,11},{10,... | collective-permute-start | bytes 503816 | tf_op jit(solution)/shard_map/ppermute | solution.py:186
  18.5 9.8 %collective-permute-start.5 = (bf16[656,128]{1,0:T(8,128)(2,1)S(1)}, bf16[656,128]{1,0:T(8,128)(2,1)S(1)}, u32[]{:S(2)}, u32[]{:S(2)}) collective-permute-start(bf16[656,128]{1,0:T(8,128)(2,1)S(1)} %get-tuple-element.24.refs_2_), channel_id=1, source_target_pairs={{0,2},{1,3},{2,0},{3,1},{4,6},{5,7},{6,4},{7,5},{8,10},{9,11},{10,... | collective-permute-start | bytes 503816 | tf_op jit(solution)/shard_map/ppermute | solution.py:186
  21.3 8.7 %collective-permute-start.6 = (bf16[656,128]{1,0:T(8,128)(2,1)S(1)}, bf16[656,128]{1,0:T(8,128)(2,1)S(1)}, u32[]{:S(2)}, u32[]{:S(2)}) collective-permute-start(bf16[656,128]{1,0:T(8,128)(2,1)S(1)} %collective-permute-done.3.refs_6_), channel_id=1, source_target_pairs={{0,2},{1,3},{2,0},{3,1},{4,6},{5,7},{6,4},{7,5},{8,10},{9,11},{10,... | collective-permute-start | bytes 503816 | tf_op jit(solution)/shard_map/ppermute | solution.py:186
  28.3 1.8 %collective-permute-start.7 = (bf16[656,128]{1,0:T(8,128)(2,1)S(1)}, bf16[656,128]{1,0:T(8,128)(2,1)S(1)}, u32[]{:S(2)}, u32[]{:S(2)}) collective-permute-start(bf16[656,128]{1,0:T(8,128)(2,1)S(1)} %get-tuple-element.22.refs_0_), channel_id=1, source_target_pairs={{0,1},{1,0},{2,3},{3,2},{4,5},{5,4},{6,7},{7,6},{8,9},{9,8},{10,11... | collective-permute-start | bytes 503816 | tf_op jit(solution)/shard_map/ppermute | solution.py:186
  28.3 2.3 %collective-permute-start.8 = (bf16[656,128]{1,0:T(8,128)(2,1)S(1)}, bf16[656,128]{1,0:T(8,128)(2,1)S(1)}, u32[]{:S(2)}, u32[]{:S(2)}) collective-permute-start(bf16[656,128]{1,0:T(8,128)(2,1)S(1)} %collective-permute-done.refs_1_), channel_id=1, source_target_pairs={{0,1},{1,0},{2,3},{3,2},{4,5},{5,4},{6,7},{7,6},{8,9},{9,8},{10,11... | collective-permute-start | bytes 503816 | tf_op jit(solution)/shard_map/ppermute | solution.py:186
  28.8 1.9 %collective-permute-start.9 = (bf16[656,128]{1,0:T(8,128)(2,1)S(1)}, bf16[656,128]{1,0:T(8,128)(2,1)S(1)}, u32[]{:S(2)}, u32[]{:S(2)}) collective-permute-start(bf16[656,128]{1,0:T(8,128)(2,1)S(1)} %get-tuple-element.24.refs_2_), channel_id=1, source_target_pairs={{0,1},{1,0},{2,3},{3,2},{4,5},{5,4},{6,7},{7,6},{8,9},{9,8},{10,11... | collective-permute-start | bytes 503816 | tf_op jit(solution)/shard_map/ppermute | solution.py:186
  28.8 2.3 %collective-permute-start.10 = (bf16[656,128]{1,0:T(8,128)(2,1)S(1)}, bf16[656,128]{1,0:T(8,128)(2,1)S(1)}, u32[]{:S(2)}, u32[]{:S(2)}) collective-permute-start(bf16[656,128]{1,0:T(8,128)(2,1)S(1)} %collective-permute-done.2.refs_3_), channel_id=1, source_target_pairs={{0,1},{1,0},{2,3},{3,2},{4,5},{5,4},{6,7},{7,6},{8,9},{9,8},{10,11... | collective-permute-start | bytes 503816 | tf_op jit(solution)/shard_map/ppermute | solution.py:186
  30.1 1.4 %collective-permute-start.11 = (bf16[656,128]{1,0:T(8,128)(2,1)S(1)}, bf16[656,128]{1,0:T(8,128)(2,1)S(1)}, u32[]{:S(2)}, u32[]{:S(2)}) collective-permute-start(bf16[656,128]{1,0:T(8,128)(2,1)S(1)} %collective-permute-done.4.refs_4_), channel_id=1, source_target_pairs={{0,1},{1,0},{2,3},{3,2},{4,5},{5,4},{6,7},{7,6},{8,9},{9,8},{10,11... | collective-permute-start | bytes 503816 | tf_op jit(solution)/shard_map/ppermute | solution.py:186
  30.1 1.6 %collective-permute-start.12 = (bf16[656,128]{1,0:T(8,128)(2,1)S(1)}, bf16[656,128]{1,0:T(8,128)(2,1)S(1)}, u32[]{:S(2)}, u32[]{:S(2)}) collective-permute-start(bf16[656,128]{1,0:T(8,128)(2,1)S(1)} %collective-permute-done.5.refs_5_), channel_id=1, source_target_pairs={{0,1},{1,0},{2,3},{3,2},{4,5},{5,4},{6,7},{7,6},{8,9},{9,8},{10,11... | collective-permute-start | bytes 503816 | tf_op jit(solution)/shard_map/ppermute | solution.py:186
  30.6 1.4 %collective-permute-start.13 = (bf16[656,128]{1,0:T(8,128)(2,1)S(1)}, bf16[656,128]{1,0:T(8,128)(2,1)S(1)}, u32[]{:S(2)}, u32[]{:S(2)}) collective-permute-start(bf16[656,128]{1,0:T(8,128)(2,1)S(1)} %collective-permute-done.3.refs_6_), channel_id=1, source_target_pairs={{0,1},{1,0},{2,3},{3,2},{4,5},{5,4},{6,7},{7,6},{8,9},{9,8},{10,11... | collective-permute-start | bytes 503816 | tf_op jit(solution)/shard_map/ppermute | solution.py:186
  30.7 1.6 %collective-permute-start.14 = (bf16[656,128]{1,0:T(8,128)(2,1)S(1)}, bf16[656,128]{1,0:T(8,128)(2,1)S(1)}, u32[]{:S(2)}, u32[]{:S(2)}) collective-permute-start(bf16[656,128]{1,0:T(8,128)(2,1)S(1)} %collective-permute-done.6.refs_7_), channel_id=1, source_target_pairs={{0,1},{1,0},{2,3},{3,2},{4,5},{5,4},{6,7},{7,6},{8,9},{9,8},{10,11... | collective-permute-start | bytes 503816 | tf_op jit(solution)/shard_map/ppermute | solution.py:186

commit v11 on v10

--- a/solution.py
+++ b/solution.py
@@ -192,16 +192,21 @@
     orbitals = coeff.shape[1]
     if n_orb == 4 and n_pair == 4:
         own, one_off, two_off = pack(n_pair, integrals, mu_block, nu_block, counts, coeff)
+        size = own.shape[0]
         two = flip(two_off, "pair", n_pair, 2)
         one = flip(one_off, "pair", n_pair, 1)
-        last = flip(two[: own.shape[0]], "pair", n_pair, 1)
-        lines = [own, one, two[two.shape[0] - own.shape[0] :]]
-        across = [flip(line, "orb", n_orb, 2) for line in lines]
-        last, across[1] = lax.optimization_barrier((last, across[1]))
-        across.append(flip(last, "orb", n_orb, 2))
-        early = lax.optimization_barrier(tuple(lines + across[:3] + [last]))
-        pieces = list(early) + across[3:]
-        pieces += [flip(piece, "orb", n_orb, 1) for piece in pieces]
+        own_across = flip(own, "orb", n_orb, 2)
+        one, own_across = lax.optimization_barrier((one, own_across))
+        one_across = flip(one, "orb", n_orb, 2)
+        three = flip(two[:size], "pair", n_pair, 1)
+        two = two[two.shape[0] - size :]
+        two_across = flip(two, "orb", n_orb, 2)
+        pieces = [own, one, two, own_across, one_across]
+        swapped = [flip(piece, "orb", n_orb, 1) for piece in pieces]
+        three, *swapped = lax.optimization_barrier((three, *swapped))
+        pieces += [two_across, three, flip(three, "orb", n_orb, 2)]
+        swapped += [flip(piece, "orb", n_orb, 1) for piece in pieces[5:]]
+        pieces += swapped
         came = [(0, 0, 0), (1, 0, 0), (2, 0, 0), (0, 2, 0), (1, 2, 0), (2, 2, 0), (3, 0, 1), (3, 2, 1)]
         came += [(s, side ^ 1, ahead) for s, side, ahead in came]
     else:

time: 36.1 us -> 36.2 us (level)
  starting transfers between devices: 14.9 us -> 14 us
  waiting for transfers between devices: 15.5 us -> 16.4 us
    ppermute x15, waiting for transfers between devices: 15.5 us -> 16.4 us  [flip(): return lax.ppermute(array, axis, [(i, i ^ bit) for i in range(size)])]
    ppermute x15, starting transfers between devices: 14.9 us -> 14 us  [flip(): return lax.ppermute(array, axis, [(i, i ^ bit) for i in range(size)])]
  transfers between devices with their start and end apart: 15 -> 15, of which waited for: 9 -> 6; matrix products, arithmetic and copies ran while one was open for 0% -> 0% of each run, Pallas kernels for 0% -> 0%
where the time goes in v11:
time: 36.2 us; the launch traced here: 36 us
  waiting for transfers between devices  16.4 us (45%)
  starting transfers between devices  14 us (39%)
  Pallas kernels  4.88 us (13%)
  between operations  0.68 us (2%)
    ppermute x15, waiting for transfers between devices, flip(): return lax.ppermute(array, axis, [(i, i ^ bit) for i in range(size)])  16.4 us
    ppermute x15, starting transfers between devices, flip(): return lax.ppermute(array, axis, [(i, i ^ bit) for i in range(size)])  14 us
    pallas_call x1, Pallas kernels, transform(): pl.pallas_call(functools.partial(transform_kernel, came, n_orb, orbitals,...  3.7 us
    pallas_call x1, Pallas kernels, pack(): pl.pallas_call(functools.partial(pack_kernel, n_pair), out_shape=[pltpu.V...  1.17 us
  transfers between devices with their start and end apart: 15, of which 6 were waited for; matrix products, arithmetic and copies ran while one was open for 0% of the time, Pallas kernels for 0%

profile of v11, /device:TPU:0, one launch (start us, length us, event | category | flops | bytes accessed | tf_op | source)
XLA Modules:
  0.0 36.0 jit_solution(1243918318834370910)
XLA Ops:
  0.7 1.2 %pack.1 = (bf16[656,128]{1,0:T(8,128)(2,1)S(1)}, bf16[656,128]{1,0:T(8,128)(2,1)S(1)}, bf16[800,128]{1,0:T(8,128)(2,1)S(1)}) custom-call(bf16[2,8,4096]{2,1,0:T(8,128)(2,1)} %integrals.1, s32[2]{0:T(128)} %mu.1, s32[2]{0:T(128)} %nu.1, s32[1]{0:T(128)S(6)} %copy.7.counts, bf16[128,512]{1,0:T(8,128)(2,1)} %coeff.1), custom_call_target="tpu_custom_call" | custom-call | tf_op jit(solution)/shard_map/pack/pallas_call | solution.py:76
  1.8 4.1 %collective-permute-start.2 = (bf16[800,128]{1,0:T(8,128)(2,1)S(1)}, bf16[800,128]{1,0:T(8,128)(2,1)S(1)}, u32[]{:S(2)}, u32[]{:S(2)}) collective-permute-start(bf16[800,128]{1,0:T(8,128)(2,1)S(1)} %get-tuple-element.19), channel_id=1, source_target_pairs={{0,8},{4,12},{8,0},{12,4},{1,9},{5,13},{9,1},{13,5},{2,10},{6,14},... | collective-permute-start | bytes 614408 | tf_op jit(solution)/shard_map/ppermute | solution.py:186
  5.9 1.6 %collective-permute-start = (bf16[656,128]{1,0:T(8,128)(2,1)S(1)}, bf16[656,128]{1,0:T(8,128)(2,1)S(1)}, u32[]{:S(2)}, u32[]{:S(2)}) collective-permute-start(bf16[656,128]{1,0:T(8,128)(2,1)S(1)} %get-tuple-element.17), channel_id=1, source_target_pairs={{0,4},{4,0},{8,12},{12,8},{1,5},{5,1},{9,13},{13,9},{2,6},{6,2},{1... | collective-permute-start | bytes 503816 | tf_op jit(solution)/shard_map/ppermute | solution.py:186
  7.5 1.5 %collective-permute-start.1 = (bf16[656,128]{1,0:T(8,128)(2,1)S(1)}, bf16[656,128]{1,0:T(8,128)(2,1)S(1)}, u32[]{:S(2)}, u32[]{:S(2)}) collective-permute-start(bf16[656,128]{1,0:T(8,128)(2,1)S(1)} %get-tuple-element.16.refs_0_), channel_id=1, source_target_pairs={{0,2},{1,3},{2,0},{3,1},{4,6},{5,7},{6,4},{7,5},{8,10},{9,11},{10,... | collective-permute-start | bytes 503816 | tf_op jit(solution)/shard_map/ppermute | solution.py:186
  9.0 0.0 collective-permute-start.6
  9.0 4.9 %collective-permute-done.refs_1_ = bf16[656,128]{1,0:T(8,128)(2,1)S(1)} collective-permute-done((bf16[656,128]{1,0:T(8,128)(2,1)S(1)}, bf16[656,128]{1,0:T(8,128)(2,1)S(1)}, u32[]{:S(2)}, u32[]{:S(2)}) %collective-permute-start) | collective-permute-done | bytes 167968 | tf_op jit(solution)/shard_map/ppermute | solution.py:186
  13.9 0.0 collective-permute-done.1.refs_3_
  13.9 0.0 collective-permute-start.7
  13.9 1.5 %collective-permute-start.3 = (bf16[656,128]{1,0:T(8,128)(2,1)S(1)}, bf16[656,128]{1,0:T(8,128)(2,1)S(1)}, u32[]{:S(2)}, u32[]{:S(2)}) collective-permute-start(bf16[656,128]{1,0:T(8,128)(2,1)S(1)} %collective-permute-done.refs_1_), channel_id=1, source_target_pairs={{0,2},{1,3},{2,0},{3,1},{4,6},{5,7},{6,4},{7,5},{8,10},{9,11},{10,... | collective-permute-start | bytes 503816 | tf_op jit(solution)/shard_map/ppermute | solution.py:186
  15.4 0.2 collective-permute-start.9
  15.6 0.0 collective-permute-done.2
  15.7 2.5 %collective-permute-start.5 = (bf16[656,128]{1,0:T(8,128)(2,1)S(1)}, bf16[656,128]{1,0:T(8,128)(2,1)S(1)}, u32[]{:S(2)}, u32[]{:S(2)}) collective-permute-start(bf16[656,128]{1,0:T(8,128)(2,1)S(1)} %get-tuple-element.27), channel_id=1, source_target_pairs={{0,4},{4,0},{8,12},{12,8},{1,5},{5,1},{9,13},{13,9},{2,6},{6,2},{1... | collective-permute-start | bytes 503816 | tf_op jit(solution)/shard_map/ppermute | solution.py:186
  18.2 0.0 collective-permute-done.6.refs_8_
  18.2 0.0 collective-permute-start.8
  18.2 2.4 %collective-permute-done.3.refs_4_ = bf16[656,128]{1,0:T(8,128)(2,1)S(1)} collective-permute-done((bf16[656,128]{1,0:T(8,128)(2,1)S(1)}, bf16[656,128]{1,0:T(8,128)(2,1)S(1)}, u32[]{:S(2)}, u32[]{:S(2)}) %collective-permute-start.3) | collective-permute-done | bytes 167968 | tf_op jit(solution)/shard_map/ppermute | solution.py:186
  20.6 0.0 collective-permute-start.10
  20.6 0.0 collective-permute-done.9.refs_11_
  20.6 1.5 %collective-permute-start.4 = (bf16[656,128]{1,0:T(8,128)(2,1)S(1)}, bf16[656,128]{1,0:T(8,128)(2,1)S(1)}, u32[]{:S(2)}, u32[]{:S(2)}) collective-permute-start(bf16[656,128]{1,0:T(8,128)(2,1)S(1)} %get-tuple-element.28.refs_2_), channel_id=1, source_target_pairs={{0,2},{1,3},{2,0},{3,1},{4,6},{5,7},{6,4},{7,5},{8,10},{9,11},{10,... | collective-permute-start | bytes 503816 | tf_op jit(solution)/shard_map/ppermute | solution.py:186
  22.1 0.0 collective-permute-done.7.refs_9_
  22.1 0.8 %collective-permute-done.5.refs_6_ = bf16[656,128]{1,0:T(8,128)(2,1)S(1)} collective-permute-done((bf16[656,128]{1,0:T(8,128)(2,1)S(1)}, bf16[656,128]{1,0:T(8,128)(2,1)S(1)}, u32[]{:S(2)}, u32[]{:S(2)}) %collective-permute-start.5) | collective-permute-done | bytes 167968 | tf_op jit(solution)/shard_map/ppermute | solution.py:186
  23.0 0.0 collective-permute-done.8.refs_10_
  23.0 0.0 collective-permute-done.10.refs_12_
  23.0 0.6 %collective-permute-start.11 = (bf16[656,128]{1,0:T(8,128)(2,1)S(1)}, bf16[656,128]{1,0:T(8,128)(2,1)S(1)}, u32[]{:S(2)}, u32[]{:S(2)}) collective-permute-start(bf16[656,128]{1,0:T(8,128)(2,1)S(1)} %collective-permute-done.5.refs_6_), channel_id=1, source_target_pairs={{0,2},{1,3},{2,0},{3,1},{4,6},{5,7},{6,4},{7,5},{8,10},{9,11},{10,... | collective-permute-start | bytes 503816 | tf_op jit(solution)/shard_map/ppermute | solution.py:186
  23.5 4.2 %collective-permute-done.4.refs_5_ = bf16[656,128]{1,0:T(8,128)(2,1)S(1)} collective-permute-done((bf16[656,128]{1,0:T(8,128)(2,1)S(1)}, bf16[656,128]{1,0:T(8,128)(2,1)S(1)}, u32[]{:S(2)}, u32[]{:S(2)}) %collective-permute-start.4) | collective-permute-done | bytes 167968 | tf_op jit(solution)/shard_map/ppermute | solution.py:186
  27.7 0.0 collective-permute-start.12
  27.7 0.5 %collective-permute-start.13 = (bf16[656,128]{1,0:T(8,128)(2,1)S(1)}, bf16[656,128]{1,0:T(8,128)(2,1)S(1)}, u32[]{:S(2)}, u32[]{:S(2)}) collective-permute-start(bf16[656,128]{1,0:T(8,128)(2,1)S(1)} %collective-permute-done.5.refs_6_), channel_id=1, source_target_pairs={{0,1},{1,0},{2,3},{3,2},{4,5},{5,4},{6,7},{7,6},{8,9},{9,8},{10,11... | collective-permute-start | bytes 503816 | tf_op jit(solution)/shard_map/ppermute | solution.py:186
  28.2 2.7 %collective-permute-done.11.refs_7_ = bf16[656,128]{1,0:T(8,128)(2,1)S(1)} collective-permute-done((bf16[656,128]{1,0:T(8,128)(2,1)S(1)}, bf16[656,128]{1,0:T(8,128)(2,1)S(1)}, u32[]{:S(2)}, u32[]{:S(2)}) %collective-permute-start.11) | collective-permute-done | bytes 167968 | tf_op jit(solution)/shard_map/ppermute | solution.py:186
  30.9 0.0 collective-permute-start.14
  30.9 0.0 collective-permute-done.12.refs_13_
  30.9 0.0 collective-permute-done.13.refs_14_
  30.9 1.4 %collective-permute-done.14.refs_15_ = bf16[656,128]{1,0:T(8,128)(2,1)S(1)} collective-permute-done((bf16[656,128]{1,0:T(8,128)(2,1)S(1)}, bf16[656,128]{1,0:T(8,128)(2,1)S(1)}, u32[]{:S(2)}, u32[]{:S(2)}) %collective-permute-start.14) | collective-permute-done | bytes 167968 | tf_op jit(solution)/shard_map/ppermute | solution.py:186
  32.3 3.7 %transform.1 = f32[1024,128]{1,0:T(8,128)} custom-call(bf16[656,128]{1,0:T(8,128)(2,1)S(1)} %get-tuple-element.16.refs_0_, bf16[656,128]{1,0:T(8,128)(2,1)S(1)} %collective-permute-done.refs_1_, bf16[656,128]{1,0:T(8,128)(2,1)S(1)} %get-tuple-element.28.refs_2_, bf16[656,128]{1,0:T(8,128)(2,1)S(1)} %collective-permute-done.1.refs_3_, ...), custom_call_target="tpu_custom_call" | custom-call | tf_op jit(solution)/shard_map/transform/pallas_call | solution.py:167
  (1 shorter events, 0.0 us)
Async XLA Ops:
  1.8 13.8 %collective-permute-start.2 = (bf16[800,128]{1,0:T(8,128)(2,1)S(1)}, bf16[800,128]{1,0:T(8,128)(2,1)S(1)}, u32[]{:S(2)}, u32[]{:S(2)}) collective-permute-start(bf16[800,128]{1,0:T(8,128)(2,1)S(1)} %get-tuple-element.19), channel_id=1, source_target_pairs={{0,8},{4,12},{8,0},{12,4},{1,9},{5,13},{9,1},{13,5},{2,10},{6,14},... | collective-permute-start | bytes 614408 | tf_op jit(solution)/shard_map/ppermute | solution.py:186
  5.9 8.0 %collective-permute-start = (bf16[656,128]{1,0:T(8,128)(2,1)S(1)}, bf16[656,128]{1,0:T(8,128)(2,1)S(1)}, u32[]{:S(2)}, u32[]{:S(2)}) collective-permute-start(bf16[656,128]{1,0:T(8,128)(2,1)S(1)} %get-tuple-element.17), channel_id=1, source_target_pairs={{0,4},{4,0},{8,12},{12,8},{1,5},{5,1},{9,13},{13,9},{2,6},{6,2},{1... | collective-permute-start | bytes 503816 | tf_op jit(solution)/shard_map/ppermute | solution.py:186
  7.5 6.4 %collective-permute-start.1 = (bf16[656,128]{1,0:T(8,128)(2,1)S(1)}, bf16[656,128]{1,0:T(8,128)(2,1)S(1)}, u32[]{:S(2)}, u32[]{:S(2)}) collective-permute-start(bf16[656,128]{1,0:T(8,128)(2,1)S(1)} %get-tuple-element.16.refs_0_), channel_id=1, source_target_pairs={{0,2},{1,3},{2,0},{3,1},{4,6},{5,7},{6,4},{7,5},{8,10},{9,11},{10,... | collective-permute-start | bytes 503816 | tf_op jit(solution)/shard_map/ppermute | solution.py:186
  9.0 9.2 %collective-permute-start.6 = (bf16[656,128]{1,0:T(8,128)(2,1)S(1)}, bf16[656,128]{1,0:T(8,128)(2,1)S(1)}, u32[]{:S(2)}, u32[]{:S(2)}) collective-permute-start(bf16[656,128]{1,0:T(8,128)(2,1)S(1)} %get-tuple-element.16.refs_0_), channel_id=1, source_target_pairs={{0,1},{1,0},{2,3},{3,2},{4,5},{5,4},{6,7},{7,6},{8,9},{9,8},{10,11... | collective-permute-start | bytes 503816 | tf_op jit(solution)/shard_map/ppermute | solution.py:186
  13.9 8.2 %collective-permute-start.7 = (bf16[656,128]{1,0:T(8,128)(2,1)S(1)}, bf16[656,128]{1,0:T(8,128)(2,1)S(1)}, u32[]{:S(2)}, u32[]{:S(2)}) collective-permute-start(bf16[656,128]{1,0:T(8,128)(2,1)S(1)} %collective-permute-done.refs_1_), channel_id=1, source_target_pairs={{0,1},{1,0},{2,3},{3,2},{4,5},{5,4},{6,7},{7,6},{8,9},{9,8},{10,11... | collective-permute-start | bytes 503816 | tf_op jit(solution)/shard_map/ppermute | solution.py:186
  13.9 6.7 %collective-permute-start.3 = (bf16[656,128]{1,0:T(8,128)(2,1)S(1)}, bf16[656,128]{1,0:T(8,128)(2,1)S(1)}, u32[]{:S(2)}, u32[]{:S(2)}) collective-permute-start(bf16[656,128]{1,0:T(8,128)(2,1)S(1)} %collective-permute-done.refs_1_), channel_id=1, source_target_pairs={{0,2},{1,3},{2,0},{3,1},{4,6},{5,7},{6,4},{7,5},{8,10},{9,11},{10,... | collective-permute-start | bytes 503816 | tf_op jit(solution)/shard_map/ppermute | solution.py:186
  15.4 5.2 %collective-permute-start.9 = (bf16[656,128]{1,0:T(8,128)(2,1)S(1)}, bf16[656,128]{1,0:T(8,128)(2,1)S(1)}, u32[]{:S(2)}, u32[]{:S(2)}) collective-permute-start(bf16[656,128]{1,0:T(8,128)(2,1)S(1)} %collective-permute-done.1.refs_3_), channel_id=1, source_target_pairs={{0,1},{1,0},{2,3},{3,2},{4,5},{5,4},{6,7},{7,6},{8,9},{9,8},{10,11... | collective-permute-start | bytes 503816 | tf_op jit(solution)/shard_map/ppermute | solution.py:186
  15.7 7.3 %collective-permute-start.5 = (bf16[656,128]{1,0:T(8,128)(2,1)S(1)}, bf16[656,128]{1,0:T(8,128)(2,1)S(1)}, u32[]{:S(2)}, u32[]{:S(2)}) collective-permute-start(bf16[656,128]{1,0:T(8,128)(2,1)S(1)} %get-tuple-element.27), channel_id=1, source_target_pairs={{0,4},{4,0},{8,12},{12,8},{1,5},{5,1},{9,13},{13,9},{2,6},{6,2},{1... | collective-permute-start | bytes 503816 | tf_op jit(solution)/shard_map/ppermute | solution.py:186
  18.2 4.7 %collective-permute-start.8 = (bf16[656,128]{1,0:T(8,128)(2,1)S(1)}, bf16[656,128]{1,0:T(8,128)(2,1)S(1)}, u32[]{:S(2)}, u32[]{:S(2)}) collective-permute-start(bf16[656,128]{1,0:T(8,128)(2,1)S(1)} %get-tuple-element.28.refs_2_), channel_id=1, source_target_pairs={{0,1},{1,0},{2,3},{3,2},{4,5},{5,4},{6,7},{7,6},{8,9},{9,8},{10,11... | collective-permute-start | bytes 503816 | tf_op jit(solution)/shard_map/ppermute | solution.py:186
  20.6 2.3 %collective-permute-start.10 = (bf16[656,128]{1,0:T(8,128)(2,1)S(1)}, bf16[656,128]{1,0:T(8,128)(2,1)S(1)}, u32[]{:S(2)}, u32[]{:S(2)}) collective-permute-start(bf16[656,128]{1,0:T(8,128)(2,1)S(1)} %collective-permute-done.3.refs_4_), channel_id=1, source_target_pairs={{0,1},{1,0},{2,3},{3,2},{4,5},{5,4},{6,7},{7,6},{8,9},{9,8},{10,11... | collective-permute-start | bytes 503816 | tf_op jit(solution)/shard_map/ppermute | solution.py:186
  20.6 7.1 %collective-permute-start.4 = (bf16[656,128]{1,0:T(8,128)(2,1)S(1)}, bf16[656,128]{1,0:T(8,128)(2,1)S(1)}, u32[]{:S(2)}, u32[]{:S(2)}) collective-permute-start(bf16[656,128]{1,0:T(8,128)(2,1)S(1)} %get-tuple-element.28.refs_2_), channel_id=1, source_target_pairs={{0,2},{1,3},{2,0},{3,1},{4,6},{5,7},{6,4},{7,5},{8,10},{9,11},{10,... | collective-permute-start | bytes 503816 | tf_op jit(solution)/shard_map/ppermute | solution.py:186
  23.0 8.0 %collective-permute-start.11 = (bf16[656,128]{1,0:T(8,128)(2,1)S(1)}, bf16[656,128]{1,0:T(8,128)(2,1)S(1)}, u32[]{:S(2)}, u32[]{:S(2)}) collective-permute-start(bf16[656,128]{1,0:T(8,128)(2,1)S(1)} %collective-permute-done.5.refs_6_), channel_id=1, source_target_pairs={{0,2},{1,3},{2,0},{3,1},{4,6},{5,7},{6,4},{7,5},{8,10},{9,11},{10,... | collective-permute-start | bytes 503816 | tf_op jit(solution)/shard_map/ppermute | solution.py:186
  27.7 3.2 %collective-permute-start.12 = (bf16[656,128]{1,0:T(8,128)(2,1)S(1)}, bf16[656,128]{1,0:T(8,128)(2,1)S(1)}, u32[]{:S(2)}, u32[]{:S(2)}) collective-permute-start(bf16[656,128]{1,0:T(8,128)(2,1)S(1)} %collective-permute-done.4.refs_5_), channel_id=1, source_target_pairs={{0,1},{1,0},{2,3},{3,2},{4,5},{5,4},{6,7},{7,6},{8,9},{9,8},{10,11... | collective-permute-start | bytes 503816 | tf_op jit(solution)/shard_map/ppermute | solution.py:186
  27.7 3.2 %collective-permute-start.13 = (bf16[656,128]{1,0:T(8,128)(2,1)S(1)}, bf16[656,128]{1,0:T(8,128)(2,1)S(1)}, u32[]{:S(2)}, u32[]{:S(2)}) collective-permute-start(bf16[656,128]{1,0:T(8,128)(2,1)S(1)} %collective-permute-done.5.refs_6_), channel_id=1, source_target_pairs={{0,1},{1,0},{2,3},{3,2},{4,5},{5,4},{6,7},{7,6},{8,9},{9,8},{10,11... | collective-permute-start | bytes 503816 | tf_op jit(solution)/shard_map/ppermute | solution.py:186
  30.9 1.4 %collective-permute-start.14 = (bf16[656,128]{1,0:T(8,128)(2,1)S(1)}, bf16[656,128]{1,0:T(8,128)(2,1)S(1)}, u32[]{:S(2)}, u32[]{:S(2)}) collective-permute-start(bf16[656,128]{1,0:T(8,128)(2,1)S(1)} %collective-permute-done.11.refs_7_), channel_id=1, source_target_pairs={{0,1},{1,0},{2,3},{3,2},{4,5},{5,4},{6,7},{7,6},{8,9},{9,8},{10,11... | collective-permute-start | bytes 503816 | tf_op jit(solution)/shard_map/ppermute | solution.py:186

commit v12 on v9

--- a/solution.py
+++ b/solution.py
@@ -187,13 +187,18 @@
     if n_orb == 4 and n_pair == 4:
         packed = list(pack(n_pair, integrals, mu_block, nu_block, counts, coeff))
         lines = packed[:1] + [flip(packed[s], "pair", n_pair, s) for s in range(1, n_pair)]
-        across = [flip(line, "orb", n_orb, 2) for line in lines[:3]]
-        last, across[1] = lax.optimization_barrier((lines[3], across[1]))
+        across = [None, flip(lines[1], "orb", n_orb, 2)]
+        lines[0], lines[1] = lax.optimization_barrier((lines[0], lines[1]))
+        across[0] = flip(lines[0], "orb", n_orb, 2)
+        lines[2], across[1] = lax.optimization_barrier((lines[2], across[1]))
+        across.append(flip(lines[2], "orb", n_orb, 2))
+        swapped = [flip(piece, "orb", n_orb, 1) for piece in lines[:2]]
+        last, across[1], *swapped = lax.optimization_barrier((lines[3], across[1], *swapped))
         across.append(flip(last, "orb", n_orb, 2))
-        early = lax.optimization_barrier(tuple(lines[:3] + across[:3] + [last]))
-        pieces = list(early) + across[3:]
-        pieces += [flip(piece, "orb", n_orb, 1) for piece in pieces]
-        came = [(0, 0), (1, 0), (2, 0), (0, 2), (1, 2), (2, 2), (3, 0), (3, 2)]
+        later = list(lax.optimization_barrier(tuple([lines[2], last] + across[:3]))) + across[3:]
+        swapped += [flip(piece, "orb", n_orb, 1) for piece in later]
+        pieces = lines[:2] + later + swapped
+        came = [(0, 0), (1, 0), (2, 0), (3, 0), (0, 2), (1, 2), (2, 2), (3, 2)]
         came += [(s, side ^ 1) for s, side in came]
     else:
         kept = jnp.arange(slots, dtype=jnp.int32) < counts[0]

time: 33.8 us -> 36.3 us (1.074)
  starting transfers between devices: 11.8 us -> 14.4 us
    ppermute x15, starting transfers between devices: 11.8 us -> 14.4 us  [flip(): return lax.ppermute(array, axis, [(i, i ^ bit) for i in range(size)])]
  transfers between devices with their start and end apart: 15 -> 15, of which waited for: 9 -> 8; matrix products, arithmetic and copies ran while one was open for 0% -> 0% of each run, Pallas kernels for 0% -> 0%
where the time goes in v12:
time: 36.3 us; the launch traced here: 36.1 us
  waiting for transfers between devices  16.1 us (44%)
  starting transfers between devices  14.4 us (40%)
  Pallas kernels  4.9 us (13%)
  between operations  0.68 us (2%)
    ppermute x15, waiting for transfers between devices, flip(): return lax.ppermute(array, axis, [(i, i ^ bit) for i in range(size)])  16.1 us
    ppermute x15, starting transfers between devices, flip(): return lax.ppermute(array, axis, [(i, i ^ bit) for i in range(size)])  14.4 us
    pallas_call x1, Pallas kernels, transform(): pl.pallas_call(functools.partial(transform_kernel, came, n_orb, orbitals,...  3.71 us
    pallas_call x1, Pallas kernels, pack(): pl.pallas_call(functools.partial(pack_kernel, n_pair), out_shape=[pltpu.V...  1.19 us
  transfers between devices with their start and end apart: 15, of which 8 were waited for; matrix products, arithmetic and copies ran while one was open for 0% of the time, Pallas kernels for 0%

profile of v12, /device:TPU:0, one launch (start us, length us, event | category | flops | bytes accessed | tf_op | source)
XLA Modules:
  0.0 36.1 jit_solution(1390770542455279982)
XLA Ops:
  0.7 1.2 %pack.1 = (bf16[656,128]{1,0:T(8,128)(2,1)S(1)}, bf16[656,128]{1,0:T(8,128)(2,1)S(1)}, bf16[656,128]{1,0:T(8,128)(2,1)S(1)}, bf16[656,128]{1,0:T(8,128)(2,1)S(1)}) custom-call(bf16[2,8,4096]{2,1,0:T(8,128)(2,1)} %integrals.1, s32[2]{0:T(128)} %mu.1, s32[2]{0:T(128)} %nu.1, s32[1]{0:T(128)S(6)} %copy.7.counts, bf16[128,512]{1,0:T(8,128)(2,1)} %coeff.1), custom_call_target="tpu_custom_call" | custom-call | tf_op jit(solution)/shard_map/pack/pallas_call | solution.py:71
  1.9 3.1 %collective-permute-start = (bf16[656,128]{1,0:T(8,128)(2,1)S(1)}, bf16[656,128]{1,0:T(8,128)(2,1)S(1)}, u32[]{:S(2)}, u32[]{:S(2)}) collective-permute-start(bf16[656,128]{1,0:T(8,128)(2,1)S(1)} %get-tuple-element.23), channel_id=1, source_target_pairs={{0,4},{4,0},{8,12},{12,8},{1,5},{5,1},{9,13},{13,9},{2,6},{6,2},{1... | collective-permute-start | bytes 503816 | tf_op jit(solution)/shard_map/ppermute | solution.py:180
  4.9 2.6 %collective-permute-start.1 = (bf16[656,128]{1,0:T(8,128)(2,1)S(1)}, bf16[656,128]{1,0:T(8,128)(2,1)S(1)}, u32[]{:S(2)}, u32[]{:S(2)}) collective-permute-start(bf16[656,128]{1,0:T(8,128)(2,1)S(1)} %get-tuple-element.26), channel_id=1, source_target_pairs={{0,8},{4,12},{8,0},{12,4},{1,9},{5,13},{9,1},{13,5},{2,10},{6,14},... | collective-permute-start | bytes 503816 | tf_op jit(solution)/shard_map/ppermute | solution.py:180
  7.5 5.2 %collective-permute-done.refs_1_ = bf16[656,128]{1,0:T(8,128)(2,1)S(1)} collective-permute-done((bf16[656,128]{1,0:T(8,128)(2,1)S(1)}, bf16[656,128]{1,0:T(8,128)(2,1)S(1)}, u32[]{:S(2)}, u32[]{:S(2)}) %collective-permute-start) | collective-permute-done | bytes 167968 | tf_op jit(solution)/shard_map/ppermute | solution.py:180
  12.7 1.7 %collective-permute-start.2 = (bf16[656,128]{1,0:T(8,128)(2,1)S(1)}, bf16[656,128]{1,0:T(8,128)(2,1)S(1)}, u32[]{:S(2)}, u32[]{:S(2)}) collective-permute-start(bf16[656,128]{1,0:T(8,128)(2,1)S(1)} %collective-permute-done.refs_1_), channel_id=1, source_target_pairs={{0,2},{1,3},{2,0},{3,1},{4,6},{5,7},{6,4},{7,5},{8,10},{9,11},{10,... | collective-permute-start | bytes 503816 | tf_op jit(solution)/shard_map/ppermute | solution.py:180
  14.4 2.5 %collective-permute-start.3 = (bf16[656,128]{1,0:T(8,128)(2,1)S(1)}, bf16[656,128]{1,0:T(8,128)(2,1)S(1)}, u32[]{:S(2)}, u32[]{:S(2)}) collective-permute-start(bf16[656,128]{1,0:T(8,128)(2,1)S(1)} %get-tuple-element.28), channel_id=1, source_target_pairs={{0,12},{4,8},{8,4},{12,0},{1,13},{5,9},{9,5},{13,1},{2,14},{6,10},... | collective-permute-start | bytes 503816 | tf_op jit(solution)/shard_map/ppermute | solution.py:180
  16.8 0.0 collective-permute-start.5
  16.8 0.5 %collective-permute-start.4 = (bf16[656,128]{1,0:T(8,128)(2,1)S(1)}, bf16[656,128]{1,0:T(8,128)(2,1)S(1)}, u32[]{:S(2)}, u32[]{:S(2)}) collective-permute-start(bf16[656,128]{1,0:T(8,128)(2,1)S(1)} %get-tuple-element.24.refs_0_), channel_id=1, source_target_pairs={{0,1},{1,0},{2,3},{3,2},{4,5},{5,4},{6,7},{7,6},{8,9},{9,8},{10,11... | collective-permute-start | bytes 503816 | tf_op jit(solution)/shard_map/ppermute | solution.py:180
  17.4 0.0 collective-permute-done.1.refs_2_
  17.4 0.5 %collective-permute-start.6 = (bf16[656,128]{1,0:T(8,128)(2,1)S(1)}, bf16[656,128]{1,0:T(8,128)(2,1)S(1)}, u32[]{:S(2)}, u32[]{:S(2)}) collective-permute-start(bf16[656,128]{1,0:T(8,128)(2,1)S(1)} %get-tuple-element.24.refs_0_), channel_id=1, source_target_pairs={{0,2},{1,3},{2,0},{3,1},{4,6},{5,7},{6,4},{7,5},{8,10},{9,11},{10,... | collective-permute-start | bytes 503816 | tf_op jit(solution)/shard_map/ppermute | solution.py:180
  17.9 0.2 collective-permute-done.2.refs_5_
  18.1 1.7 %collective-permute-start.7 = (bf16[656,128]{1,0:T(8,128)(2,1)S(1)}, bf16[656,128]{1,0:T(8,128)(2,1)S(1)}, u32[]{:S(2)}, u32[]{:S(2)}) collective-permute-start(bf16[656,128]{1,0:T(8,128)(2,1)S(1)} %collective-permute-done.1.refs_2_), channel_id=1, source_target_pairs={{0,2},{1,3},{2,0},{3,1},{4,6},{5,7},{6,4},{7,5},{8,10},{9,11},{10,... | collective-permute-start | bytes 503816 | tf_op jit(solution)/shard_map/ppermute | solution.py:180
  19.7 1.9 %collective-permute-done.3.refs_3_ = bf16[656,128]{1,0:T(8,128)(2,1)S(1)} collective-permute-done((bf16[656,128]{1,0:T(8,128)(2,1)S(1)}, bf16[656,128]{1,0:T(8,128)(2,1)S(1)}, u32[]{:S(2)}, u32[]{:S(2)}) %collective-permute-start.3) | collective-permute-done | bytes 167968 | tf_op jit(solution)/shard_map/ppermute | solution.py:180
  21.6 0.0 collective-permute-done.5.refs_9_
  21.6 0.0 collective-permute-done.4.refs_8_
  21.6 0.4 %collective-permute-start.8 = (bf16[656,128]{1,0:T(8,128)(2,1)S(1)}, bf16[656,128]{1,0:T(8,128)(2,1)S(1)}, u32[]{:S(2)}, u32[]{:S(2)}) collective-permute-start(bf16[656,128]{1,0:T(8,128)(2,1)S(1)} %collective-permute-done.3.refs_3_), channel_id=1, source_target_pairs={{0,2},{1,3},{2,0},{3,1},{4,6},{5,7},{6,4},{7,5},{8,10},{9,11},{10,... | collective-permute-start | bytes 503816 | tf_op jit(solution)/shard_map/ppermute | solution.py:180
  22.0 2.5 %collective-permute-done.6.refs_4_ = bf16[656,128]{1,0:T(8,128)(2,1)S(1)} collective-permute-done((bf16[656,128]{1,0:T(8,128)(2,1)S(1)}, bf16[656,128]{1,0:T(8,128)(2,1)S(1)}, u32[]{:S(2)}, u32[]{:S(2)}) %collective-permute-start.6) | collective-permute-done | bytes 167968 | tf_op jit(solution)/shard_map/ppermute | solution.py:180
  24.5 3.6 %collective-permute-done.7.refs_6_ = bf16[656,128]{1,0:T(8,128)(2,1)S(1)} collective-permute-done((bf16[656,128]{1,0:T(8,128)(2,1)S(1)}, bf16[656,128]{1,0:T(8,128)(2,1)S(1)}, u32[]{:S(2)}, u32[]{:S(2)}) %collective-permute-start.7) | collective-permute-done | bytes 167968 | tf_op jit(solution)/shard_map/ppermute | solution.py:180
  28.1 0.0 collective-permute-start.9
  28.1 0.5 %collective-permute-start.10 = (bf16[656,128]{1,0:T(8,128)(2,1)S(1)}, bf16[656,128]{1,0:T(8,128)(2,1)S(1)}, u32[]{:S(2)}, u32[]{:S(2)}) collective-permute-start(bf16[656,128]{1,0:T(8,128)(2,1)S(1)} %collective-permute-done.3.refs_3_), channel_id=1, source_target_pairs={{0,1},{1,0},{2,3},{3,2},{4,5},{5,4},{6,7},{7,6},{8,9},{9,8},{10,11... | collective-permute-start | bytes 503816 | tf_op jit(solution)/shard_map/ppermute | solution.py:180
  28.6 0.0 collective-permute-start.11
  28.6 0.5 %collective-permute-start.12 = (bf16[656,128]{1,0:T(8,128)(2,1)S(1)}, bf16[656,128]{1,0:T(8,128)(2,1)S(1)}, u32[]{:S(2)}, u32[]{:S(2)}) collective-permute-start(bf16[656,128]{1,0:T(8,128)(2,1)S(1)} %collective-permute-done.2.refs_5_), channel_id=1, source_target_pairs={{0,1},{1,0},{2,3},{3,2},{4,5},{5,4},{6,7},{7,6},{8,9},{9,8},{10,11... | collective-permute-start | bytes 503816 | tf_op jit(solution)/shard_map/ppermute | solution.py:180
  29.1 1.6 %collective-permute-done.8.refs_7_ = bf16[656,128]{1,0:T(8,128)(2,1)S(1)} collective-permute-done((bf16[656,128]{1,0:T(8,128)(2,1)S(1)}, bf16[656,128]{1,0:T(8,128)(2,1)S(1)}, u32[]{:S(2)}, u32[]{:S(2)}) %collective-permute-start.8) | collective-permute-done | bytes 167968 | tf_op jit(solution)/shard_map/ppermute | solution.py:180
  30.8 0.0 collective-permute-start.13
  30.8 0.0 collective-permute-done.9.refs_10_
  30.8 0.5 %collective-permute-start.14 = (bf16[656,128]{1,0:T(8,128)(2,1)S(1)}, bf16[656,128]{1,0:T(8,128)(2,1)S(1)}, u32[]{:S(2)}, u32[]{:S(2)}) collective-permute-start(bf16[656,128]{1,0:T(8,128)(2,1)S(1)} %collective-permute-done.8.refs_7_), channel_id=1, source_target_pairs={{0,1},{1,0},{2,3},{3,2},{4,5},{5,4},{6,7},{7,6},{8,9},{9,8},{10,11... | collective-permute-start | bytes 503816 | tf_op jit(solution)/shard_map/ppermute | solution.py:180
  31.3 0.0 collective-permute-done.10.refs_11_
  31.3 0.0 collective-permute-done.11.refs_12_
  31.3 0.0 collective-permute-done.12.refs_13_
  31.3 0.9 %collective-permute-done.13.refs_14_ = bf16[656,128]{1,0:T(8,128)(2,1)S(1)} collective-permute-done((bf16[656,128]{1,0:T(8,128)(2,1)S(1)}, bf16[656,128]{1,0:T(8,128)(2,1)S(1)}, u32[]{:S(2)}, u32[]{:S(2)}) %collective-permute-start.13) | collective-permute-done | bytes 167968 | tf_op jit(solution)/shard_map/ppermute | solution.py:180
  32.2 0.2 collective-permute-done.14.refs_15_
  32.4 3.7 %transform.1 = f32[1024,128]{1,0:T(8,128)} custom-call(bf16[656,128]{1,0:T(8,128)(2,1)S(1)} %get-tuple-element.24.refs_0_, bf16[656,128]{1,0:T(8,128)(2,1)S(1)} %collective-permute-done.refs_1_, bf16[656,128]{1,0:T(8,128)(2,1)S(1)} %collective-permute-done.1.refs_2_, bf16[656,128]{1,0:T(8,128)(2,1)S(1)} %collective-permute-done.3.refs_3_, ...), custom_call_target="tpu_custom_call" | custom-call | tf_op jit(solution)/shard_map/transform/pallas_call | solution.py:161
Async XLA Ops:
  1.9 10.9 %collective-permute-start = (bf16[656,128]{1,0:T(8,128)(2,1)S(1)}, bf16[656,128]{1,0:T(8,128)(2,1)S(1)}, u32[]{:S(2)}, u32[]{:S(2)}) collective-permute-start(bf16[656,128]{1,0:T(8,128)(2,1)S(1)} %get-tuple-element.23), channel_id=1, source_target_pairs={{0,4},{4,0},{8,12},{12,8},{1,5},{5,1},{9,13},{13,9},{2,6},{6,2},{1... | collective-permute-start | bytes 503816 | tf_op jit(solution)/shard_map/ppermute | solution.py:180
  4.9 12.4 %collective-permute-start.1 = (bf16[656,128]{1,0:T(8,128)(2,1)S(1)}, bf16[656,128]{1,0:T(8,128)(2,1)S(1)}, u32[]{:S(2)}, u32[]{:S(2)}) collective-permute-start(bf16[656,128]{1,0:T(8,128)(2,1)S(1)} %get-tuple-element.26), channel_id=1, source_target_pairs={{0,8},{4,12},{8,0},{12,4},{1,9},{5,13},{9,1},{13,5},{2,10},{6,14},... | collective-permute-start | bytes 503816 | tf_op jit(solution)/shard_map/ppermute | solution.py:180
  12.7 5.4 %collective-permute-start.2 = (bf16[656,128]{1,0:T(8,128)(2,1)S(1)}, bf16[656,128]{1,0:T(8,128)(2,1)S(1)}, u32[]{:S(2)}, u32[]{:S(2)}) collective-permute-start(bf16[656,128]{1,0:T(8,128)(2,1)S(1)} %collective-permute-done.refs_1_), channel_id=1, source_target_pairs={{0,2},{1,3},{2,0},{3,1},{4,6},{5,7},{6,4},{7,5},{8,10},{9,11},{10,... | collective-permute-start | bytes 503816 | tf_op jit(solution)/shard_map/ppermute | solution.py:180
  14.4 7.3 %collective-permute-start.3 = (bf16[656,128]{1,0:T(8,128)(2,1)S(1)}, bf16[656,128]{1,0:T(8,128)(2,1)S(1)}, u32[]{:S(2)}, u32[]{:S(2)}) collective-permute-start(bf16[656,128]{1,0:T(8,128)(2,1)S(1)} %get-tuple-element.28), channel_id=1, source_target_pairs={{0,12},{4,8},{8,4},{12,0},{1,13},{5,9},{9,5},{13,1},{2,14},{6,10},... | collective-permute-start | bytes 503816 | tf_op jit(solution)/shard_map/ppermute | solution.py:180
  16.8 4.8 %collective-permute-start.5 = (bf16[656,128]{1,0:T(8,128)(2,1)S(1)}, bf16[656,128]{1,0:T(8,128)(2,1)S(1)}, u32[]{:S(2)}, u32[]{:S(2)}) collective-permute-start(bf16[656,128]{1,0:T(8,128)(2,1)S(1)} %collective-permute-done.refs_1_), channel_id=1, source_target_pairs={{0,1},{1,0},{2,3},{3,2},{4,5},{5,4},{6,7},{7,6},{8,9},{9,8},{10,11... | collective-permute-start | bytes 503816 | tf_op jit(solution)/shard_map/ppermute | solution.py:180
  16.8 4.8 %collective-permute-start.4 = (bf16[656,128]{1,0:T(8,128)(2,1)S(1)}, bf16[656,128]{1,0:T(8,128)(2,1)S(1)}, u32[]{:S(2)}, u32[]{:S(2)}) collective-permute-start(bf16[656,128]{1,0:T(8,128)(2,1)S(1)} %get-tuple-element.24.refs_0_), channel_id=1, source_target_pairs={{0,1},{1,0},{2,3},{3,2},{4,5},{5,4},{6,7},{7,6},{8,9},{9,8},{10,11... | collective-permute-start | bytes 503816 | tf_op jit(solution)/shard_map/ppermute | solution.py:180
  17.4 7.2 %collective-permute-start.6 = (bf16[656,128]{1,0:T(8,128)(2,1)S(1)}, bf16[656,128]{1,0:T(8,128)(2,1)S(1)}, u32[]{:S(2)}, u32[]{:S(2)}) collective-permute-start(bf16[656,128]{1,0:T(8,128)(2,1)S(1)} %get-tuple-element.24.refs_0_), channel_id=1, source_target_pairs={{0,2},{1,3},{2,0},{3,1},{4,6},{5,7},{6,4},{7,5},{8,10},{9,11},{10,... | collective-permute-start | bytes 503816 | tf_op jit(solution)/shard_map/ppermute | solution.py:180
  18.1 10.0 %collective-permute-start.7 = (bf16[656,128]{1,0:T(8,128)(2,1)S(1)}, bf16[656,128]{1,0:T(8,128)(2,1)S(1)}, u32[]{:S(2)}, u32[]{:S(2)}) collective-permute-start(bf16[656,128]{1,0:T(8,128)(2,1)S(1)} %collective-permute-done.1.refs_2_), channel_id=1, source_target_pairs={{0,2},{1,3},{2,0},{3,1},{4,6},{5,7},{6,4},{7,5},{8,10},{9,11},{10,... | collective-permute-start | bytes 503816 | tf_op jit(solution)/shard_map/ppermute | solution.py:180
  21.6 9.1 %collective-permute-start.8 = (bf16[656,128]{1,0:T(8,128)(2,1)S(1)}, bf16[656,128]{1,0:T(8,128)(2,1)S(1)}, u32[]{:S(2)}, u32[]{:S(2)}) collective-permute-start(bf16[656,128]{1,0:T(8,128)(2,1)S(1)} %collective-permute-done.3.refs_3_), channel_id=1, source_target_pairs={{0,2},{1,3},{2,0},{3,1},{4,6},{5,7},{6,4},{7,5},{8,10},{9,11},{10,... | collective-permute-start | bytes 503816 | tf_op jit(solution)/shard_map/ppermute | solution.py:180
  28.1 2.6 %collective-permute-start.9 = (bf16[656,128]{1,0:T(8,128)(2,1)S(1)}, bf16[656,128]{1,0:T(8,128)(2,1)S(1)}, u32[]{:S(2)}, u32[]{:S(2)}) collective-permute-start(bf16[656,128]{1,0:T(8,128)(2,1)S(1)} %collective-permute-done.1.refs_2_), channel_id=1, source_target_pairs={{0,1},{1,0},{2,3},{3,2},{4,5},{5,4},{6,7},{7,6},{8,9},{9,8},{10,11... | collective-permute-start | bytes 503816 | tf_op jit(solution)/shard_map/ppermute | solution.py:180
  28.1 3.2 %collective-permute-start.10 = (bf16[656,128]{1,0:T(8,128)(2,1)S(1)}, bf16[656,128]{1,0:T(8,128)(2,1)S(1)}, u32[]{:S(2)}, u32[]{:S(2)}) collective-permute-start(bf16[656,128]{1,0:T(8,128)(2,1)S(1)} %collective-permute-done.3.refs_3_), channel_id=1, source_target_pairs={{0,1},{1,0},{2,3},{3,2},{4,5},{5,4},{6,7},{7,6},{8,9},{9,8},{10,11... | collective-permute-start | bytes 503816 | tf_op jit(solution)/shard_map/ppermute | solution.py:180
  28.6 2.6 %collective-permute-start.11 = (bf16[656,128]{1,0:T(8,128)(2,1)S(1)}, bf16[656,128]{1,0:T(8,128)(2,1)S(1)}, u32[]{:S(2)}, u32[]{:S(2)}) collective-permute-start(bf16[656,128]{1,0:T(8,128)(2,1)S(1)} %collective-permute-done.6.refs_4_), channel_id=1, source_target_pairs={{0,1},{1,0},{2,3},{3,2},{4,5},{5,4},{6,7},{7,6},{8,9},{9,8},{10,11... | collective-permute-start | bytes 503816 | tf_op jit(solution)/shard_map/ppermute | solution.py:180
  28.6 2.6 %collective-permute-start.12 = (bf16[656,128]{1,0:T(8,128)(2,1)S(1)}, bf16[656,128]{1,0:T(8,128)(2,1)S(1)}, u32[]{:S(2)}, u32[]{:S(2)}) collective-permute-start(bf16[656,128]{1,0:T(8,128)(2,1)S(1)} %collective-permute-done.2.refs_5_), channel_id=1, source_target_pairs={{0,1},{1,0},{2,3},{3,2},{4,5},{5,4},{6,7},{7,6},{8,9},{9,8},{10,11... | collective-permute-start | bytes 503816 | tf_op jit(solution)/shard_map/ppermute | solution.py:180
  30.8 1.4 %collective-permute-start.13 = (bf16[656,128]{1,0:T(8,128)(2,1)S(1)}, bf16[656,128]{1,0:T(8,128)(2,1)S(1)}, u32[]{:S(2)}, u32[]{:S(2)}) collective-permute-start(bf16[656,128]{1,0:T(8,128)(2,1)S(1)} %collective-permute-done.7.refs_6_), channel_id=1, source_target_pairs={{0,1},{1,0},{2,3},{3,2},{4,5},{5,4},{6,7},{7,6},{8,9},{9,8},{10,11... | collective-permute-start | bytes 503816 | tf_op jit(solution)/shard_map/ppermute | solution.py:180
  30.8 1.6 %collective-permute-start.14 = (bf16[656,128]{1,0:T(8,128)(2,1)S(1)}, bf16[656,128]{1,0:T(8,128)(2,1)S(1)}, u32[]{:S(2)}, u32[]{:S(2)}) collective-permute-start(bf16[656,128]{1,0:T(8,128)(2,1)S(1)} %collective-permute-done.8.refs_7_), channel_id=1, source_target_pairs={{0,1},{1,0},{2,3},{3,2},{4,5},{5,4},{6,7},{7,6},{8,9},{9,8},{10,11... | collective-permute-start | bytes 503816 | tf_op jit(solution)/shard_map/ppermute | solution.py:180

commit v13 on v9

--- a/solution.py
+++ b/solution.py
@@ -190,10 +190,12 @@
         across = [flip(line, "orb", n_orb, 2) for line in lines[:3]]
         last, across[1] = lax.optimization_barrier((lines[3], across[1]))
         across.append(flip(last, "orb", n_orb, 2))
-        early = lax.optimization_barrier(tuple(lines[:3] + across[:3] + [last]))
-        pieces = list(early) + across[3:]
-        pieces += [flip(piece, "orb", n_orb, 1) for piece in pieces]
-        came = [(0, 0), (1, 0), (2, 0), (0, 2), (1, 2), (2, 2), (3, 0), (3, 2)]
+        first = list(lax.optimization_barrier((lines[0], lines[1], last)))[:2]
+        swapped = [flip(piece, "orb", n_orb, 1) for piece in first]
+        later = list(lax.optimization_barrier((lines[2], last, *across[:3]))) + across[3:]
+        swapped += [flip(piece, "orb", n_orb, 1) for piece in later]
+        pieces = first + later + swapped
+        came = [(0, 0), (1, 0), (2, 0), (3, 0), (0, 2), (1, 2), (2, 2), (3, 2)]
         came += [(s, side ^ 1) for s, side in came]
     else:
         kept = jnp.arange(slots, dtype=jnp.int32) < counts[0]

time: 33.8 us -> 33.3 us (0.985)
  waiting for transfers between devices: 16.3 us -> 15.8 us
    ppermute x15, waiting for transfers between devices: 16.3 us -> 15.8 us  [flip(): return lax.ppermute(array, axis, [(i, i ^ bit) for i in range(size)])]
  transfers between devices with their start and end apart: 15 -> 15, of which waited for: 9 -> 6; matrix products, arithmetic and copies ran while one was open for 0% -> 0% of each run, Pallas kernels for 0% -> 0%
where the time goes in v13:
time: 33.3 us; the launch traced here: 33.2 us
  waiting for transfers between devices  15.8 us (47%)
  starting transfers between devices  11.8 us (35%)
  Pallas kernels  4.9 us (15%)
  between operations  0.68 us (2%)
    ppermute x15, waiting for transfers between devices, flip(): return lax.ppermute(array, axis, [(i, i ^ bit) for i in range(size)])  15.8 us
    ppermute x15, starting transfers between devices, flip(): return lax.ppermute(array, axis, [(i, i ^ bit) for i in range(size)])  11.8 us
    pallas_call x1, Pallas kernels, transform(): pl.pallas_call(functools.partial(transform_kernel, came, n_orb, orbitals,...  3.71 us
    pallas_call x1, Pallas kernels, pack(): pl.pallas_call(functools.partial(pack_kernel, n_pair), out_shape=[pltpu.V...  1.19 us
  transfers between devices with their start and end apart: 15, of which 6 were waited for; matrix products, arithmetic and copies ran while one was open for 0% of the time, Pallas kernels for 0%

profile of v13, /device:TPU:0, one launch (start us, length us, event | category | flops | bytes accessed | tf_op | source)
XLA Modules:
  0.0 33.2 jit_solution(4944049641954834575)
XLA Ops:
  0.7 1.2 %pack.1 = (bf16[656,128]{1,0:T(8,128)(2,1)S(1)}, bf16[656,128]{1,0:T(8,128)(2,1)S(1)}, bf16[656,128]{1,0:T(8,128)(2,1)S(1)}, bf16[656,128]{1,0:T(8,128)(2,1)S(1)}) custom-call(bf16[2,8,4096]{2,1,0:T(8,128)(2,1)} %integrals.1, s32[2]{0:T(128)} %mu.1, s32[2]{0:T(128)} %nu.1, s32[1]{0:T(128)S(6)} %copy.7.counts, bf16[128,512]{1,0:T(8,128)(2,1)} %coeff.1), custom_call_target="tpu_custom_call" | custom-call | tf_op jit(solution)/shard_map/pack/pallas_call | solution.py:71
  1.9 3.1 %collective-permute-start = (bf16[656,128]{1,0:T(8,128)(2,1)S(1)}, bf16[656,128]{1,0:T(8,128)(2,1)S(1)}, u32[]{:S(2)}, u32[]{:S(2)}) collective-permute-start(bf16[656,128]{1,0:T(8,128)(2,1)S(1)} %get-tuple-element.19), channel_id=1, source_target_pairs={{0,4},{4,0},{8,12},{12,8},{1,5},{5,1},{9,13},{13,9},{2,6},{6,2},{1... | collective-permute-start | bytes 503816 | tf_op jit(solution)/shard_map/ppermute | solution.py:180
  4.9 2.6 %collective-permute-start.3 = (bf16[656,128]{1,0:T(8,128)(2,1)S(1)}, bf16[656,128]{1,0:T(8,128)(2,1)S(1)}, u32[]{:S(2)}, u32[]{:S(2)}) collective-permute-start(bf16[656,128]{1,0:T(8,128)(2,1)S(1)} %get-tuple-element.24), channel_id=1, source_target_pairs={{0,8},{4,12},{8,0},{12,4},{1,9},{5,13},{9,1},{13,5},{2,10},{6,14},... | collective-permute-start | bytes 503816 | tf_op jit(solution)/shard_map/ppermute | solution.py:180
  7.5 0.0 collective-permute-start.1
  7.5 4.3 %collective-permute-done.refs_1_ = bf16[656,128]{1,0:T(8,128)(2,1)S(1)} collective-permute-done((bf16[656,128]{1,0:T(8,128)(2,1)S(1)}, bf16[656,128]{1,0:T(8,128)(2,1)S(1)}, u32[]{:S(2)}, u32[]{:S(2)}) %collective-permute-start) | collective-permute-done | bytes 167968 | tf_op jit(solution)/shard_map/ppermute | solution.py:180
  11.8 1.7 %collective-permute-start.2 = (bf16[656,128]{1,0:T(8,128)(2,1)S(1)}, bf16[656,128]{1,0:T(8,128)(2,1)S(1)}, u32[]{:S(2)}, u32[]{:S(2)}) collective-permute-start(bf16[656,128]{1,0:T(8,128)(2,1)S(1)} %collective-permute-done.refs_1_), channel_id=1, source_target_pairs={{0,2},{1,3},{2,0},{3,1},{4,6},{5,7},{6,4},{7,5},{8,10},{9,11},{10,... | collective-permute-start | bytes 503816 | tf_op jit(solution)/shard_map/ppermute | solution.py:180
  13.5 0.3 collective-permute-start.4
  13.8 6.4 %collective-permute-done.3.refs_2_ = bf16[656,128]{1,0:T(8,128)(2,1)S(1)} collective-permute-done((bf16[656,128]{1,0:T(8,128)(2,1)S(1)}, bf16[656,128]{1,0:T(8,128)(2,1)S(1)}, u32[]{:S(2)}, u32[]{:S(2)}) %collective-permute-start.3) | collective-permute-done | bytes 167968 | tf_op jit(solution)/shard_map/ppermute | solution.py:180
  20.3 1.5 %collective-permute-start.5 = (bf16[656,128]{1,0:T(8,128)(2,1)S(1)}, bf16[656,128]{1,0:T(8,128)(2,1)S(1)}, u32[]{:S(2)}, u32[]{:S(2)}) collective-permute-start(bf16[656,128]{1,0:T(8,128)(2,1)S(1)} %collective-permute-done.3.refs_2_), channel_id=1, source_target_pairs={{0,2},{1,3},{2,0},{3,1},{4,6},{5,7},{6,4},{7,5},{8,10},{9,11},{10,... | collective-permute-start | bytes 503816 | tf_op jit(solution)/shard_map/ppermute | solution.py:180
  21.7 0.0 collective-permute-done.1.refs_3_
  21.7 0.0 collective-permute-done.2.refs_5_
  21.7 0.5 %collective-permute-start.6 = (bf16[656,128]{1,0:T(8,128)(2,1)S(1)}, bf16[656,128]{1,0:T(8,128)(2,1)S(1)}, u32[]{:S(2)}, u32[]{:S(2)}) collective-permute-start(bf16[656,128]{1,0:T(8,128)(2,1)S(1)} %collective-permute-done.1.refs_3_), channel_id=1, source_target_pairs={{0,2},{1,3},{2,0},{3,1},{4,6},{5,7},{6,4},{7,5},{8,10},{9,11},{10,... | collective-permute-start | bytes 503816 | tf_op jit(solution)/shard_map/ppermute | solution.py:180
  22.3 0.0 collective-permute-start.7
  22.3 0.5 %collective-permute-start.8 = (bf16[656,128]{1,0:T(8,128)(2,1)S(1)}, bf16[656,128]{1,0:T(8,128)(2,1)S(1)}, u32[]{:S(2)}, u32[]{:S(2)}) collective-permute-start(bf16[656,128]{1,0:T(8,128)(2,1)S(1)} %collective-permute-done.refs_1_), channel_id=1, source_target_pairs={{0,1},{1,0},{2,3},{3,2},{4,5},{5,4},{6,7},{7,6},{8,9},{9,8},{10,11... | collective-permute-start | bytes 503816 | tf_op jit(solution)/shard_map/ppermute | solution.py:180
  22.8 0.0 collective-permute-done.4.refs_4_
  22.8 3.2 %collective-permute-done.5.refs_6_ = bf16[656,128]{1,0:T(8,128)(2,1)S(1)} collective-permute-done((bf16[656,128]{1,0:T(8,128)(2,1)S(1)}, bf16[656,128]{1,0:T(8,128)(2,1)S(1)}, u32[]{:S(2)}, u32[]{:S(2)}) %collective-permute-start.5) | collective-permute-done | bytes 167968 | tf_op jit(solution)/shard_map/ppermute | solution.py:180
  26.0 0.0 collective-permute-start.9
  26.0 0.5 %collective-permute-start.10 = (bf16[656,128]{1,0:T(8,128)(2,1)S(1)}, bf16[656,128]{1,0:T(8,128)(2,1)S(1)}, u32[]{:S(2)}, u32[]{:S(2)}) collective-permute-start(bf16[656,128]{1,0:T(8,128)(2,1)S(1)} %collective-permute-done.1.refs_3_), channel_id=1, source_target_pairs={{0,1},{1,0},{2,3},{3,2},{4,5},{5,4},{6,7},{7,6},{8,9},{9,8},{10,11... | collective-permute-start | bytes 503816 | tf_op jit(solution)/shard_map/ppermute | solution.py:180
  26.5 0.0 collective-permute-done.7.refs_8_
  26.5 0.0 collective-permute-start.11
  26.5 0.0 collective-permute-done.8.refs_9_
  26.5 0.5 %collective-permute-start.12 = (bf16[656,128]{1,0:T(8,128)(2,1)S(1)}, bf16[656,128]{1,0:T(8,128)(2,1)S(1)}, u32[]{:S(2)}, u32[]{:S(2)}) collective-permute-start(bf16[656,128]{1,0:T(8,128)(2,1)S(1)} %collective-permute-done.2.refs_5_), channel_id=1, source_target_pairs={{0,1},{1,0},{2,3},{3,2},{4,5},{5,4},{6,7},{7,6},{8,9},{9,8},{10,11... | collective-permute-start | bytes 503816 | tf_op jit(solution)/shard_map/ppermute | solution.py:180
  27.0 0.8 %collective-permute-done.6.refs_7_ = bf16[656,128]{1,0:T(8,128)(2,1)S(1)} collective-permute-done((bf16[656,128]{1,0:T(8,128)(2,1)S(1)}, bf16[656,128]{1,0:T(8,128)(2,1)S(1)}, u32[]{:S(2)}, u32[]{:S(2)}) %collective-permute-start.6) | collective-permute-done | bytes 167968 | tf_op jit(solution)/shard_map/ppermute | solution.py:180
  27.8 0.0 collective-permute-start.13
  27.8 0.0 collective-permute-done.9.refs_10_
  27.8 0.5 %collective-permute-start.14 = (bf16[656,128]{1,0:T(8,128)(2,1)S(1)}, bf16[656,128]{1,0:T(8,128)(2,1)S(1)}, u32[]{:S(2)}, u32[]{:S(2)}) collective-permute-start(bf16[656,128]{1,0:T(8,128)(2,1)S(1)} %collective-permute-done.6.refs_7_), channel_id=1, source_target_pairs={{0,1},{1,0},{2,3},{3,2},{4,5},{5,4},{6,7},{7,6},{8,9},{9,8},{10,11... | collective-permute-start | bytes 503816 | tf_op jit(solution)/shard_map/ppermute | solution.py:180
  28.3 0.0 collective-permute-done.10.refs_11_
  28.3 0.0 collective-permute-done.11.refs_12_
  28.3 0.0 collective-permute-done.12.refs_13_
  28.3 0.9 %collective-permute-done.13.refs_14_ = bf16[656,128]{1,0:T(8,128)(2,1)S(1)} collective-permute-done((bf16[656,128]{1,0:T(8,128)(2,1)S(1)}, bf16[656,128]{1,0:T(8,128)(2,1)S(1)}, u32[]{:S(2)}, u32[]{:S(2)}) %collective-permute-start.13) | collective-permute-done | bytes 167968 | tf_op jit(solution)/shard_map/ppermute | solution.py:180
  29.2 0.2 collective-permute-done.14.refs_15_
  29.5 3.7 %transform.1 = f32[1024,128]{1,0:T(8,128)} custom-call(bf16[656,128]{1,0:T(8,128)(2,1)S(1)} %get-tuple-element.22.refs_0_, bf16[656,128]{1,0:T(8,128)(2,1)S(1)} %collective-permute-done.refs_1_, bf16[656,128]{1,0:T(8,128)(2,1)S(1)} %collective-permute-done.3.refs_2_, bf16[656,128]{1,0:T(8,128)(2,1)S(1)} %collective-permute-done.1.refs_3_, ...), custom_call_target="tpu_custom_call" | custom-call | tf_op jit(solution)/shard_map/transform/pallas_call | solution.py:161
Async XLA Ops:
  1.9 10.0 %collective-permute-start = (bf16[656,128]{1,0:T(8,128)(2,1)S(1)}, bf16[656,128]{1,0:T(8,128)(2,1)S(1)}, u32[]{:S(2)}, u32[]{:S(2)}) collective-permute-start(bf16[656,128]{1,0:T(8,128)(2,1)S(1)} %get-tuple-element.19), channel_id=1, source_target_pairs={{0,4},{4,0},{8,12},{12,8},{1,5},{5,1},{9,13},{13,9},{2,6},{6,2},{1... | collective-permute-start | bytes 503816 | tf_op jit(solution)/shard_map/ppermute | solution.py:180
  4.9 15.3 %collective-permute-start.3 = (bf16[656,128]{1,0:T(8,128)(2,1)S(1)}, bf16[656,128]{1,0:T(8,128)(2,1)S(1)}, u32[]{:S(2)}, u32[]{:S(2)}) collective-permute-start(bf16[656,128]{1,0:T(8,128)(2,1)S(1)} %get-tuple-element.24), channel_id=1, source_target_pairs={{0,8},{4,12},{8,0},{12,4},{1,9},{5,13},{9,1},{13,5},{2,10},{6,14},... | collective-permute-start | bytes 503816 | tf_op jit(solution)/shard_map/ppermute | solution.py:180
  7.5 14.2 %collective-permute-start.1 = (bf16[656,128]{1,0:T(8,128)(2,1)S(1)}, bf16[656,128]{1,0:T(8,128)(2,1)S(1)}, u32[]{:S(2)}, u32[]{:S(2)}) collective-permute-start(bf16[656,128]{1,0:T(8,128)(2,1)S(1)} %get-tuple-element.20), channel_id=1, source_target_pairs={{0,12},{4,8},{8,4},{12,0},{1,13},{5,9},{9,5},{13,1},{2,14},{6,10},... | collective-permute-start | bytes 503816 | tf_op jit(solution)/shard_map/ppermute | solution.py:180
  11.8 9.9 %collective-permute-start.2 = (bf16[656,128]{1,0:T(8,128)(2,1)S(1)}, bf16[656,128]{1,0:T(8,128)(2,1)S(1)}, u32[]{:S(2)}, u32[]{:S(2)}) collective-permute-start(bf16[656,128]{1,0:T(8,128)(2,1)S(1)} %collective-permute-done.refs_1_), channel_id=1, source_target_pairs={{0,2},{1,3},{2,0},{3,1},{4,6},{5,7},{6,4},{7,5},{8,10},{9,11},{10,... | collective-permute-start | bytes 503816 | tf_op jit(solution)/shard_map/ppermute | solution.py:180
  13.5 9.3 %collective-permute-start.4 = (bf16[656,128]{1,0:T(8,128)(2,1)S(1)}, bf16[656,128]{1,0:T(8,128)(2,1)S(1)}, u32[]{:S(2)}, u32[]{:S(2)}) collective-permute-start(bf16[656,128]{1,0:T(8,128)(2,1)S(1)} %get-tuple-element.22.refs_0_), channel_id=1, source_target_pairs={{0,2},{1,3},{2,0},{3,1},{4,6},{5,7},{6,4},{7,5},{8,10},{9,11},{10,... | collective-permute-start | bytes 503816 | tf_op jit(solution)/shard_map/ppermute | solution.py:180
  20.3 5.8 %collective-permute-start.5 = (bf16[656,128]{1,0:T(8,128)(2,1)S(1)}, bf16[656,128]{1,0:T(8,128)(2,1)S(1)}, u32[]{:S(2)}, u32[]{:S(2)}) collective-permute-start(bf16[656,128]{1,0:T(8,128)(2,1)S(1)} %collective-permute-done.3.refs_2_), channel_id=1, source_target_pairs={{0,2},{1,3},{2,0},{3,1},{4,6},{5,7},{6,4},{7,5},{8,10},{9,11},{10,... | collective-permute-start | bytes 503816 | tf_op jit(solution)/shard_map/ppermute | solution.py:180
  21.7 6.1 %collective-permute-start.6 = (bf16[656,128]{1,0:T(8,128)(2,1)S(1)}, bf16[656,128]{1,0:T(8,128)(2,1)S(1)}, u32[]{:S(2)}, u32[]{:S(2)}) collective-permute-start(bf16[656,128]{1,0:T(8,128)(2,1)S(1)} %collective-permute-done.1.refs_3_), channel_id=1, source_target_pairs={{0,2},{1,3},{2,0},{3,1},{4,6},{5,7},{6,4},{7,5},{8,10},{9,11},{10,... | collective-permute-start | bytes 503816 | tf_op jit(solution)/shard_map/ppermute | solution.py:180
  22.3 4.2 %collective-permute-start.7 = (bf16[656,128]{1,0:T(8,128)(2,1)S(1)}, bf16[656,128]{1,0:T(8,128)(2,1)S(1)}, u32[]{:S(2)}, u32[]{:S(2)}) collective-permute-start(bf16[656,128]{1,0:T(8,128)(2,1)S(1)} %get-tuple-element.22.refs_0_), channel_id=1, source_target_pairs={{0,1},{1,0},{2,3},{3,2},{4,5},{5,4},{6,7},{7,6},{8,9},{9,8},{10,11... | collective-permute-start | bytes 503816 | tf_op jit(solution)/shard_map/ppermute | solution.py:180
  22.3 4.2 %collective-permute-start.8 = (bf16[656,128]{1,0:T(8,128)(2,1)S(1)}, bf16[656,128]{1,0:T(8,128)(2,1)S(1)}, u32[]{:S(2)}, u32[]{:S(2)}) collective-permute-start(bf16[656,128]{1,0:T(8,128)(2,1)S(1)} %collective-permute-done.refs_1_), channel_id=1, source_target_pairs={{0,1},{1,0},{2,3},{3,2},{4,5},{5,4},{6,7},{7,6},{8,9},{9,8},{10,11... | collective-permute-start | bytes 503816 | tf_op jit(solution)/shard_map/ppermute | solution.py:180
  26.0 1.8 %collective-permute-start.9 = (bf16[656,128]{1,0:T(8,128)(2,1)S(1)}, bf16[656,128]{1,0:T(8,128)(2,1)S(1)}, u32[]{:S(2)}, u32[]{:S(2)}) collective-permute-start(bf16[656,128]{1,0:T(8,128)(2,1)S(1)} %collective-permute-done.3.refs_2_), channel_id=1, source_target_pairs={{0,1},{1,0},{2,3},{3,2},{4,5},{5,4},{6,7},{7,6},{8,9},{9,8},{10,11... | collective-permute-start | bytes 503816 | tf_op jit(solution)/shard_map/ppermute | solution.py:180
  26.0 2.3 %collective-permute-start.10 = (bf16[656,128]{1,0:T(8,128)(2,1)S(1)}, bf16[656,128]{1,0:T(8,128)(2,1)S(1)}, u32[]{:S(2)}, u32[]{:S(2)}) collective-permute-start(bf16[656,128]{1,0:T(8,128)(2,1)S(1)} %collective-permute-done.1.refs_3_), channel_id=1, source_target_pairs={{0,1},{1,0},{2,3},{3,2},{4,5},{5,4},{6,7},{7,6},{8,9},{9,8},{10,11... | collective-permute-start | bytes 503816 | tf_op jit(solution)/shard_map/ppermute | solution.py:180
  26.5 1.8 %collective-permute-start.11 = (bf16[656,128]{1,0:T(8,128)(2,1)S(1)}, bf16[656,128]{1,0:T(8,128)(2,1)S(1)}, u32[]{:S(2)}, u32[]{:S(2)}) collective-permute-start(bf16[656,128]{1,0:T(8,128)(2,1)S(1)} %collective-permute-done.4.refs_4_), channel_id=1, source_target_pairs={{0,1},{1,0},{2,3},{3,2},{4,5},{5,4},{6,7},{7,6},{8,9},{9,8},{10,11... | collective-permute-start | bytes 503816 | tf_op jit(solution)/shard_map/ppermute | solution.py:180
  26.5 1.8 %collective-permute-start.12 = (bf16[656,128]{1,0:T(8,128)(2,1)S(1)}, bf16[656,128]{1,0:T(8,128)(2,1)S(1)}, u32[]{:S(2)}, u32[]{:S(2)}) collective-permute-start(bf16[656,128]{1,0:T(8,128)(2,1)S(1)} %collective-permute-done.2.refs_5_), channel_id=1, source_target_pairs={{0,1},{1,0},{2,3},{3,2},{4,5},{5,4},{6,7},{7,6},{8,9},{9,8},{10,11... | collective-permute-start | bytes 503816 | tf_op jit(solution)/shard_map/ppermute | solution.py:180
  27.8 1.4 %collective-permute-start.13 = (bf16[656,128]{1,0:T(8,128)(2,1)S(1)}, bf16[656,128]{1,0:T(8,128)(2,1)S(1)}, u32[]{:S(2)}, u32[]{:S(2)}) collective-permute-start(bf16[656,128]{1,0:T(8,128)(2,1)S(1)} %collective-permute-done.5.refs_6_), channel_id=1, source_target_pairs={{0,1},{1,0},{2,3},{3,2},{4,5},{5,4},{6,7},{7,6},{8,9},{9,8},{10,11... | collective-permute-start | bytes 503816 | tf_op jit(solution)/shard_map/ppermute | solution.py:180
  27.8 1.6 %collective-permute-start.14 = (bf16[656,128]{1,0:T(8,128)(2,1)S(1)}, bf16[656,128]{1,0:T(8,128)(2,1)S(1)}, u32[]{:S(2)}, u32[]{:S(2)}) collective-permute-start(bf16[656,128]{1,0:T(8,128)(2,1)S(1)} %collective-permute-done.6.refs_7_), channel_id=1, source_target_pairs={{0,1},{1,0},{2,3},{3,2},{4,5},{5,4},{6,7},{7,6},{8,9},{9,8},{10,11... | collective-permute-start | bytes 503816 | tf_op jit(solution)/shard_map/ppermute | solution.py:180

commit v14 on v13

--- a/solution.py
+++ b/solution.py
@@ -136,10 +136,8 @@
             at = pl.ds(d * 2 * SB, 2 * SB)
             half[at, :orbitals] = moved[: 2 * SB]
             half[at, orbitals:] = moved[2 * SB :]
-            left[at, :] = jnp.concatenate([c_all[rows_of(mu_one), mine], c_all[rows_of(mu_two), mine]], 0)
-        part = lax.dot_general(
-            left[...], half[...], (((0,), (0,)), ((), ())), preferred_element_type=jnp.float32
-        )
+            left[:, at] = jnp.concatenate([c_all[rows_of(mu_one), mine], c_all[rows_of(mu_two), mine]], 0).T
+        part = jnp.dot(left[...], half[...], preferred_element_type=jnp.float32)
         for k in range(2):
             for j in range(blocks):
                 at = pl.ds(2 * j + k, LANES, stride=2 * blocks)
@@ -168,7 +166,7 @@
             pltpu.VMEM((devices, LANES), jnp.int32),
             pltpu.SMEM((devices, LANES), jnp.int32),
             pltpu.VMEM((wide, 2 * orbitals), jnp.bfloat16),
-            pltpu.VMEM((wide, LANES), jnp.bfloat16),
+            pltpu.VMEM((LANES, wide), jnp.bfloat16),
             pltpu.SemaphoreType.DMA,
         ],
         compiler_params=pltpu.CompilerParams(vmem_limit_bytes=40 << 20),

time: 33.3 us -> 33.3 us (level)
  no operation moved by 1% of the time
where the time goes in v14:
time: 33.3 us; the launch traced here: 33.1 us
  waiting for transfers between devices  15.8 us (47%)
  starting transfers between devices  11.8 us (35%)
  Pallas kernels  4.85 us (15%)
  between operations  0.68 us (2%)
    ppermute x15, waiting for transfers between devices, flip(): return lax.ppermute(array, axis, [(i, i ^ bit) for i in range(size)])  15.8 us
    ppermute x15, starting transfers between devices, flip(): return lax.ppermute(array, axis, [(i, i ^ bit) for i in range(size)])  11.8 us
    pallas_call x1, Pallas kernels, transform(): pl.pallas_call(functools.partial(transform_kernel, came, n_orb, orbitals,...  3.66 us
    pallas_call x1, Pallas kernels, pack(): pl.pallas_call(functools.partial(pack_kernel, n_pair), out_shape=[pltpu.V...  1.19 us
  transfers between devices with their start and end apart: 15, of which 6 were waited for; matrix products, arithmetic and copies ran while one was open for 0% of the time, Pallas kernels for 0%

profile of v14, /device:TPU:0, one launch (start us, length us, event | category | flops | bytes accessed | tf_op | source)
XLA Modules:
  0.0 33.1 jit_solution(13229037489364537026)
XLA Ops:
  0.7 1.2 %pack.1 = (bf16[656,128]{1,0:T(8,128)(2,1)S(1)}, bf16[656,128]{1,0:T(8,128)(2,1)S(1)}, bf16[656,128]{1,0:T(8,128)(2,1)S(1)}, bf16[656,128]{1,0:T(8,128)(2,1)S(1)}) custom-call(bf16[2,8,4096]{2,1,0:T(8,128)(2,1)} %integrals.1, s32[2]{0:T(128)} %mu.1, s32[2]{0:T(128)} %nu.1, s32[1]{0:T(128)S(6)} %copy.7.counts, bf16[128,512]{1,0:T(8,128)(2,1)} %coeff.1), custom_call_target="tpu_custom_call" | custom-call | tf_op jit(solution)/shard_map/pack/pallas_call | solution.py:71
  1.9 3.1 %collective-permute-start = (bf16[656,128]{1,0:T(8,128)(2,1)S(1)}, bf16[656,128]{1,0:T(8,128)(2,1)S(1)}, u32[]{:S(2)}, u32[]{:S(2)}) collective-permute-start(bf16[656,128]{1,0:T(8,128)(2,1)S(1)} %get-tuple-element.19), channel_id=1, source_target_pairs={{0,4},{4,0},{8,12},{12,8},{1,5},{5,1},{9,13},{13,9},{2,6},{6,2},{1... | collective-permute-start | bytes 503816 | tf_op jit(solution)/shard_map/ppermute | solution.py:178
  4.9 2.6 %collective-permute-start.3 = (bf16[656,128]{1,0:T(8,128)(2,1)S(1)}, bf16[656,128]{1,0:T(8,128)(2,1)S(1)}, u32[]{:S(2)}, u32[]{:S(2)}) collective-permute-start(bf16[656,128]{1,0:T(8,128)(2,1)S(1)} %get-tuple-element.24), channel_id=1, source_target_pairs={{0,8},{4,12},{8,0},{12,4},{1,9},{5,13},{9,1},{13,5},{2,10},{6,14},... | collective-permute-start | bytes 503816 | tf_op jit(solution)/shard_map/ppermute | solution.py:178
  7.5 0.0 collective-permute-start.1
  7.5 4.3 %collective-permute-done.refs_1_ = bf16[656,128]{1,0:T(8,128)(2,1)S(1)} collective-permute-done((bf16[656,128]{1,0:T(8,128)(2,1)S(1)}, bf16[656,128]{1,0:T(8,128)(2,1)S(1)}, u32[]{:S(2)}, u32[]{:S(2)}) %collective-permute-start) | collective-permute-done | bytes 167968 | tf_op jit(solution)/shard_map/ppermute | solution.py:178
  11.8 1.7 %collective-permute-start.2 = (bf16[656,128]{1,0:T(8,128)(2,1)S(1)}, bf16[656,128]{1,0:T(8,128)(2,1)S(1)}, u32[]{:S(2)}, u32[]{:S(2)}) collective-permute-start(bf16[656,128]{1,0:T(8,128)(2,1)S(1)} %collective-permute-done.refs_1_), channel_id=1, source_target_pairs={{0,2},{1,3},{2,0},{3,1},{4,6},{5,7},{6,4},{7,5},{8,10},{9,11},{10,... | collective-permute-start | bytes 503816 | tf_op jit(solution)/shard_map/ppermute | solution.py:178
  13.5 0.3 collective-permute-start.4
  13.8 6.4 %collective-permute-done.3.refs_2_ = bf16[656,128]{1,0:T(8,128)(2,1)S(1)} collective-permute-done((bf16[656,128]{1,0:T(8,128)(2,1)S(1)}, bf16[656,128]{1,0:T(8,128)(2,1)S(1)}, u32[]{:S(2)}, u32[]{:S(2)}) %collective-permute-start.3) | collective-permute-done | bytes 167968 | tf_op jit(solution)/shard_map/ppermute | solution.py:178
  20.3 1.5 %collective-permute-start.5 = (bf16[656,128]{1,0:T(8,128)(2,1)S(1)}, bf16[656,128]{1,0:T(8,128)(2,1)S(1)}, u32[]{:S(2)}, u32[]{:S(2)}) collective-permute-start(bf16[656,128]{1,0:T(8,128)(2,1)S(1)} %collective-permute-done.3.refs_2_), channel_id=1, source_target_pairs={{0,2},{1,3},{2,0},{3,1},{4,6},{5,7},{6,4},{7,5},{8,10},{9,11},{10,... | collective-permute-start | bytes 503816 | tf_op jit(solution)/shard_map/ppermute | solution.py:178
  21.7 0.0 collective-permute-done.1.refs_3_
  21.7 0.0 collective-permute-done.2.refs_5_
  21.7 0.5 %collective-permute-start.6 = (bf16[656,128]{1,0:T(8,128)(2,1)S(1)}, bf16[656,128]{1,0:T(8,128)(2,1)S(1)}, u32[]{:S(2)}, u32[]{:S(2)}) collective-permute-start(bf16[656,128]{1,0:T(8,128)(2,1)S(1)} %collective-permute-done.1.refs_3_), channel_id=1, source_target_pairs={{0,2},{1,3},{2,0},{3,1},{4,6},{5,7},{6,4},{7,5},{8,10},{9,11},{10,... | collective-permute-start | bytes 503816 | tf_op jit(solution)/shard_map/ppermute | solution.py:178
  22.3 0.0 collective-permute-start.7
  22.3 0.5 %collective-permute-start.8 = (bf16[656,128]{1,0:T(8,128)(2,1)S(1)}, bf16[656,128]{1,0:T(8,128)(2,1)S(1)}, u32[]{:S(2)}, u32[]{:S(2)}) collective-permute-start(bf16[656,128]{1,0:T(8,128)(2,1)S(1)} %collective-permute-done.refs_1_), channel_id=1, source_target_pairs={{0,1},{1,0},{2,3},{3,2},{4,5},{5,4},{6,7},{7,6},{8,9},{9,8},{10,11... | collective-permute-start | bytes 503816 | tf_op jit(solution)/shard_map/ppermute | solution.py:178
  22.8 0.0 collective-permute-done.4.refs_4_
  22.8 3.2 %collective-permute-done.5.refs_6_ = bf16[656,128]{1,0:T(8,128)(2,1)S(1)} collective-permute-done((bf16[656,128]{1,0:T(8,128)(2,1)S(1)}, bf16[656,128]{1,0:T(8,128)(2,1)S(1)}, u32[]{:S(2)}, u32[]{:S(2)}) %collective-permute-start.5) | collective-permute-done | bytes 167968 | tf_op jit(solution)/shard_map/ppermute | solution.py:178
  26.0 0.0 collective-permute-start.9
  26.0 0.5 %collective-permute-start.10 = (bf16[656,128]{1,0:T(8,128)(2,1)S(1)}, bf16[656,128]{1,0:T(8,128)(2,1)S(1)}, u32[]{:S(2)}, u32[]{:S(2)}) collective-permute-start(bf16[656,128]{1,0:T(8,128)(2,1)S(1)} %collective-permute-done.1.refs_3_), channel_id=1, source_target_pairs={{0,1},{1,0},{2,3},{3,2},{4,5},{5,4},{6,7},{7,6},{8,9},{9,8},{10,11... | collective-permute-start | bytes 503816 | tf_op jit(solution)/shard_map/ppermute | solution.py:178
  26.5 0.0 collective-permute-done.7.refs_8_
  26.5 0.0 collective-permute-start.11
  26.5 0.0 collective-permute-done.8.refs_9_
  26.5 0.5 %collective-permute-start.12 = (bf16[656,128]{1,0:T(8,128)(2,1)S(1)}, bf16[656,128]{1,0:T(8,128)(2,1)S(1)}, u32[]{:S(2)}, u32[]{:S(2)}) collective-permute-start(bf16[656,128]{1,0:T(8,128)(2,1)S(1)} %collective-permute-done.2.refs_5_), channel_id=1, source_target_pairs={{0,1},{1,0},{2,3},{3,2},{4,5},{5,4},{6,7},{7,6},{8,9},{9,8},{10,11... | collective-permute-start | bytes 503816 | tf_op jit(solution)/shard_map/ppermute | solution.py:178
  27.0 0.8 %collective-permute-done.6.refs_7_ = bf16[656,128]{1,0:T(8,128)(2,1)S(1)} collective-permute-done((bf16[656,128]{1,0:T(8,128)(2,1)S(1)}, bf16[656,128]{1,0:T(8,128)(2,1)S(1)}, u32[]{:S(2)}, u32[]{:S(2)}) %collective-permute-start.6) | collective-permute-done | bytes 167968 | tf_op jit(solution)/shard_map/ppermute | solution.py:178
  27.8 0.0 collective-permute-start.13
  27.8 0.0 collective-permute-done.9.refs_10_
  27.8 0.5 %collective-permute-start.14 = (bf16[656,128]{1,0:T(8,128)(2,1)S(1)}, bf16[656,128]{1,0:T(8,128)(2,1)S(1)}, u32[]{:S(2)}, u32[]{:S(2)}) collective-permute-start(bf16[656,128]{1,0:T(8,128)(2,1)S(1)} %collective-permute-done.6.refs_7_), channel_id=1, source_target_pairs={{0,1},{1,0},{2,3},{3,2},{4,5},{5,4},{6,7},{7,6},{8,9},{9,8},{10,11... | collective-permute-start | bytes 503816 | tf_op jit(solution)/shard_map/ppermute | solution.py:178
  28.3 0.0 collective-permute-done.10.refs_11_
  28.3 0.0 collective-permute-done.11.refs_12_
  28.3 0.0 collective-permute-done.12.refs_13_
  28.3 0.9 %collective-permute-done.13.refs_14_ = bf16[656,128]{1,0:T(8,128)(2,1)S(1)} collective-permute-done((bf16[656,128]{1,0:T(8,128)(2,1)S(1)}, bf16[656,128]{1,0:T(8,128)(2,1)S(1)}, u32[]{:S(2)}, u32[]{:S(2)}) %collective-permute-start.13) | collective-permute-done | bytes 167968 | tf_op jit(solution)/shard_map/ppermute | solution.py:178
  29.2 0.2 collective-permute-done.14.refs_15_
  29.5 3.7 %transform.1 = f32[1024,128]{1,0:T(8,128)} custom-call(bf16[656,128]{1,0:T(8,128)(2,1)S(1)} %get-tuple-element.22.refs_0_, bf16[656,128]{1,0:T(8,128)(2,1)S(1)} %collective-permute-done.refs_1_, bf16[656,128]{1,0:T(8,128)(2,1)S(1)} %collective-permute-done.3.refs_2_, bf16[656,128]{1,0:T(8,128)(2,1)S(1)} %collective-permute-done.1.refs_3_, ...), custom_call_target="tpu_custom_call" | custom-call | tf_op jit(solution)/shard_map/transform/pallas_call | solution.py:159
Async XLA Ops:
  1.9 10.0 %collective-permute-start = (bf16[656,128]{1,0:T(8,128)(2,1)S(1)}, bf16[656,128]{1,0:T(8,128)(2,1)S(1)}, u32[]{:S(2)}, u32[]{:S(2)}) collective-permute-start(bf16[656,128]{1,0:T(8,128)(2,1)S(1)} %get-tuple-element.19), channel_id=1, source_target_pairs={{0,4},{4,0},{8,12},{12,8},{1,5},{5,1},{9,13},{13,9},{2,6},{6,2},{1... | collective-permute-start | bytes 503816 | tf_op jit(solution)/shard_map/ppermute | solution.py:178
  4.9 15.3 %collective-permute-start.3 = (bf16[656,128]{1,0:T(8,128)(2,1)S(1)}, bf16[656,128]{1,0:T(8,128)(2,1)S(1)}, u32[]{:S(2)}, u32[]{:S(2)}) collective-permute-start(bf16[656,128]{1,0:T(8,128)(2,1)S(1)} %get-tuple-element.24), channel_id=1, source_target_pairs={{0,8},{4,12},{8,0},{12,4},{1,9},{5,13},{9,1},{13,5},{2,10},{6,14},... | collective-permute-start | bytes 503816 | tf_op jit(solution)/shard_map/ppermute | solution.py:178
  7.5 14.2 %collective-permute-start.1 = (bf16[656,128]{1,0:T(8,128)(2,1)S(1)}, bf16[656,128]{1,0:T(8,128)(2,1)S(1)}, u32[]{:S(2)}, u32[]{:S(2)}) collective-permute-start(bf16[656,128]{1,0:T(8,128)(2,1)S(1)} %get-tuple-element.20), channel_id=1, source_target_pairs={{0,12},{4,8},{8,4},{12,0},{1,13},{5,9},{9,5},{13,1},{2,14},{6,10},... | collective-permute-start | bytes 503816 | tf_op jit(solution)/shard_map/ppermute | solution.py:178
  11.8 9.9 %collective-permute-start.2 = (bf16[656,128]{1,0:T(8,128)(2,1)S(1)}, bf16[656,128]{1,0:T(8,128)(2,1)S(1)}, u32[]{:S(2)}, u32[]{:S(2)}) collective-permute-start(bf16[656,128]{1,0:T(8,128)(2,1)S(1)} %collective-permute-done.refs_1_), channel_id=1, source_target_pairs={{0,2},{1,3},{2,0},{3,1},{4,6},{5,7},{6,4},{7,5},{8,10},{9,11},{10,... | collective-permute-start | bytes 503816 | tf_op jit(solution)/shard_map/ppermute | solution.py:178
  13.5 9.3 %collective-permute-start.4 = (bf16[656,128]{1,0:T(8,128)(2,1)S(1)}, bf16[656,128]{1,0:T(8,128)(2,1)S(1)}, u32[]{:S(2)}, u32[]{:S(2)}) collective-permute-start(bf16[656,128]{1,0:T(8,128)(2,1)S(1)} %get-tuple-element.22.refs_0_), channel_id=1, source_target_pairs={{0,2},{1,3},{2,0},{3,1},{4,6},{5,7},{6,4},{7,5},{8,10},{9,11},{10,... | collective-permute-start | bytes 503816 | tf_op jit(solution)/shard_map/ppermute | solution.py:178
  20.3 5.8 %collective-permute-start.5 = (bf16[656,128]{1,0:T(8,128)(2,1)S(1)}, bf16[656,128]{1,0:T(8,128)(2,1)S(1)}, u32[]{:S(2)}, u32[]{:S(2)}) collective-permute-start(bf16[656,128]{1,0:T(8,128)(2,1)S(1)} %collective-permute-done.3.refs_2_), channel_id=1, source_target_pairs={{0,2},{1,3},{2,0},{3,1},{4,6},{5,7},{6,4},{7,5},{8,10},{9,11},{10,... | collective-permute-start | bytes 503816 | tf_op jit(solution)/shard_map/ppermute | solution.py:178
  21.7 6.1 %collective-permute-start.6 = (bf16[656,128]{1,0:T(8,128)(2,1)S(1)}, bf16[656,128]{1,0:T(8,128)(2,1)S(1)}, u32[]{:S(2)}, u32[]{:S(2)}) collective-permute-start(bf16[656,128]{1,0:T(8,128)(2,1)S(1)} %collective-permute-done.1.refs_3_), channel_id=1, source_target_pairs={{0,2},{1,3},{2,0},{3,1},{4,6},{5,7},{6,4},{7,5},{8,10},{9,11},{10,... | collective-permute-start | bytes 503816 | tf_op jit(solution)/shard_map/ppermute | solution.py:178
  22.3 4.2 %collective-permute-start.7 = (bf16[656,128]{1,0:T(8,128)(2,1)S(1)}, bf16[656,128]{1,0:T(8,128)(2,1)S(1)}, u32[]{:S(2)}, u32[]{:S(2)}) collective-permute-start(bf16[656,128]{1,0:T(8,128)(2,1)S(1)} %get-tuple-element.22.refs_0_), channel_id=1, source_target_pairs={{0,1},{1,0},{2,3},{3,2},{4,5},{5,4},{6,7},{7,6},{8,9},{9,8},{10,11... | collective-permute-start | bytes 503816 | tf_op jit(solution)/shard_map/ppermute | solution.py:178
  22.3 4.2 %collective-permute-start.8 = (bf16[656,128]{1,0:T(8,128)(2,1)S(1)}, bf16[656,128]{1,0:T(8,128)(2,1)S(1)}, u32[]{:S(2)}, u32[]{:S(2)}) collective-permute-start(bf16[656,128]{1,0:T(8,128)(2,1)S(1)} %collective-permute-done.refs_1_), channel_id=1, source_target_pairs={{0,1},{1,0},{2,3},{3,2},{4,5},{5,4},{6,7},{7,6},{8,9},{9,8},{10,11... | collective-permute-start | bytes 503816 | tf_op jit(solution)/shard_map/ppermute | solution.py:178
  26.0 1.8 %collective-permute-start.9 = (bf16[656,128]{1,0:T(8,128)(2,1)S(1)}, bf16[656,128]{1,0:T(8,128)(2,1)S(1)}, u32[]{:S(2)}, u32[]{:S(2)}) collective-permute-start(bf16[656,128]{1,0:T(8,128)(2,1)S(1)} %collective-permute-done.3.refs_2_), channel_id=1, source_target_pairs={{0,1},{1,0},{2,3},{3,2},{4,5},{5,4},{6,7},{7,6},{8,9},{9,8},{10,11... | collective-permute-start | bytes 503816 | tf_op jit(solution)/shard_map/ppermute | solution.py:178
  26.0 2.3 %collective-permute-start.10 = (bf16[656,128]{1,0:T(8,128)(2,1)S(1)}, bf16[656,128]{1,0:T(8,128)(2,1)S(1)}, u32[]{:S(2)}, u32[]{:S(2)}) collective-permute-start(bf16[656,128]{1,0:T(8,128)(2,1)S(1)} %collective-permute-done.1.refs_3_), channel_id=1, source_target_pairs={{0,1},{1,0},{2,3},{3,2},{4,5},{5,4},{6,7},{7,6},{8,9},{9,8},{10,11... | collective-permute-start | bytes 503816 | tf_op jit(solution)/shard_map/ppermute | solution.py:178
  26.5 1.8 %collective-permute-start.11 = (bf16[656,128]{1,0:T(8,128)(2,1)S(1)}, bf16[656,128]{1,0:T(8,128)(2,1)S(1)}, u32[]{:S(2)}, u32[]{:S(2)}) collective-permute-start(bf16[656,128]{1,0:T(8,128)(2,1)S(1)} %collective-permute-done.4.refs_4_), channel_id=1, source_target_pairs={{0,1},{1,0},{2,3},{3,2},{4,5},{5,4},{6,7},{7,6},{8,9},{9,8},{10,11... | collective-permute-start | bytes 503816 | tf_op jit(solution)/shard_map/ppermute | solution.py:178
  26.5 1.8 %collective-permute-start.12 = (bf16[656,128]{1,0:T(8,128)(2,1)S(1)}, bf16[656,128]{1,0:T(8,128)(2,1)S(1)}, u32[]{:S(2)}, u32[]{:S(2)}) collective-permute-start(bf16[656,128]{1,0:T(8,128)(2,1)S(1)} %collective-permute-done.2.refs_5_), channel_id=1, source_target_pairs={{0,1},{1,0},{2,3},{3,2},{4,5},{5,4},{6,7},{7,6},{8,9},{9,8},{10,11... | collective-permute-start | bytes 503816 | tf_op jit(solution)/shard_map/ppermute | solution.py:178
  27.8 1.4 %collective-permute-start.13 = (bf16[656,128]{1,0:T(8,128)(2,1)S(1)}, bf16[656,128]{1,0:T(8,128)(2,1)S(1)}, u32[]{:S(2)}, u32[]{:S(2)}) collective-permute-start(bf16[656,128]{1,0:T(8,128)(2,1)S(1)} %collective-permute-done.5.refs_6_), channel_id=1, source_target_pairs={{0,1},{1,0},{2,3},{3,2},{4,5},{5,4},{6,7},{7,6},{8,9},{9,8},{10,11... | collective-permute-start | bytes 503816 | tf_op jit(solution)/shard_map/ppermute | solution.py:178
  27.8 1.6 %collective-permute-start.14 = (bf16[656,128]{1,0:T(8,128)(2,1)S(1)}, bf16[656,128]{1,0:T(8,128)(2,1)S(1)}, u32[]{:S(2)}, u32[]{:S(2)}) collective-permute-start(bf16[656,128]{1,0:T(8,128)(2,1)S(1)} %collective-permute-done.6.refs_7_), channel_id=1, source_target_pairs={{0,1},{1,0},{2,3},{3,2},{4,5},{5,4},{6,7},{7,6},{8,9},{9,8},{10,11... | collective-permute-start | bytes 503816 | tf_op jit(solution)/shard_map/ppermute | solution.py:178

commit v15 on v14

--- a/solution.py
+++ b/solution.py
@@ -10,6 +10,7 @@
 SB = 64
 LANES = 128
 TAG = 16
+PARTS = 8
 CHUNK = 16
 
 
@@ -17,17 +18,21 @@
     outs = refs[:n_pair]
     tiles, shard, mu_in, nu_in, spread, woven, sems = refs[n_pair:]
     p = lax.axis_index("pair")
-    copies = [
-        pltpu.make_async_copy(source, target, sems.at[n])
-        for n, (source, target) in enumerate(((integrals, tiles), (mu, mu_in), (nu, nu_in), (coeff, shard)))
-    ]
+    slots, kets, flat = tiles.shape
+    ends = [(mu, mu_in), (nu, nu_in)]
+    for n in range(PARTS):
+        lanes = pl.ds(n * (flat // PARTS), flat // PARTS)
+        ends.append((integrals.at[:, :, lanes], tiles.at[:, :, lanes]))
+    for n in range(PARTS):
+        part = pl.ds(n * (shard.shape[0] // PARTS), shard.shape[0] // PARTS)
+        ends.append((coeff.at[part], shard.at[part]))
+    copies = [pltpu.make_async_copy(source, target, sems.at[n]) for n, (source, target) in enumerate(ends)]
     for copy in copies:
         copy.start()
-    slots, kets, flat = tiles.shape
     wide = flat // LANES
     columns = kets // n_pair
     held, orbitals = shard.shape
-    for copy in copies[1:3]:
+    for copy in copies[:2]:
         copy.wait()
     count = counts[0]
     lane = lax.broadcasted_iota(jnp.int32, (wide, LANES), 1)
@@ -38,9 +43,10 @@
         tag = jnp.where((lane == 2 * t) & (t < count), mu_in[t], tag)
         tag = jnp.where((lane == 2 * t + 1) & (t < count), nu_in[t], tag)
     tag = tag.astype(jnp.float32).astype(jnp.bfloat16)
-    copies[0].wait()
-    for t in range(slots):
-        for j in range(wide):
+    for j in range(wide):
+        if j % (wide // PARTS) == 0:
+            copies[2 + j // (wide // PARTS)].wait()
+        for t in range(slots):
             at = pl.ds((t * wide + j) * kets, kets)
             spread[at, :] = tiles[t, :, j * LANES : (j + 1) * LANES].astype(jnp.float32)
     tile_at, rows = orbitals // LANES * held, columns * SB
@@ -57,7 +63,8 @@
             woven[pl.ds(begin + 1, wide, stride=2), :] = jnp.where(kept, odd, 0.0)
         outs[s][tile_at : tile_at + rows] = woven[pl.ds(s * rows, rows), :].astype(jnp.bfloat16)
         outs[s][tile_at + rows :] = tag
-    copies[3].wait()
+    for copy in copies[2 + PARTS :]:
+        copy.wait()
     for j in range(orbitals // LANES):
         lanes = shard[:, j * LANES : (j + 1) * LANES]
         for s in range(n_pair):
@@ -80,7 +87,7 @@
             pltpu.SMEM(nu.shape, jnp.int32),
             pltpu.VMEM((slots * kets * flat // LANES, LANES), jnp.float32),
             pltpu.VMEM((kets * SB, LANES), jnp.float32),
-            pltpu.SemaphoreType.DMA((4,)),
+            pltpu.SemaphoreType.DMA((2 + 2 * PARTS,)),
         ],
         compiler_params=pltpu.CompilerParams(vmem_limit_bytes=56 << 20),
         name="pack",

time: 33.3 us -> 33.4 us (level)
  no operation moved by 1% of the time
where the time goes in v15:
time: 33.4 us; the launch traced here: 33.2 us
  waiting for transfers between devices  15.8 us (47%)
  starting transfers between devices  11.8 us (35%)
  Pallas kernels  4.92 us (15%)
  between operations  0.68 us (2%)
    ppermute x15, waiting for transfers between devices, flip(): return lax.ppermute(array, axis, [(i, i ^ bit) for i in range(size)])  15.8 us
    ppermute x15, starting transfers between devices, flip(): return lax.ppermute(array, axis, [(i, i ^ bit) for i in range(size)])  11.8 us
    pallas_call x1, Pallas kernels, transform(): pl.pallas_call(functools.partial(transform_kernel, came, n_orb, orbitals,...  3.66 us
    pallas_call x1, Pallas kernels, pack(): pl.pallas_call(functools.partial(pack_kernel, n_pair), out_shape=[pltpu.V...  1.26 us
  transfers between devices with their start and end apart: 15, of which 6 were waited for; matrix products, arithmetic and copies ran while one was open for 0% of the time, Pallas kernels for 0%

profile of v15, /device:TPU:0, one launch (start us, length us, event | category | flops | bytes accessed | tf_op | source)
XLA Modules:
  0.0 33.2 jit_solution(12374174264110253164)
XLA Ops:
  0.7 1.3 %pack.1 = (bf16[656,128]{1,0:T(8,128)(2,1)S(1)}, bf16[656,128]{1,0:T(8,128)(2,1)S(1)}, bf16[656,128]{1,0:T(8,128)(2,1)S(1)}, bf16[656,128]{1,0:T(8,128)(2,1)S(1)}) custom-call(bf16[2,8,4096]{2,1,0:T(8,128)(2,1)} %integrals.1, s32[2]{0:T(128)} %mu.1, s32[2]{0:T(128)} %nu.1, s32[1]{0:T(128)S(6)} %copy.7.counts, bf16[128,512]{1,0:T(8,128)(2,1)} %coeff.1), custom_call_target="tpu_custom_call" | custom-call | tf_op jit(solution)/shard_map/pack/pallas_call | solution.py:78
  1.9 3.1 %collective-permute-start = (bf16[656,128]{1,0:T(8,128)(2,1)S(1)}, bf16[656,128]{1,0:T(8,128)(2,1)S(1)}, u32[]{:S(2)}, u32[]{:S(2)}) collective-permute-start(bf16[656,128]{1,0:T(8,128)(2,1)S(1)} %get-tuple-element.19), channel_id=1, source_target_pairs={{0,4},{4,0},{8,12},{12,8},{1,5},{5,1},{9,13},{13,9},{2,6},{6,2},{1... | collective-permute-start | bytes 503816 | tf_op jit(solution)/shard_map/ppermute | solution.py:185
  5.0 2.6 %collective-permute-start.3 = (bf16[656,128]{1,0:T(8,128)(2,1)S(1)}, bf16[656,128]{1,0:T(8,128)(2,1)S(1)}, u32[]{:S(2)}, u32[]{:S(2)}) collective-permute-start(bf16[656,128]{1,0:T(8,128)(2,1)S(1)} %get-tuple-element.24), channel_id=1, source_target_pairs={{0,8},{4,12},{8,0},{12,4},{1,9},{5,13},{9,1},{13,5},{2,10},{6,14},... | collective-permute-start | bytes 503816 | tf_op jit(solution)/shard_map/ppermute | solution.py:185
  7.6 0.0 collective-permute-start.1
  7.6 4.3 %collective-permute-done.refs_1_ = bf16[656,128]{1,0:T(8,128)(2,1)S(1)} collective-permute-done((bf16[656,128]{1,0:T(8,128)(2,1)S(1)}, bf16[656,128]{1,0:T(8,128)(2,1)S(1)}, u32[]{:S(2)}, u32[]{:S(2)}) %collective-permute-start) | collective-permute-done | bytes 167968 | tf_op jit(solution)/shard_map/ppermute | solution.py:185
  11.9 1.7 %collective-permute-start.2 = (bf16[656,128]{1,0:T(8,128)(2,1)S(1)}, bf16[656,128]{1,0:T(8,128)(2,1)S(1)}, u32[]{:S(2)}, u32[]{:S(2)}) collective-permute-start(bf16[656,128]{1,0:T(8,128)(2,1)S(1)} %collective-permute-done.refs_1_), channel_id=1, source_target_pairs={{0,2},{1,3},{2,0},{3,1},{4,6},{5,7},{6,4},{7,5},{8,10},{9,11},{10,... | collective-permute-start | bytes 503816 | tf_op jit(solution)/shard_map/ppermute | solution.py:185
  13.6 0.3 collective-permute-start.4
  13.9 6.4 %collective-permute-done.3.refs_2_ = bf16[656,128]{1,0:T(8,128)(2,1)S(1)} collective-permute-done((bf16[656,128]{1,0:T(8,128)(2,1)S(1)}, bf16[656,128]{1,0:T(8,128)(2,1)S(1)}, u32[]{:S(2)}, u32[]{:S(2)}) %collective-permute-start.3) | collective-permute-done | bytes 167968 | tf_op jit(solution)/shard_map/ppermute | solution.py:185
  20.3 1.5 %collective-permute-start.5 = (bf16[656,128]{1,0:T(8,128)(2,1)S(1)}, bf16[656,128]{1,0:T(8,128)(2,1)S(1)}, u32[]{:S(2)}, u32[]{:S(2)}) collective-permute-start(bf16[656,128]{1,0:T(8,128)(2,1)S(1)} %collective-permute-done.3.refs_2_), channel_id=1, source_target_pairs={{0,2},{1,3},{2,0},{3,1},{4,6},{5,7},{6,4},{7,5},{8,10},{9,11},{10,... | collective-permute-start | bytes 503816 | tf_op jit(solution)/shard_map/ppermute | solution.py:185
  21.8 0.0 collective-permute-done.1.refs_3_
  21.8 0.0 collective-permute-done.2.refs_5_
  21.8 0.5 %collective-permute-start.6 = (bf16[656,128]{1,0:T(8,128)(2,1)S(1)}, bf16[656,128]{1,0:T(8,128)(2,1)S(1)}, u32[]{:S(2)}, u32[]{:S(2)}) collective-permute-start(bf16[656,128]{1,0:T(8,128)(2,1)S(1)} %collective-permute-done.1.refs_3_), channel_id=1, source_target_pairs={{0,2},{1,3},{2,0},{3,1},{4,6},{5,7},{6,4},{7,5},{8,10},{9,11},{10,... | collective-permute-start | bytes 503816 | tf_op jit(solution)/shard_map/ppermute | solution.py:185
  22.4 0.0 collective-permute-start.7
  22.4 0.5 %collective-permute-start.8 = (bf16[656,128]{1,0:T(8,128)(2,1)S(1)}, bf16[656,128]{1,0:T(8,128)(2,1)S(1)}, u32[]{:S(2)}, u32[]{:S(2)}) collective-permute-start(bf16[656,128]{1,0:T(8,128)(2,1)S(1)} %collective-permute-done.refs_1_), channel_id=1, source_target_pairs={{0,1},{1,0},{2,3},{3,2},{4,5},{5,4},{6,7},{7,6},{8,9},{9,8},{10,11... | collective-permute-start | bytes 503816 | tf_op jit(solution)/shard_map/ppermute | solution.py:185
  22.9 0.0 collective-permute-done.4.refs_4_
  22.9 3.2 %collective-permute-done.5.refs_6_ = bf16[656,128]{1,0:T(8,128)(2,1)S(1)} collective-permute-done((bf16[656,128]{1,0:T(8,128)(2,1)S(1)}, bf16[656,128]{1,0:T(8,128)(2,1)S(1)}, u32[]{:S(2)}, u32[]{:S(2)}) %collective-permute-start.5) | collective-permute-done | bytes 167968 | tf_op jit(solution)/shard_map/ppermute | solution.py:185
  26.1 0.0 collective-permute-start.9
  26.1 0.5 %collective-permute-start.10 = (bf16[656,128]{1,0:T(8,128)(2,1)S(1)}, bf16[656,128]{1,0:T(8,128)(2,1)S(1)}, u32[]{:S(2)}, u32[]{:S(2)}) collective-permute-start(bf16[656,128]{1,0:T(8,128)(2,1)S(1)} %collective-permute-done.1.refs_3_), channel_id=1, source_target_pairs={{0,1},{1,0},{2,3},{3,2},{4,5},{5,4},{6,7},{7,6},{8,9},{9,8},{10,11... | collective-permute-start | bytes 503816 | tf_op jit(solution)/shard_map/ppermute | solution.py:185
  26.6 0.0 collective-permute-done.7.refs_8_
  26.6 0.0 collective-permute-start.11
  26.6 0.0 collective-permute-done.8.refs_9_
  26.6 0.5 %collective-permute-start.12 = (bf16[656,128]{1,0:T(8,128)(2,1)S(1)}, bf16[656,128]{1,0:T(8,128)(2,1)S(1)}, u32[]{:S(2)}, u32[]{:S(2)}) collective-permute-start(bf16[656,128]{1,0:T(8,128)(2,1)S(1)} %collective-permute-done.2.refs_5_), channel_id=1, source_target_pairs={{0,1},{1,0},{2,3},{3,2},{4,5},{5,4},{6,7},{7,6},{8,9},{9,8},{10,11... | collective-permute-start | bytes 503816 | tf_op jit(solution)/shard_map/ppermute | solution.py:185
  27.1 0.8 %collective-permute-done.6.refs_7_ = bf16[656,128]{1,0:T(8,128)(2,1)S(1)} collective-permute-done((bf16[656,128]{1,0:T(8,128)(2,1)S(1)}, bf16[656,128]{1,0:T(8,128)(2,1)S(1)}, u32[]{:S(2)}, u32[]{:S(2)}) %collective-permute-start.6) | collective-permute-done | bytes 167968 | tf_op jit(solution)/shard_map/ppermute | solution.py:185
  27.9 0.0 collective-permute-start.13
  27.9 0.0 collective-permute-done.9.refs_10_
  27.9 0.5 %collective-permute-start.14 = (bf16[656,128]{1,0:T(8,128)(2,1)S(1)}, bf16[656,128]{1,0:T(8,128)(2,1)S(1)}, u32[]{:S(2)}, u32[]{:S(2)}) collective-permute-start(bf16[656,128]{1,0:T(8,128)(2,1)S(1)} %collective-permute-done.6.refs_7_), channel_id=1, source_target_pairs={{0,1},{1,0},{2,3},{3,2},{4,5},{5,4},{6,7},{7,6},{8,9},{9,8},{10,11... | collective-permute-start | bytes 503816 | tf_op jit(solution)/shard_map/ppermute | solution.py:185
  28.4 0.0 collective-permute-done.10.refs_11_
  28.4 0.0 collective-permute-done.11.refs_12_
  28.4 0.0 collective-permute-done.12.refs_13_
  28.4 0.9 %collective-permute-done.13.refs_14_ = bf16[656,128]{1,0:T(8,128)(2,1)S(1)} collective-permute-done((bf16[656,128]{1,0:T(8,128)(2,1)S(1)}, bf16[656,128]{1,0:T(8,128)(2,1)S(1)}, u32[]{:S(2)}, u32[]{:S(2)}) %collective-permute-start.13) | collective-permute-done | bytes 167968 | tf_op jit(solution)/shard_map/ppermute | solution.py:185
  29.3 0.2 collective-permute-done.14.refs_15_
  29.5 3.7 %transform.1 = f32[1024,128]{1,0:T(8,128)} custom-call(bf16[656,128]{1,0:T(8,128)(2,1)S(1)} %get-tuple-element.22.refs_0_, bf16[656,128]{1,0:T(8,128)(2,1)S(1)} %collective-permute-done.refs_1_, bf16[656,128]{1,0:T(8,128)(2,1)S(1)} %collective-permute-done.3.refs_2_, bf16[656,128]{1,0:T(8,128)(2,1)S(1)} %collective-permute-done.1.refs_3_, ...), custom_call_target="tpu_custom_call" | custom-call | tf_op jit(solution)/shard_map/transform/pallas_call | solution.py:166
Async XLA Ops:
  1.9 10.0 %collective-permute-start = (bf16[656,128]{1,0:T(8,128)(2,1)S(1)}, bf16[656,128]{1,0:T(8,128)(2,1)S(1)}, u32[]{:S(2)}, u32[]{:S(2)}) collective-permute-start(bf16[656,128]{1,0:T(8,128)(2,1)S(1)} %get-tuple-element.19), channel_id=1, source_target_pairs={{0,4},{4,0},{8,12},{12,8},{1,5},{5,1},{9,13},{13,9},{2,6},{6,2},{1... | collective-permute-start | bytes 503816 | tf_op jit(solution)/shard_map/ppermute | solution.py:185
  5.0 15.3 %collective-permute-start.3 = (bf16[656,128]{1,0:T(8,128)(2,1)S(1)}, bf16[656,128]{1,0:T(8,128)(2,1)S(1)}, u32[]{:S(2)}, u32[]{:S(2)}) collective-permute-start(bf16[656,128]{1,0:T(8,128)(2,1)S(1)} %get-tuple-element.24), channel_id=1, source_target_pairs={{0,8},{4,12},{8,0},{12,4},{1,9},{5,13},{9,1},{13,5},{2,10},{6,14},... | collective-permute-start | bytes 503816 | tf_op jit(solution)/shard_map/ppermute | solution.py:185
  7.6 14.2 %collective-permute-start.1 = (bf16[656,128]{1,0:T(8,128)(2,1)S(1)}, bf16[656,128]{1,0:T(8,128)(2,1)S(1)}, u32[]{:S(2)}, u32[]{:S(2)}) collective-permute-start(bf16[656,128]{1,0:T(8,128)(2,1)S(1)} %get-tuple-element.20), channel_id=1, source_target_pairs={{0,12},{4,8},{8,4},{12,0},{1,13},{5,9},{9,5},{13,1},{2,14},{6,10},... | collective-permute-start | bytes 503816 | tf_op jit(solution)/shard_map/ppermute | solution.py:185
  11.9 9.9 %collective-permute-start.2 = (bf16[656,128]{1,0:T(8,128)(2,1)S(1)}, bf16[656,128]{1,0:T(8,128)(2,1)S(1)}, u32[]{:S(2)}, u32[]{:S(2)}) collective-permute-start(bf16[656,128]{1,0:T(8,128)(2,1)S(1)} %collective-permute-done.refs_1_), channel_id=1, source_target_pairs={{0,2},{1,3},{2,0},{3,1},{4,6},{5,7},{6,4},{7,5},{8,10},{9,11},{10,... | collective-permute-start | bytes 503816 | tf_op jit(solution)/shard_map/ppermute | solution.py:185
  13.6 9.3 %collective-permute-start.4 = (bf16[656,128]{1,0:T(8,128)(2,1)S(1)}, bf16[656,128]{1,0:T(8,128)(2,1)S(1)}, u32[]{:S(2)}, u32[]{:S(2)}) collective-permute-start(bf16[656,128]{1,0:T(8,128)(2,1)S(1)} %get-tuple-element.22.refs_0_), channel_id=1, source_target_pairs={{0,2},{1,3},{2,0},{3,1},{4,6},{5,7},{6,4},{7,5},{8,10},{9,11},{10,... | collective-permute-start | bytes 503816 | tf_op jit(solution)/shard_map/ppermute | solution.py:185
  20.3 5.8 %collective-permute-start.5 = (bf16[656,128]{1,0:T(8,128)(2,1)S(1)}, bf16[656,128]{1,0:T(8,128)(2,1)S(1)}, u32[]{:S(2)}, u32[]{:S(2)}) collective-permute-start(bf16[656,128]{1,0:T(8,128)(2,1)S(1)} %collective-permute-done.3.refs_2_), channel_id=1, source_target_pairs={{0,2},{1,3},{2,0},{3,1},{4,6},{5,7},{6,4},{7,5},{8,10},{9,11},{10,... | collective-permute-start | bytes 503816 | tf_op jit(solution)/shard_map/ppermute | solution.py:185
  21.8 6.1 %collective-permute-start.6 = (bf16[656,128]{1,0:T(8,128)(2,1)S(1)}, bf16[656,128]{1,0:T(8,128)(2,1)S(1)}, u32[]{:S(2)}, u32[]{:S(2)}) collective-permute-start(bf16[656,128]{1,0:T(8,128)(2,1)S(1)} %collective-permute-done.1.refs_3_), channel_id=1, source_target_pairs={{0,2},{1,3},{2,0},{3,1},{4,6},{5,7},{6,4},{7,5},{8,10},{9,11},{10,... | collective-permute-start | bytes 503816 | tf_op jit(solution)/shard_map/ppermute | solution.py:185
  22.4 4.2 %collective-permute-start.7 = (bf16[656,128]{1,0:T(8,128)(2,1)S(1)}, bf16[656,128]{1,0:T(8,128)(2,1)S(1)}, u32[]{:S(2)}, u32[]{:S(2)}) collective-permute-start(bf16[656,128]{1,0:T(8,128)(2,1)S(1)} %get-tuple-element.22.refs_0_), channel_id=1, source_target_pairs={{0,1},{1,0},{2,3},{3,2},{4,5},{5,4},{6,7},{7,6},{8,9},{9,8},{10,11... | collective-permute-start | bytes 503816 | tf_op jit(solution)/shard_map/ppermute | solution.py:185
  22.4 4.2 %collective-permute-start.8 = (bf16[656,128]{1,0:T(8,128)(2,1)S(1)}, bf16[656,128]{1,0:T(8,128)(2,1)S(1)}, u32[]{:S(2)}, u32[]{:S(2)}) collective-permute-start(bf16[656,128]{1,0:T(8,128)(2,1)S(1)} %collective-permute-done.refs_1_), channel_id=1, source_target_pairs={{0,1},{1,0},{2,3},{3,2},{4,5},{5,4},{6,7},{7,6},{8,9},{9,8},{10,11... | collective-permute-start | bytes 503816 | tf_op jit(solution)/shard_map/ppermute | solution.py:185
  26.1 1.8 %collective-permute-start.9 = (bf16[656,128]{1,0:T(8,128)(2,1)S(1)}, bf16[656,128]{1,0:T(8,128)(2,1)S(1)}, u32[]{:S(2)}, u32[]{:S(2)}) collective-permute-start(bf16[656,128]{1,0:T(8,128)(2,1)S(1)} %collective-permute-done.3.refs_2_), channel_id=1, source_target_pairs={{0,1},{1,0},{2,3},{3,2},{4,5},{5,4},{6,7},{7,6},{8,9},{9,8},{10,11... | collective-permute-start | bytes 503816 | tf_op jit(solution)/shard_map/ppermute | solution.py:185
  26.1 2.3 %collective-permute-start.10 = (bf16[656,128]{1,0:T(8,128)(2,1)S(1)}, bf16[656,128]{1,0:T(8,128)(2,1)S(1)}, u32[]{:S(2)}, u32[]{:S(2)}) collective-permute-start(bf16[656,128]{1,0:T(8,128)(2,1)S(1)} %collective-permute-done.1.refs_3_), channel_id=1, source_target_pairs={{0,1},{1,0},{2,3},{3,2},{4,5},{5,4},{6,7},{7,6},{8,9},{9,8},{10,11... | collective-permute-start | bytes 503816 | tf_op jit(solution)/shard_map/ppermute | solution.py:185
  26.6 1.8 %collective-permute-start.11 = (bf16[656,128]{1,0:T(8,128)(2,1)S(1)}, bf16[656,128]{1,0:T(8,128)(2,1)S(1)}, u32[]{:S(2)}, u32[]{:S(2)}) collective-permute-start(bf16[656,128]{1,0:T(8,128)(2,1)S(1)} %collective-permute-done.4.refs_4_), channel_id=1, source_target_pairs={{0,1},{1,0},{2,3},{3,2},{4,5},{5,4},{6,7},{7,6},{8,9},{9,8},{10,11... | collective-permute-start | bytes 503816 | tf_op jit(solution)/shard_map/ppermute | solution.py:185
  26.6 1.8 %collective-permute-start.12 = (bf16[656,128]{1,0:T(8,128)(2,1)S(1)}, bf16[656,128]{1,0:T(8,128)(2,1)S(1)}, u32[]{:S(2)}, u32[]{:S(2)}) collective-permute-start(bf16[656,128]{1,0:T(8,128)(2,1)S(1)} %collective-permute-done.2.refs_5_), channel_id=1, source_target_pairs={{0,1},{1,0},{2,3},{3,2},{4,5},{5,4},{6,7},{7,6},{8,9},{9,8},{10,11... | collective-permute-start | bytes 503816 | tf_op jit(solution)/shard_map/ppermute | solution.py:185
  27.9 1.4 %collective-permute-start.13 = (bf16[656,128]{1,0:T(8,128)(2,1)S(1)}, bf16[656,128]{1,0:T(8,128)(2,1)S(1)}, u32[]{:S(2)}, u32[]{:S(2)}) collective-permute-start(bf16[656,128]{1,0:T(8,128)(2,1)S(1)} %collective-permute-done.5.refs_6_), channel_id=1, source_target_pairs={{0,1},{1,0},{2,3},{3,2},{4,5},{5,4},{6,7},{7,6},{8,9},{9,8},{10,11... | collective-permute-start | bytes 503816 | tf_op jit(solution)/shard_map/ppermute | solution.py:185
  27.9 1.6 %collective-permute-start.14 = (bf16[656,128]{1,0:T(8,128)(2,1)S(1)}, bf16[656,128]{1,0:T(8,128)(2,1)S(1)}, u32[]{:S(2)}, u32[]{:S(2)}) collective-permute-start(bf16[656,128]{1,0:T(8,128)(2,1)S(1)} %collective-permute-done.6.refs_7_), channel_id=1, source_target_pairs={{0,1},{1,0},{2,3},{3,2},{4,5},{5,4},{6,7},{7,6},{8,9},{9,8},{10,11... | collective-permute-start | bytes 503816 | tf_op jit(solution)/shard_map/ppermute | solution.py:185

commit v16 on v14

--- a/solution.py
+++ b/solution.py
@@ -120,6 +120,7 @@
         return pl.ds(pl.multiple_of(block * SB, SB), SB)
 
     def chunk_step(chunk, carry):
+        part = None
         for d in range(CHUNK):
             device = chunk * CHUNK + d
             stacked = []
@@ -137,7 +138,10 @@
             half[at, :orbitals] = moved[: 2 * SB]
             half[at, orbitals:] = moved[2 * SB :]
             left[:, at] = jnp.concatenate([c_all[rows_of(mu_one), mine], c_all[rows_of(mu_two), mine]], 0).T
-        part = jnp.dot(left[...], half[...], preferred_element_type=jnp.float32)
+            if d % (CHUNK // 2) == CHUNK // 2 - 1:
+                done = slice((d + 1 - CHUNK // 2) * 2 * SB, (d + 1) * 2 * SB)
+                term = jnp.dot(left[:, done], half[done, :], preferred_element_type=jnp.float32)
+                part = term if part is None else part + term
         for k in range(2):
             for j in range(blocks):
                 at = pl.ds(2 * j + k, LANES, stride=2 * blocks)

time: 33.3 us -> 33.2 us (level)
  no operation moved by 1% of the time
where the time goes in v16:
time: 33.2 us; the launch traced here: 33.1 us
  waiting for transfers between devices  15.8 us (48%)
  starting transfers between devices  11.8 us (36%)
  Pallas kernels  4.82 us (15%)
  between operations  0.68 us (2%)
    ppermute x15, waiting for transfers between devices, flip(): return lax.ppermute(array, axis, [(i, i ^ bit) for i in range(size)])  15.8 us
    ppermute x15, starting transfers between devices, flip(): return lax.ppermute(array, axis, [(i, i ^ bit) for i in range(size)])  11.8 us
    pallas_call x1, Pallas kernels, transform(): pl.pallas_call(functools.partial(transform_kernel, came, n_orb, orbitals,...  3.63 us
    pallas_call x1, Pallas kernels, pack(): pl.pallas_call(functools.partial(pack_kernel, n_pair), out_shape=[pltpu.V...  1.19 us
  transfers between devices with their start and end apart: 15, of which 6 were waited for; matrix products, arithmetic and copies ran while one was open for 0% of the time, Pallas kernels for 0%

profile of v16, /device:TPU:0, one launch (start us, length us, event | category | flops | bytes accessed | tf_op | source)
XLA Modules:
  0.0 33.1 jit_solution(12187694002690877898)
XLA Ops:
  0.7 1.2 %pack.1 = (bf16[656,128]{1,0:T(8,128)(2,1)S(1)}, bf16[656,128]{1,0:T(8,128)(2,1)S(1)}, bf16[656,128]{1,0:T(8,128)(2,1)S(1)}, bf16[656,128]{1,0:T(8,128)(2,1)S(1)}) custom-call(bf16[2,8,4096]{2,1,0:T(8,128)(2,1)} %integrals.1, s32[2]{0:T(128)} %mu.1, s32[2]{0:T(128)} %nu.1, s32[1]{0:T(128)S(6)} %copy.7.counts, bf16[128,512]{1,0:T(8,128)(2,1)} %coeff.1), custom_call_target="tpu_custom_call" | custom-call | tf_op jit(solution)/shard_map/pack/pallas_call | solution.py:71
  1.9 3.1 %collective-permute-start = (bf16[656,128]{1,0:T(8,128)(2,1)S(1)}, bf16[656,128]{1,0:T(8,128)(2,1)S(1)}, u32[]{:S(2)}, u32[]{:S(2)}) collective-permute-start(bf16[656,128]{1,0:T(8,128)(2,1)S(1)} %get-tuple-element.19), channel_id=1, source_target_pairs={{0,4},{4,0},{8,12},{12,8},{1,5},{5,1},{9,13},{13,9},{2,6},{6,2},{1... | collective-permute-start | bytes 503816 | tf_op jit(solution)/shard_map/ppermute | solution.py:182
  4.9 2.6 %collective-permute-start.3 = (bf16[656,128]{1,0:T(8,128)(2,1)S(1)}, bf16[656,128]{1,0:T(8,128)(2,1)S(1)}, u32[]{:S(2)}, u32[]{:S(2)}) collective-permute-start(bf16[656,128]{1,0:T(8,128)(2,1)S(1)} %get-tuple-element.24), channel_id=1, source_target_pairs={{0,8},{4,12},{8,0},{12,4},{1,9},{5,13},{9,1},{13,5},{2,10},{6,14},... | collective-permute-start | bytes 503816 | tf_op jit(solution)/shard_map/ppermute | solution.py:182
  7.5 0.0 collective-permute-start.1
  7.5 4.3 %collective-permute-done.refs_1_ = bf16[656,128]{1,0:T(8,128)(2,1)S(1)} collective-permute-done((bf16[656,128]{1,0:T(8,128)(2,1)S(1)}, bf16[656,128]{1,0:T(8,128)(2,1)S(1)}, u32[]{:S(2)}, u32[]{:S(2)}) %collective-permute-start) | collective-permute-done | bytes 167968 | tf_op jit(solution)/shard_map/ppermute | solution.py:182
  11.8 1.7 %collective-permute-start.2 = (bf16[656,128]{1,0:T(8,128)(2,1)S(1)}, bf16[656,128]{1,0:T(8,128)(2,1)S(1)}, u32[]{:S(2)}, u32[]{:S(2)}) collective-permute-start(bf16[656,128]{1,0:T(8,128)(2,1)S(1)} %collective-permute-done.refs_1_), channel_id=1, source_target_pairs={{0,2},{1,3},{2,0},{3,1},{4,6},{5,7},{6,4},{7,5},{8,10},{9,11},{10,... | collective-permute-start | bytes 503816 | tf_op jit(solution)/shard_map/ppermute | solution.py:182
  13.5 0.3 collective-permute-start.4
  13.8 6.4 %collective-permute-done.3.refs_2_ = bf16[656,128]{1,0:T(8,128)(2,1)S(1)} collective-permute-done((bf16[656,128]{1,0:T(8,128)(2,1)S(1)}, bf16[656,128]{1,0:T(8,128)(2,1)S(1)}, u32[]{:S(2)}, u32[]{:S(2)}) %collective-permute-start.3) | collective-permute-done | bytes 167968 | tf_op jit(solution)/shard_map/ppermute | solution.py:182
  20.3 1.5 %collective-permute-start.5 = (bf16[656,128]{1,0:T(8,128)(2,1)S(1)}, bf16[656,128]{1,0:T(8,128)(2,1)S(1)}, u32[]{:S(2)}, u32[]{:S(2)}) collective-permute-start(bf16[656,128]{1,0:T(8,128)(2,1)S(1)} %collective-permute-done.3.refs_2_), channel_id=1, source_target_pairs={{0,2},{1,3},{2,0},{3,1},{4,6},{5,7},{6,4},{7,5},{8,10},{9,11},{10,... | collective-permute-start | bytes 503816 | tf_op jit(solution)/shard_map/ppermute | solution.py:182
  21.7 0.0 collective-permute-done.1.refs_3_
  21.7 0.0 collective-permute-done.2.refs_5_
  21.7 0.5 %collective-permute-start.6 = (bf16[656,128]{1,0:T(8,128)(2,1)S(1)}, bf16[656,128]{1,0:T(8,128)(2,1)S(1)}, u32[]{:S(2)}, u32[]{:S(2)}) collective-permute-start(bf16[656,128]{1,0:T(8,128)(2,1)S(1)} %collective-permute-done.1.refs_3_), channel_id=1, source_target_pairs={{0,2},{1,3},{2,0},{3,1},{4,6},{5,7},{6,4},{7,5},{8,10},{9,11},{10,... | collective-permute-start | bytes 503816 | tf_op jit(solution)/shard_map/ppermute | solution.py:182
  22.3 0.0 collective-permute-start.7
  22.3 0.5 %collective-permute-start.8 = (bf16[656,128]{1,0:T(8,128)(2,1)S(1)}, bf16[656,128]{1,0:T(8,128)(2,1)S(1)}, u32[]{:S(2)}, u32[]{:S(2)}) collective-permute-start(bf16[656,128]{1,0:T(8,128)(2,1)S(1)} %collective-permute-done.refs_1_), channel_id=1, source_target_pairs={{0,1},{1,0},{2,3},{3,2},{4,5},{5,4},{6,7},{7,6},{8,9},{9,8},{10,11... | collective-permute-start | bytes 503816 | tf_op jit(solution)/shard_map/ppermute | solution.py:182
  22.8 0.0 collective-permute-done.4.refs_4_
  22.8 3.2 %collective-permute-done.5.refs_6_ = bf16[656,128]{1,0:T(8,128)(2,1)S(1)} collective-permute-done((bf16[656,128]{1,0:T(8,128)(2,1)S(1)}, bf16[656,128]{1,0:T(8,128)(2,1)S(1)}, u32[]{:S(2)}, u32[]{:S(2)}) %collective-permute-start.5) | collective-permute-done | bytes 167968 | tf_op jit(solution)/shard_map/ppermute | solution.py:182
  26.0 0.0 collective-permute-start.9
  26.0 0.5 %collective-permute-start.10 = (bf16[656,128]{1,0:T(8,128)(2,1)S(1)}, bf16[656,128]{1,0:T(8,128)(2,1)S(1)}, u32[]{:S(2)}, u32[]{:S(2)}) collective-permute-start(bf16[656,128]{1,0:T(8,128)(2,1)S(1)} %collective-permute-done.1.refs_3_), channel_id=1, source_target_pairs={{0,1},{1,0},{2,3},{3,2},{4,5},{5,4},{6,7},{7,6},{8,9},{9,8},{10,11... | collective-permute-start | bytes 503816 | tf_op jit(solution)/shard_map/ppermute | solution.py:182
  26.5 0.0 collective-permute-done.7.refs_8_
  26.5 0.0 collective-permute-start.11
  26.5 0.0 collective-permute-done.8.refs_9_
  26.5 0.5 %collective-permute-start.12 = (bf16[656,128]{1,0:T(8,128)(2,1)S(1)}, bf16[656,128]{1,0:T(8,128)(2,1)S(1)}, u32[]{:S(2)}, u32[]{:S(2)}) collective-permute-start(bf16[656,128]{1,0:T(8,128)(2,1)S(1)} %collective-permute-done.2.refs_5_), channel_id=1, source_target_pairs={{0,1},{1,0},{2,3},{3,2},{4,5},{5,4},{6,7},{7,6},{8,9},{9,8},{10,11... | collective-permute-start | bytes 503816 | tf_op jit(solution)/shard_map/ppermute | solution.py:182
  27.0 0.8 %collective-permute-done.6.refs_7_ = bf16[656,128]{1,0:T(8,128)(2,1)S(1)} collective-permute-done((bf16[656,128]{1,0:T(8,128)(2,1)S(1)}, bf16[656,128]{1,0:T(8,128)(2,1)S(1)}, u32[]{:S(2)}, u32[]{:S(2)}) %collective-permute-start.6) | collective-permute-done | bytes 167968 | tf_op jit(solution)/shard_map/ppermute | solution.py:182
  27.8 0.0 collective-permute-start.13
  27.8 0.0 collective-permute-done.9.refs_10_
  27.8 0.5 %collective-permute-start.14 = (bf16[656,128]{1,0:T(8,128)(2,1)S(1)}, bf16[656,128]{1,0:T(8,128)(2,1)S(1)}, u32[]{:S(2)}, u32[]{:S(2)}) collective-permute-start(bf16[656,128]{1,0:T(8,128)(2,1)S(1)} %collective-permute-done.6.refs_7_), channel_id=1, source_target_pairs={{0,1},{1,0},{2,3},{3,2},{4,5},{5,4},{6,7},{7,6},{8,9},{9,8},{10,11... | collective-permute-start | bytes 503816 | tf_op jit(solution)/shard_map/ppermute | solution.py:182
  28.3 0.0 collective-permute-done.10.refs_11_
  28.3 0.0 collective-permute-done.11.refs_12_
  28.3 0.0 collective-permute-done.12.refs_13_
  28.3 0.9 %collective-permute-done.13.refs_14_ = bf16[656,128]{1,0:T(8,128)(2,1)S(1)} collective-permute-done((bf16[656,128]{1,0:T(8,128)(2,1)S(1)}, bf16[656,128]{1,0:T(8,128)(2,1)S(1)}, u32[]{:S(2)}, u32[]{:S(2)}) %collective-permute-start.13) | collective-permute-done | bytes 167968 | tf_op jit(solution)/shard_map/ppermute | solution.py:182
  29.2 0.2 collective-permute-done.14.refs_15_
  29.5 3.6 %transform.1 = f32[1024,128]{1,0:T(8,128)} custom-call(bf16[656,128]{1,0:T(8,128)(2,1)S(1)} %get-tuple-element.22.refs_0_, bf16[656,128]{1,0:T(8,128)(2,1)S(1)} %collective-permute-done.refs_1_, bf16[656,128]{1,0:T(8,128)(2,1)S(1)} %collective-permute-done.3.refs_2_, bf16[656,128]{1,0:T(8,128)(2,1)S(1)} %collective-permute-done.1.refs_3_, ...), custom_call_target="tpu_custom_call" | custom-call | tf_op jit(solution)/shard_map/transform/pallas_call | solution.py:163
Async XLA Ops:
  1.9 10.0 %collective-permute-start = (bf16[656,128]{1,0:T(8,128)(2,1)S(1)}, bf16[656,128]{1,0:T(8,128)(2,1)S(1)}, u32[]{:S(2)}, u32[]{:S(2)}) collective-permute-start(bf16[656,128]{1,0:T(8,128)(2,1)S(1)} %get-tuple-element.19), channel_id=1, source_target_pairs={{0,4},{4,0},{8,12},{12,8},{1,5},{5,1},{9,13},{13,9},{2,6},{6,2},{1... | collective-permute-start | bytes 503816 | tf_op jit(solution)/shard_map/ppermute | solution.py:182
  4.9 15.3 %collective-permute-start.3 = (bf16[656,128]{1,0:T(8,128)(2,1)S(1)}, bf16[656,128]{1,0:T(8,128)(2,1)S(1)}, u32[]{:S(2)}, u32[]{:S(2)}) collective-permute-start(bf16[656,128]{1,0:T(8,128)(2,1)S(1)} %get-tuple-element.24), channel_id=1, source_target_pairs={{0,8},{4,12},{8,0},{12,4},{1,9},{5,13},{9,1},{13,5},{2,10},{6,14},... | collective-permute-start | bytes 503816 | tf_op jit(solution)/shard_map/ppermute | solution.py:182
  7.5 14.2 %collective-permute-start.1 = (bf16[656,128]{1,0:T(8,128)(2,1)S(1)}, bf16[656,128]{1,0:T(8,128)(2,1)S(1)}, u32[]{:S(2)}, u32[]{:S(2)}) collective-permute-start(bf16[656,128]{1,0:T(8,128)(2,1)S(1)} %get-tuple-element.20), channel_id=1, source_target_pairs={{0,12},{4,8},{8,4},{12,0},{1,13},{5,9},{9,5},{13,1},{2,14},{6,10},... | collective-permute-start | bytes 503816 | tf_op jit(solution)/shard_map/ppermute | solution.py:182
  11.8 9.9 %collective-permute-start.2 = (bf16[656,128]{1,0:T(8,128)(2,1)S(1)}, bf16[656,128]{1,0:T(8,128)(2,1)S(1)}, u32[]{:S(2)}, u32[]{:S(2)}) collective-permute-start(bf16[656,128]{1,0:T(8,128)(2,1)S(1)} %collective-permute-done.refs_1_), channel_id=1, source_target_pairs={{0,2},{1,3},{2,0},{3,1},{4,6},{5,7},{6,4},{7,5},{8,10},{9,11},{10,... | collective-permute-start | bytes 503816 | tf_op jit(solution)/shard_map/ppermute | solution.py:182
  13.5 9.3 %collective-permute-start.4 = (bf16[656,128]{1,0:T(8,128)(2,1)S(1)}, bf16[656,128]{1,0:T(8,128)(2,1)S(1)}, u32[]{:S(2)}, u32[]{:S(2)}) collective-permute-start(bf16[656,128]{1,0:T(8,128)(2,1)S(1)} %get-tuple-element.22.refs_0_), channel_id=1, source_target_pairs={{0,2},{1,3},{2,0},{3,1},{4,6},{5,7},{6,4},{7,5},{8,10},{9,11},{10,... | collective-permute-start | bytes 503816 | tf_op jit(solution)/shard_map/ppermute | solution.py:182
  20.3 5.8 %collective-permute-start.5 = (bf16[656,128]{1,0:T(8,128)(2,1)S(1)}, bf16[656,128]{1,0:T(8,128)(2,1)S(1)}, u32[]{:S(2)}, u32[]{:S(2)}) collective-permute-start(bf16[656,128]{1,0:T(8,128)(2,1)S(1)} %collective-permute-done.3.refs_2_), channel_id=1, source_target_pairs={{0,2},{1,3},{2,0},{3,1},{4,6},{5,7},{6,4},{7,5},{8,10},{9,11},{10,... | collective-permute-start | bytes 503816 | tf_op jit(solution)/shard_map/ppermute | solution.py:182
  21.7 6.1 %collective-permute-start.6 = (bf16[656,128]{1,0:T(8,128)(2,1)S(1)}, bf16[656,128]{1,0:T(8,128)(2,1)S(1)}, u32[]{:S(2)}, u32[]{:S(2)}) collective-permute-start(bf16[656,128]{1,0:T(8,128)(2,1)S(1)} %collective-permute-done.1.refs_3_), channel_id=1, source_target_pairs={{0,2},{1,3},{2,0},{3,1},{4,6},{5,7},{6,4},{7,5},{8,10},{9,11},{10,... | collective-permute-start | bytes 503816 | tf_op jit(solution)/shard_map/ppermute | solution.py:182
  22.3 4.2 %collective-permute-start.7 = (bf16[656,128]{1,0:T(8,128)(2,1)S(1)}, bf16[656,128]{1,0:T(8,128)(2,1)S(1)}, u32[]{:S(2)}, u32[]{:S(2)}) collective-permute-start(bf16[656,128]{1,0:T(8,128)(2,1)S(1)} %get-tuple-element.22.refs_0_), channel_id=1, source_target_pairs={{0,1},{1,0},{2,3},{3,2},{4,5},{5,4},{6,7},{7,6},{8,9},{9,8},{10,11... | collective-permute-start | bytes 503816 | tf_op jit(solution)/shard_map/ppermute | solution.py:182
  22.3 4.2 %collective-permute-start.8 = (bf16[656,128]{1,0:T(8,128)(2,1)S(1)}, bf16[656,128]{1,0:T(8,128)(2,1)S(1)}, u32[]{:S(2)}, u32[]{:S(2)}) collective-permute-start(bf16[656,128]{1,0:T(8,128)(2,1)S(1)} %collective-permute-done.refs_1_), channel_id=1, source_target_pairs={{0,1},{1,0},{2,3},{3,2},{4,5},{5,4},{6,7},{7,6},{8,9},{9,8},{10,11... | collective-permute-start | bytes 503816 | tf_op jit(solution)/shard_map/ppermute | solution.py:182
  26.0 1.8 %collective-permute-start.9 = (bf16[656,128]{1,0:T(8,128)(2,1)S(1)}, bf16[656,128]{1,0:T(8,128)(2,1)S(1)}, u32[]{:S(2)}, u32[]{:S(2)}) collective-permute-start(bf16[656,128]{1,0:T(8,128)(2,1)S(1)} %collective-permute-done.3.refs_2_), channel_id=1, source_target_pairs={{0,1},{1,0},{2,3},{3,2},{4,5},{5,4},{6,7},{7,6},{8,9},{9,8},{10,11... | collective-permute-start | bytes 503816 | tf_op jit(solution)/shard_map/ppermute | solution.py:182
  26.0 2.3 %collective-permute-start.10 = (bf16[656,128]{1,0:T(8,128)(2,1)S(1)}, bf16[656,128]{1,0:T(8,128)(2,1)S(1)}, u32[]{:S(2)}, u32[]{:S(2)}) collective-permute-start(bf16[656,128]{1,0:T(8,128)(2,1)S(1)} %collective-permute-done.1.refs_3_), channel_id=1, source_target_pairs={{0,1},{1,0},{2,3},{3,2},{4,5},{5,4},{6,7},{7,6},{8,9},{9,8},{10,11... | collective-permute-start | bytes 503816 | tf_op jit(solution)/shard_map/ppermute | solution.py:182
  26.5 1.8 %collective-permute-start.11 = (bf16[656,128]{1,0:T(8,128)(2,1)S(1)}, bf16[656,128]{1,0:T(8,128)(2,1)S(1)}, u32[]{:S(2)}, u32[]{:S(2)}) collective-permute-start(bf16[656,128]{1,0:T(8,128)(2,1)S(1)} %collective-permute-done.4.refs_4_), channel_id=1, source_target_pairs={{0,1},{1,0},{2,3},{3,2},{4,5},{5,4},{6,7},{7,6},{8,9},{9,8},{10,11... | collective-permute-start | bytes 503816 | tf_op jit(solution)/shard_map/ppermute | solution.py:182
  26.5 1.8 %collective-permute-start.12 = (bf16[656,128]{1,0:T(8,128)(2,1)S(1)}, bf16[656,128]{1,0:T(8,128)(2,1)S(1)}, u32[]{:S(2)}, u32[]{:S(2)}) collective-permute-start(bf16[656,128]{1,0:T(8,128)(2,1)S(1)} %collective-permute-done.2.refs_5_), channel_id=1, source_target_pairs={{0,1},{1,0},{2,3},{3,2},{4,5},{5,4},{6,7},{7,6},{8,9},{9,8},{10,11... | collective-permute-start | bytes 503816 | tf_op jit(solution)/shard_map/ppermute | solution.py:182
  27.8 1.4 %collective-permute-start.13 = (bf16[656,128]{1,0:T(8,128)(2,1)S(1)}, bf16[656,128]{1,0:T(8,128)(2,1)S(1)}, u32[]{:S(2)}, u32[]{:S(2)}) collective-permute-start(bf16[656,128]{1,0:T(8,128)(2,1)S(1)} %collective-permute-done.5.refs_6_), channel_id=1, source_target_pairs={{0,1},{1,0},{2,3},{3,2},{4,5},{5,4},{6,7},{7,6},{8,9},{9,8},{10,11... | collective-permute-start | bytes 503816 | tf_op jit(solution)/shard_map/ppermute | solution.py:182
  27.8 1.6 %collective-permute-start.14 = (bf16[656,128]{1,0:T(8,128)(2,1)S(1)}, bf16[656,128]{1,0:T(8,128)(2,1)S(1)}, u32[]{:S(2)}, u32[]{:S(2)}) collective-permute-start(bf16[656,128]{1,0:T(8,128)(2,1)S(1)} %collective-permute-done.6.refs_7_), channel_id=1, source_target_pairs={{0,1},{1,0},{2,3},{3,2},{4,5},{5,4},{6,7},{7,6},{8,9},{9,8},{10,11... | collective-permute-start | bytes 503816 | tf_op jit(solution)/shard_map/ppermute | solution.py:182

commit v17 on v16

--- a/solution.py
+++ b/solution.py
@@ -138,8 +138,8 @@
             half[at, :orbitals] = moved[: 2 * SB]
             half[at, orbitals:] = moved[2 * SB :]
             left[:, at] = jnp.concatenate([c_all[rows_of(mu_one), mine], c_all[rows_of(mu_two), mine]], 0).T
-            if d % (CHUNK // 2) == CHUNK // 2 - 1:
-                done = slice((d + 1 - CHUNK // 2) * 2 * SB, (d + 1) * 2 * SB)
+            if d % (CHUNK // 4) == CHUNK // 4 - 1:
+                done = slice((d + 1 - CHUNK // 4) * 2 * SB, (d + 1) * 2 * SB)
                 term = jnp.dot(left[:, done], half[done, :], preferred_element_type=jnp.float32)
                 part = term if part is None else part + term
         for k in range(2):

time: 33.2 us -> 33.5 us (level)
  no operation moved by 1% of the time
where the time goes in v17:
time: 33.5 us; the launch traced here: 33.3 us
  waiting for transfers between devices  15.8 us (47%)
  starting transfers between devices  11.8 us (35%)
  Pallas kernels  5.05 us (15%)
  between operations  0.68 us (2%)
    ppermute x15, waiting for transfers between devices, flip(): return lax.ppermute(array, axis, [(i, i ^ bit) for i in range(size)])  15.8 us
    ppermute x15, starting transfers between devices, flip(): return lax.ppermute(array, axis, [(i, i ^ bit) for i in range(size)])  11.8 us
    pallas_call x1, Pallas kernels, transform(): pl.pallas_call(functools.partial(transform_kernel, came, n_orb, orbitals,...  3.86 us
    pallas_call x1, Pallas kernels, pack(): pl.pallas_call(functools.partial(pack_kernel, n_pair), out_shape=[pltpu.V...  1.19 us
  transfers between devices with their start and end apart: 15, of which 6 were waited for; matrix products, arithmetic and copies ran while one was open for 0% of the time, Pallas kernels for 0%

profile of v17, /device:TPU:0, one launch (start us, length us, event | category | flops | bytes accessed | tf_op | source)
XLA Modules:
  0.0 33.3 jit_solution(7183906318829171489)
XLA Ops:
  0.7 1.2 %pack.1 = (bf16[656,128]{1,0:T(8,128)(2,1)S(1)}, bf16[656,128]{1,0:T(8,128)(2,1)S(1)}, bf16[656,128]{1,0:T(8,128)(2,1)S(1)}, bf16[656,128]{1,0:T(8,128)(2,1)S(1)}) custom-call(bf16[2,8,4096]{2,1,0:T(8,128)(2,1)} %integrals.1, s32[2]{0:T(128)} %mu.1, s32[2]{0:T(128)} %nu.1, s32[1]{0:T(128)S(6)} %copy.7.counts, bf16[128,512]{1,0:T(8,128)(2,1)} %coeff.1), custom_call_target="tpu_custom_call" | custom-call | tf_op jit(solution)/shard_map/pack/pallas_call | solution.py:71
  1.9 3.1 %collective-permute-start = (bf16[656,128]{1,0:T(8,128)(2,1)S(1)}, bf16[656,128]{1,0:T(8,128)(2,1)S(1)}, u32[]{:S(2)}, u32[]{:S(2)}) collective-permute-start(bf16[656,128]{1,0:T(8,128)(2,1)S(1)} %get-tuple-element.19), channel_id=1, source_target_pairs={{0,4},{4,0},{8,12},{12,8},{1,5},{5,1},{9,13},{13,9},{2,6},{6,2},{1... | collective-permute-start | bytes 503816 | tf_op jit(solution)/shard_map/ppermute | solution.py:182
  4.9 2.6 %collective-permute-start.3 = (bf16[656,128]{1,0:T(8,128)(2,1)S(1)}, bf16[656,128]{1,0:T(8,128)(2,1)S(1)}, u32[]{:S(2)}, u32[]{:S(2)}) collective-permute-start(bf16[656,128]{1,0:T(8,128)(2,1)S(1)} %get-tuple-element.24), channel_id=1, source_target_pairs={{0,8},{4,12},{8,0},{12,4},{1,9},{5,13},{9,1},{13,5},{2,10},{6,14},... | collective-permute-start | bytes 503816 | tf_op jit(solution)/shard_map/ppermute | solution.py:182
  7.5 0.0 collective-permute-start.1
  7.5 4.3 %collective-permute-done.refs_1_ = bf16[656,128]{1,0:T(8,128)(2,1)S(1)} collective-permute-done((bf16[656,128]{1,0:T(8,128)(2,1)S(1)}, bf16[656,128]{1,0:T(8,128)(2,1)S(1)}, u32[]{:S(2)}, u32[]{:S(2)}) %collective-permute-start) | collective-permute-done | bytes 167968 | tf_op jit(solution)/shard_map/ppermute | solution.py:182
  11.8 1.7 %collective-permute-start.2 = (bf16[656,128]{1,0:T(8,128)(2,1)S(1)}, bf16[656,128]{1,0:T(8,128)(2,1)S(1)}, u32[]{:S(2)}, u32[]{:S(2)}) collective-permute-start(bf16[656,128]{1,0:T(8,128)(2,1)S(1)} %collective-permute-done.refs_1_), channel_id=1, source_target_pairs={{0,2},{1,3},{2,0},{3,1},{4,6},{5,7},{6,4},{7,5},{8,10},{9,11},{10,... | collective-permute-start | bytes 503816 | tf_op jit(solution)/shard_map/ppermute | solution.py:182
  13.5 0.3 collective-permute-start.4
  13.8 6.4 %collective-permute-done.3.refs_2_ = bf16[656,128]{1,0:T(8,128)(2,1)S(1)} collective-permute-done((bf16[656,128]{1,0:T(8,128)(2,1)S(1)}, bf16[656,128]{1,0:T(8,128)(2,1)S(1)}, u32[]{:S(2)}, u32[]{:S(2)}) %collective-permute-start.3) | collective-permute-done | bytes 167968 | tf_op jit(solution)/shard_map/ppermute | solution.py:182
  20.3 1.5 %collective-permute-start.5 = (bf16[656,128]{1,0:T(8,128)(2,1)S(1)}, bf16[656,128]{1,0:T(8,128)(2,1)S(1)}, u32[]{:S(2)}, u32[]{:S(2)}) collective-permute-start(bf16[656,128]{1,0:T(8,128)(2,1)S(1)} %collective-permute-done.3.refs_2_), channel_id=1, source_target_pairs={{0,2},{1,3},{2,0},{3,1},{4,6},{5,7},{6,4},{7,5},{8,10},{9,11},{10,... | collective-permute-start | bytes 503816 | tf_op jit(solution)/shard_map/ppermute | solution.py:182
  21.7 0.0 collective-permute-done.1.refs_3_
  21.7 0.0 collective-permute-done.2.refs_5_
  21.7 0.5 %collective-permute-start.6 = (bf16[656,128]{1,0:T(8,128)(2,1)S(1)}, bf16[656,128]{1,0:T(8,128)(2,1)S(1)}, u32[]{:S(2)}, u32[]{:S(2)}) collective-permute-start(bf16[656,128]{1,0:T(8,128)(2,1)S(1)} %collective-permute-done.1.refs_3_), channel_id=1, source_target_pairs={{0,2},{1,3},{2,0},{3,1},{4,6},{5,7},{6,4},{7,5},{8,10},{9,11},{10,... | collective-permute-start | bytes 503816 | tf_op jit(solution)/shard_map/ppermute | solution.py:182
  22.3 0.0 collective-permute-start.7
  22.3 0.5 %collective-permute-start.8 = (bf16[656,128]{1,0:T(8,128)(2,1)S(1)}, bf16[656,128]{1,0:T(8,128)(2,1)S(1)}, u32[]{:S(2)}, u32[]{:S(2)}) collective-permute-start(bf16[656,128]{1,0:T(8,128)(2,1)S(1)} %collective-permute-done.refs_1_), channel_id=1, source_target_pairs={{0,1},{1,0},{2,3},{3,2},{4,5},{5,4},{6,7},{7,6},{8,9},{9,8},{10,11... | collective-permute-start | bytes 503816 | tf_op jit(solution)/shard_map/ppermute | solution.py:182
  22.8 0.0 collective-permute-done.4.refs_4_
  22.8 3.2 %collective-permute-done.5.refs_6_ = bf16[656,128]{1,0:T(8,128)(2,1)S(1)} collective-permute-done((bf16[656,128]{1,0:T(8,128)(2,1)S(1)}, bf16[656,128]{1,0:T(8,128)(2,1)S(1)}, u32[]{:S(2)}, u32[]{:S(2)}) %collective-permute-start.5) | collective-permute-done | bytes 167968 | tf_op jit(solution)/shard_map/ppermute | solution.py:182
  26.0 0.0 collective-permute-start.9
  26.0 0.5 %collective-permute-start.10 = (bf16[656,128]{1,0:T(8,128)(2,1)S(1)}, bf16[656,128]{1,0:T(8,128)(2,1)S(1)}, u32[]{:S(2)}, u32[]{:S(2)}) collective-permute-start(bf16[656,128]{1,0:T(8,128)(2,1)S(1)} %collective-permute-done.1.refs_3_), channel_id=1, source_target_pairs={{0,1},{1,0},{2,3},{3,2},{4,5},{5,4},{6,7},{7,6},{8,9},{9,8},{10,11... | collective-permute-start | bytes 503816 | tf_op jit(solution)/shard_map/ppermute | solution.py:182
  26.5 0.0 collective-permute-done.7.refs_8_
  26.5 0.0 collective-permute-start.11
  26.5 0.0 collective-permute-done.8.refs_9_
  26.5 0.5 %collective-permute-start.12 = (bf16[656,128]{1,0:T(8,128)(2,1)S(1)}, bf16[656,128]{1,0:T(8,128)(2,1)S(1)}, u32[]{:S(2)}, u32[]{:S(2)}) collective-permute-start(bf16[656,128]{1,0:T(8,128)(2,1)S(1)} %collective-permute-done.2.refs_5_), channel_id=1, source_target_pairs={{0,1},{1,0},{2,3},{3,2},{4,5},{5,4},{6,7},{7,6},{8,9},{9,8},{10,11... | collective-permute-start | bytes 503816 | tf_op jit(solution)/shard_map/ppermute | solution.py:182
  27.0 0.8 %collective-permute-done.6.refs_7_ = bf16[656,128]{1,0:T(8,128)(2,1)S(1)} collective-permute-done((bf16[656,128]{1,0:T(8,128)(2,1)S(1)}, bf16[656,128]{1,0:T(8,128)(2,1)S(1)}, u32[]{:S(2)}, u32[]{:S(2)}) %collective-permute-start.6) | collective-permute-done | bytes 167968 | tf_op jit(solution)/shard_map/ppermute | solution.py:182
  27.8 0.0 collective-permute-start.13
  27.8 0.0 collective-permute-done.9.refs_10_
  27.8 0.5 %collective-permute-start.14 = (bf16[656,128]{1,0:T(8,128)(2,1)S(1)}, bf16[656,128]{1,0:T(8,128)(2,1)S(1)}, u32[]{:S(2)}, u32[]{:S(2)}) collective-permute-start(bf16[656,128]{1,0:T(8,128)(2,1)S(1)} %collective-permute-done.6.refs_7_), channel_id=1, source_target_pairs={{0,1},{1,0},{2,3},{3,2},{4,5},{5,4},{6,7},{7,6},{8,9},{9,8},{10,11... | collective-permute-start | bytes 503816 | tf_op jit(solution)/shard_map/ppermute | solution.py:182
  28.3 0.0 collective-permute-done.10.refs_11_
  28.3 0.0 collective-permute-done.11.refs_12_
  28.3 0.0 collective-permute-done.12.refs_13_
  28.3 0.9 %collective-permute-done.13.refs_14_ = bf16[656,128]{1,0:T(8,128)(2,1)S(1)} collective-permute-done((bf16[656,128]{1,0:T(8,128)(2,1)S(1)}, bf16[656,128]{1,0:T(8,128)(2,1)S(1)}, u32[]{:S(2)}, u32[]{:S(2)}) %collective-permute-start.13) | collective-permute-done | bytes 167968 | tf_op jit(solution)/shard_map/ppermute | solution.py:182
  29.2 0.2 collective-permute-done.14.refs_15_
  29.5 3.9 %transform.1 = f32[1024,128]{1,0:T(8,128)} custom-call(bf16[656,128]{1,0:T(8,128)(2,1)S(1)} %get-tuple-element.22.refs_0_, bf16[656,128]{1,0:T(8,128)(2,1)S(1)} %collective-permute-done.refs_1_, bf16[656,128]{1,0:T(8,128)(2,1)S(1)} %collective-permute-done.3.refs_2_, bf16[656,128]{1,0:T(8,128)(2,1)S(1)} %collective-permute-done.1.refs_3_, ...), custom_call_target="tpu_custom_call" | custom-call | tf_op jit(solution)/shard_map/transform/pallas_call | solution.py:163
Async XLA Ops:
  1.9 10.0 %collective-permute-start = (bf16[656,128]{1,0:T(8,128)(2,1)S(1)}, bf16[656,128]{1,0:T(8,128)(2,1)S(1)}, u32[]{:S(2)}, u32[]{:S(2)}) collective-permute-start(bf16[656,128]{1,0:T(8,128)(2,1)S(1)} %get-tuple-element.19), channel_id=1, source_target_pairs={{0,4},{4,0},{8,12},{12,8},{1,5},{5,1},{9,13},{13,9},{2,6},{6,2},{1... | collective-permute-start | bytes 503816 | tf_op jit(solution)/shard_map/ppermute | solution.py:182
  4.9 15.3 %collective-permute-start.3 = (bf16[656,128]{1,0:T(8,128)(2,1)S(1)}, bf16[656,128]{1,0:T(8,128)(2,1)S(1)}, u32[]{:S(2)}, u32[]{:S(2)}) collective-permute-start(bf16[656,128]{1,0:T(8,128)(2,1)S(1)} %get-tuple-element.24), channel_id=1, source_target_pairs={{0,8},{4,12},{8,0},{12,4},{1,9},{5,13},{9,1},{13,5},{2,10},{6,14},... | collective-permute-start | bytes 503816 | tf_op jit(solution)/shard_map/ppermute | solution.py:182
  7.5 14.2 %collective-permute-start.1 = (bf16[656,128]{1,0:T(8,128)(2,1)S(1)}, bf16[656,128]{1,0:T(8,128)(2,1)S(1)}, u32[]{:S(2)}, u32[]{:S(2)}) collective-permute-start(bf16[656,128]{1,0:T(8,128)(2,1)S(1)} %get-tuple-element.20), channel_id=1, source_target_pairs={{0,12},{4,8},{8,4},{12,0},{1,13},{5,9},{9,5},{13,1},{2,14},{6,10},... | collective-permute-start | bytes 503816 | tf_op jit(solution)/shard_map/ppermute | solution.py:182
  11.8 9.9 %collective-permute-start.2 = (bf16[656,128]{1,0:T(8,128)(2,1)S(1)}, bf16[656,128]{1,0:T(8,128)(2,1)S(1)}, u32[]{:S(2)}, u32[]{:S(2)}) collective-permute-start(bf16[656,128]{1,0:T(8,128)(2,1)S(1)} %collective-permute-done.refs_1_), channel_id=1, source_target_pairs={{0,2},{1,3},{2,0},{3,1},{4,6},{5,7},{6,4},{7,5},{8,10},{9,11},{10,... | collective-permute-start | bytes 503816 | tf_op jit(solution)/shard_map/ppermute | solution.py:182
  13.5 9.3 %collective-permute-start.4 = (bf16[656,128]{1,0:T(8,128)(2,1)S(1)}, bf16[656,128]{1,0:T(8,128)(2,1)S(1)}, u32[]{:S(2)}, u32[]{:S(2)}) collective-permute-start(bf16[656,128]{1,0:T(8,128)(2,1)S(1)} %get-tuple-element.22.refs_0_), channel_id=1, source_target_pairs={{0,2},{1,3},{2,0},{3,1},{4,6},{5,7},{6,4},{7,5},{8,10},{9,11},{10,... | collective-permute-start | bytes 503816 | tf_op jit(solution)/shard_map/ppermute | solution.py:182
  20.3 5.8 %collective-permute-start.5 = (bf16[656,128]{1,0:T(8,128)(2,1)S(1)}, bf16[656,128]{1,0:T(8,128)(2,1)S(1)}, u32[]{:S(2)}, u32[]{:S(2)}) collective-permute-start(bf16[656,128]{1,0:T(8,128)(2,1)S(1)} %collective-permute-done.3.refs_2_), channel_id=1, source_target_pairs={{0,2},{1,3},{2,0},{3,1},{4,6},{5,7},{6,4},{7,5},{8,10},{9,11},{10,... | collective-permute-start | bytes 503816 | tf_op jit(solution)/shard_map/ppermute | solution.py:182
  21.7 6.1 %collective-permute-start.6 = (bf16[656,128]{1,0:T(8,128)(2,1)S(1)}, bf16[656,128]{1,0:T(8,128)(2,1)S(1)}, u32[]{:S(2)}, u32[]{:S(2)}) collective-permute-start(bf16[656,128]{1,0:T(8,128)(2,1)S(1)} %collective-permute-done.1.refs_3_), channel_id=1, source_target_pairs={{0,2},{1,3},{2,0},{3,1},{4,6},{5,7},{6,4},{7,5},{8,10},{9,11},{10,... | collective-permute-start | bytes 503816 | tf_op jit(solution)/shard_map/ppermute | solution.py:182
  22.3 4.2 %collective-permute-start.7 = (bf16[656,128]{1,0:T(8,128)(2,1)S(1)}, bf16[656,128]{1,0:T(8,128)(2,1)S(1)}, u32[]{:S(2)}, u32[]{:S(2)}) collective-permute-start(bf16[656,128]{1,0:T(8,128)(2,1)S(1)} %get-tuple-element.22.refs_0_), channel_id=1, source_target_pairs={{0,1},{1,0},{2,3},{3,2},{4,5},{5,4},{6,7},{7,6},{8,9},{9,8},{10,11... | collective-permute-start | bytes 503816 | tf_op jit(solution)/shard_map/ppermute | solution.py:182
  22.3 4.2 %collective-permute-start.8 = (bf16[656,128]{1,0:T(8,128)(2,1)S(1)}, bf16[656,128]{1,0:T(8,128)(2,1)S(1)}, u32[]{:S(2)}, u32[]{:S(2)}) collective-permute-start(bf16[656,128]{1,0:T(8,128)(2,1)S(1)} %collective-permute-done.refs_1_), channel_id=1, source_target_pairs={{0,1},{1,0},{2,3},{3,2},{4,5},{5,4},{6,7},{7,6},{8,9},{9,8},{10,11... | collective-permute-start | bytes 503816 | tf_op jit(solution)/shard_map/ppermute | solution.py:182
  26.0 1.8 %collective-permute-start.9 = (bf16[656,128]{1,0:T(8,128)(2,1)S(1)}, bf16[656,128]{1,0:T(8,128)(2,1)S(1)}, u32[]{:S(2)}, u32[]{:S(2)}) collective-permute-start(bf16[656,128]{1,0:T(8,128)(2,1)S(1)} %collective-permute-done.3.refs_2_), channel_id=1, source_target_pairs={{0,1},{1,0},{2,3},{3,2},{4,5},{5,4},{6,7},{7,6},{8,9},{9,8},{10,11... | collective-permute-start | bytes 503816 | tf_op jit(solution)/shard_map/ppermute | solution.py:182
  26.0 2.3 %collective-permute-start.10 = (bf16[656,128]{1,0:T(8,128)(2,1)S(1)}, bf16[656,128]{1,0:T(8,128)(2,1)S(1)}, u32[]{:S(2)}, u32[]{:S(2)}) collective-permute-start(bf16[656,128]{1,0:T(8,128)(2,1)S(1)} %collective-permute-done.1.refs_3_), channel_id=1, source_target_pairs={{0,1},{1,0},{2,3},{3,2},{4,5},{5,4},{6,7},{7,6},{8,9},{9,8},{10,11... | collective-permute-start | bytes 503816 | tf_op jit(solution)/shard_map/ppermute | solution.py:182
  26.5 1.8 %collective-permute-start.11 = (bf16[656,128]{1,0:T(8,128)(2,1)S(1)}, bf16[656,128]{1,0:T(8,128)(2,1)S(1)}, u32[]{:S(2)}, u32[]{:S(2)}) collective-permute-start(bf16[656,128]{1,0:T(8,128)(2,1)S(1)} %collective-permute-done.4.refs_4_), channel_id=1, source_target_pairs={{0,1},{1,0},{2,3},{3,2},{4,5},{5,4},{6,7},{7,6},{8,9},{9,8},{10,11... | collective-permute-start | bytes 503816 | tf_op jit(solution)/shard_map/ppermute | solution.py:182
  26.5 1.8 %collective-permute-start.12 = (bf16[656,128]{1,0:T(8,128)(2,1)S(1)}, bf16[656,128]{1,0:T(8,128)(2,1)S(1)}, u32[]{:S(2)}, u32[]{:S(2)}) collective-permute-start(bf16[656,128]{1,0:T(8,128)(2,1)S(1)} %collective-permute-done.2.refs_5_), channel_id=1, source_target_pairs={{0,1},{1,0},{2,3},{3,2},{4,5},{5,4},{6,7},{7,6},{8,9},{9,8},{10,11... | collective-permute-start | bytes 503816 | tf_op jit(solution)/shard_map/ppermute | solution.py:182
  27.8 1.4 %collective-permute-start.13 = (bf16[656,128]{1,0:T(8,128)(2,1)S(1)}, bf16[656,128]{1,0:T(8,128)(2,1)S(1)}, u32[]{:S(2)}, u32[]{:S(2)}) collective-permute-start(bf16[656,128]{1,0:T(8,128)(2,1)S(1)} %collective-permute-done.5.refs_6_), channel_id=1, source_target_pairs={{0,1},{1,0},{2,3},{3,2},{4,5},{5,4},{6,7},{7,6},{8,9},{9,8},{10,11... | collective-permute-start | bytes 503816 | tf_op jit(solution)/shard_map/ppermute | solution.py:182
  27.8 1.6 %collective-permute-start.14 = (bf16[656,128]{1,0:T(8,128)(2,1)S(1)}, bf16[656,128]{1,0:T(8,128)(2,1)S(1)}, u32[]{:S(2)}, u32[]{:S(2)}) collective-permute-start(bf16[656,128]{1,0:T(8,128)(2,1)S(1)} %collective-permute-done.6.refs_7_), channel_id=1, source_target_pairs={{0,1},{1,0},{2,3},{3,2},{4,5},{5,4},{6,7},{7,6},{8,9},{9,8},{10,11... | collective-permute-start | bytes 503816 | tf_op jit(solution)/shard_map/ppermute | solution.py:182

commit v18 on v16

--- a/solution.py
+++ b/solution.py
@@ -38,6 +38,11 @@
         tag = jnp.where((lane == 2 * t) & (t < count), mu_in[t], tag)
         tag = jnp.where((lane == 2 * t + 1) & (t < count), nu_in[t], tag)
     tag = tag.astype(jnp.float32).astype(jnp.bfloat16)
+    copies[3].wait()
+    for j in range(orbitals // LANES):
+        lanes = shard[:, j * LANES : (j + 1) * LANES]
+        for s in range(n_pair):
+            outs[s][j * held : (j + 1) * held] = lanes
     copies[0].wait()
     for t in range(slots):
         for j in range(wide):
@@ -57,11 +62,6 @@
             woven[pl.ds(begin + 1, wide, stride=2), :] = jnp.where(kept, odd, 0.0)
         outs[s][tile_at : tile_at + rows] = woven[pl.ds(s * rows, rows), :].astype(jnp.bfloat16)
         outs[s][tile_at + rows :] = tag
-    copies[3].wait()
-    for j in range(orbitals // LANES):
-        lanes = shard[:, j * LANES : (j + 1) * LANES]
-        for s in range(n_pair):
-            outs[s][j * held : (j + 1) * held] = lanes
 
 
 def pack(n_pair, integrals, mu, nu, counts, coeff):

time: 33.2 us -> 33.3 us (level)
  no operation moved by 1% of the time
where the time goes in v18:
time: 33.3 us; the launch traced here: 33.2 us
  waiting for transfers between devices  15.8 us (47%)
  starting transfers between devices  11.8 us (35%)
  Pallas kernels  4.89 us (15%)
  between operations  0.68 us (2%)
    ppermute x15, waiting for transfers between devices, flip(): return lax.ppermute(array, axis, [(i, i ^ bit) for i in range(size)])  15.8 us
    ppermute x15, starting transfers between devices, flip(): return lax.ppermute(array, axis, [(i, i ^ bit) for i in range(size)])  11.8 us
    pallas_call x1, Pallas kernels, transform(): pl.pallas_call(functools.partial(transform_kernel, came, n_orb, orbitals,...  3.64 us
    pallas_call x1, Pallas kernels, pack(): pl.pallas_call(functools.partial(pack_kernel, n_pair), out_shape=[pltpu.V...  1.26 us
  transfers between devices with their start and end apart: 15, of which 6 were waited for; matrix products, arithmetic and copies ran while one was open for 0% of the time, Pallas kernels for 0%

profile of v18, /device:TPU:0, one launch (start us, length us, event | category | flops | bytes accessed | tf_op | source)
XLA Modules:
  0.0 33.2 jit_solution(10334172149765932506)
XLA Ops:
  0.7 1.3 %pack.1 = (bf16[656,128]{1,0:T(8,128)(2,1)S(1)}, bf16[656,128]{1,0:T(8,128)(2,1)S(1)}, bf16[656,128]{1,0:T(8,128)(2,1)S(1)}, bf16[656,128]{1,0:T(8,128)(2,1)S(1)}) custom-call(bf16[2,8,4096]{2,1,0:T(8,128)(2,1)} %integrals.1, s32[2]{0:T(128)} %mu.1, s32[2]{0:T(128)} %nu.1, s32[1]{0:T(128)S(6)} %copy.7.counts, bf16[128,512]{1,0:T(8,128)(2,1)} %coeff.1), custom_call_target="tpu_custom_call" | custom-call | tf_op jit(solution)/shard_map/pack/pallas_call | solution.py:71
  1.9 3.1 %collective-permute-start = (bf16[656,128]{1,0:T(8,128)(2,1)S(1)}, bf16[656,128]{1,0:T(8,128)(2,1)S(1)}, u32[]{:S(2)}, u32[]{:S(2)}) collective-permute-start(bf16[656,128]{1,0:T(8,128)(2,1)S(1)} %get-tuple-element.19), channel_id=1, source_target_pairs={{0,4},{4,0},{8,12},{12,8},{1,5},{5,1},{9,13},{13,9},{2,6},{6,2},{1... | collective-permute-start | bytes 503816 | tf_op jit(solution)/shard_map/ppermute | solution.py:182
  5.0 2.6 %collective-permute-start.3 = (bf16[656,128]{1,0:T(8,128)(2,1)S(1)}, bf16[656,128]{1,0:T(8,128)(2,1)S(1)}, u32[]{:S(2)}, u32[]{:S(2)}) collective-permute-start(bf16[656,128]{1,0:T(8,128)(2,1)S(1)} %get-tuple-element.24), channel_id=1, source_target_pairs={{0,8},{4,12},{8,0},{12,4},{1,9},{5,13},{9,1},{13,5},{2,10},{6,14},... | collective-permute-start | bytes 503816 | tf_op jit(solution)/shard_map/ppermute | solution.py:182
  7.6 0.0 collective-permute-start.1
  7.6 4.3 %collective-permute-done.refs_1_ = bf16[656,128]{1,0:T(8,128)(2,1)S(1)} collective-permute-done((bf16[656,128]{1,0:T(8,128)(2,1)S(1)}, bf16[656,128]{1,0:T(8,128)(2,1)S(1)}, u32[]{:S(2)}, u32[]{:S(2)}) %collective-permute-start) | collective-permute-done | bytes 167968 | tf_op jit(solution)/shard_map/ppermute | solution.py:182
  11.9 1.7 %collective-permute-start.2 = (bf16[656,128]{1,0:T(8,128)(2,1)S(1)}, bf16[656,128]{1,0:T(8,128)(2,1)S(1)}, u32[]{:S(2)}, u32[]{:S(2)}) collective-permute-start(bf16[656,128]{1,0:T(8,128)(2,1)S(1)} %collective-permute-done.refs_1_), channel_id=1, source_target_pairs={{0,2},{1,3},{2,0},{3,1},{4,6},{5,7},{6,4},{7,5},{8,10},{9,11},{10,... | collective-permute-start | bytes 503816 | tf_op jit(solution)/shard_map/ppermute | solution.py:182
  13.6 0.3 collective-permute-start.4
  13.9 6.4 %collective-permute-done.3.refs_2_ = bf16[656,128]{1,0:T(8,128)(2,1)S(1)} collective-permute-done((bf16[656,128]{1,0:T(8,128)(2,1)S(1)}, bf16[656,128]{1,0:T(8,128)(2,1)S(1)}, u32[]{:S(2)}, u32[]{:S(2)}) %collective-permute-start.3) | collective-permute-done | bytes 167968 | tf_op jit(solution)/shard_map/ppermute | solution.py:182
  20.3 1.5 %collective-permute-start.5 = (bf16[656,128]{1,0:T(8,128)(2,1)S(1)}, bf16[656,128]{1,0:T(8,128)(2,1)S(1)}, u32[]{:S(2)}, u32[]{:S(2)}) collective-permute-start(bf16[656,128]{1,0:T(8,128)(2,1)S(1)} %collective-permute-done.3.refs_2_), channel_id=1, source_target_pairs={{0,2},{1,3},{2,0},{3,1},{4,6},{5,7},{6,4},{7,5},{8,10},{9,11},{10,... | collective-permute-start | bytes 503816 | tf_op jit(solution)/shard_map/ppermute | solution.py:182
  21.8 0.0 collective-permute-done.1.refs_3_
  21.8 0.0 collective-permute-done.2.refs_5_
  21.8 0.5 %collective-permute-start.6 = (bf16[656,128]{1,0:T(8,128)(2,1)S(1)}, bf16[656,128]{1,0:T(8,128)(2,1)S(1)}, u32[]{:S(2)}, u32[]{:S(2)}) collective-permute-start(bf16[656,128]{1,0:T(8,128)(2,1)S(1)} %collective-permute-done.1.refs_3_), channel_id=1, source_target_pairs={{0,2},{1,3},{2,0},{3,1},{4,6},{5,7},{6,4},{7,5},{8,10},{9,11},{10,... | collective-permute-start | bytes 503816 | tf_op jit(solution)/shard_map/ppermute | solution.py:182
  22.4 0.0 collective-permute-start.7
  22.4 0.5 %collective-permute-start.8 = (bf16[656,128]{1,0:T(8,128)(2,1)S(1)}, bf16[656,128]{1,0:T(8,128)(2,1)S(1)}, u32[]{:S(2)}, u32[]{:S(2)}) collective-permute-start(bf16[656,128]{1,0:T(8,128)(2,1)S(1)} %collective-permute-done.refs_1_), channel_id=1, source_target_pairs={{0,1},{1,0},{2,3},{3,2},{4,5},{5,4},{6,7},{7,6},{8,9},{9,8},{10,11... | collective-permute-start | bytes 503816 | tf_op jit(solution)/shard_map/ppermute | solution.py:182
  22.9 0.0 collective-permute-done.4.refs_4_
  22.9 3.2 %collective-permute-done.5.refs_6_ = bf16[656,128]{1,0:T(8,128)(2,1)S(1)} collective-permute-done((bf16[656,128]{1,0:T(8,128)(2,1)S(1)}, bf16[656,128]{1,0:T(8,128)(2,1)S(1)}, u32[]{:S(2)}, u32[]{:S(2)}) %collective-permute-start.5) | collective-permute-done | bytes 167968 | tf_op jit(solution)/shard_map/ppermute | solution.py:182
  26.1 0.0 collective-permute-start.9
  26.1 0.5 %collective-permute-start.10 = (bf16[656,128]{1,0:T(8,128)(2,1)S(1)}, bf16[656,128]{1,0:T(8,128)(2,1)S(1)}, u32[]{:S(2)}, u32[]{:S(2)}) collective-permute-start(bf16[656,128]{1,0:T(8,128)(2,1)S(1)} %collective-permute-done.1.refs_3_), channel_id=1, source_target_pairs={{0,1},{1,0},{2,3},{3,2},{4,5},{5,4},{6,7},{7,6},{8,9},{9,8},{10,11... | collective-permute-start | bytes 503816 | tf_op jit(solution)/shard_map/ppermute | solution.py:182
  26.6 0.0 collective-permute-done.7.refs_8_
  26.6 0.0 collective-permute-start.11
  26.6 0.0 collective-permute-done.8.refs_9_
  26.6 0.5 %collective-permute-start.12 = (bf16[656,128]{1,0:T(8,128)(2,1)S(1)}, bf16[656,128]{1,0:T(8,128)(2,1)S(1)}, u32[]{:S(2)}, u32[]{:S(2)}) collective-permute-start(bf16[656,128]{1,0:T(8,128)(2,1)S(1)} %collective-permute-done.2.refs_5_), channel_id=1, source_target_pairs={{0,1},{1,0},{2,3},{3,2},{4,5},{5,4},{6,7},{7,6},{8,9},{9,8},{10,11... | collective-permute-start | bytes 503816 | tf_op jit(solution)/shard_map/ppermute | solution.py:182
  27.1 0.8 %collective-permute-done.6.refs_7_ = bf16[656,128]{1,0:T(8,128)(2,1)S(1)} collective-permute-done((bf16[656,128]{1,0:T(8,128)(2,1)S(1)}, bf16[656,128]{1,0:T(8,128)(2,1)S(1)}, u32[]{:S(2)}, u32[]{:S(2)}) %collective-permute-start.6) | collective-permute-done | bytes 167968 | tf_op jit(solution)/shard_map/ppermute | solution.py:182
  27.9 0.0 collective-permute-start.13
  27.9 0.0 collective-permute-done.9.refs_10_
  27.9 0.5 %collective-permute-start.14 = (bf16[656,128]{1,0:T(8,128)(2,1)S(1)}, bf16[656,128]{1,0:T(8,128)(2,1)S(1)}, u32[]{:S(2)}, u32[]{:S(2)}) collective-permute-start(bf16[656,128]{1,0:T(8,128)(2,1)S(1)} %collective-permute-done.6.refs_7_), channel_id=1, source_target_pairs={{0,1},{1,0},{2,3},{3,2},{4,5},{5,4},{6,7},{7,6},{8,9},{9,8},{10,11... | collective-permute-start | bytes 503816 | tf_op jit(solution)/shard_map/ppermute | solution.py:182
  28.4 0.0 collective-permute-done.10.refs_11_
  28.4 0.0 collective-permute-done.11.refs_12_
  28.4 0.0 collective-permute-done.12.refs_13_
  28.4 0.9 %collective-permute-done.13.refs_14_ = bf16[656,128]{1,0:T(8,128)(2,1)S(1)} collective-permute-done((bf16[656,128]{1,0:T(8,128)(2,1)S(1)}, bf16[656,128]{1,0:T(8,128)(2,1)S(1)}, u32[]{:S(2)}, u32[]{:S(2)}) %collective-permute-start.13) | collective-permute-done | bytes 167968 | tf_op jit(solution)/shard_map/ppermute | solution.py:182
  29.3 0.2 collective-permute-done.14.refs_15_
  29.5 3.6 %transform.1 = f32[1024,128]{1,0:T(8,128)} custom-call(bf16[656,128]{1,0:T(8,128)(2,1)S(1)} %get-tuple-element.22.refs_0_, bf16[656,128]{1,0:T(8,128)(2,1)S(1)} %collective-permute-done.refs_1_, bf16[656,128]{1,0:T(8,128)(2,1)S(1)} %collective-permute-done.3.refs_2_, bf16[656,128]{1,0:T(8,128)(2,1)S(1)} %collective-permute-done.1.refs_3_, ...), custom_call_target="tpu_custom_call" | custom-call | tf_op jit(solution)/shard_map/transform/pallas_call | solution.py:163
Async XLA Ops:
  1.9 10.0 %collective-permute-start = (bf16[656,128]{1,0:T(8,128)(2,1)S(1)}, bf16[656,128]{1,0:T(8,128)(2,1)S(1)}, u32[]{:S(2)}, u32[]{:S(2)}) collective-permute-start(bf16[656,128]{1,0:T(8,128)(2,1)S(1)} %get-tuple-element.19), channel_id=1, source_target_pairs={{0,4},{4,0},{8,12},{12,8},{1,5},{5,1},{9,13},{13,9},{2,6},{6,2},{1... | collective-permute-start | bytes 503816 | tf_op jit(solution)/shard_map/ppermute | solution.py:182
  5.0 15.3 %collective-permute-start.3 = (bf16[656,128]{1,0:T(8,128)(2,1)S(1)}, bf16[656,128]{1,0:T(8,128)(2,1)S(1)}, u32[]{:S(2)}, u32[]{:S(2)}) collective-permute-start(bf16[656,128]{1,0:T(8,128)(2,1)S(1)} %get-tuple-element.24), channel_id=1, source_target_pairs={{0,8},{4,12},{8,0},{12,4},{1,9},{5,13},{9,1},{13,5},{2,10},{6,14},... | collective-permute-start | bytes 503816 | tf_op jit(solution)/shard_map/ppermute | solution.py:182
  7.6 14.2 %collective-permute-start.1 = (bf16[656,128]{1,0:T(8,128)(2,1)S(1)}, bf16[656,128]{1,0:T(8,128)(2,1)S(1)}, u32[]{:S(2)}, u32[]{:S(2)}) collective-permute-start(bf16[656,128]{1,0:T(8,128)(2,1)S(1)} %get-tuple-element.20), channel_id=1, source_target_pairs={{0,12},{4,8},{8,4},{12,0},{1,13},{5,9},{9,5},{13,1},{2,14},{6,10},... | collective-permute-start | bytes 503816 | tf_op jit(solution)/shard_map/ppermute | solution.py:182
  11.9 9.9 %collective-permute-start.2 = (bf16[656,128]{1,0:T(8,128)(2,1)S(1)}, bf16[656,128]{1,0:T(8,128)(2,1)S(1)}, u32[]{:S(2)}, u32[]{:S(2)}) collective-permute-start(bf16[656,128]{1,0:T(8,128)(2,1)S(1)} %collective-permute-done.refs_1_), channel_id=1, source_target_pairs={{0,2},{1,3},{2,0},{3,1},{4,6},{5,7},{6,4},{7,5},{8,10},{9,11},{10,... | collective-permute-start | bytes 503816 | tf_op jit(solution)/shard_map/ppermute | solution.py:182
  13.6 9.3 %collective-permute-start.4 = (bf16[656,128]{1,0:T(8,128)(2,1)S(1)}, bf16[656,128]{1,0:T(8,128)(2,1)S(1)}, u32[]{:S(2)}, u32[]{:S(2)}) collective-permute-start(bf16[656,128]{1,0:T(8,128)(2,1)S(1)} %get-tuple-element.22.refs_0_), channel_id=1, source_target_pairs={{0,2},{1,3},{2,0},{3,1},{4,6},{5,7},{6,4},{7,5},{8,10},{9,11},{10,... | collective-permute-start | bytes 503816 | tf_op jit(solution)/shard_map/ppermute | solution.py:182
  20.3 5.8 %collective-permute-start.5 = (bf16[656,128]{1,0:T(8,128)(2,1)S(1)}, bf16[656,128]{1,0:T(8,128)(2,1)S(1)}, u32[]{:S(2)}, u32[]{:S(2)}) collective-permute-start(bf16[656,128]{1,0:T(8,128)(2,1)S(1)} %collective-permute-done.3.refs_2_), channel_id=1, source_target_pairs={{0,2},{1,3},{2,0},{3,1},{4,6},{5,7},{6,4},{7,5},{8,10},{9,11},{10,... | collective-permute-start | bytes 503816 | tf_op jit(solution)/shard_map/ppermute | solution.py:182
  21.8 6.1 %collective-permute-start.6 = (bf16[656,128]{1,0:T(8,128)(2,1)S(1)}, bf16[656,128]{1,0:T(8,128)(2,1)S(1)}, u32[]{:S(2)}, u32[]{:S(2)}) collective-permute-start(bf16[656,128]{1,0:T(8,128)(2,1)S(1)} %collective-permute-done.1.refs_3_), channel_id=1, source_target_pairs={{0,2},{1,3},{2,0},{3,1},{4,6},{5,7},{6,4},{7,5},{8,10},{9,11},{10,... | collective-permute-start | bytes 503816 | tf_op jit(solution)/shard_map/ppermute | solution.py:182
  22.4 4.2 %collective-permute-start.7 = (bf16[656,128]{1,0:T(8,128)(2,1)S(1)}, bf16[656,128]{1,0:T(8,128)(2,1)S(1)}, u32[]{:S(2)}, u32[]{:S(2)}) collective-permute-start(bf16[656,128]{1,0:T(8,128)(2,1)S(1)} %get-tuple-element.22.refs_0_), channel_id=1, source_target_pairs={{0,1},{1,0},{2,3},{3,2},{4,5},{5,4},{6,7},{7,6},{8,9},{9,8},{10,11... | collective-permute-start | bytes 503816 | tf_op jit(solution)/shard_map/ppermute | solution.py:182
  22.4 4.2 %collective-permute-start.8 = (bf16[656,128]{1,0:T(8,128)(2,1)S(1)}, bf16[656,128]{1,0:T(8,128)(2,1)S(1)}, u32[]{:S(2)}, u32[]{:S(2)}) collective-permute-start(bf16[656,128]{1,0:T(8,128)(2,1)S(1)} %collective-permute-done.refs_1_), channel_id=1, source_target_pairs={{0,1},{1,0},{2,3},{3,2},{4,5},{5,4},{6,7},{7,6},{8,9},{9,8},{10,11... | collective-permute-start | bytes 503816 | tf_op jit(solution)/shard_map/ppermute | solution.py:182
  26.1 1.8 %collective-permute-start.9 = (bf16[656,128]{1,0:T(8,128)(2,1)S(1)}, bf16[656,128]{1,0:T(8,128)(2,1)S(1)}, u32[]{:S(2)}, u32[]{:S(2)}) collective-permute-start(bf16[656,128]{1,0:T(8,128)(2,1)S(1)} %collective-permute-done.3.refs_2_), channel_id=1, source_target_pairs={{0,1},{1,0},{2,3},{3,2},{4,5},{5,4},{6,7},{7,6},{8,9},{9,8},{10,11... | collective-permute-start | bytes 503816 | tf_op jit(solution)/shard_map/ppermute | solution.py:182
  26.1 2.3 %collective-permute-start.10 = (bf16[656,128]{1,0:T(8,128)(2,1)S(1)}, bf16[656,128]{1,0:T(8,128)(2,1)S(1)}, u32[]{:S(2)}, u32[]{:S(2)}) collective-permute-start(bf16[656,128]{1,0:T(8,128)(2,1)S(1)} %collective-permute-done.1.refs_3_), channel_id=1, source_target_pairs={{0,1},{1,0},{2,3},{3,2},{4,5},{5,4},{6,7},{7,6},{8,9},{9,8},{10,11... | collective-permute-start | bytes 503816 | tf_op jit(solution)/shard_map/ppermute | solution.py:182
  26.6 1.8 %collective-permute-start.11 = (bf16[656,128]{1,0:T(8,128)(2,1)S(1)}, bf16[656,128]{1,0:T(8,128)(2,1)S(1)}, u32[]{:S(2)}, u32[]{:S(2)}) collective-permute-start(bf16[656,128]{1,0:T(8,128)(2,1)S(1)} %collective-permute-done.4.refs_4_), channel_id=1, source_target_pairs={{0,1},{1,0},{2,3},{3,2},{4,5},{5,4},{6,7},{7,6},{8,9},{9,8},{10,11... | collective-permute-start | bytes 503816 | tf_op jit(solution)/shard_map/ppermute | solution.py:182
  26.6 1.8 %collective-permute-start.12 = (bf16[656,128]{1,0:T(8,128)(2,1)S(1)}, bf16[656,128]{1,0:T(8,128)(2,1)S(1)}, u32[]{:S(2)}, u32[]{:S(2)}) collective-permute-start(bf16[656,128]{1,0:T(8,128)(2,1)S(1)} %collective-permute-done.2.refs_5_), channel_id=1, source_target_pairs={{0,1},{1,0},{2,3},{3,2},{4,5},{5,4},{6,7},{7,6},{8,9},{9,8},{10,11... | collective-permute-start | bytes 503816 | tf_op jit(solution)/shard_map/ppermute | solution.py:182
  27.9 1.4 %collective-permute-start.13 = (bf16[656,128]{1,0:T(8,128)(2,1)S(1)}, bf16[656,128]{1,0:T(8,128)(2,1)S(1)}, u32[]{:S(2)}, u32[]{:S(2)}) collective-permute-start(bf16[656,128]{1,0:T(8,128)(2,1)S(1)} %collective-permute-done.5.refs_6_), channel_id=1, source_target_pairs={{0,1},{1,0},{2,3},{3,2},{4,5},{5,4},{6,7},{7,6},{8,9},{9,8},{10,11... | collective-permute-start | bytes 503816 | tf_op jit(solution)/shard_map/ppermute | solution.py:182
  27.9 1.6 %collective-permute-start.14 = (bf16[656,128]{1,0:T(8,128)(2,1)S(1)}, bf16[656,128]{1,0:T(8,128)(2,1)S(1)}, u32[]{:S(2)}, u32[]{:S(2)}) collective-permute-start(bf16[656,128]{1,0:T(8,128)(2,1)S(1)} %collective-permute-done.6.refs_7_), channel_id=1, source_target_pairs={{0,1},{1,0},{2,3},{3,2},{4,5},{5,4},{6,7},{7,6},{8,9},{9,8},{10,11... | collective-permute-start | bytes 503816 | tf_op jit(solution)/shard_map/ppermute | solution.py:182

commit v19 on v16

--- a/solution.py
+++ b/solution.py
@@ -194,7 +194,7 @@
         across.append(flip(last, "orb", n_orb, 2))
         first = list(lax.optimization_barrier((lines[0], lines[1], last)))[:2]
         swapped = [flip(piece, "orb", n_orb, 1) for piece in first]
-        later = list(lax.optimization_barrier((lines[2], last, *across[:3]))) + across[3:]
+        later = [*lax.optimization_barrier((lines[2], last)), *lax.optimization_barrier(tuple(across[:3])), across[3]]
         swapped += [flip(piece, "orb", n_orb, 1) for piece in later]
         pieces = first + later + swapped
         came = [(0, 0), (1, 0), (2, 0), (3, 0), (0, 2), (1, 2), (2, 2), (3, 2)]

time: 33.2 us -> 34.6 us (1.042)
  waiting for transfers between devices: 15.8 us -> 17.7 us
  starting transfers between devices: 11.8 us -> 11.3 us
    ppermute x15, waiting for transfers between devices: 15.8 us -> 17.7 us  [flip(): return lax.ppermute(array, axis, [(i, i ^ bit) for i in range(size)])]
    ppermute x15, starting transfers between devices: 11.8 us -> 11.3 us  [flip(): return lax.ppermute(array, axis, [(i, i ^ bit) for i in range(size)])]
where the time goes in v19:
time: 34.6 us; the launch traced here: 34.5 us
  waiting for transfers between devices  17.7 us (51%)
  starting transfers between devices  11.3 us (33%)
  Pallas kernels  4.82 us (14%)
  between operations  0.68 us (2%)
    ppermute x15, waiting for transfers between devices, flip(): return lax.ppermute(array, axis, [(i, i ^ bit) for i in range(size)])  17.7 us
    ppermute x15, starting transfers between devices, flip(): return lax.ppermute(array, axis, [(i, i ^ bit) for i in range(size)])  11.3 us
    pallas_call x1, Pallas kernels, transform(): pl.pallas_call(functools.partial(transform_kernel, came, n_orb, orbitals,...  3.63 us
    pallas_call x1, Pallas kernels, pack(): pl.pallas_call(functools.partial(pack_kernel, n_pair), out_shape=[pltpu.V...  1.19 us
  transfers between devices with their start and end apart: 15, of which 6 were waited for; matrix products, arithmetic and copies ran while one was open for 0% of the time, Pallas kernels for 0%

profile of v19, /device:TPU:0, one launch (start us, length us, event | category | flops | bytes accessed | tf_op | source)
XLA Modules:
  0.0 34.5 jit_solution(15972806403913665143)
XLA Ops:
  0.7 1.2 %pack.1 = (bf16[656,128]{1,0:T(8,128)(2,1)S(1)}, bf16[656,128]{1,0:T(8,128)(2,1)S(1)}, bf16[656,128]{1,0:T(8,128)(2,1)S(1)}, bf16[656,128]{1,0:T(8,128)(2,1)S(1)}) custom-call(bf16[2,8,4096]{2,1,0:T(8,128)(2,1)} %integrals.1, s32[2]{0:T(128)} %mu.1, s32[2]{0:T(128)} %nu.1, s32[1]{0:T(128)S(6)} %copy.7.counts, bf16[128,512]{1,0:T(8,128)(2,1)} %coeff.1), custom_call_target="tpu_custom_call" | custom-call | tf_op jit(solution)/shard_map/pack/pallas_call | solution.py:71
  1.9 3.1 %collective-permute-start = (bf16[656,128]{1,0:T(8,128)(2,1)S(1)}, bf16[656,128]{1,0:T(8,128)(2,1)S(1)}, u32[]{:S(2)}, u32[]{:S(2)}) collective-permute-start(bf16[656,128]{1,0:T(8,128)(2,1)S(1)} %get-tuple-element.19), channel_id=1, source_target_pairs={{0,4},{4,0},{8,12},{12,8},{1,5},{5,1},{9,13},{13,9},{2,6},{6,2},{1... | collective-permute-start | bytes 503816 | tf_op jit(solution)/shard_map/ppermute | solution.py:182
  4.9 2.6 %collective-permute-start.3 = (bf16[656,128]{1,0:T(8,128)(2,1)S(1)}, bf16[656,128]{1,0:T(8,128)(2,1)S(1)}, u32[]{:S(2)}, u32[]{:S(2)}) collective-permute-start(bf16[656,128]{1,0:T(8,128)(2,1)S(1)} %get-tuple-element.24), channel_id=1, source_target_pairs={{0,8},{4,12},{8,0},{12,4},{1,9},{5,13},{9,1},{13,5},{2,10},{6,14},... | collective-permute-start | bytes 503816 | tf_op jit(solution)/shard_map/ppermute | solution.py:182
  7.5 0.0 collective-permute-start.1
  7.5 4.3 %collective-permute-done.refs_1_ = bf16[656,128]{1,0:T(8,128)(2,1)S(1)} collective-permute-done((bf16[656,128]{1,0:T(8,128)(2,1)S(1)}, bf16[656,128]{1,0:T(8,128)(2,1)S(1)}, u32[]{:S(2)}, u32[]{:S(2)}) %collective-permute-start) | collective-permute-done | bytes 167968 | tf_op jit(solution)/shard_map/ppermute | solution.py:182
  11.8 1.7 %collective-permute-start.2 = (bf16[656,128]{1,0:T(8,128)(2,1)S(1)}, bf16[656,128]{1,0:T(8,128)(2,1)S(1)}, u32[]{:S(2)}, u32[]{:S(2)}) collective-permute-start(bf16[656,128]{1,0:T(8,128)(2,1)S(1)} %collective-permute-done.refs_1_), channel_id=1, source_target_pairs={{0,2},{1,3},{2,0},{3,1},{4,6},{5,7},{6,4},{7,5},{8,10},{9,11},{10,... | collective-permute-start | bytes 503816 | tf_op jit(solution)/shard_map/ppermute | solution.py:182
  13.5 0.3 collective-permute-start.4
  13.8 6.4 %collective-permute-done.3.refs_2_ = bf16[656,128]{1,0:T(8,128)(2,1)S(1)} collective-permute-done((bf16[656,128]{1,0:T(8,128)(2,1)S(1)}, bf16[656,128]{1,0:T(8,128)(2,1)S(1)}, u32[]{:S(2)}, u32[]{:S(2)}) %collective-permute-start.3) | collective-permute-done | bytes 167968 | tf_op jit(solution)/shard_map/ppermute | solution.py:182
  20.3 1.5 %collective-permute-start.5 = (bf16[656,128]{1,0:T(8,128)(2,1)S(1)}, bf16[656,128]{1,0:T(8,128)(2,1)S(1)}, u32[]{:S(2)}, u32[]{:S(2)}) collective-permute-start(bf16[656,128]{1,0:T(8,128)(2,1)S(1)} %collective-permute-done.3.refs_2_), channel_id=1, source_target_pairs={{0,2},{1,3},{2,0},{3,1},{4,6},{5,7},{6,4},{7,5},{8,10},{9,11},{10,... | collective-permute-start | bytes 503816 | tf_op jit(solution)/shard_map/ppermute | solution.py:182
  21.7 0.0 collective-permute-done.1.refs_3_
  21.7 0.0 collective-permute-done.2.refs_5_
  21.7 0.0 collective-permute-start.7
  21.8 0.5 %collective-permute-start.8 = (bf16[656,128]{1,0:T(8,128)(2,1)S(1)}, bf16[656,128]{1,0:T(8,128)(2,1)S(1)}, u32[]{:S(2)}, u32[]{:S(2)}) collective-permute-start(bf16[656,128]{1,0:T(8,128)(2,1)S(1)} %collective-permute-done.refs_1_), channel_id=1, source_target_pairs={{0,1},{1,0},{2,3},{3,2},{4,5},{5,4},{6,7},{7,6},{8,9},{9,8},{10,11... | collective-permute-start | bytes 503816 | tf_op jit(solution)/shard_map/ppermute | solution.py:182
  22.3 0.5 %collective-permute-start.6 = (bf16[656,128]{1,0:T(8,128)(2,1)S(1)}, bf16[656,128]{1,0:T(8,128)(2,1)S(1)}, u32[]{:S(2)}, u32[]{:S(2)}) collective-permute-start(bf16[656,128]{1,0:T(8,128)(2,1)S(1)} %collective-permute-done.1.refs_3_), channel_id=1, source_target_pairs={{0,2},{1,3},{2,0},{3,1},{4,6},{5,7},{6,4},{7,5},{8,10},{9,11},{10,... | collective-permute-start | bytes 503816 | tf_op jit(solution)/shard_map/ppermute | solution.py:182
  22.8 0.0 collective-permute-done.4.refs_4_
  22.8 0.0 collective-permute-start.9
  22.8 3.5 %collective-permute-done.5.refs_6_ = bf16[656,128]{1,0:T(8,128)(2,1)S(1)} collective-permute-done((bf16[656,128]{1,0:T(8,128)(2,1)S(1)}, bf16[656,128]{1,0:T(8,128)(2,1)S(1)}, u32[]{:S(2)}, u32[]{:S(2)}) %collective-permute-start.5) | collective-permute-done | bytes 167968 | tf_op jit(solution)/shard_map/ppermute | solution.py:182
  26.3 0.0 collective-permute-start.10
  26.3 0.0 collective-permute-done.7.refs_8_
  26.3 0.5 %collective-permute-start.11 = (bf16[656,128]{1,0:T(8,128)(2,1)S(1)}, bf16[656,128]{1,0:T(8,128)(2,1)S(1)}, u32[]{:S(2)}, u32[]{:S(2)}) collective-permute-start(bf16[656,128]{1,0:T(8,128)(2,1)S(1)} %collective-permute-done.4.refs_4_), channel_id=1, source_target_pairs={{0,1},{1,0},{2,3},{3,2},{4,5},{5,4},{6,7},{7,6},{8,9},{9,8},{10,11... | collective-permute-start | bytes 503816 | tf_op jit(solution)/shard_map/ppermute | solution.py:182
  26.8 0.0 collective-permute-done.8.refs_9_
  26.8 0.1 collective-permute-start.12
  26.9 2.3 %collective-permute-done.6.refs_7_ = bf16[656,128]{1,0:T(8,128)(2,1)S(1)} collective-permute-done((bf16[656,128]{1,0:T(8,128)(2,1)S(1)}, bf16[656,128]{1,0:T(8,128)(2,1)S(1)}, u32[]{:S(2)}, u32[]{:S(2)}) %collective-permute-start.6) | collective-permute-done | bytes 167968 | tf_op jit(solution)/shard_map/ppermute | solution.py:182
  29.2 0.0 collective-permute-start.13
  29.2 0.0 collective-permute-done.9.refs_10_
  29.2 0.5 %collective-permute-start.14 = (bf16[656,128]{1,0:T(8,128)(2,1)S(1)}, bf16[656,128]{1,0:T(8,128)(2,1)S(1)}, u32[]{:S(2)}, u32[]{:S(2)}) collective-permute-start(bf16[656,128]{1,0:T(8,128)(2,1)S(1)} %collective-permute-done.6.refs_7_), channel_id=1, source_target_pairs={{0,1},{1,0},{2,3},{3,2},{4,5},{5,4},{6,7},{7,6},{8,9},{9,8},{10,11... | collective-permute-start | bytes 503816 | tf_op jit(solution)/shard_map/ppermute | solution.py:182
  29.7 0.0 collective-permute-done.10.refs_11_
  29.7 0.0 collective-permute-done.11.refs_12_
  29.7 0.0 collective-permute-done.12.refs_13_
  29.7 0.9 %collective-permute-done.13.refs_14_ = bf16[656,128]{1,0:T(8,128)(2,1)S(1)} collective-permute-done((bf16[656,128]{1,0:T(8,128)(2,1)S(1)}, bf16[656,128]{1,0:T(8,128)(2,1)S(1)}, u32[]{:S(2)}, u32[]{:S(2)}) %collective-permute-start.13) | collective-permute-done | bytes 167968 | tf_op jit(solution)/shard_map/ppermute | solution.py:182
  30.6 0.2 collective-permute-done.14.refs_15_
  30.9 3.6 %transform.1 = f32[1024,128]{1,0:T(8,128)} custom-call(bf16[656,128]{1,0:T(8,128)(2,1)S(1)} %get-tuple-element.22.refs_0_, bf16[656,128]{1,0:T(8,128)(2,1)S(1)} %collective-permute-done.refs_1_, bf16[656,128]{1,0:T(8,128)(2,1)S(1)} %collective-permute-done.3.refs_2_, bf16[656,128]{1,0:T(8,128)(2,1)S(1)} %collective-permute-done.1.refs_3_, ...), custom_call_target="tpu_custom_call" | custom-call | tf_op jit(solution)/shard_map/transform/pallas_call | solution.py:163
Async XLA Ops:
  1.9 10.0 %collective-permute-start = (bf16[656,128]{1,0:T(8,128)(2,1)S(1)}, bf16[656,128]{1,0:T(8,128)(2,1)S(1)}, u32[]{:S(2)}, u32[]{:S(2)}) collective-permute-start(bf16[656,128]{1,0:T(8,128)(2,1)S(1)} %get-tuple-element.19), channel_id=1, source_target_pairs={{0,4},{4,0},{8,12},{12,8},{1,5},{5,1},{9,13},{13,9},{2,6},{6,2},{1... | collective-permute-start | bytes 503816 | tf_op jit(solution)/shard_map/ppermute | solution.py:182
  4.9 15.3 %collective-permute-start.3 = (bf16[656,128]{1,0:T(8,128)(2,1)S(1)}, bf16[656,128]{1,0:T(8,128)(2,1)S(1)}, u32[]{:S(2)}, u32[]{:S(2)}) collective-permute-start(bf16[656,128]{1,0:T(8,128)(2,1)S(1)} %get-tuple-element.24), channel_id=1, source_target_pairs={{0,8},{4,12},{8,0},{12,4},{1,9},{5,13},{9,1},{13,5},{2,10},{6,14},... | collective-permute-start | bytes 503816 | tf_op jit(solution)/shard_map/ppermute | solution.py:182
  7.5 14.2 %collective-permute-start.1 = (bf16[656,128]{1,0:T(8,128)(2,1)S(1)}, bf16[656,128]{1,0:T(8,128)(2,1)S(1)}, u32[]{:S(2)}, u32[]{:S(2)}) collective-permute-start(bf16[656,128]{1,0:T(8,128)(2,1)S(1)} %get-tuple-element.20), channel_id=1, source_target_pairs={{0,12},{4,8},{8,4},{12,0},{1,13},{5,9},{9,5},{13,1},{2,14},{6,10},... | collective-permute-start | bytes 503816 | tf_op jit(solution)/shard_map/ppermute | solution.py:182
  11.8 9.9 %collective-permute-start.2 = (bf16[656,128]{1,0:T(8,128)(2,1)S(1)}, bf16[656,128]{1,0:T(8,128)(2,1)S(1)}, u32[]{:S(2)}, u32[]{:S(2)}) collective-permute-start(bf16[656,128]{1,0:T(8,128)(2,1)S(1)} %collective-permute-done.refs_1_), channel_id=1, source_target_pairs={{0,2},{1,3},{2,0},{3,1},{4,6},{5,7},{6,4},{7,5},{8,10},{9,11},{10,... | collective-permute-start | bytes 503816 | tf_op jit(solution)/shard_map/ppermute | solution.py:182
  13.5 9.3 %collective-permute-start.4 = (bf16[656,128]{1,0:T(8,128)(2,1)S(1)}, bf16[656,128]{1,0:T(8,128)(2,1)S(1)}, u32[]{:S(2)}, u32[]{:S(2)}) collective-permute-start(bf16[656,128]{1,0:T(8,128)(2,1)S(1)} %get-tuple-element.22.refs_0_), channel_id=1, source_target_pairs={{0,2},{1,3},{2,0},{3,1},{4,6},{5,7},{6,4},{7,5},{8,10},{9,11},{10,... | collective-permute-start | bytes 503816 | tf_op jit(solution)/shard_map/ppermute | solution.py:182
  20.3 6.0 %collective-permute-start.5 = (bf16[656,128]{1,0:T(8,128)(2,1)S(1)}, bf16[656,128]{1,0:T(8,128)(2,1)S(1)}, u32[]{:S(2)}, u32[]{:S(2)}) collective-permute-start(bf16[656,128]{1,0:T(8,128)(2,1)S(1)} %collective-permute-done.3.refs_2_), channel_id=1, source_target_pairs={{0,2},{1,3},{2,0},{3,1},{4,6},{5,7},{6,4},{7,5},{8,10},{9,11},{10,... | collective-permute-start | bytes 503816 | tf_op jit(solution)/shard_map/ppermute | solution.py:182
  21.7 4.5 %collective-permute-start.7 = (bf16[656,128]{1,0:T(8,128)(2,1)S(1)}, bf16[656,128]{1,0:T(8,128)(2,1)S(1)}, u32[]{:S(2)}, u32[]{:S(2)}) collective-permute-start(bf16[656,128]{1,0:T(8,128)(2,1)S(1)} %get-tuple-element.22.refs_0_), channel_id=1, source_target_pairs={{0,1},{1,0},{2,3},{3,2},{4,5},{5,4},{6,7},{7,6},{8,9},{9,8},{10,11... | collective-permute-start | bytes 503816 | tf_op jit(solution)/shard_map/ppermute | solution.py:182
  21.8 5.0 %collective-permute-start.8 = (bf16[656,128]{1,0:T(8,128)(2,1)S(1)}, bf16[656,128]{1,0:T(8,128)(2,1)S(1)}, u32[]{:S(2)}, u32[]{:S(2)}) collective-permute-start(bf16[656,128]{1,0:T(8,128)(2,1)S(1)} %collective-permute-done.refs_1_), channel_id=1, source_target_pairs={{0,1},{1,0},{2,3},{3,2},{4,5},{5,4},{6,7},{7,6},{8,9},{9,8},{10,11... | collective-permute-start | bytes 503816 | tf_op jit(solution)/shard_map/ppermute | solution.py:182
  22.3 7.0 %collective-permute-start.6 = (bf16[656,128]{1,0:T(8,128)(2,1)S(1)}, bf16[656,128]{1,0:T(8,128)(2,1)S(1)}, u32[]{:S(2)}, u32[]{:S(2)}) collective-permute-start(bf16[656,128]{1,0:T(8,128)(2,1)S(1)} %collective-permute-done.1.refs_3_), channel_id=1, source_target_pairs={{0,2},{1,3},{2,0},{3,1},{4,6},{5,7},{6,4},{7,5},{8,10},{9,11},{10,... | collective-permute-start | bytes 503816 | tf_op jit(solution)/shard_map/ppermute | solution.py:182
  22.8 6.4 %collective-permute-start.9 = (bf16[656,128]{1,0:T(8,128)(2,1)S(1)}, bf16[656,128]{1,0:T(8,128)(2,1)S(1)}, u32[]{:S(2)}, u32[]{:S(2)}) collective-permute-start(bf16[656,128]{1,0:T(8,128)(2,1)S(1)} %collective-permute-done.3.refs_2_), channel_id=1, source_target_pairs={{0,1},{1,0},{2,3},{3,2},{4,5},{5,4},{6,7},{7,6},{8,9},{9,8},{10,11... | collective-permute-start | bytes 503816 | tf_op jit(solution)/shard_map/ppermute | solution.py:182
  26.3 3.4 %collective-permute-start.10 = (bf16[656,128]{1,0:T(8,128)(2,1)S(1)}, bf16[656,128]{1,0:T(8,128)(2,1)S(1)}, u32[]{:S(2)}, u32[]{:S(2)}) collective-permute-start(bf16[656,128]{1,0:T(8,128)(2,1)S(1)} %collective-permute-done.1.refs_3_), channel_id=1, source_target_pairs={{0,1},{1,0},{2,3},{3,2},{4,5},{5,4},{6,7},{7,6},{8,9},{9,8},{10,11... | collective-permute-start | bytes 503816 | tf_op jit(solution)/shard_map/ppermute | solution.py:182
  26.3 3.4 %collective-permute-start.11 = (bf16[656,128]{1,0:T(8,128)(2,1)S(1)}, bf16[656,128]{1,0:T(8,128)(2,1)S(1)}, u32[]{:S(2)}, u32[]{:S(2)}) collective-permute-start(bf16[656,128]{1,0:T(8,128)(2,1)S(1)} %collective-permute-done.4.refs_4_), channel_id=1, source_target_pairs={{0,1},{1,0},{2,3},{3,2},{4,5},{5,4},{6,7},{7,6},{8,9},{9,8},{10,11... | collective-permute-start | bytes 503816 | tf_op jit(solution)/shard_map/ppermute | solution.py:182
  26.8 2.9 %collective-permute-start.12 = (bf16[656,128]{1,0:T(8,128)(2,1)S(1)}, bf16[656,128]{1,0:T(8,128)(2,1)S(1)}, u32[]{:S(2)}, u32[]{:S(2)}) collective-permute-start(bf16[656,128]{1,0:T(8,128)(2,1)S(1)} %collective-permute-done.2.refs_5_), channel_id=1, source_target_pairs={{0,1},{1,0},{2,3},{3,2},{4,5},{5,4},{6,7},{7,6},{8,9},{9,8},{10,11... | collective-permute-start | bytes 503816 | tf_op jit(solution)/shard_map/ppermute | solution.py:182
  29.2 1.4 %collective-permute-start.13 = (bf16[656,128]{1,0:T(8,128)(2,1)S(1)}, bf16[656,128]{1,0:T(8,128)(2,1)S(1)}, u32[]{:S(2)}, u32[]{:S(2)}) collective-permute-start(bf16[656,128]{1,0:T(8,128)(2,1)S(1)} %collective-permute-done.5.refs_6_), channel_id=1, source_target_pairs={{0,1},{1,0},{2,3},{3,2},{4,5},{5,4},{6,7},{7,6},{8,9},{9,8},{10,11... | collective-permute-start | bytes 503816 | tf_op jit(solution)/shard_map/ppermute | solution.py:182
  29.2 1.6 %collective-permute-start.14 = (bf16[656,128]{1,0:T(8,128)(2,1)S(1)}, bf16[656,128]{1,0:T(8,128)(2,1)S(1)}, u32[]{:S(2)}, u32[]{:S(2)}) collective-permute-start(bf16[656,128]{1,0:T(8,128)(2,1)S(1)} %collective-permute-done.6.refs_7_), channel_id=1, source_target_pairs={{0,1},{1,0},{2,3},{3,2},{4,5},{5,4},{6,7},{7,6},{8,9},{9,8},{10,11... | collective-permute-start | bytes 503816 | tf_op jit(solution)/shard_map/ppermute | solution.py:182
